TPU v7x, 256 devices: a whole 4x4x8 slice. The times are simulated.
256 devices in a mesh: atom: 32 (over x, y, core), aux: 8 (over z).
Axes of the slice: x: 4, y: 4, z: 8, core: 2. Of those that a mesh axis runs over, the one named last changes fastest.
Arguments:
- integrals: bfloat16 [64, 8192, 512], P('aux', 'atom'), may hold values from -0.25 to 0.25
- coeffs: bfloat16 [8192, 2, 384], P('atom'), may hold values from -6 to 6
- metric: bfloat16 [64, 8], P('aux'), may hold values from -0.84852814 to 1.4, as said below
- atom_sizes: int32 [32, 32], P('atom'), may hold values from 1 to 16, 256 in all within a row
- pair_device: int32 [1024, 1], P('atom'), may hold values from 0 to 31; in each aligned block of 32 rows (0 to 31, 32 to 63, ...) at most 2 rows name the same one
- pair_atom: int32 [1024], P('atom'), may hold values from 0 to 31
Outputs:
- exchange_term: float32 [8192, 2, 384], P('atom', None, 'aux')
Inputs may be any that keep to these rules, and one draw needn't show every extreme that they name: `metric`: within each block of 8 rows, entry (q, p) is zero where q % 8 > p. `atom_sizes`: each row sums to 256. `pair_device`: rows 2k and 2k + 1 are the two ends of pair k, owned by the device that holds them; among the (32) rows of one device, at most 2 name the same block. A pair may name one atom twice, and a pair may repeat; every entry counts.
All inputs are finite; a program needn't handle non-finite values.
Results may differ from a plain program's by a relative error of at most 0.0061.
Values may be sent and summed in bfloat16 or wider, within the bound.
No kernel may reach another device: no remote copies, remote signals or barrier semaphores. Data moves between devices by JAX's collectives and lax.ppermute only.
A program may use at most 128 MiB of HBM per device.

v0:
```python
import math

import jax
import jax.numpy as jnp
from jax import lax
from jax.sharding import PartitionSpec as P

MAXBF = 16


def with_halo(block, sides, width):
    for axis, dim in sides:
        count = lax.axis_size(axis)
        forward = [(i, i + 1) for i in range(count - 1)]
        backward = [(target, source) for source, target in forward]
        low = lax.ppermute(
            lax.slice_in_dim(block, block.shape[dim] - width, None, axis=dim), axis, forward
        )
        high = lax.ppermute(lax.slice_in_dim(block, 0, width, axis=dim), axis, backward)
        block = jnp.concatenate([low, block, high], axis=dim)
    return block


def end_ranks(targets):
    ref_count = targets.shape[0]
    same_block = targets[:, None] == targets[None, :]
    positions = jnp.arange(ref_count)
    earlier = positions[None, :] < positions[:, None]
    return jnp.sum((same_block & earlier).astype(jnp.int32), axis=1)


def request_table(targets, ranks, atom_ids, groups, capacity):
    block_hit = targets[None, None, :] == jnp.arange(groups, dtype=jnp.int32)[:, None, None]
    slot_hit = ranks[None, None, :] == jnp.arange(capacity, dtype=jnp.int32)[None, :, None]
    chosen = jnp.where(block_hit & slot_hit, atom_ids[None, None, :] + 1, 0)
    return jnp.sum(chosen, axis=2) - 1


def lookup_small(values, atom_ids, atom_count):
    matches = atom_ids[..., None] == jnp.arange(atom_count, dtype=jnp.int32)
    return jnp.sum(jnp.where(matches, values, 0), axis=-1)


def per_device(integrals, coeffs, metric, atom_sizes, pair_device, pair_atom):
    aux_dev, bas_dev, window = integrals.shape
    occ_width = coeffs.shape[2]
    groups = lax.axis_size("atom")
    aux_count = lax.axis_size("aux")
    occ_part = occ_width // aux_count
    atom_count = atom_sizes.shape[1]
    ref_count = pair_atom.shape[0]
    pair_count = ref_count // 2
    capacity = 2 * atom_count // groups
    row_span = MAXBF
    halo_width = (window - bas_dev) // 2
    pair_scale = 1.0 / math.sqrt(2 * occ_width * aux_dev * aux_count * row_span)
    zero_half = jnp.zeros((), jnp.bfloat16)
    padded = with_halo(coeffs, (("atom", 0),), halo_width)
    half_coef = jnp.dot(
        integrals.reshape(aux_dev * bas_dev, window),
        padded.reshape(window, 2 * occ_width),
        preferred_element_type=jnp.float32,
    ).astype(jnp.bfloat16)
    fitted = lax.dot_general(
        metric,
        half_coef.reshape(aux_dev, bas_dev * 2 * occ_width),
        (((0,), (0,)), ((), ())),
        preferred_element_type=jnp.float32,
    )
    fitted = fitted.astype(jnp.bfloat16).reshape(aux_dev, bas_dev, 2 * occ_width)
    local_sizes = atom_sizes[0]
    starts = jnp.cumsum(local_sizes) - local_sizes
    targets = pair_device[:, 0]
    ranks = end_ranks(targets)
    asked = request_table(targets, ranks, pair_atom, groups, capacity)
    requested = lax.all_to_all(asked, "atom", split_axis=0, concat_axis=0, tiled=True)
    is_live = requested >= 0
    wanted = jnp.maximum(requested, 0)
    row_first = lookup_small(starts, wanted, atom_count)
    row_count = jnp.where(is_live, lookup_small(local_sizes, wanted, atom_count), 0)
    offsets = jnp.arange(row_span, dtype=jnp.int32)
    is_valid = offsets[None, None, :] < row_count[..., None]
    row_ids = jnp.minimum(row_first[..., None] + offsets, bas_dev - 1)
    sent_rows = jnp.where(is_valid[None, ..., None], jnp.take(fitted, row_ids, axis=1), zero_half)
    aux_index = lax.axis_index("aux")
    coef_part = lax.dynamic_slice_in_dim(coeffs, aux_index * occ_part, occ_part, 2).reshape(
        bas_dev, 2 * occ_part
    )
    sent_coef = jnp.where(is_valid[..., None], jnp.take(coef_part, row_ids, axis=0), zero_half)[
        None
    ]
    got_rows, got_coef = (
        lax.all_to_all(sent_rows, "atom", split_axis=1, concat_axis=1, tiled=True),
        lax.all_to_all(sent_coef, "atom", split_axis=1, concat_axis=1, tiled=True),
    )
    slot_index = targets * capacity + ranks
    flat_rows = got_rows.reshape(aux_dev, groups * capacity, row_span, 2 * occ_width)
    chosen = jnp.take(flat_rows, slot_index, axis=1).reshape(
        aux_dev, pair_count, 2, row_span, 2 * occ_width
    )
    first_rows = chosen[:, :, 0]
    second_rows = chosen[:, :, 1]
    turned = jnp.concatenate([-second_rows[..., occ_width:], second_rows[..., :occ_width]], axis=-1)
    paired = jnp.stack([second_rows, turned], axis=2)
    partial_value = jnp.einsum(
        "qpaj,qpkbj->pkab", first_rows, paired, preferred_element_type=jnp.float32
    )
    summed = lax.psum(partial_value, "aux")
    kernel = (summed * pair_scale).astype(jnp.bfloat16)
    real_k = kernel[:, 0]
    imag_k = kernel[:, 1]
    coef_flat = got_coef.reshape(groups * capacity, row_span, 2, occ_part)
    coef_pick = jnp.take(coef_flat, slot_index, axis=0).reshape(
        pair_count, 2, row_span, 2, occ_part
    )
    first_coef = coef_pick[:, 0]
    second_coef = coef_pick[:, 1]
    real_on_second = jnp.einsum(
        "pab,pbci->paci", real_k, second_coef, preferred_element_type=jnp.float32
    )
    imag_on_second = jnp.einsum(
        "pab,pbci->paci", imag_k, second_coef, preferred_element_type=jnp.float32
    )
    first_gain = jnp.stack(
        [
            real_on_second[:, :, 0] - imag_on_second[:, :, 1],
            real_on_second[:, :, 1] + imag_on_second[:, :, 0],
        ],
        axis=2,
    )
    real_on_first = jnp.einsum(
        "pab,paci->pbci", real_k, first_coef, preferred_element_type=jnp.float32
    )
    imag_on_first = jnp.einsum(
        "pab,paci->pbci", imag_k, first_coef, preferred_element_type=jnp.float32
    )
    second_gain = jnp.stack(
        [
            real_on_first[:, :, 0] + imag_on_first[:, :, 1],
            real_on_first[:, :, 1] - imag_on_first[:, :, 0],
        ],
        axis=2,
    )
    gains = jnp.stack([first_gain, second_gain], axis=1).reshape(ref_count, row_span, 2 * occ_part)
    all_sizes = lax.all_gather(atom_sizes, "atom", axis=0, tiled=True)
    all_starts = jnp.cumsum(all_sizes, axis=1) - all_sizes
    block_match = targets[:, None, None] == jnp.arange(groups, dtype=jnp.int32)[None, :, None]
    atom_match = pair_atom[:, None, None] == jnp.arange(atom_count, dtype=jnp.int32)[None, None, :]
    end_first = jnp.sum(jnp.where(block_match & atom_match, all_starts[None], 0), axis=(1, 2))
    global_rows = targets[:, None] * bas_dev + jnp.minimum(
        end_first[:, None] + offsets, bas_dev - 1
    )
    dense_term = jnp.zeros((groups * bas_dev, 2 * occ_part), jnp.float32)
    dense_term = dense_term.at[global_rows.reshape(-1)].add(
        gains.reshape(ref_count * row_span, 2 * occ_part)
    )
    mixed = lax.psum_scatter(dense_term, "atom", scatter_dimension=0, tiled=True)
    return mixed.reshape(bas_dev, 2, occ_part)


def solution(mesh):
    placed = (
        P("aux", "atom", None),
        P("atom", None, None),
        P("aux", None),
        P("atom", None),
        P("atom", None),
        P("atom"),
    )
    return jax.shard_map(
        per_device, mesh=mesh, in_specs=placed, out_specs=P("atom", None, "aux"), check_vma=False
    )
```

profile of v0, /device:TPU:1, one launch (start us, length us, event | category | flops | bytes accessed | tf_op | source)
XLA Modules:
  0.0 461.7 jit_solution(14822297524024786324)
XLA Ops:
  6.5 1.0 convert_reduce_fusion
  7.5 0.8 iota_compare_fusion.2
  9.9 8.6 %all-to-all-start = ((s32[32,1,2]{2,1,0:T(1,128)}), s32[32,1,2]{2,1,0:T(1,128)S(1)}, u32[]{:S(2)}, u32[]{:S(2)}) async-start(s32[32,1,2]{2,1,0:T(1,128)} %copy.122), calls=%async_computation | async-start | bytes 32768 | tf_op jit(solution)/shard_map/all_to_all | solution.py:76
  18.5 2.0 fusion.14
  20.5 3.5 collective-permute-start
  24.0 1.9 collective-permute-start.1
  26.0 0.7 copy.126
  27.5 1.2 constant_dynamic-slice_fusion
  29.0 0.9 select_reduce_fusion.2
  30.5 3.2 gather_fusion.2
  33.7 1.0 select_select_fusion
  34.8 7.5 %all-to-all-start.2 = ((bf16[1,32,2,16,96]{4,3,2,0,1:T(8,128)(2,1)}), bf16[1,32,2,16,96]{4,3,2,0,1:T(8,128)(2,1)S(1)}, u32[]{:S(2)}, u32[]{:S(2)}) async-start(bf16[1,32,2,16,96]{4,3,2,0,1:T(8,128)(2,1)} %select_select_fusion), calls=%async_computation.2 | async-start | bytes 524288 | tf_op jit(solution)/shard_map/all_to_all | solution.py:94
  42.3 2.0 pad_maximum_fusion.1
  44.5 3.5 fusion.2
  48.0 3.2 copy.128
  51.2 3.1 reshape.285
  54.2 2.9 convolution_convert_fusion
  57.1 11.0 %gather_fusion = bf16[1024,8,768]{2,1,0:T(8,128)(2,1)} fusion(bf16[8,256,768]{2,0,1:T(8,128)(2,1)S(1)} %bitcast.104, s32[1024]{0:T(1024)S(1)} %broadcast_clamp_fusion), kind=kCustom, calls=%fused_computation | custom fusion | bytes 25169920 | tf_op jit(solution)/shard_map/jit(_take)/gather | solution.py:84
  68.2 6.0 %select_bitcast_fusion = bf16[8,32,2,16,768]{4,0,3,2,1:T(8,128)(2,1)S(1)} fusion(bf16[32,2,16,8,768]{4,3,2,1,0:T(8,128)(2,1)} %bitcast.105, pred[32,2,16]{2,1,0:T(4,128)(4,1)S(1)} %iota_compare_fusion.1, pred[32,2,16]{2,1,0:T(4,128)(4,1)S(1)} %compare_and_fusion), kind=kLoop, calls=%fused_computation.6 | loop fusion | flops 12582912 | bytes 25167872 | tf_op jit(solution)/shard_map/jit(_where)/select_n | solution.py:84
  74.2 6.9 %copy.130 = bf16[8,32,2,16,768]{4,3,2,0,1:T(8,128)(2,1)} copy(bf16[8,32,2,16,768]{4,0,3,2,1:T(8,128)(2,1)S(1)} %select_bitcast_fusion) | data formatting | bytes 25165824 | tf_op jit(solution)/shard_map/jit(_where)/select_n | solution.py:84
  81.1 7.6 %all-to-all-start.1 = ((bf16[8,32,2,16,768]{4,3,2,0,1:T(8,128)(2,1)}), bf16[8,32,2,16,768]{4,3,2,0,1:T(8,128)(2,1)}, u32[]{:S(2)}, u32[]{:S(2)}) async-start(bf16[8,32,2,16,768]{4,3,2,0,1:T(8,128)(2,1)} %copy.130), calls=%async_computation.1 | async-start | bytes 25165824 | tf_op jit(solution)/shard_map/all_to_all | solution.py:93
  89.0 208.4 %all-gather = s32[32,1,32]{2,1,0:T(1,128)S(1)} all-gather(s32[1,1,32]{2,1,0:T(1,128)S(1)} %bitcast.119), channel_id=1, replica_groups=mesh['atom'=32,'aux'=8] {'atom'}, dimensions={0}, use_global_device_ids=true | all-gather | bytes 4224 | tf_op jit(solution)/shard_map/all_gather | solution.py:145
  297.5 0.8 select_reduce_fusion
  298.8 1.1 gather_fusion.3
  300.0 10.9 %copy.131 = bf16[8,32,2,16,768]{4,3,2,1,0:T(8,128)(2,1)} copy(bf16[8,32,2,16,768]{4,3,2,0,1:T(8,128)(2,1)} %all-to-all-done.1) | data formatting | bytes 25165824 | tf_op jit(solution)/shard_map/all_to_all | solution.py:93
  310.9 8.2 %gather_fusion.1 = bf16[32,8,16,768]{3,2,1,0:T(8,128)(2,1)} fusion(bf16[8,64,16,768]{3,2,1,0:T(8,128)(2,1)} %bitcast.106, s32[1024]{0:T(1024)S(1)} %pad_clamp_fusion), kind=kCustom, calls=%fused_computation.1 | custom fusion | bytes 12583040 | tf_op jit(solution)/shard_map/jit(_take)/gather | solution.py:98
  319.1 3.4 copy_select_fusion
  323.7 2.3 fusion.5
  325.9 28.9 %psum.7 = f32[16,2,16,16]{2,3,1,0:T(8,128)S(1)} all-reduce(f32[16,2,16,16]{2,3,1,0:T(8,128)S(1)} %fusion.5), channel_id=1, replica_groups=mesh['atom'=32,'aux'=8] {'aux'}, use_global_device_ids=true, to_apply=%region_7.8 | all-reduce | flops 8192 | bytes 65536 | tf_op jit(solution)/shard_map/psum | solution.py:108
  356.5 4.4 scatter_custom_fusion
  360.9 92.3 %reduce-scatter.2.cloned.1.call-done = f32[256,96]{1,0:T(8,128)} async-done(((f32[8192,96]{1,0:T(8,128)}), f32[256,96]{1,0:T(8,128)}) %reduce-scatter.2.cloned.1.call-update) | async-done | bytes 98320 | tf_op jit(solution)/shard_map/reduce_scatter | solution.py:157
  453.2 1.6 copy.144
  (67 shorter events, 7.0 us)
Async XLA Ops:
  6.5 37.9 %copy-start = (bf16[8,256,512]{2,1,0:T(8,128)(2,1)S(1)}, bf16[8,256,512]{2,1,0:T(8,128)(2,1)}, u32[]{:S(2)}) copy-start(bf16[8,256,512]{2,1,0:T(8,128)(2,1)} %param.6) | copy-start | bytes 6291460
  6.5 35.8 %copy-start.2 = (bf16[256,2,384]{2,1,0:T(2,128)(2,1)S(1)}, bf16[256,2,384]{2,1,0:T(2,128)(2,1)}, u32[]{:S(2)}) copy-start(bf16[256,2,384]{2,1,0:T(2,128)(2,1)} %param.7) | copy-start | bytes 1179652
  9.9 19.1 %all-to-all-start = ((s32[32,1,2]{2,1,0:T(1,128)}), s32[32,1,2]{2,1,0:T(1,128)S(1)}, u32[]{:S(2)}, u32[]{:S(2)}) async-start(s32[32,1,2]{2,1,0:T(1,128)} %copy.122), calls=%async_computation | async-start | bytes 32768 | tf_op jit(solution)/shard_map/all_to_all | solution.py:76
  20.5 21.8 %collective-permute-start = (bf16[128,2,384]{2,1,0:T(2,128)(2,1)}, bf16[128,2,384]{2,1,0:T(2,128)(2,1)S(1)}, u32[]{:S(2)}, u32[]{:S(2)}) collective-permute-start(bf16[128,2,384]{2,1,0:T(2,128)(2,1)} %get-tuple-element.17), channel_id=1, source_target_pairs={{0,8},{8,16},{16,24},{24,32},{32,40},{40,48},{48,56},{56,64},{64,7... | collective-permute-start | bytes 589832 | tf_op jit(solution)/shard_map/ppermute | solution.py:16
  24.0 18.3 %collective-permute-start.1 = (bf16[128,2,384]{2,1,0:T(2,128)(2,1)}, bf16[128,2,384]{2,1,0:T(2,128)(2,1)}, u32[]{:S(2)}, u32[]{:S(2)}) collective-permute-start(bf16[128,2,384]{2,1,0:T(2,128)(2,1)} %get-tuple-element.18), channel_id=1, source_target_pairs={{8,0},{16,8},{24,16},{32,24},{40,32},{48,40},{56,48},{64,56},{72,6... | collective-permute-start | bytes 589832 | tf_op jit(solution)/shard_map/ppermute | solution.py:19
  34.8 46.3 %all-to-all-start.2 = ((bf16[1,32,2,16,96]{4,3,2,0,1:T(8,128)(2,1)}), bf16[1,32,2,16,96]{4,3,2,0,1:T(8,128)(2,1)S(1)}, u32[]{:S(2)}, u32[]{:S(2)}) async-start(bf16[1,32,2,16,96]{4,3,2,0,1:T(8,128)(2,1)} %select_select_fusion), calls=%async_computation.2 | async-start | bytes 524288 | tf_op jit(solution)/shard_map/all_to_all | solution.py:94
  51.1 3.1 copy-start.5
  81.1 7.6 %copy-start.3 = (s32[32,1]{0,1:T(1,128)S(1)}, s32[32,1]{0,1:T(1,128)}, u32[]{:S(2)}) copy-start(s32[32,1]{0,1:T(1,128)} %param.10) | copy-start | bytes 388
  81.1 7.9 %copy-start.4 = (s32[1,32]{1,0:T(1,128)S(1)}, s32[1,32]{1,0:T(1,128)}, u32[]{:S(2)}) copy-start(s32[1,32]{1,0:T(1,128)} %param.9) | copy-start | bytes 388
  81.1 218.9 %all-to-all-start.1 = ((bf16[8,32,2,16,768]{4,3,2,0,1:T(8,128)(2,1)}), bf16[8,32,2,16,768]{4,3,2,0,1:T(8,128)(2,1)}, u32[]{:S(2)}, u32[]{:S(2)}) async-start(bf16[8,32,2,16,768]{4,3,2,0,1:T(8,128)(2,1)} %copy.130), calls=%async_computation.1 | async-start | bytes 25165824 | tf_op jit(solution)/shard_map/all_to_all | solution.py:93
  88.7 364.5 %reduce-scatter.2.cloned.1.call-start = ((), (), s32[]{:S(2)}) async-start(), calls=%async_computation.4 | async-start | bytes 4325376 | tf_op jit(solution)/shard_map/reduce_scatter | solution.py:157
  356.5 98.4 %copy-start.1 = (bf16[8,256,512]{2,1,0:T(8,128)(2,1)S(1)}, bf16[8,256,512]{2,1,0:T(8,128)(2,1)}, u32[]{:S(2)}) copy-start(bf16[8,256,512]{2,1,0:T(8,128)(2,1)} %param.6) | copy-start | bytes 6291460
Sparse Core Ops, SparseCore 0:
  361.0 92.1 reduce-scatter.1
where the time goes:
time: 463 us; the launch traced here: 462 us
  blocking collectives  237 us (51%)
  waiting for transfers between devices  92.3 us (20%)
  local copies, waits for them, and re-layouts  56.1 us (12%)
  starting transfers between devices  29.1 us (6%)
  other arithmetic  23.6 us (5%)
  between operations  13.8 us (3%)
  matrix products  9.44 us (2%)
    all_gather x1, blocking collectives, per_device(): all_sizes = lax.all_gather(atom_sizes, 'atom', axis=0, tiled=True)  208 us
    reduce_scatter x1, waiting for transfers between devices, per_device(): lax.psum_scatter(dense_term, 'atom', scatter_dimension=0, tiled=True)  92.3 us
    psum x1, blocking collectives, per_device(): summed = lax.psum(partial_value, 'aux')  28.9 us
    gather x1, local copies, waits for them, and re-layouts, per_device(): jnp.take(fitted, row_ids, axis=1)  11 us
    all_to_all x1, local copies, waits for them, and re-layouts, per_device(): lax.all_to_all(sent_rows, 'atom', split_axis=1, concat_axis=1, tiled=True)  10.9 us
  transfers between devices with their start and end apart: 6, of which 1 were waited for; matrix products, arithmetic and copies ran while one was open for 11% of the time, Pallas kernels for 0%

commit v1 on v0

v1 whole, which is shorter than its diff:
```python
import math

import jax
import jax.numpy as jnp
from jax import lax
from jax.experimental import pallas as pl
from jax.experimental.pallas import tpu as pltpu
from jax.sharding import PartitionSpec as P

MAXBF = 16
ROWBLK = 32
PACKED = ROWBLK + ROWBLK // 2
MIB = 1 << 20


def iota(shape, dim):
    return lax.broadcasted_iota(jnp.int32, shape, dim)


def dot(a, b):
    return jnp.dot(a, b, preferred_element_type=jnp.float32)


def dot_nt(a, b):
    return lax.dot_general(a, b, (((1,), (1,)), ((), ())), preferred_element_type=jnp.float32)


def dot_tn(a, b):
    return lax.dot_general(a, b, (((0,), (0,)), ((), ())), preferred_element_type=jnp.float32)


def fit_kernel(ints_ref, low_ref, own_ref, high_ref, mix_ref, out_ref, window_ref):
    @pl.when(pl.program_id(0) == 0)
    def _():
        window_ref[0:128] = low_ref[...]
        window_ref[128:384] = own_ref[...]
        window_ref[384:512] = high_ref[...]

    aux_dev = ints_ref.shape[0]
    half = dot(ints_ref[...].reshape(aux_dev * ROWBLK, ints_ref.shape[2]), window_ref[...])
    fitted = dot(mix_ref[...], half.astype(jnp.bfloat16))
    left = iota((ROWBLK // 2, 128), 1) < 64
    for p in range(aux_dev):
        rows = fitted[p * ROWBLK : (p + 1) * ROWBLK]
        for k in range(4):
            out_ref[p * 4 + k, 0, 0:ROWBLK] = rows[:, k * 128 : (k + 1) * 128].astype(jnp.bfloat16)
        for k in range(2):
            shared = rows[:, 512 + k * 128 : 640 + k * 128]
            top, bottom = shared[: ROWBLK // 2], shared[ROWBLK // 2 :]
            even = jnp.where(left, top, pltpu.roll(bottom, 64, 1))
            odd = jnp.where(left, pltpu.roll(top, 64, 1), bottom)
            out_ref[p * 4 + 2 * k, 0, ROWBLK:PACKED] = even.astype(jnp.bfloat16)
            out_ref[p * 4 + 2 * k + 1, 0, ROWBLK:PACKED] = odd.astype(jnp.bfloat16)


def pair_kernel(row_ref, got_ref, out_ref, main_ref, side_ref, first_ref, second_ref):
    groups, _, _, _ = got_ref.shape
    blocks = got_ref.shape[1]
    left = iota((ROWBLK // 2, 128), 1) < 64

    def unpack(b, carry):
        for i in range(blocks):
            base = pl.multiple_of(b * (blocks * ROWBLK) + i * ROWBLK, ROWBLK)
            main_ref[pl.ds(base, ROWBLK)] = got_ref[b, i, 0:ROWBLK].astype(jnp.float32)
            shared = got_ref[b, i, ROWBLK:PACKED].astype(jnp.float32)
            side_ref[pl.ds(base, ROWBLK // 2)] = jnp.where(left, shared, 0.0)
            side_ref[pl.ds(base + ROWBLK // 2, ROWBLK // 2)] = jnp.where(
                left, pltpu.roll(shared, 64, 1), 0.0
            )
        return carry

    lax.fori_loop(0, groups, unpack, 0)
    tail = groups * blocks * ROWBLK
    main_ref[tail : tail + MAXBF] = jnp.zeros((MAXBF, 128), jnp.float32)
    side_ref[tail : tail + MAXBF] = jnp.zeros((MAXBF, 128), jnp.float32)

    u, v = iota((256, 256), 0), iota((256, 256), 1)
    span = jnp.where(v < 128, 64, 32)
    is_real = (v < 64) | ((v >= 128) & (v < 160))
    source = jnp.where(is_real, v + span, v - span)
    turn = jnp.where((u == source) & (v < 192), jnp.where(is_real, -1.0, 1.0), 0.0)
    turn = turn.astype(jnp.bfloat16)
    same = iota((MAXBF, MAXBF, 256), 0) == iota((MAXBF, MAXBF, 256), 2) // MAXBF

    def group(g, carry):
        for j in range(2 * MAXBF):
            row = row_ref[g * (2 * MAXBF) + j]
            dest = first_ref if j % 2 == 0 else second_ref
            place = (j // 2) * MAXBF
            dest[place : place + MAXBF, 0:128] = main_ref[pl.ds(row, MAXBF)].astype(jnp.bfloat16)
            dest[place : place + MAXBF, 128:256] = side_ref[pl.ds(row, MAXBF)].astype(jnp.bfloat16)
        first = first_ref[...]
        second = second_ref[...]
        real = dot_nt(first, second)
        imag = dot_nt(first, dot(second, turn).astype(jnp.bfloat16))
        for c, value in ((0, real), (1, imag)):
            value = jnp.where(same, value.reshape(MAXBF, MAXBF, 256), 0.0)
            out_ref[g, c * MAXBF : (c + 1) * MAXBF] = jnp.sum(value, axis=0)
        return carry

    lax.fori_loop(0, groups, group, 0)


def slot_kernel(scale, place_ref, parts_ref, out_ref, tile_ref):
    total = parts_ref[0]
    for z in range(1, parts_ref.shape[0]):
        total = total + parts_ref[z]
    kernel = (total * scale).astype(jnp.bfloat16)
    same = iota((256, 256), 0) // MAXBF == iota((256, 256), 1) // MAXBF
    u, v = iota((256, 128), 0), iota((256, 128), 1)
    spot = v % 64 - (v // 64) * MAXBF
    first = jnp.zeros((256, 128), jnp.float32)
    for c in range(2):
        half = kernel[c * MAXBF : (c + 1) * MAXBF].astype(jnp.float32)
        wide = jnp.concatenate([half] * MAXBF, axis=0)
        wide = jnp.where(same, wide, 0.0).astype(jnp.bfloat16)
        fold = jnp.where(spot == c * 32 + u % MAXBF, 1.0, 0.0).astype(jnp.bfloat16)
        first = first + dot(wide, fold)
    u, v = iota((32, 128), 0), iota((32, 128), 1)
    spot = v % 64 - (v // 64) * MAXBF
    fold = jnp.where(spot == (u // MAXBF) * 32 + u % MAXBF, jnp.where(u < MAXBF, 1.0, -1.0), 0.0)
    tile_ref[0:256] = first
    tile_ref[256:512] = dot_tn(kernel, fold.astype(jnp.bfloat16))
    tile_ref[512:528] = jnp.zeros((MAXBF, 128), jnp.float32)
    for d in range(out_ref.shape[0]):
        one = tile_ref[pl.ds(pl.multiple_of(place_ref[2 * d], MAXBF), MAXBF)]
        two = tile_ref[pl.ds(pl.multiple_of(place_ref[2 * d + 1], MAXBF), MAXBF)]
        both = one + pltpu.roll(two, 64, 1)
        out_ref[d] = both[:, 0:64].astype(jnp.bfloat16)


def coef_kernel(row_ref, count_ref, coef_ref, out_ref):
    u, v = iota((96, 96), 0), iota((96, 96), 1)
    turn = jnp.where(u == (v + 48) % 96, jnp.where(v < 48, -1.0, 1.0), 0.0).astype(jnp.bfloat16)
    row_id = iota((MAXBF, 96), 0)

    def owner(g, carry):
        picked = []
        for r in range(2):
            row = row_ref[2 * g + r]
            base = pl.multiple_of((row // 16) * 16, 16)
            wide = coef_ref[pl.ds(base, 32)].astype(jnp.float32)
            rows = pltpu.roll(wide, 32 - (row - base), 0)[0:MAXBF]
            picked.append(jnp.where(row_id < count_ref[2 * g + r], rows, 0.0))
        rows = jnp.concatenate(picked, axis=0).astype(jnp.bfloat16)
        out_ref[g, 0:32] = rows
        out_ref[g, 32:64] = dot(rows, turn).astype(jnp.bfloat16)
        return carry

    lax.fori_loop(0, out_ref.shape[0], owner, 0)


def gain_kernel(row_ref, count_ref, slot_ref, coef_ref, out_ref, sum_ref):
    sum_ref[...] = jnp.zeros(sum_ref.shape, jnp.float32)
    lane = iota((MAXBF, 64), 1) % 32
    row_id = iota((MAXBF, 96), 0)
    for g in range(slot_ref.shape[0]):
        tile = slot_ref[g].astype(jnp.float32)
        upper = jnp.where(lane < MAXBF, tile, 0.0)
        lower = jnp.where(lane >= MAXBF, tile, 0.0)
        both = jnp.concatenate([upper, lower], axis=0).astype(jnp.bfloat16)
        gains = dot(both, coef_ref[g])
        for r in range(2):
            part = gains[r * MAXBF : (r + 1) * MAXBF]
            part = jnp.where(row_id < count_ref[2 * g + r], part, 0.0)
            where = pl.ds(row_ref[2 * g + r], MAXBF)
            sum_ref[where, 0:96] = sum_ref[where, 0:96] + part
    out_ref[...] = sum_ref[0:256].T[0:96]


def vmem_spec():
    return pl.BlockSpec(memory_space=pltpu.VMEM)


def smem_spec():
    return pl.BlockSpec(memory_space=pltpu.SMEM)


def limit(mib):
    return pltpu.CompilerParams(vmem_limit_bytes=mib * MIB)


def fit(integrals, low, own, high, mix):
    aux_dev, bas_dev, window = integrals.shape
    width = own.shape[1]
    steps = bas_dev // ROWBLK
    return pl.pallas_call(
        fit_kernel,
        grid=(steps,),
        in_specs=[
            pl.BlockSpec((aux_dev, ROWBLK, window), lambda i: (0, i, 0)),
            pl.BlockSpec(low.shape, lambda i: (0, 0)),
            pl.BlockSpec(own.shape, lambda i: (0, 0)),
            pl.BlockSpec(high.shape, lambda i: (0, 0)),
            pl.BlockSpec(mix.shape, lambda i: (0, 0)),
        ],
        out_specs=pl.BlockSpec((4 * aux_dev, 1, PACKED, 128), lambda i: (0, i, 0, 0)),
        out_shape=jax.ShapeDtypeStruct((4 * aux_dev, steps, PACKED, 128), jnp.bfloat16),
        scratch_shapes=[pltpu.VMEM((window, width), jnp.bfloat16)],
        compiler_params=limit(32),
        cost_estimate=pl.CostEstimate(
            flops=2 * aux_dev * bas_dev * width * (window + 256),
            bytes_accessed=6 * MIB,
            transcendentals=0,
        ),
        name="fit",
    )(integrals, low, own, high, mix)


def pair_sums(end_rows, got):
    groups, steps, _, _ = got.shape
    rows = groups * steps * ROWBLK + MAXBF
    return pl.pallas_call(
        pair_kernel,
        in_specs=[smem_spec(), vmem_spec()],
        out_specs=vmem_spec(),
        out_shape=jax.ShapeDtypeStruct((groups, 2 * MAXBF, 256), jnp.float32),
        scratch_shapes=[
            pltpu.VMEM((rows, 128), jnp.float32),
            pltpu.VMEM((rows, 128), jnp.float32),
            pltpu.VMEM((256, 256), jnp.bfloat16),
            pltpu.VMEM((256, 256), jnp.bfloat16),
        ],
        compiler_params=limit(40),
        name="pair_sums",
    )(end_rows, got)


def make_slots(scale, places, parts, groups):
    def body(*refs):
        slot_kernel(scale, *refs)

    return pl.pallas_call(
        body,
        in_specs=[smem_spec(), vmem_spec()],
        out_specs=vmem_spec(),
        out_shape=jax.ShapeDtypeStruct((groups, MAXBF, 64), jnp.bfloat16),
        scratch_shapes=[pltpu.VMEM((528, 128), jnp.float32)],
        compiler_params=limit(16),
        name="make_slots",
    )(places, parts)


def partner_coef(rows, counts, coef, groups):
    return pl.pallas_call(
        coef_kernel,
        in_specs=[smem_spec(), smem_spec(), vmem_spec()],
        out_specs=vmem_spec(),
        out_shape=jax.ShapeDtypeStruct((groups, 64, coef.shape[1]), jnp.bfloat16),
        compiler_params=limit(16),
        name="partner_coef",
    )(rows, counts, coef)


def add_gains(rows, counts, slots, partner, bas_dev):
    return pl.pallas_call(
        gain_kernel,
        in_specs=[smem_spec(), smem_spec(), vmem_spec(), vmem_spec()],
        out_specs=vmem_spec(),
        out_shape=jax.ShapeDtypeStruct((partner.shape[2], bas_dev), jnp.float32),
        scratch_shapes=[pltpu.VMEM((bas_dev + MAXBF, 128), jnp.float32)],
        compiler_params=limit(16),
        name="add_gains",
    )(rows, counts, slots, partner)


def pick(hit, values):
    return jnp.sum(jnp.where(hit, values, 0), axis=-1)


def per_device(integrals, coeffs, metric, atom_sizes, pair_device, pair_atom):
    aux_dev, bas_dev, window = integrals.shape
    occ = coeffs.shape[2]
    groups = lax.axis_size("atom")
    aux_count = lax.axis_size("aux")
    occ_part = occ // aux_count
    atom_count = atom_sizes.shape[1]
    ref_count = pair_atom.shape[0]
    halo = (window - bas_dev) // 2
    scale = 1.0 / math.sqrt(2 * occ * aux_dev * aux_count * MAXBF)
    me = lax.axis_index("atom")

    wide = coeffs[:, :, :256].reshape(bas_dev, 2, 4, 64).transpose(0, 2, 1, 3)
    narrow = coeffs[:, :, 256:].reshape(bas_dev, 2, 4, 32).transpose(0, 2, 1, 3)
    own = jnp.concatenate([wide.reshape(bas_dev, 512), narrow.reshape(bas_dev, 256)], axis=1)
    forward = [(i, i + 1) for i in range(groups - 1)]
    backward = [(i + 1, i) for i in range(groups - 1)]
    low = lax.ppermute(own[bas_dev - halo :], "atom", forward)
    high = lax.ppermute(own[:halo], "atom", backward)

    meta = jnp.concatenate([atom_sizes[0], pair_device[:, 0], pair_atom]).astype(jnp.bfloat16)
    coef_part = lax.dynamic_slice_in_dim(
        coeffs, lax.axis_index("aux") * occ_part, occ_part, 2
    ).reshape(bas_dev, 2 * occ_part)
    meta_rows = jnp.pad(meta[None], ((0, 15), (0, 0)))
    sent = jnp.concatenate([coef_part, meta_rows], axis=0)
    block_rows = bas_dev + 16
    all_coef = lax.all_gather(sent, "atom", axis=0, tiled=True)

    mix = metric.T[:, None, :, None] * jnp.eye(ROWBLK, dtype=jnp.bfloat16)[None, :, None, :]
    mix = mix.reshape(aux_dev * ROWBLK, aux_dev * ROWBLK)
    packed = fit(integrals, low, own, high, mix)
    got = lax.all_to_all(packed, "atom", split_axis=0, concat_axis=0, tiled=True)

    all_meta = all_coef.reshape(groups, block_rows, 2 * occ_part)[:, bas_dev].astype(jnp.int32)
    sizes = all_meta[:, :atom_count]
    devices = all_meta[:, atom_count : atom_count + ref_count]
    atoms = all_meta[:, atom_count + ref_count :]
    starts = jnp.cumsum(sizes, axis=1) - sizes
    atom_range = jnp.arange(atom_count, dtype=jnp.int32)
    block_range = jnp.arange(groups, dtype=jnp.int32)
    flat_dev, flat_atom = devices.reshape(-1), atoms.reshape(-1)
    both = (starts * 32 + sizes).astype(jnp.int32)
    hit = (flat_dev[:, None, None] == block_range[None, :, None]) & (
        flat_atom[:, None, None] == atom_range[None, None, :]
    )
    found = jnp.sum(jnp.where(hit, both[None], 0), axis=(1, 2))
    end_start = found // 32
    end_size = found % 32
    end_rows = flat_dev * bas_dev + end_start

    here = devices == me
    rank = jnp.cumsum(here.astype(jnp.int32), axis=1) - 1
    slot = here[:, None, :] & (rank[:, None, :] == jnp.arange(2, dtype=jnp.int32)[None, :, None])
    end_start, end_size = end_start.reshape(groups, ref_count), end_size.reshape(groups, ref_count)

    def partner(x):
        return x.reshape(groups, ref_count // 2, 2)[:, :, ::-1].reshape(groups, ref_count)

    gather_rows = devices * block_rows + end_start
    slot_start = pick(slot, end_start[:, None, :]).reshape(-1)
    slot_size = pick(slot, end_size[:, None, :]).reshape(-1)
    other_row = pick(slot, partner(gather_rows)[:, None, :]).reshape(-1)
    other_size = pick(slot, partner(end_size)[:, None, :]).reshape(-1)

    targets = pair_device[:, 0]
    order = jnp.arange(ref_count, dtype=jnp.int32)
    earlier = (targets[:, None] == targets[None, :]) & (order[None, :] < order[:, None])
    ranks = jnp.sum(earlier.astype(jnp.int32), axis=1)
    asked = targets * 2 + ranks
    place = (order % 2) * 256 + (order // 2) * MAXBF
    asked_hit = asked[None, :] == jnp.arange(2 * groups, dtype=jnp.int32)[:, None]
    places = 512 + pick(asked_hit, place[None, :] - 512)

    partial_sums = pair_sums(end_rows, got)
    owned = lax.all_to_all(partial_sums, "atom", split_axis=0, concat_axis=0, tiled=True)
    partner_rows = partner_coef(other_row, other_size, all_coef, groups)
    owned = jnp.sum(owned, axis=0)
    shared = jnp.broadcast_to(owned[None], (aux_count,) + owned.shape)
    parts = lax.all_to_all(shared, "aux", split_axis=0, concat_axis=0, tiled=True)
    slots = make_slots(scale, places, parts, groups)
    slots = lax.all_to_all(slots, "atom", split_axis=0, concat_axis=0, tiled=True)
    gains = add_gains(slot_start, slot_size, slots, partner_rows, bas_dev)
    return gains.reshape(2, occ_part, bas_dev).transpose(2, 0, 1)


def solution(mesh):
    placed = (
        P("aux", "atom", None),
        P("atom", None, None),
        P("aux", None),
        P("atom", None),
        P("atom", None),
        P("atom"),
    )
    return jax.shard_map(
        per_device, mesh=mesh, in_specs=placed, out_specs=P("atom", None, "aux"), check_vma=False
    )
```

time: 463 us -> 172 us (0.37)
  blocking collectives: 237 us -> 0 us
  local copies, waits for them, and re-layouts: 56.1 us -> 11.4 us
  Pallas kernels: 0 us -> 29.6 us
  other arithmetic: 23.6 us -> 6.87 us
  waiting for transfers between devices: 92.3 us -> 76.9 us
  matrix products: 9.44 us -> 0 us
    all_gather x1 -> x0, blocking collectives: 208 us -> none  [per_device(): all_sizes = lax.all_gather(atom_sizes, 'atom', axis=0, tiled=True)]
    reduce_scatter x1 -> x0, waiting for transfers between devices: 92.3 us -> none  [per_device(): lax.psum_scatter(dense_term, 'atom', scatter_dimension=0, tiled=True)]
    all_gather x0 -> x1, waiting for transfers between devices: none -> 45.3 us  [per_device(): all_coef = lax.all_gather(sent, 'atom', axis=0, tiled=True)]
    pallas_call x0 -> x5, Pallas kernels: none -> 29.6 us  [the longest x1 16.1 us: pair_sums(): pl.pallas_call(pair_kernel, in_specs=[smem_spec(), vmem_spec()], out_spec...]
    all_to_all x3 -> x4, waiting for transfers between devices: 0.01 us -> 29.2 us  [the longest x1 16.1 us: per_device(): lax.all_to_all(partial_sums, 'atom', split_axis=0, concat_axis=0, tiled=T...]
    psum x1 -> x0, blocking collectives: 28.9 us -> none  [per_device(): summed = lax.psum(partial_value, 'aux')]
    gather x4 -> x0, local copies, waits for them, and re-layouts: 23.5 us -> none  [the longest x1 11 us: per_device(): jnp.take(fitted, row_ids, axis=1)]
    all_to_all x2 -> x0, local copies, waits for them, and re-layouts: 10.9 us -> none  [the longest x1 10.9 us: per_device(): lax.all_to_all(sent_rows, 'atom', split_axis=1, concat_axis=1, tiled=True)]
  transfers between devices with their start and end apart: 6 -> 7, of which waited for: 1 -> 6; matrix products, arithmetic and copies ran while one was open for 11% -> 5% of each run, Pallas kernels for 0% -> 6%
where the time goes in v1:
time: 172 us
  waiting for transfers between devices  76.9 us (45%)
  starting transfers between devices  33.1 us (19%)
  Pallas kernels  29.6 us (17%)
  between operations  13.7 us (8%)
  local copies, waits for them, and re-layouts  11.4 us (7%)
  other arithmetic  6.87 us (4%)
    all_gather x1, waiting for transfers between devices, per_device(): all_coef = lax.all_gather(sent, 'atom', axis=0, tiled=True)  45.3 us
    pallas_call x1, Pallas kernels, pair_sums(): pl.pallas_call(pair_kernel, in_specs=[smem_spec(), vmem_spec()], out_spec...  16.1 us
    all_to_all x1, waiting for transfers between devices, per_device(): lax.all_to_all(partial_sums, 'atom', split_axis=0, concat_axis=0, tiled=T...  16.1 us
    all_to_all x1, waiting for transfers between devices, per_device(): lax.all_to_all(shared, 'aux', split_axis=0, concat_axis=0, tiled=True)  11.8 us
    all_to_all x1, starting transfers between devices, per_device(): lax.all_to_all(packed, 'atom', split_axis=0, concat_axis=0, tiled=True)  9.78 us
    all_to_all x1, starting transfers between devices, per_device(): lax.all_to_all(shared, 'aux', split_axis=0, concat_axis=0, tiled=True)  7.54 us
    pallas_call x1, Pallas kernels, fit(): pl.pallas_call(fit_kernel, grid=(steps,), in_specs=[pl.BlockSpec((aux_dev...  5.73 us
    ppermute x1, starting transfers between devices, per_device(): high = lax.ppermute(own[:halo], 'atom', backward)  5.14 us
  transfers between devices with their start and end apart: 7, of which 6 were waited for; matrix products, arithmetic and copies ran while one was open for 5% of the time, Pallas kernels for 6%

profile of v1, /device:TPU:1, one launch (start us, length us, event | category | flops | bytes accessed | tf_op | source)
XLA Modules:
  0.0 171.6 jit_solution(7704264794055756984)
XLA Ops:
  6.5 0.7 convert.12
  7.2 0.7 convert_bitcast_fusion
  7.9 0.7 convert_bitcast_fusion.1
  8.5 1.2 constant_dynamic-slice_fusion
  10.0 0.7 pad_maximum_fusion.1
  10.7 1.0 slice.29
  11.7 1.1 slice.28
  13.4 0.8 fusion.2
  14.2 5.1 %collective-permute-start.1 = (bf16[128,768]{1,0:T(8,128)(2,1)}, bf16[128,768]{1,0:T(8,128)(2,1)S(1)}, u32[]{:S(2)}, u32[]{:S(2)}) collective-permute-start(bf16[128,768]{1,0:T(8,128)(2,1)} %get-tuple-element.11), channel_id=1, source_target_pairs={{8,0},{16,8},{24,16},{32,24},{40,32},{48,40},{56,48},{64,56},{72,6... | collective-permute-start | bytes 589832 | tf_op jit(solution)/shard_map/ppermute | solution.py:289
  19.3 1.9 %collective-permute-start = (bf16[128,768]{1,0:T(8,128)(2,1)}, bf16[128,768]{1,0:T(8,128)(2,1)S(1)}, u32[]{:S(2)}, u32[]{:S(2)}) collective-permute-start(bf16[128,768]{1,0:T(8,128)(2,1)} %get-tuple-element.12), channel_id=1, source_target_pairs={{0,8},{8,16},{16,24},{24,32},{32,40},{40,48},{48,56},{56,64},{64,7... | collective-permute-start | bytes 589832 | tf_op jit(solution)/shard_map/ppermute | solution.py:288
  21.9 0.5 collective-permute-done.1.high_ref
  22.3 1.8 %collective-permute-done.low_ref = bf16[128,768]{1,0:T(8,128)(2,1)S(1)} collective-permute-done((bf16[128,768]{1,0:T(8,128)(2,1)}, bf16[128,768]{1,0:T(8,128)(2,1)S(1)}, u32[]{:S(2)}, u32[]{:S(2)}) %collective-permute-start) | collective-permute-done | bytes 196640 | tf_op jit(solution)/shard_map/ppermute | solution.py:288
  24.2 5.7 %fit.1 = bf16[32,8,48,128]{3,2,1,0:T(8,128)(2,1)S(1)} custom-call(bf16[8,256,512]{2,1,0:T(8,128)(2,1)S(1)} %copy-done.3, bf16[128,768]{1,0:T(8,128)(2,1)S(1)} %collective-permute-done.low_ref, bf16[256,768]{1,0:T(8,128)(2,1)S(1)} %pad_maximum_fusion.own_ref, bf16[128,768]{1,0:T(8,128)(2,1)S(1)} %collective-permute-done.1.high_ref, ...), custom_call_target="tpu_custom_call" | custom-call | flops 2415919104 | bytes 6291456 | tf_op jit(solution)/shard_map/fit/pallas_call | solution.py:187
  29.9 1.7 copy-done.1
  31.6 9.8 %all-to-all-start = ((bf16[32,8,48,128]{3,2,1,0:T(8,128)(2,1)}), bf16[32,8,48,128]{3,2,1,0:T(8,128)(2,1)S(1)}, u32[]{:S(2)}, u32[]{:S(2)}) async-start(bf16[32,8,48,128]{3,2,1,0:T(8,128)(2,1)} %copy-done.1), calls=%async_computation | async-start | bytes 6291456 | tf_op jit(solution)/shard_map/all_to_all | solution.py:303
  41.5 45.3 %all-gather.2.cloned.1.call-done.coef_ref = bf16[8704,96]{1,0:T(8,128)(2,1)} async-done(((bf16[272,96]{1,0:T(8,128)(2,1)}), bf16[8704,96]{1,0:T(8,128)(2,1)}) %all-gather.2.cloned.1.call-update) | async-done | bytes 1671184 | tf_op jit(solution)/shard_map/all_gather | solution.py:298
  86.9 0.8 slice.32
  88.2 0.7 select_reduce_fusion
  88.9 16.1 %pair_sums.1 = f32[32,32,256]{2,1,0:T(8,128)S(1)} custom-call(s32[1024]{0:T(1024)S(1)} %fusion.13.row_ref, bf16[32,8,48,128]{3,2,1,0:T(8,128)(2,1)S(1)} %all-to-all-done.got_ref), custom_call_target="tpu_custom_call" | custom-call | tf_op jit(solution)/shard_map/pair_sums/pallas_call | solution.py:213
  105.1 1.0 copy-done
  106.1 4.6 %all-to-all-start.1 = ((f32[32,32,256]{2,1,0:T(8,128)}), f32[32,32,256]{2,1,0:T(8,128)}, u32[]{:S(2)}, u32[]{:S(2)}) async-start(f32[32,32,256]{2,1,0:T(8,128)} %copy-done), calls=%async_computation.1 | async-start | bytes 2097152 | tf_op jit(solution)/shard_map/all_to_all | solution.py:346
  111.7 16.1 %all-to-all-done.1 = f32[32,32,256]{2,1,0:T(8,128)} async-done(((f32[32,32,256]{2,1,0:T(8,128)}), f32[32,32,256]{2,1,0:T(8,128)}, u32[]{:S(2)}, u32[]{:S(2)}) %all-to-all-start.1) | async-done | bytes 1048608 | tf_op jit(solution)/shard_map/all_to_all | solution.py:346
  127.8 1.3 reduce_sum.82
  129.1 0.7 broadcast_in_dim.85
  129.8 7.5 %all-to-all-start.2 = ((f32[8,32,256]{2,1,0:T(8,128)}), f32[8,32,256]{2,1,0:T(8,128)S(1)}, u32[]{:S(2)}, u32[]{:S(2)}) async-start(f32[8,32,256]{2,1,0:T(8,128)} %broadcast_in_dim.85), calls=%async_computation.2 | async-start | bytes 524288 | tf_op jit(solution)/shard_map/all_to_all | solution.py:350
  137.8 11.8 %all-to-all-done.2.refs_1_ = f32[8,32,256]{2,1,0:T(8,128)S(1)} async-done(((f32[8,32,256]{2,1,0:T(8,128)}), f32[8,32,256]{2,1,0:T(8,128)S(1)}, u32[]{:S(2)}, u32[]{:S(2)}) %all-to-all-start.2) | async-done | bytes 262176 | tf_op jit(solution)/shard_map/all_to_all | solution.py:350
  149.6 0.9 make_slots.1
  150.5 0.8 reshape.258
  151.3 4.1 %all-to-all-start.3 = ((bf16[32,2,512]{2,1,0:T(2,128)(2,1)}), bf16[32,2,512]{2,1,0:T(2,128)(2,1)S(1)}, u32[]{:S(2)}, u32[]{:S(2)}) async-start(bf16[32,2,512]{2,1,0:T(2,128)(2,1)} %reshape.258), calls=%async_computation.3 | async-start | bytes 131072 | tf_op jit(solution)/shard_map/all_to_all | solution.py:352
  156.4 5.1 %partner_coef.1.coef_ref = bf16[32,64,96]{2,1,0:T(8,128)(2,1)S(1)} custom-call(s32[64]{0:T(128)S(1)} %reshape.254.row_ref, s32[64]{0:T(128)S(1)} %reshape.255.count_ref, bf16[8704,96]{1,0:T(8,128)(2,1)S(1)} %copy-done.2), custom_call_target="tpu_custom_call" | custom-call | tf_op jit(solution)/shard_map/partner_coef/pallas_call | solution.py:245
  161.5 1.4 all-to-all-done.3
  163.0 1.7 %add_gains.1 = f32[96,256]{1,0:T(8,128)} custom-call(s32[64]{0:T(128)S(1)} %reshape.247.row_ref, s32[64]{0:T(128)S(1)} %reshape.248.count_ref, bf16[32,16,64]{2,1,0:T(8,128)(2,1)S(1)} %reshape.259.slot_ref, bf16[32,64,96]{2,1,0:T(8,128)(2,1)S(1)} %partner_coef.1.coef_ref), custom_call_target="tpu_custom_call" | custom-call | tf_op jit(solution)/shard_map/add_gains/pallas_call | solution.py:256
  (62 shorter events, 4.7 us)
Async XLA Ops:
  6.5 14.7 %copy-start.4 = (bf16[8,8]{1,0:T(8,128)(2,1)S(1)}, bf16[8,8]{1,0:T(8,128)(2,1)}, u32[]{:S(2)}) copy-start(bf16[8,8]{1,0:T(8,128)(2,1)} %param.8) | copy-start | bytes 388
  6.5 80.3 %all-gather.2.cloned.1.call-start = ((), (), s32[]{:S(2)}) async-start(), calls=%async_computation.4 | async-start | bytes 2297856 | tf_op jit(solution)/shard_map/all_gather | solution.py:298
  9.8 14.4 %copy-start.3 = (bf16[8,256,512]{2,1,0:T(8,128)(2,1)S(1)}, bf16[8,256,512]{2,1,0:T(8,128)(2,1)}, u32[]{:S(2)}) copy-start(bf16[8,256,512]{2,1,0:T(8,128)(2,1)} %ints_ref.1) | copy-start | bytes 6291460
  14.2 8.1 %collective-permute-start.1 = (bf16[128,768]{1,0:T(8,128)(2,1)}, bf16[128,768]{1,0:T(8,128)(2,1)S(1)}, u32[]{:S(2)}, u32[]{:S(2)}) collective-permute-start(bf16[128,768]{1,0:T(8,128)(2,1)} %get-tuple-element.11), channel_id=1, source_target_pairs={{8,0},{16,8},{24,16},{32,24},{40,32},{48,40},{56,48},{64,56},{72,6... | collective-permute-start | bytes 589832 | tf_op jit(solution)/shard_map/ppermute | solution.py:289
  19.3 4.8 %collective-permute-start = (bf16[128,768]{1,0:T(8,128)(2,1)}, bf16[128,768]{1,0:T(8,128)(2,1)S(1)}, u32[]{:S(2)}, u32[]{:S(2)}) collective-permute-start(bf16[128,768]{1,0:T(8,128)(2,1)} %get-tuple-element.12), channel_id=1, source_target_pairs={{0,8},{8,16},{16,24},{24,32},{32,40},{40,48},{48,56},{56,64},{64,7... | collective-permute-start | bytes 589832 | tf_op jit(solution)/shard_map/ppermute | solution.py:288
  29.9 1.7 copy-start.1
  31.6 9.8 %copy-start.5 = (s32[32,1]{0,1:T(1,128)S(1)}, s32[32,1]{0,1:T(1,128)}, u32[]{:S(2)}) copy-start(s32[32,1]{0,1:T(1,128)} %param.10) | copy-start | bytes 388
  31.6 57.3 %all-to-all-start = ((bf16[32,8,48,128]{3,2,1,0:T(8,128)(2,1)}), bf16[32,8,48,128]{3,2,1,0:T(8,128)(2,1)S(1)}, u32[]{:S(2)}, u32[]{:S(2)}) async-start(bf16[32,8,48,128]{3,2,1,0:T(8,128)(2,1)} %copy-done.1), calls=%async_computation | async-start | bytes 6291456 | tf_op jit(solution)/shard_map/all_to_all | solution.py:303
  105.0 1.0 copy-start
  106.1 50.3 %copy-start.2 = (bf16[8704,96]{1,0:T(8,128)(2,1)S(1)}, bf16[8704,96]{1,0:T(8,128)(2,1)}, u32[]{:S(2)}) copy-start(bf16[8704,96]{1,0:T(8,128)(2,1)} %all-gather.2.cloned.1.call-done.coef_ref) | copy-start | bytes 5013508
  106.1 21.7 %all-to-all-start.1 = ((f32[32,32,256]{2,1,0:T(8,128)}), f32[32,32,256]{2,1,0:T(8,128)}, u32[]{:S(2)}, u32[]{:S(2)}) async-start(f32[32,32,256]{2,1,0:T(8,128)} %copy-done), calls=%async_computation.1 | async-start | bytes 2097152 | tf_op jit(solution)/shard_map/all_to_all | solution.py:346
  129.8 19.8 %all-to-all-start.2 = ((f32[8,32,256]{2,1,0:T(8,128)}), f32[8,32,256]{2,1,0:T(8,128)S(1)}, u32[]{:S(2)}, u32[]{:S(2)}) async-start(f32[8,32,256]{2,1,0:T(8,128)} %broadcast_in_dim.85), calls=%async_computation.2 | async-start | bytes 524288 | tf_op jit(solution)/shard_map/all_to_all | solution.py:350
  151.3 11.5 %all-to-all-start.3 = ((bf16[32,2,512]{2,1,0:T(2,128)(2,1)}), bf16[32,2,512]{2,1,0:T(2,128)(2,1)S(1)}, u32[]{:S(2)}, u32[]{:S(2)}) async-start(bf16[32,2,512]{2,1,0:T(2,128)(2,1)} %reshape.258), calls=%async_computation.3 | async-start | bytes 131072 | tf_op jit(solution)/shard_map/all_to_all | solution.py:352
Sparse Core Ops, SparseCore 0:
  10.8 76.0 all-gather.1

commit v2 on v1

v2 whole, which is shorter than its diff:
```python
import math

import jax
import jax.numpy as jnp
import numpy as np
from jax import lax
from jax.experimental import pallas as pl
from jax.experimental.pallas import tpu as pltpu
from jax.sharding import PartitionSpec as P

MAXBF = 16
ROWBLK = 32
PACKED = ROWBLK + ROWBLK // 2
BATCH = 8
MIB = 1 << 20


def iota(shape, dim):
    return lax.broadcasted_iota(jnp.int32, shape, dim)


def dot(a, b):
    return jnp.dot(a, b, preferred_element_type=jnp.float32)


def dot_nt(a, b):
    return lax.dot_general(a, b, (((1,), (1,)), ((), ())), preferred_element_type=jnp.float32)


def dot_tn(a, b):
    return lax.dot_general(a, b, (((0,), (0,)), ((), ())), preferred_element_type=jnp.float32)


def fit_kernel(
    ints_ref, low_ref, own_ref, high_ref, order_ref, mix_ref, meta_ref, out_ref,
    window_ref, packed_ref, sem_ref,
):
    at = 0
    for part_ref in (low_ref, own_ref, high_ref):
        rows = part_ref.shape[0]
        window_ref[at : at + rows] = dot(part_ref[...], order_ref[...]).astype(jnp.bfloat16)
        at += rows
    aux_dev, bas_dev, span = ints_ref.shape
    blocks = bas_dev // ROWBLK
    left = iota((ROWBLK // 2, 128), 1) < 64
    copies = []
    for u in range(blocks):
        ints = ints_ref[:, u * ROWBLK : (u + 1) * ROWBLK].reshape(aux_dev * ROWBLK, span)
        half = dot(ints, window_ref[...]).astype(jnp.bfloat16)
        fitted = dot(mix_ref[...], half)
        main = slice(u * PACKED, u * PACKED + ROWBLK)
        side = slice(u * PACKED + ROWBLK, (u + 1) * PACKED)
        for p in range(aux_dev):
            rows = fitted[p * ROWBLK : (p + 1) * ROWBLK]
            for k in range(4):
                tile = rows[:, k * 128 : (k + 1) * 128]
                packed_ref[p * 4 + k, main] = tile.astype(jnp.bfloat16)
            for k in range(2):
                shared = rows[:, 512 + k * 128 : 640 + k * 128]
                top, bottom = shared[: ROWBLK // 2], shared[ROWBLK // 2 :]
                even = jnp.where(left, top, pltpu.roll(bottom, 64, 1))
                odd = jnp.where(left, pltpu.roll(top, 64, 1), bottom)
                packed_ref[p * 4 + 2 * k, side] = even.astype(jnp.bfloat16)
                packed_ref[p * 4 + 2 * k + 1, side] = odd.astype(jnp.bfloat16)
        if u == blocks - 1:
            for d in range(4 * aux_dev):
                packed_ref[d, blocks * PACKED : blocks * PACKED + 16] = meta_ref[...]
        if u % 2 == 1:
            first = (u - 1) * PACKED
            span_rows = pl.ds(first, 2 * PACKED + (16 if u == blocks - 1 else 0))
            copies.append(
                pltpu.make_async_copy(
                    packed_ref.at[:, span_rows], out_ref.at[:, span_rows], sem_ref.at[u // 2]
                )
            )
            copies[-1].start()
    for copy in copies:
        copy.wait()


def pair_kernel(row_ref, got_ref, out_ref, real_ref, imag_ref, sums_ref, sem_ref, *sides):
    groups, blocks = got_ref.shape[0], got_ref.shape[1] // PACKED
    lane = iota((ROWBLK // 2, 128), 1)
    left, valid = lane < 64, lane < 96

    def unpack(b, carry):
        for i in range(blocks):
            base = pl.multiple_of(b * (blocks * ROWBLK) + i * ROWBLK, ROWBLK)
            shared = got_ref[b, i * PACKED + ROWBLK : (i + 1) * PACKED].astype(jnp.float32)
            for h in range(2):
                at = i * PACKED + h * 16
                main = got_ref[b, at : at + 16].astype(jnp.float32)
                real = shared if h else pltpu.roll(shared, 64, 1)
                imag = pltpu.roll(shared, 96 if h else 32, 1)
                real = jnp.where(left, main, jnp.where(valid, real, 0.0))
                imag = jnp.where(left, pltpu.roll(main, 64, 1), jnp.where(valid, imag, 0.0))
                real_ref[pl.ds(base + h * 16, 16)] = real
                imag_ref[pl.ds(base + h * 16, 16)] = imag
        return carry

    lax.fori_loop(0, groups, unpack, 0, unroll=2)
    tail = groups * blocks * ROWBLK
    real_ref[tail : tail + MAXBF] = jnp.zeros((MAXBF, 128), jnp.float32)
    imag_ref[tail : tail + MAXBF] = jnp.zeros((MAXBF, 128), jnp.float32)
    lane_pair = lane // MAXBF
    batch = len(sides) // 4

    def group(step, carry):
        for u in range(batch):
            g = step * batch + u
            for h in range(2):
                first_ref, second_ref = sides[u * 4 + h * 2], sides[u * 4 + h * 2 + 1]
                for j in range(16):
                    row = row_ref[g * (2 * MAXBF) + h * 16 + j]
                    dest = second_ref if j % 2 else first_ref
                    place = (j // 2) * MAXBF
                    dest[place : place + 16] = real_ref[pl.ds(row, 16)].astype(jnp.bfloat16)
                    dest[128 + place : 144 + place] = imag_ref[pl.ds(row, 16)].astype(jnp.bfloat16)
                value = dot_nt(first_ref[...], second_ref[...])
                parts = []
                for top in (0, 128):
                    for at in (0, 128):
                        part = value[top : top + 16, at : at + 128]
                        for j in range(1, 8):
                            here = value[top + j * 16 : top + j * 16 + 16, at : at + 128]
                            part = jnp.where(lane_pair == j, here, part)
                        parts.append(part)
                sums_ref[g, 0:16, h * 128 : (h + 1) * 128] = parts[0] + parts[3]
                sums_ref[g, 16:32, h * 128 : (h + 1) * 128] = parts[2] - parts[1]
        send(step).start()
        return carry

    def send(step):
        done = pl.ds(step * batch, batch)
        return pltpu.make_async_copy(sums_ref.at[done], out_ref.at[done], sem_ref.at[step])

    lax.fori_loop(0, groups // batch, group, 0)
    for step in range(groups // batch):
        send(step).wait()


def slot_kernel(scale, place_ref, parts_ref, out_ref, tile_ref):
    total = parts_ref[0].astype(jnp.float32)
    for z in range(1, parts_ref.shape[0]):
        total = total + parts_ref[z].astype(jnp.float32)
    kernel = (total * scale).astype(jnp.bfloat16)
    same = iota((256, 256), 0) // MAXBF == iota((256, 256), 1) // MAXBF
    u, v = iota((256, 128), 0), iota((256, 128), 1)
    spot = v % 64 - (v // 64) * MAXBF
    first = jnp.zeros((256, 128), jnp.float32)
    for c in range(2):
        half = kernel[c * MAXBF : (c + 1) * MAXBF].astype(jnp.float32)
        wide = jnp.concatenate([half] * MAXBF, axis=0)
        wide = jnp.where(same, wide, 0.0).astype(jnp.bfloat16)
        fold = jnp.where(spot == c * 32 + u % MAXBF, 1.0, 0.0).astype(jnp.bfloat16)
        first = first + dot(wide, fold)
    u, v = iota((32, 128), 0), iota((32, 128), 1)
    spot = v % 64 - (v // 64) * MAXBF
    fold = jnp.where(spot == (u // MAXBF) * 32 + u % MAXBF, jnp.where(u < MAXBF, 1.0, -1.0), 0.0)
    tile_ref[0:256] = first
    tile_ref[256:512] = dot_tn(kernel, fold.astype(jnp.bfloat16))
    tile_ref[512:528] = jnp.zeros((MAXBF, 128), jnp.float32)
    left = iota((8, 128), 1) < 64
    for d in range(out_ref.shape[0]):
        one = tile_ref[pl.ds(pl.multiple_of(place_ref[2 * d], MAXBF), MAXBF)]
        two = tile_ref[pl.ds(pl.multiple_of(place_ref[2 * d + 1], MAXBF), MAXBF)]
        both = one + pltpu.roll(two, 64, 1)
        out_ref[d] = jnp.where(left, both[0:8], pltpu.roll(both[8:16], 64, 1))


def coef_kernel(row_ref, count_ref, coef_ref, out_ref):
    u, v = iota((96, 96), 0), iota((96, 96), 1)
    turn = jnp.where(u == (v + 48) % 96, jnp.where(v < 48, -1.0, 1.0), 0.0).astype(jnp.bfloat16)
    row_id = iota((MAXBF, 96), 0)

    def owner(g, carry):
        picked = []
        for r in range(2):
            row = row_ref[2 * g + r]
            base = jnp.minimum((row // 16) * 16, coef_ref.shape[0] - 32)
            base = pl.multiple_of(base, 16)
            wide = coef_ref[pl.ds(base, 32)].astype(jnp.float32)
            rows = pltpu.roll(wide, lax.rem(32 - (row - base), 32), 0)[0:MAXBF]
            picked.append(jnp.where(row_id < count_ref[2 * g + r], rows, 0.0))
        rows = jnp.concatenate(picked, axis=0).astype(jnp.bfloat16)
        out_ref[g, 0:32] = rows
        out_ref[g, 32:64] = dot(rows, turn).astype(jnp.bfloat16)
        return carry

    lax.fori_loop(0, out_ref.shape[0], owner, 0)


def gain_kernel(row_ref, count_ref, slot_ref, coef_ref, out_ref, sum_ref):
    sum_ref[...] = jnp.zeros(sum_ref.shape, jnp.float32)
    lane = iota((MAXBF, 64), 1) % 32
    row_id = iota((MAXBF, 96), 0)
    for g in range(slot_ref.shape[0]):
        pair = slot_ref[g]
        tile = jnp.concatenate([pair, pltpu.roll(pair, 64, 1)], axis=0)[:, 0:64]
        upper = jnp.where(lane < MAXBF, tile, 0.0)
        lower = jnp.where(lane >= MAXBF, tile, 0.0)
        both = jnp.concatenate([upper, lower], axis=0).astype(jnp.bfloat16)
        gains = dot(both, coef_ref[g])
        for r in range(2):
            part = gains[r * MAXBF : (r + 1) * MAXBF]
            part = jnp.where(row_id < count_ref[2 * g + r], part, 0.0)
            where = pl.ds(row_ref[2 * g + r], MAXBF)
            sum_ref[where, 0:96] = sum_ref[where, 0:96] + part
    out_ref[...] = sum_ref[0:256].T[0:96]


def vmem_spec():
    return pl.BlockSpec(memory_space=pltpu.VMEM)


def smem_spec():
    return pl.BlockSpec(memory_space=pltpu.SMEM)


def limit(mib):
    return pltpu.CompilerParams(vmem_limit_bytes=mib * MIB)


def fit(integrals, low, own, high, order, mix, meta):
    aux_dev, bas_dev, window = integrals.shape
    width = own.shape[1]
    blocks = bas_dev // ROWBLK
    shape = (4 * aux_dev, blocks * PACKED + 16, 128)
    return pl.pallas_call(
        fit_kernel,
        in_specs=[vmem_spec()] * 7,
        out_specs=pl.BlockSpec(memory_space=pltpu.HBM),
        out_shape=jax.ShapeDtypeStruct(shape, jnp.bfloat16),
        scratch_shapes=[
            pltpu.VMEM((window, width), jnp.bfloat16),
            pltpu.VMEM(shape, jnp.bfloat16),
            pltpu.SemaphoreType.DMA((blocks // 2,)),
        ],
        compiler_params=limit(32),
        cost_estimate=pl.CostEstimate(
            flops=2 * aux_dev * bas_dev * width * (window + 256),
            bytes_accessed=6 * MIB,
            transcendentals=0,
        ),
        name="fit",
    )(integrals, low, own, high, order, mix, meta)


def pair_sums(end_rows, got):
    groups = got.shape[0]
    rows = groups * (got.shape[1] // PACKED) * ROWBLK + MAXBF
    return pl.pallas_call(
        pair_kernel,
        in_specs=[smem_spec(), vmem_spec()],
        out_specs=pl.BlockSpec(memory_space=pltpu.HBM),
        out_shape=jax.ShapeDtypeStruct((groups, 2 * MAXBF, 256), jnp.float32),
        scratch_shapes=[
            pltpu.VMEM((rows, 128), jnp.float32),
            pltpu.VMEM((rows, 128), jnp.float32),
            pltpu.VMEM((groups, 2 * MAXBF, 256), jnp.float32),
            pltpu.SemaphoreType.DMA((groups // BATCH,)),
        ]
        + [pltpu.VMEM((256, 128), jnp.bfloat16)] * (4 * BATCH),
        compiler_params=limit(40),
        name="pair_sums",
    )(end_rows, got)


def make_slots(scale, places, parts, groups):
    def body(*refs):
        slot_kernel(scale, *refs)

    return pl.pallas_call(
        body,
        in_specs=[smem_spec(), vmem_spec()],
        out_specs=vmem_spec(),
        out_shape=jax.ShapeDtypeStruct((groups, 8, 128), jnp.float32),
        scratch_shapes=[pltpu.VMEM((528, 128), jnp.float32)],
        compiler_params=limit(16),
        name="make_slots",
    )(places, parts)


def partner_coef(rows, counts, coef, groups):
    return pl.pallas_call(
        coef_kernel,
        in_specs=[smem_spec(), smem_spec(), vmem_spec()],
        out_specs=vmem_spec(),
        out_shape=jax.ShapeDtypeStruct((groups, 64, coef.shape[1]), jnp.bfloat16),
        compiler_params=limit(16),
        name="partner_coef",
    )(rows, counts, coef)


def add_gains(rows, counts, slots, partner, bas_dev):
    return pl.pallas_call(
        gain_kernel,
        in_specs=[smem_spec(), smem_spec(), vmem_spec(), vmem_spec()],
        out_specs=vmem_spec(),
        out_shape=jax.ShapeDtypeStruct((partner.shape[2], bas_dev), jnp.float32),
        scratch_shapes=[pltpu.VMEM((bas_dev + MAXBF, 128), jnp.float32)],
        compiler_params=limit(16),
        name="add_gains",
    )(rows, counts, slots, partner)


def pick(hit, values):
    return jnp.sum(jnp.where(hit, values, 0), axis=-1)


def column_order(occ):
    order = np.zeros((2 * occ, 2 * occ), np.float32)
    spot = 0
    for first, count in ((0, 64), (4 * 64, 32)):
        for k in range(4):
            for c in range(2):
                for i in range(count):
                    order[c * occ + first + k * count + i, spot] = 1.0
                    spot += 1
    return order.astype(jnp.bfloat16)


def per_device(integrals, coeffs, metric, atom_sizes, pair_device, pair_atom):
    aux_dev, bas_dev, window = integrals.shape
    occ = coeffs.shape[2]
    groups = lax.axis_size("atom")
    aux_count = lax.axis_size("aux")
    occ_part = occ // aux_count
    atom_count = atom_sizes.shape[1]
    ref_count = pair_atom.shape[0]
    halo = (window - bas_dev) // 2
    scale = 1.0 / math.sqrt(2 * occ * aux_dev * aux_count * MAXBF)
    me = lax.axis_index("atom")

    own = coeffs.reshape(bas_dev, 2 * occ)
    forward = [(i, i + 1) for i in range(groups - 1)]
    backward = [(i + 1, i) for i in range(groups - 1)]
    low = lax.ppermute(own[bas_dev - halo :], "atom", forward)
    high = lax.ppermute(own[:halo], "atom", backward)

    meta = jnp.concatenate([atom_sizes[0], pair_device[:, 0], pair_atom]).astype(jnp.bfloat16)
    meta = jnp.pad(meta[None], ((0, 15), (0, 128 - meta.shape[0])))
    mix = metric.T[:, None, :, None] * jnp.eye(ROWBLK, dtype=jnp.bfloat16)[None, :, None, :]
    mix = mix.reshape(aux_dev * ROWBLK, aux_dev * ROWBLK)
    packed = fit(integrals, low, own, high, jnp.asarray(column_order(occ)), mix, meta)
    coef_part, packed = lax.optimization_barrier((coeffs, packed))
    got = lax.all_to_all(packed, "atom", split_axis=0, concat_axis=0, tiled=True)
    coef_part = lax.dynamic_slice_in_dim(
        coef_part, lax.axis_index("aux") * occ_part, occ_part, 2
    ).reshape(bas_dev, 2 * occ_part)
    all_coef = lax.all_gather(coef_part, "atom", axis=0, tiled=True)

    all_meta = got[:, got.shape[1] - 16, : 2 * occ_part].astype(jnp.int32)
    sizes = all_meta[:, :atom_count]
    devices = all_meta[:, atom_count : atom_count + ref_count]
    atoms = all_meta[:, atom_count + ref_count :]
    starts = jnp.cumsum(sizes, axis=1) - sizes
    atom_range = jnp.arange(atom_count, dtype=jnp.int32)
    block_range = jnp.arange(groups, dtype=jnp.int32)
    flat_dev, flat_atom = devices.reshape(-1), atoms.reshape(-1)
    both = (starts * 32 + sizes).astype(jnp.int32)
    hit = (flat_dev[:, None, None] == block_range[None, :, None]) & (
        flat_atom[:, None, None] == atom_range[None, None, :]
    )
    found = jnp.sum(jnp.where(hit, both[None], 0), axis=(1, 2))
    end_start = found // 32
    end_size = found % 32
    end_rows = flat_dev * bas_dev + end_start

    here = devices == me
    rank = jnp.cumsum(here.astype(jnp.int32), axis=1) - 1
    slot = here[:, None, :] & (rank[:, None, :] == jnp.arange(2, dtype=jnp.int32)[None, :, None])
    end_start, end_size = end_start.reshape(groups, ref_count), end_size.reshape(groups, ref_count)

    def partner(x):
        return x.reshape(groups, ref_count // 2, 2)[:, :, ::-1].reshape(groups, ref_count)

    gather_rows = devices * bas_dev + end_start
    slot_start = pick(slot, end_start[:, None, :]).reshape(-1)
    slot_size = pick(slot, end_size[:, None, :]).reshape(-1)
    other_row = pick(slot, partner(gather_rows)[:, None, :]).reshape(-1)
    other_size = pick(slot, partner(end_size)[:, None, :]).reshape(-1)

    targets = pair_device[:, 0]
    order = jnp.arange(ref_count, dtype=jnp.int32)
    earlier = (targets[:, None] == targets[None, :]) & (order[None, :] < order[:, None])
    ranks = jnp.sum(earlier.astype(jnp.int32), axis=1)
    asked = targets * 2 + ranks
    place = (order % 2) * 256 + (order // 2) * MAXBF
    asked_hit = asked[None, :] == jnp.arange(2 * groups, dtype=jnp.int32)[:, None]
    places = 512 + pick(asked_hit, place[None, :] - 512)

    partial_sums = pair_sums(end_rows, got)
    owned = lax.all_to_all(partial_sums, "atom", split_axis=0, concat_axis=0, tiled=True)
    partner_rows = partner_coef(other_row, other_size, all_coef, groups)
    owned = jnp.sum(owned, axis=0).astype(jnp.bfloat16)
    shared = jnp.broadcast_to(owned[None], (aux_count,) + owned.shape)
    parts = lax.all_to_all(shared, "aux", split_axis=0, concat_axis=0, tiled=True)
    slots = make_slots(scale, places, parts, groups)
    slots = lax.all_to_all(slots, "atom", split_axis=0, concat_axis=0, tiled=True)
    gains = add_gains(slot_start, slot_size, slots, partner_rows, bas_dev)
    return gains.reshape(2, occ_part, bas_dev).transpose(2, 0, 1)


def solution(mesh):
    placed = (
        P("aux", "atom", None),
        P("atom", None, None),
        P("aux", None),
        P("atom", None),
        P("atom", None),
        P("atom"),
    )
    return jax.shard_map(
        per_device, mesh=mesh, in_specs=placed, out_specs=P("atom", None, "aux"), check_vma=False
    )
```

time: 172 us -> 153 us (0.89)
  waiting for transfers between devices: 76.9 us -> 66.2 us
  Pallas kernels: 29.6 us -> 20.5 us
  local copies, waits for them, and re-layouts: 11.4 us -> 15.1 us
  other arithmetic: 6.87 us -> 3.55 us
    all_gather x1, waiting for transfers between devices: 45.3 us -> 0.02 us  [per_device(): all_coef = lax.all_gather(coef_part, 'atom', axis=0, tiled=True)]
    all_to_all x1, waiting for transfers between devices: 0.01 us -> 38.6 us  [per_device(): lax.all_to_all(packed, 'atom', split_axis=0, concat_axis=0, tiled=True)]
    pallas_call x1, Pallas kernels: 16.1 us -> 6.67 us  [pair_sums(): pl.pallas_call(pair_kernel, in_specs=[smem_spec(), vmem_spec()], out_spec...]
    all_to_all x1, waiting for transfers between devices: 11.8 us -> 7.36 us  [per_device(): lax.all_to_all(shared, 'aux', split_axis=0, concat_axis=0, tiled=True)]
    ppermute x1, starting transfers between devices: 5.14 us -> 1.92 us  [per_device(): high = lax.ppermute(own[:halo], 'atom', backward)]
    all_to_all x1, waiting for transfers between devices: 16.1 us -> 18.9 us  [per_device(): lax.all_to_all(partial_sums, 'atom', split_axis=0, concat_axis=0, tiled=T...]
    ppermute x1, starting transfers between devices: 1.92 us -> 4.59 us  [per_device(): low = lax.ppermute(own[bas_dev - halo:], 'atom', forward)]
    unnamed x17, local copies, waits for them, and re-layouts: 3.97 us -> 6.63 us
  transfers between devices with their start and end apart: 7 -> 7, of which waited for: 6 -> 4; matrix products, arithmetic and copies ran while one was open for 5% -> 8% of each run, Pallas kernels for 6% -> 9%
where the time goes in v2:
time: 153 us; the launch traced here: 152 us
  waiting for transfers between devices  66.2 us (43%)
  starting transfers between devices  33.3 us (22%)
  Pallas kernels  20.5 us (13%)
  local copies, waits for them, and re-layouts  15.1 us (10%)
  between operations  13.7 us (9%)
  other arithmetic  3.55 us (2%)
    all_to_all x1, waiting for transfers between devices, per_device(): lax.all_to_all(packed, 'atom', split_axis=0, concat_axis=0, tiled=True)  38.6 us
    all_to_all x1, waiting for transfers between devices, per_device(): lax.all_to_all(partial_sums, 'atom', split_axis=0, concat_axis=0, tiled=T...  18.9 us
    all_to_all x1, starting transfers between devices, per_device(): lax.all_to_all(packed, 'atom', split_axis=0, concat_axis=0, tiled=True)  8.41 us
    all_to_all x1, starting transfers between devices, per_device(): lax.all_to_all(shared, 'aux', split_axis=0, concat_axis=0, tiled=True)  7.71 us
    all_to_all x1, waiting for transfers between devices, per_device(): lax.all_to_all(shared, 'aux', split_axis=0, concat_axis=0, tiled=True)  7.36 us
    pallas_call x1, Pallas kernels, pair_sums(): pl.pallas_call(pair_kernel, in_specs=[smem_spec(), vmem_spec()], out_spec...  6.67 us
    unnamed x17, local copies, waits for them, and re-layouts  6.63 us
    all_to_all x1, starting transfers between devices, per_device(): lax.all_to_all(slots, 'atom', split_axis=0, concat_axis=0, tiled=True)  5.9 us
  transfers between devices with their start and end apart: 7, of which 4 were waited for; matrix products, arithmetic and copies ran while one was open for 8% of the time, Pallas kernels for 9%

profile of v2, /device:TPU:1, one launch (start us, length us, event | category | flops | bytes accessed | tf_op | source)
XLA Modules:
  0.0 152.3 jit_solution(16228923340503253651)
XLA Ops:
  6.5 1.4 fusion.23
  8.0 4.6 %collective-permute-start = (bf16[128,768]{1,0:T(8,128)(2,1)S(1)}, bf16[128,768]{1,0:T(8,128)(2,1)S(1)}, u32[]{:S(2)}, u32[]{:S(2)}) collective-permute-start(bf16[128,768]{1,0:T(8,128)(2,1)S(1)} %bitcast.33), channel_id=1, source_target_pairs={{0,8},{8,16},{16,24},{24,32},{32,40},{40,48},{48,56},{56,64},{64,7... | collective-permute-start | bytes 589832 | tf_op jit(solution)/shard_map/ppermute | solution.py:338
  12.7 1.9 %collective-permute-start.1 = (bf16[128,768]{1,0:T(8,128)(2,1)S(1)}, bf16[128,768]{1,0:T(8,128)(2,1)S(1)}, u32[]{:S(2)}, u32[]{:S(2)}) collective-permute-start(bf16[128,768]{1,0:T(8,128)(2,1)S(1)} %bitcast.34), channel_id=1, source_target_pairs={{8,0},{16,8},{24,16},{32,24},{40,32},{48,40},{56,48},{64,56},{72,6... | collective-permute-start | bytes 589832 | tf_op jit(solution)/shard_map/ppermute | solution.py:339
  14.6 0.8 copy.16
  15.4 0.7 convert_bitcast_fusion
  16.1 0.7 convert_bitcast_fusion.1
  16.8 0.3 mul.71.mix_ref
  17.1 1.0 copy.28
  18.3 1.3 collective-permute-done.1.high_ref
  19.6 1.3 copy-done.4
  20.9 5.3 %fit.1 = bf16[32,400,128]{2,1,0:T(8,128)(2,1)S(1)} custom-call(bf16[8,256,512]{2,1,0:T(8,128)(2,1)S(1)} %copy-done.3, bf16[128,768]{1,0:T(8,128)(2,1)S(1)} %collective-permute-done.low_ref, bf16[256,768]{1,0:T(8,128)(2,1)S(1)} %bitcast.24, bf16[128,768]{1,0:T(8,128)(2,1)S(1)} %collective-permute-done.1.high_ref, bf16[768,768]{1,0:T(8,128)(2,1)S(1)} %copy-done.4, ...), custom_call_target="tpu_custom_call" | custom-call | flops 2415919104 | bytes 6291456 | tf_op jit(solution)/shard_map/fit/pallas_call | solution.py:229
  26.2 1.7 %copy-done.1 = bf16[32,400,128]{2,1,0:T(8,128)(2,1)} copy-done((bf16[32,400,128]{2,1,0:T(8,128)(2,1)}, bf16[32,400,128]{2,1,0:T(8,128)(2,1)S(1)}, u32[]{:S(2)}) %copy-start.1) | copy-done | bytes 3276824
  27.9 8.4 %all-to-all-start = ((bf16[32,400,128]{2,1,0:T(8,128)(2,1)}), bf16[32,400,128]{2,1,0:T(8,128)(2,1)S(1)}, u32[]{:S(2)}, u32[]{:S(2)}) async-start(bf16[32,400,128]{2,1,0:T(8,128)(2,1)} %copy-done.1), calls=%async_computation | async-start | bytes 6553600 | tf_op jit(solution)/shard_map/all_to_all | solution.py:347
  36.4 1.9 %copy.25 = bf16[256,2,384]{0,2,1:T(8,128)(2,1)} copy(bf16[256,2,384]{2,1,0:T(2,128)(2,1)} %param.8) | data formatting | bytes 786432 | tf_op jit(solution)/shard_map/optimization_barrier | solution.py:346
  38.3 0.8 constant_dynamic-slice_fusion
  39.1 0.7 copy.26
  39.9 38.6 %all-to-all-done.got_ref = bf16[32,400,128]{2,1,0:T(8,128)(2,1)S(1)} async-done(((bf16[32,400,128]{2,1,0:T(8,128)(2,1)}), bf16[32,400,128]{2,1,0:T(8,128)(2,1)S(1)}, u32[]{:S(2)}, u32[]{:S(2)}) %all-to-all-start) | async-done | bytes 3276832 | tf_op jit(solution)/shard_map/all_to_all | solution.py:347
  79.0 0.7 select_reduce_fusion
  79.7 6.7 %pair_sums.1 = f32[32,32,256]{2,1,0:T(8,128)S(1)} custom-call(s32[1024]{0:T(1024)S(1)} %fusion.16.row_ref, bf16[32,400,128]{2,1,0:T(8,128)(2,1)S(1)} %all-to-all-done.got_ref), custom_call_target="tpu_custom_call" | custom-call | tf_op jit(solution)/shard_map/pair_sums/pallas_call | solution.py:252
  86.3 1.0 copy-done
  87.3 4.7 %all-to-all-start.1 = ((f32[32,32,256]{2,1,0:T(8,128)}), f32[32,32,256]{2,1,0:T(8,128)S(1)}, u32[]{:S(2)}, u32[]{:S(2)}) async-start(f32[32,32,256]{2,1,0:T(8,128)} %copy-done), calls=%async_computation.1 | async-start | bytes 2097152 | tf_op jit(solution)/shard_map/all_to_all | solution.py:394
  92.4 0.2 reduce_sum.84
  92.7 18.9 %all-to-all-done.1 = f32[32,32,256]{2,1,0:T(8,128)S(1)} async-done(((f32[32,32,256]{2,1,0:T(8,128)}), f32[32,32,256]{2,1,0:T(8,128)S(1)}, u32[]{:S(2)}, u32[]{:S(2)}) %all-to-all-start.1) | async-done | bytes 1048608 | tf_op jit(solution)/shard_map/all_to_all | solution.py:394
  111.6 0.6 broadcast_in_dim.85
  112.3 7.7 %all-to-all-start.2 = ((bf16[8,32,256]{2,1,0:T(8,128)(2,1)}), bf16[8,32,256]{2,1,0:T(8,128)(2,1)S(1)}, u32[]{:S(2)}, u32[]{:S(2)}) async-start(bf16[8,32,256]{2,1,0:T(8,128)(2,1)} %broadcast_in_dim.85), calls=%async_computation.2 | async-start | bytes 262144 | tf_op jit(solution)/shard_map/all_to_all | solution.py:398
  120.4 7.4 %all-to-all-done.2.refs_1_ = bf16[8,32,256]{2,1,0:T(8,128)(2,1)S(1)} async-done(((bf16[8,32,256]{2,1,0:T(8,128)(2,1)}), bf16[8,32,256]{2,1,0:T(8,128)(2,1)S(1)}, u32[]{:S(2)}, u32[]{:S(2)}) %all-to-all-start.2) | async-done | bytes 131104 | tf_op jit(solution)/shard_map/all_to_all | solution.py:398
  127.7 1.6 %make_slots.1 = f32[32,8,128]{2,1,0:T(8,128)} custom-call(s32[64]{0:T(128)S(1)} %broadcast_add_fusion.1.refs_0_, bf16[8,32,256]{2,1,0:T(8,128)(2,1)S(1)} %all-to-all-done.2.refs_1_), custom_call_target="tpu_custom_call" | custom-call | tf_op jit(solution)/shard_map/make_slots/pallas_call | solution.py:273
  129.4 5.9 %all-to-all-start.3 = ((f32[32,8,128]{2,1,0:T(8,128)}), f32[32,8,128]{2,1,0:T(8,128)S(1)}, u32[]{:S(2)}, u32[]{:S(2)}) async-start(f32[32,8,128]{2,1,0:T(8,128)} %make_slots.1), calls=%async_computation.3 | async-start | bytes 262144 | tf_op jit(solution)/shard_map/all_to_all | solution.py:400
  135.9 0.2 select_reduce_fusion.1
  137.0 1.6 %copy-done.2 = bf16[8192,96]{1,0:T(8,128)(2,1)S(1)} copy-done((bf16[8192,96]{1,0:T(8,128)(2,1)S(1)}, bf16[8192,96]{1,0:T(8,128)(2,1)}, u32[]{:S(2)}) %copy-start.2) | copy-done | bytes 1572888
  138.5 5.1 %partner_coef.1.coef_ref = bf16[32,64,96]{2,1,0:T(8,128)(2,1)S(1)} custom-call(s32[64]{0:T(128)S(1)} %reshape.241.row_ref, s32[64]{0:T(128)S(1)} %reshape.242.count_ref, bf16[8192,96]{1,0:T(8,128)(2,1)S(1)} %copy-done.2), custom_call_target="tpu_custom_call" | custom-call | tf_op jit(solution)/shard_map/partner_coef/pallas_call | solution.py:285
  143.6 1.8 %add_gains.1 = f32[96,256]{1,0:T(8,128)} custom-call(s32[64]{0:T(128)S(1)} %reshape.238.row_ref, s32[64]{0:T(128)S(1)} %reshape.239.count_ref, f32[32,8,128]{2,1,0:T(8,128)S(1)} %all-to-all-done.3.slot_ref, bf16[32,64,96]{2,1,0:T(8,128)(2,1)S(1)} %partner_coef.1.coef_ref), custom_call_target="tpu_custom_call" | custom-call | tf_op jit(solution)/shard_map/add_gains/pallas_call | solution.py:296
  (53 shorter events, 3.1 us)
Async XLA Ops:
  6.5 11.7 %copy-start.6 = (s32[1,32]{1,0:T(1,128)S(1)}, s32[1,32]{1,0:T(1,128)}, u32[]{:S(2)}) copy-start(s32[1,32]{1,0:T(1,128)} %param.10) | copy-start | bytes 388
  6.5 13.1 %copy-start.3 = (bf16[8,256,512]{2,1,0:T(8,128)(2,1)S(1)}, bf16[8,256,512]{2,1,0:T(8,128)(2,1)}, u32[]{:S(2)}) copy-start(bf16[8,256,512]{2,1,0:T(8,128)(2,1)} %ints_ref.1) | copy-start | bytes 6291460
  8.0 10.3 %collective-permute-start = (bf16[128,768]{1,0:T(8,128)(2,1)S(1)}, bf16[128,768]{1,0:T(8,128)(2,1)S(1)}, u32[]{:S(2)}, u32[]{:S(2)}) collective-permute-start(bf16[128,768]{1,0:T(8,128)(2,1)S(1)} %bitcast.33), channel_id=1, source_target_pairs={{0,8},{8,16},{16,24},{24,32},{32,40},{40,48},{48,56},{56,64},{64,7... | collective-permute-start | bytes 589832 | tf_op jit(solution)/shard_map/ppermute | solution.py:338
  12.7 7.0 %collective-permute-start.1 = (bf16[128,768]{1,0:T(8,128)(2,1)S(1)}, bf16[128,768]{1,0:T(8,128)(2,1)S(1)}, u32[]{:S(2)}, u32[]{:S(2)}) collective-permute-start(bf16[128,768]{1,0:T(8,128)(2,1)S(1)} %bitcast.34), channel_id=1, source_target_pairs={{8,0},{16,8},{24,16},{32,24},{40,32},{48,40},{56,48},{64,56},{72,6... | collective-permute-start | bytes 589832 | tf_op jit(solution)/shard_map/ppermute | solution.py:339
  19.6 1.3 copy-start.4
  26.2 1.7 %copy-start.1 = (bf16[32,400,128]{2,1,0:T(8,128)(2,1)}, bf16[32,400,128]{2,1,0:T(8,128)(2,1)S(1)}, u32[]{:S(2)}) copy-start(bf16[32,400,128]{2,1,0:T(8,128)(2,1)S(1)} %fit.1) | copy-start | bytes 9830404
  27.9 50.6 %all-to-all-start = ((bf16[32,400,128]{2,1,0:T(8,128)(2,1)}), bf16[32,400,128]{2,1,0:T(8,128)(2,1)S(1)}, u32[]{:S(2)}, u32[]{:S(2)}) async-start(bf16[32,400,128]{2,1,0:T(8,128)(2,1)} %copy-done.1), calls=%async_computation | async-start | bytes 6553600 | tf_op jit(solution)/shard_map/all_to_all | solution.py:347
  36.3 100.6 %all-gather.2.cloned.1.call-start = ((), (), s32[]{:S(2)}) async-start(), calls=%async_computation.4 | async-start | bytes 2162688 | tf_op jit(solution)/shard_map/all_gather | solution.py:351
  78.9 13.1 %copy-start.5 = (s32[32,1]{0,1:T(1,128)S(1)}, s32[32,1]{0,1:T(1,128)}, u32[]{:S(2)}) copy-start(s32[32,1]{0,1:T(1,128)} %param.11) | copy-start | bytes 388
  86.3 1.0 copy-start
  87.3 24.2 %all-to-all-start.1 = ((f32[32,32,256]{2,1,0:T(8,128)}), f32[32,32,256]{2,1,0:T(8,128)S(1)}, u32[]{:S(2)}, u32[]{:S(2)}) async-start(f32[32,32,256]{2,1,0:T(8,128)} %copy-done), calls=%async_computation.1 | async-start | bytes 2097152 | tf_op jit(solution)/shard_map/all_to_all | solution.py:394
  112.3 15.5 %all-to-all-start.2 = ((bf16[8,32,256]{2,1,0:T(8,128)(2,1)}), bf16[8,32,256]{2,1,0:T(8,128)(2,1)S(1)}, u32[]{:S(2)}, u32[]{:S(2)}) async-start(bf16[8,32,256]{2,1,0:T(8,128)(2,1)} %broadcast_in_dim.85), calls=%async_computation.2 | async-start | bytes 262144 | tf_op jit(solution)/shard_map/all_to_all | solution.py:398
  129.4 14.3 %all-to-all-start.3 = ((f32[32,8,128]{2,1,0:T(8,128)}), f32[32,8,128]{2,1,0:T(8,128)S(1)}, u32[]{:S(2)}, u32[]{:S(2)}) async-start(f32[32,8,128]{2,1,0:T(8,128)} %make_slots.1), calls=%async_computation.3 | async-start | bytes 262144 | tf_op jit(solution)/shard_map/all_to_all | solution.py:400
  136.9 1.6 %copy-start.2 = (bf16[8192,96]{1,0:T(8,128)(2,1)S(1)}, bf16[8192,96]{1,0:T(8,128)(2,1)}, u32[]{:S(2)}) copy-start(bf16[8192,96]{1,0:T(8,128)(2,1)} %all-gather.2.cloned.1.call-done.coef_ref) | copy-start | bytes 4718596
Sparse Core Ops, SparseCore 0:
  40.0 70.1 all-gather.1

commit v3 on v2

--- a/solution.py
+++ b/solution.py
@@ -78,7 +78,10 @@
         copy.wait()
 
 
-def pair_kernel(row_ref, got_ref, out_ref, real_ref, imag_ref, sums_ref, sem_ref, *sides):
+def pair_kernel(
+    row_ref, start_ref, count_ref, coef_ref, got_ref, out_ref,
+    real_ref, imag_ref, rows_ref, sums_ref, sem_ref, *sides,
+):
     groups, blocks = got_ref.shape[0], got_ref.shape[1] // PACKED
     lane = iota((ROWBLK // 2, 128), 1)
     left, valid = lane < 64, lane < 96
@@ -102,6 +105,10 @@
     tail = groups * blocks * ROWBLK
     real_ref[tail : tail + MAXBF] = jnp.zeros((MAXBF, 128), jnp.float32)
     imag_ref[tail : tail + MAXBF] = jnp.zeros((MAXBF, 128), jnp.float32)
+    bas_dev, width = coef_ref.shape
+    rows_ref[...] = jnp.zeros(rows_ref.shape, jnp.float32)
+    rows_ref[0:bas_dev, 0:width] = coef_ref[...].astype(jnp.float32)
+    row_id = iota((MAXBF, 128), 0)
     lane_pair = lane // MAXBF
     batch = len(sides) // 4
 
@@ -125,8 +132,12 @@
                             here = value[top + j * 16 : top + j * 16 + 16, at : at + 128]
                             part = jnp.where(lane_pair == j, here, part)
                         parts.append(part)
-                sums_ref[g, 0:16, h * 128 : (h + 1) * 128] = parts[0] + parts[3]
-                sums_ref[g, 16:32, h * 128 : (h + 1) * 128] = parts[2] - parts[1]
+                real, imag = parts[0] + parts[3], parts[2] - parts[1]
+                sums_ref[g, h * 32 : h * 32 + 16] = real.astype(jnp.bfloat16)
+                sums_ref[g, h * 32 + 16 : h * 32 + 32] = imag.astype(jnp.bfloat16)
+                rows = rows_ref[pl.ds(start_ref[2 * g + h], MAXBF)]
+                rows = jnp.where(row_id < count_ref[2 * g + h], rows, 0.0)
+                sums_ref[g, 64 + h * 16 : 80 + h * 16] = rows.astype(jnp.bfloat16)
         send(step).start()
         return carry
 
@@ -139,74 +150,49 @@
         send(step).wait()
 
 
-def slot_kernel(scale, place_ref, parts_ref, out_ref, tile_ref):
-    total = parts_ref[0].astype(jnp.float32)
+def gain_kernel(
+    scale, target_ref, rank_ref, place_ref, parts_ref, got_ref, out_ref,
+    first_ref, second_ref, gain_ref,
+):
+    total = parts_ref[0]
     for z in range(1, parts_ref.shape[0]):
-        total = total + parts_ref[z].astype(jnp.float32)
-    kernel = (total * scale).astype(jnp.bfloat16)
-    same = iota((256, 256), 0) // MAXBF == iota((256, 256), 1) // MAXBF
-    u, v = iota((256, 128), 0), iota((256, 128), 1)
-    spot = v % 64 - (v // 64) * MAXBF
-    first = jnp.zeros((256, 128), jnp.float32)
-    for c in range(2):
-        half = kernel[c * MAXBF : (c + 1) * MAXBF].astype(jnp.float32)
-        wide = jnp.concatenate([half] * MAXBF, axis=0)
-        wide = jnp.where(same, wide, 0.0).astype(jnp.bfloat16)
-        fold = jnp.where(spot == c * 32 + u % MAXBF, 1.0, 0.0).astype(jnp.bfloat16)
-        first = first + dot(wide, fold)
-    u, v = iota((32, 128), 0), iota((32, 128), 1)
-    spot = v % 64 - (v // 64) * MAXBF
-    fold = jnp.where(spot == (u // MAXBF) * 32 + u % MAXBF, jnp.where(u < MAXBF, 1.0, -1.0), 0.0)
-    tile_ref[0:256] = first
-    tile_ref[256:512] = dot_tn(kernel, fold.astype(jnp.bfloat16))
-    tile_ref[512:528] = jnp.zeros((MAXBF, 128), jnp.float32)
-    left = iota((8, 128), 1) < 64
-    for d in range(out_ref.shape[0]):
-        one = tile_ref[pl.ds(pl.multiple_of(place_ref[2 * d], MAXBF), MAXBF)]
-        two = tile_ref[pl.ds(pl.multiple_of(place_ref[2 * d + 1], MAXBF), MAXBF)]
-        both = one + pltpu.roll(two, 64, 1)
-        out_ref[d] = jnp.where(left, both[0:8], pltpu.roll(both[8:16], 64, 1))
-
-
-def coef_kernel(row_ref, count_ref, coef_ref, out_ref):
-    u, v = iota((96, 96), 0), iota((96, 96), 1)
-    turn = jnp.where(u == (v + 48) % 96, jnp.where(v < 48, -1.0, 1.0), 0.0).astype(jnp.bfloat16)
-    row_id = iota((MAXBF, 96), 0)
-
-    def owner(g, carry):
-        picked = []
-        for r in range(2):
-            row = row_ref[2 * g + r]
-            base = jnp.minimum((row // 16) * 16, coef_ref.shape[0] - 32)
-            base = pl.multiple_of(base, 16)
-            wide = coef_ref[pl.ds(base, 32)].astype(jnp.float32)
-            rows = pltpu.roll(wide, lax.rem(32 - (row - base), 32), 0)[0:MAXBF]
-            picked.append(jnp.where(row_id < count_ref[2 * g + r], rows, 0.0))
-        rows = jnp.concatenate(picked, axis=0).astype(jnp.bfloat16)
-        out_ref[g, 0:32] = rows
-        out_ref[g, 32:64] = dot(rows, turn).astype(jnp.bfloat16)
-        return carry
-
-    lax.fori_loop(0, out_ref.shape[0], owner, 0)
-
-
-def gain_kernel(row_ref, count_ref, slot_ref, coef_ref, out_ref, sum_ref):
+        total = total + parts_ref[z]
+    kernel = (total * scale).astype(jnp.bfloat16).astype(jnp.float32)
+    for e in range(2 * MAXBF):
+        dest = second_ref if e % 2 else first_ref
+        at = pl.multiple_of(64 + rank_ref[e] * MAXBF, MAXBF)
+        place = (e // 2) * MAXBF
+        dest[place : place + MAXBF] = got_ref[target_ref[e], pl.ds(at, MAXBF)]
+    u, v = iota((128, 128), 0), iota((128, 128), 1)
+    turn = jnp.where((v < 48) & (u == v + 48), -1.0, 0.0)
+    turn = jnp.where((v >= 48) & (v < 96) & (u == v - 48), 1.0, turn).astype(jnp.bfloat16)
+    same = u // MAXBF == v // MAXBF
+    for h in range(2):
+        rows = slice(h * 128, (h + 1) * 128)
+        first, second = first_ref[rows], second_ref[rows]
+        wide = []
+        for c in range(2):
+            tile = kernel[h * 32 + c * MAXBF : h * 32 + (c + 1) * MAXBF]
+            tile = jnp.concatenate([tile] * 8, axis=0)
+            wide.append(jnp.where(same, tile, 0.0).astype(jnp.bfloat16))
+        turned = dot(second, turn).astype(jnp.bfloat16)
+        gain_ref[rows] = dot(wide[0], second) + dot(wide[1], turned)
+        turned = dot(first, turn).astype(jnp.bfloat16)
+        gain_ref[256 + h * 128 : 384 + h * 128] = dot_tn(wide[0], first) - dot_tn(wide[1], turned)
+    gain_ref[512:528] = jnp.zeros((MAXBF, 128), jnp.float32)
+    for s in range(2 * out_ref.shape[0]):
+        at = pl.ds(pl.multiple_of(place_ref[s], MAXBF), MAXBF)
+        out_ref[s // 2, (s % 2) * MAXBF : (s % 2 + 1) * MAXBF] = gain_ref[at]
+
+
+def add_kernel(start_ref, count_ref, gain_ref, out_ref, sum_ref):
     sum_ref[...] = jnp.zeros(sum_ref.shape, jnp.float32)
-    lane = iota((MAXBF, 64), 1) % 32
-    row_id = iota((MAXBF, 96), 0)
-    for g in range(slot_ref.shape[0]):
-        pair = slot_ref[g]
-        tile = jnp.concatenate([pair, pltpu.roll(pair, 64, 1)], axis=0)[:, 0:64]
-        upper = jnp.where(lane < MAXBF, tile, 0.0)
-        lower = jnp.where(lane >= MAXBF, tile, 0.0)
-        both = jnp.concatenate([upper, lower], axis=0).astype(jnp.bfloat16)
-        gains = dot(both, coef_ref[g])
-        for r in range(2):
-            part = gains[r * MAXBF : (r + 1) * MAXBF]
-            part = jnp.where(row_id < count_ref[2 * g + r], part, 0.0)
-            where = pl.ds(row_ref[2 * g + r], MAXBF)
-            sum_ref[where, 0:96] = sum_ref[where, 0:96] + part
-    out_ref[...] = sum_ref[0:256].T[0:96]
+    row_id = iota((MAXBF, 128), 0)
+    for s in range(2 * gain_ref.shape[0]):
+        part = gain_ref[s // 2, (s % 2) * MAXBF : (s % 2 + 1) * MAXBF]
+        where = pl.ds(start_ref[s], MAXBF)
+        sum_ref[where] = sum_ref[where] + jnp.where(row_id < count_ref[s], part, 0.0)
+    out_ref[...] = sum_ref[0 : out_ref.shape[1]].T[0 : out_ref.shape[0]]
 
 
 def vmem_spec():
@@ -230,7 +216,7 @@
         fit_kernel,
         in_specs=[vmem_spec()] * 7,
         out_specs=pl.BlockSpec(memory_space=pltpu.HBM),
-        out_shape=jax.ShapeDtypeStruct(shape, jnp.bfloat16),
+        out_shape=pltpu.HBM(shape, jnp.bfloat16),
         scratch_shapes=[
             pltpu.VMEM((window, width), jnp.bfloat16),
             pltpu.VMEM(shape, jnp.bfloat16),
@@ -246,62 +232,57 @@
     )(integrals, low, own, high, order, mix, meta)
 
 
-def pair_sums(end_rows, got):
+def pair_sums(end_rows, starts, counts, coef, got):
     groups = got.shape[0]
     rows = groups * (got.shape[1] // PACKED) * ROWBLK + MAXBF
+    shape = (groups, 6 * MAXBF, 128)
     return pl.pallas_call(
         pair_kernel,
-        in_specs=[smem_spec(), vmem_spec()],
+        in_specs=[smem_spec()] * 3 + [vmem_spec()] * 2,
         out_specs=pl.BlockSpec(memory_space=pltpu.HBM),
-        out_shape=jax.ShapeDtypeStruct((groups, 2 * MAXBF, 256), jnp.float32),
+        out_shape=pltpu.HBM(shape, jnp.bfloat16),
         scratch_shapes=[
             pltpu.VMEM((rows, 128), jnp.float32),
             pltpu.VMEM((rows, 128), jnp.float32),
-            pltpu.VMEM((groups, 2 * MAXBF, 256), jnp.float32),
+            pltpu.VMEM((coef.shape[0] + MAXBF, 128), jnp.float32),
+            pltpu.VMEM(shape, jnp.bfloat16),
             pltpu.SemaphoreType.DMA((groups // BATCH,)),
         ]
         + [pltpu.VMEM((256, 128), jnp.bfloat16)] * (4 * BATCH),
         compiler_params=limit(40),
         name="pair_sums",
-    )(end_rows, got)
-
-
-def make_slots(scale, places, parts, groups):
+    )(end_rows, starts, counts, coef, got)
+
+
+def make_gains(scale, targets, ranks, places, parts, got):
     def body(*refs):
-        slot_kernel(scale, *refs)
+        gain_kernel(scale, *refs)
 
     return pl.pallas_call(
         body,
-        in_specs=[smem_spec(), vmem_spec()],
+        in_specs=[smem_spec()] * 3 + [vmem_spec()] * 2,
         out_specs=vmem_spec(),
-        out_shape=jax.ShapeDtypeStruct((groups, 8, 128), jnp.float32),
-        scratch_shapes=[pltpu.VMEM((528, 128), jnp.float32)],
+        out_shape=jax.ShapeDtypeStruct((got.shape[0], 2 * MAXBF, 128), jnp.float32),
+        scratch_shapes=[
+            pltpu.VMEM((256, 128), jnp.bfloat16),
+            pltpu.VMEM((256, 128), jnp.bfloat16),
+            pltpu.VMEM((528, 128), jnp.float32),
+        ],
         compiler_params=limit(16),
-        name="make_slots",
-    )(places, parts)
-
-
-def partner_coef(rows, counts, coef, groups):
+        name="make_gains",
+    )(targets, ranks, places, parts, got)
+
+
+def add_gains(starts, counts, gains, width, bas_dev):
     return pl.pallas_call(
-        coef_kernel,
-        in_specs=[smem_spec(), smem_spec(), vmem_spec()],
+        add_kernel,
+        in_specs=[smem_spec()] * 2 + [vmem_spec()],
         out_specs=vmem_spec(),
-        out_shape=jax.ShapeDtypeStruct((groups, 64, coef.shape[1]), jnp.bfloat16),
-        compiler_params=limit(16),
-        name="partner_coef",
-    )(rows, counts, coef)
-
-
-def add_gains(rows, counts, slots, partner, bas_dev):
-    return pl.pallas_call(
-        gain_kernel,
-        in_specs=[smem_spec(), smem_spec(), vmem_spec(), vmem_spec()],
-        out_specs=vmem_spec(),
-        out_shape=jax.ShapeDtypeStruct((partner.shape[2], bas_dev), jnp.float32),
+        out_shape=jax.ShapeDtypeStruct((width, bas_dev), jnp.float32),
         scratch_shapes=[pltpu.VMEM((bas_dev + MAXBF, 128), jnp.float32)],
         compiler_params=limit(16),
         name="add_gains",
-    )(rows, counts, slots, partner)
+    )(starts, counts, gains)
 
 
 def pick(hit, values):
@@ -343,12 +324,10 @@
     mix = metric.T[:, None, :, None] * jnp.eye(ROWBLK, dtype=jnp.bfloat16)[None, :, None, :]
     mix = mix.reshape(aux_dev * ROWBLK, aux_dev * ROWBLK)
     packed = fit(integrals, low, own, high, jnp.asarray(column_order(occ)), mix, meta)
-    coef_part, packed = lax.optimization_barrier((coeffs, packed))
     got = lax.all_to_all(packed, "atom", split_axis=0, concat_axis=0, tiled=True)
     coef_part = lax.dynamic_slice_in_dim(
-        coef_part, lax.axis_index("aux") * occ_part, occ_part, 2
+        coeffs, lax.axis_index("aux") * occ_part, occ_part, 2
     ).reshape(bas_dev, 2 * occ_part)
-    all_coef = lax.all_gather(coef_part, "atom", axis=0, tiled=True)
 
     all_meta = got[:, got.shape[1] - 16, : 2 * occ_part].astype(jnp.int32)
     sizes = all_meta[:, :atom_count]
@@ -372,14 +351,8 @@
     slot = here[:, None, :] & (rank[:, None, :] == jnp.arange(2, dtype=jnp.int32)[None, :, None])
     end_start, end_size = end_start.reshape(groups, ref_count), end_size.reshape(groups, ref_count)
 
-    def partner(x):
-        return x.reshape(groups, ref_count // 2, 2)[:, :, ::-1].reshape(groups, ref_count)
-
-    gather_rows = devices * bas_dev + end_start
     slot_start = pick(slot, end_start[:, None, :]).reshape(-1)
     slot_size = pick(slot, end_size[:, None, :]).reshape(-1)
-    other_row = pick(slot, partner(gather_rows)[:, None, :]).reshape(-1)
-    other_size = pick(slot, partner(end_size)[:, None, :]).reshape(-1)
 
     targets = pair_device[:, 0]
     order = jnp.arange(ref_count, dtype=jnp.int32)
@@ -390,16 +363,15 @@
     asked_hit = asked[None, :] == jnp.arange(2 * groups, dtype=jnp.int32)[:, None]
     places = 512 + pick(asked_hit, place[None, :] - 512)
 
-    partial_sums = pair_sums(end_rows, got)
-    owned = lax.all_to_all(partial_sums, "atom", split_axis=0, concat_axis=0, tiled=True)
-    partner_rows = partner_coef(other_row, other_size, all_coef, groups)
-    owned = jnp.sum(owned, axis=0).astype(jnp.bfloat16)
-    shared = jnp.broadcast_to(owned[None], (aux_count,) + owned.shape)
+    sent = pair_sums(end_rows, slot_start, slot_size, coef_part, got)
+    owned = lax.all_to_all(sent, "atom", split_axis=0, concat_axis=0, tiled=True)
+    own_sums = jnp.sum(owned[:, : 4 * MAXBF].astype(jnp.float32), axis=0)
+    shared = jnp.broadcast_to(own_sums[None], (aux_count,) + own_sums.shape)
     parts = lax.all_to_all(shared, "aux", split_axis=0, concat_axis=0, tiled=True)
-    slots = make_slots(scale, places, parts, groups)
-    slots = lax.all_to_all(slots, "atom", split_axis=0, concat_axis=0, tiled=True)
-    gains = add_gains(slot_start, slot_size, slots, partner_rows, bas_dev)
-    return gains.reshape(2, occ_part, bas_dev).transpose(2, 0, 1)
+    gains = make_gains(scale, targets, ranks, places, parts, owned)
+    gains = lax.all_to_all(gains, "atom", split_axis=0, concat_axis=0, tiled=True)
+    result = add_gains(slot_start, slot_size, gains, 2 * occ_part, bas_dev)
+    return result.reshape(2, occ_part, bas_dev).transpose(2, 0, 1)
 
 
 def solution(mesh):

time: 153 us -> 138 us (0.902)
  blocking collectives: 0 us -> 15.4 us
  between operations: 13.7 us -> 0.21 us
  local copies, waits for them, and re-layouts: 15.1 us -> 7.63 us
  Pallas kernels: 20.5 us -> 14.9 us
  starting transfers between devices: 33.3 us -> 28.8 us
    all_to_all x0 -> x1, blocking collectives: none -> 15.4 us  [per_device(): lax.all_to_all(gains, 'atom', split_axis=0, concat_axis=0, tiled=True)]
    pallas_call x4 -> x3, Pallas kernels: 15.2 us -> 9.86 us  [the longest x1 7.31 us: pair_sums(): pl.pallas_call(pair_kernel, in_specs=[smem_spec()] * 3 + [vmem_spec()] *...]
    all_to_all x2 -> x1, starting transfers between devices: 10.6 us -> 5.68 us  [per_device(): lax.all_to_all(sent, 'atom', split_axis=0, concat_axis=0, tiled=True)]
    all_to_all x1, waiting for transfers between devices: 7.36 us -> 12.3 us  [per_device(): lax.all_to_all(shared, 'aux', split_axis=0, concat_axis=0, tiled=True)]
    all_to_all x2 -> x1, waiting for transfers between devices: 18.9 us -> 14 us  [per_device(): lax.all_to_all(sent, 'atom', split_axis=0, concat_axis=0, tiled=True)]
    unnamed x17 -> x12, local copies, waits for them, and re-layouts: 6.63 us -> 2.47 us
    optimization_barrier x1 -> x0, local copies, waits for them, and re-layouts: 1.95 us -> none  [per_device(): coef_part, packed = lax.optimization_barrier((coeffs, packed))]
  transfers between devices with their start and end apart: 7 -> 5, of which waited for: 4 -> 4; matrix products, arithmetic and copies ran while one was open for 8% -> 4% of each run, Pallas kernels for 9% -> 0%
where the time goes in v3:
time: 138 us
  waiting for transfers between devices  67.3 us (49%)
  starting transfers between devices  28.8 us (21%)
  blocking collectives  15.4 us (11%)
  Pallas kernels  14.9 us (11%)
  local copies, waits for them, and re-layouts  7.63 us (6%)
  other arithmetic  3.34 us (2%)
    all_to_all x1, waiting for transfers between devices, per_device(): lax.all_to_all(packed, 'atom', split_axis=0, concat_axis=0, tiled=True)  39.7 us
    all_to_all x1, blocking collectives, per_device(): lax.all_to_all(gains, 'atom', split_axis=0, concat_axis=0, tiled=True)  15.4 us
    all_to_all x1, waiting for transfers between devices, per_device(): lax.all_to_all(sent, 'atom', split_axis=0, concat_axis=0, tiled=True)  14 us
    all_to_all x1, waiting for transfers between devices, per_device(): lax.all_to_all(shared, 'aux', split_axis=0, concat_axis=0, tiled=True)  12.3 us
    all_to_all x1, starting transfers between devices, per_device(): lax.all_to_all(packed, 'atom', split_axis=0, concat_axis=0, tiled=True)  8.42 us
    all_to_all x1, starting transfers between devices, per_device(): lax.all_to_all(shared, 'aux', split_axis=0, concat_axis=0, tiled=True)  8.2 us
    pallas_call x1, Pallas kernels, pair_sums(): pl.pallas_call(pair_kernel, in_specs=[smem_spec()] * 3 + [vmem_spec()] *...  7.31 us
    all_to_all x1, starting transfers between devices, per_device(): lax.all_to_all(sent, 'atom', split_axis=0, concat_axis=0, tiled=True)  5.68 us
  transfers between devices with their start and end apart: 5, of which 4 were waited for; matrix products, arithmetic and copies ran while one was open for 4% of the time, Pallas kernels for 0%

profile of v3, /device:TPU:1, one launch (start us, length us, event | category | flops | bytes accessed | tf_op | source)
XLA Modules:
  0.0 137.6 jit_solution(7984712146030093627)
XLA Ops:
  0.0 1.4 %fusion.22 = (bf16[128,2,384]{2,1,0:T(2,128)(2,1)S(1)}, bf16[128,2,384]{2,1,0:T(2,128)(2,1)S(1)}) fusion(bf16[256,2,384]{2,1,0:T(2,128)(2,1)} %param.8), kind=kLoop, calls=%fused_computation.62 | loop fusion | bytes 786432 | tf_op jit(solution)/shard_map/slice | solution.py:320
  1.5 4.6 %collective-permute-start = (bf16[128,768]{1,0:T(8,128)(2,1)S(1)}, bf16[128,768]{1,0:T(8,128)(2,1)S(1)}, u32[]{:S(2)}, u32[]{:S(2)}) collective-permute-start(bf16[128,768]{1,0:T(8,128)(2,1)S(1)} %bitcast.30), channel_id=1, source_target_pairs={{0,8},{8,16},{16,24},{24,32},{32,40},{40,48},{48,56},{56,64},{64,7... | collective-permute-start | bytes 589832 | tf_op jit(solution)/shard_map/ppermute | solution.py:319
  6.1 1.9 %collective-permute-start.1 = (bf16[128,768]{1,0:T(8,128)(2,1)S(1)}, bf16[128,768]{1,0:T(8,128)(2,1)S(1)}, u32[]{:S(2)}, u32[]{:S(2)}) collective-permute-start(bf16[128,768]{1,0:T(8,128)(2,1)S(1)} %bitcast.31), channel_id=1, source_target_pairs={{8,0},{16,8},{24,16},{32,24},{40,32},{48,40},{56,48},{64,56},{72,6... | collective-permute-start | bytes 589832 | tf_op jit(solution)/shard_map/ppermute | solution.py:320
  8.1 0.8 copy.12
  8.8 0.7 convert_bitcast_fusion
  9.5 0.1 broadcast_multiply_fusion
  9.6 0.7 convert_bitcast_fusion.1
  10.3 0.3 mul.65.mix_ref
  10.6 1.0 copy.19
  11.8 1.3 collective-permute-done.1.high_ref
  13.1 1.3 copy-done.2
  14.4 5.1 %fit.1 = bf16[32,400,128]{2,1,0:T(8,128)(2,1)} custom-call(bf16[8,256,512]{2,1,0:T(8,128)(2,1)S(1)} %copy-done.1, bf16[128,768]{1,0:T(8,128)(2,1)S(1)} %collective-permute-done.low_ref, bf16[256,768]{1,0:T(8,128)(2,1)S(1)} %bitcast.21, bf16[128,768]{1,0:T(8,128)(2,1)S(1)} %collective-permute-done.1.high_ref, bf16[768,768]{1,0:T(8,128)(2,1)S(1)} %copy-done.2, ...), custom_call_target="tpu_custom_call" | custom-call | flops 2415919104 | bytes 6291456 | tf_op jit(solution)/shard_map/fit/pallas_call | solution.py:215
  19.4 8.4 %all-to-all-start = ((bf16[32,400,128]{2,1,0:T(8,128)(2,1)}), bf16[32,400,128]{2,1,0:T(8,128)(2,1)S(1)}, u32[]{:S(2)}, u32[]{:S(2)}) async-start(bf16[32,400,128]{2,1,0:T(8,128)(2,1)} %fit.1), calls=%async_computation | async-start | bytes 6553600 | tf_op jit(solution)/shard_map/all_to_all | solution.py:327
  27.9 1.2 constant_dynamic-slice_fusion
  29.2 0.1 copy.16.coef_ref
  29.3 39.7 %all-to-all-done.got_ref = bf16[32,400,128]{2,1,0:T(8,128)(2,1)S(1)} async-done(((bf16[32,400,128]{2,1,0:T(8,128)(2,1)}), bf16[32,400,128]{2,1,0:T(8,128)(2,1)S(1)}, u32[]{:S(2)}, u32[]{:S(2)}) %all-to-all-start) | async-done | bytes 3276832 | tf_op jit(solution)/shard_map/all_to_all | solution.py:327
  69.0 0.2 reduce_window_sum.18
  69.4 0.7 select_reduce_fusion
  70.3 0.2 reduce_window_sum.17
  70.5 0.2 select_reduce_fusion.1
  70.7 0.1 reshape.222.start_ref
  71.0 0.1 reshape.223.count_ref
  71.1 7.3 %pair_sums.1 = bf16[32,96,128]{2,1,0:T(8,128)(2,1)} custom-call(s32[1024]{0:T(1024)S(1)} %fusion.15.row_ref, s32[64]{0:T(128)S(1)} %reshape.222.start_ref, s32[64]{0:T(128)S(1)} %reshape.223.count_ref, bf16[256,96]{1,0:T(8,128)(2,1)S(1)} %copy.16.coef_ref, bf16[32,400,128]{2,1,0:T(8,128)(2,1)S(1)} %all-to-all-done.got_ref), custom_call_target="tpu_custom_call" | custom-call | tf_op jit(solution)/shard_map/pair_sums/pallas_call | solution.py:239
  78.4 5.7 %all-to-all-start.1 = ((bf16[32,96,128]{2,1,0:T(8,128)(2,1)}), bf16[32,96,128]{2,1,0:T(8,128)(2,1)S(1)}, u32[]{:S(2)}, u32[]{:S(2)}) async-start(bf16[32,96,128]{2,1,0:T(8,128)(2,1)} %pair_sums.1), calls=%async_computation.1 | async-start | bytes 1572864 | tf_op jit(solution)/shard_map/all_to_all | solution.py:367
  84.1 0.2 convert_reduce_fusion.1.refs_1_
  84.3 14.0 %all-to-all-done.1.refs_4_ = bf16[32,96,128]{2,1,0:T(8,128)(2,1)S(1)} async-done(((bf16[32,96,128]{2,1,0:T(8,128)(2,1)}), bf16[32,96,128]{2,1,0:T(8,128)(2,1)S(1)}, u32[]{:S(2)}, u32[]{:S(2)}) %all-to-all-start.1) | async-done | bytes 786464 | tf_op jit(solution)/shard_map/all_to_all | solution.py:367
  98.4 0.7 broadcast_in_dim.69
  99.1 8.2 %all-to-all-start.2 = ((f32[8,64,128]{2,1,0:T(8,128)}), f32[8,64,128]{2,1,0:T(8,128)S(1)}, u32[]{:S(2)}, u32[]{:S(2)}) async-start(f32[8,64,128]{2,1,0:T(8,128)} %broadcast_in_dim.69), calls=%async_computation.2 | async-start | bytes 524288 | tf_op jit(solution)/shard_map/all_to_all | solution.py:370
  107.4 12.3 %all-to-all-done.2.refs_3_ = f32[8,64,128]{2,1,0:T(8,128)S(1)} async-done(((f32[8,64,128]{2,1,0:T(8,128)}), f32[8,64,128]{2,1,0:T(8,128)S(1)}, u32[]{:S(2)}, u32[]{:S(2)}) %all-to-all-start.2) | async-done | bytes 262176 | tf_op jit(solution)/shard_map/all_to_all | solution.py:370
  119.7 1.0 make_gains.1
  120.7 15.4 %all_to_all.20.gain_ref = f32[32,32,128]{2,1,0:T(8,128)S(1)} all-to-all(f32[32,32,128]{2,1,0:T(8,128)S(1)} %make_gains.1), channel_id=1, replica_groups=mesh['atom'=32,'aux'=8] {'atom'}, dimensions={0} | all-to-all | bytes 1048576 | tf_op jit(solution)/shard_map/all_to_all | solution.py:372
  136.0 1.6 %add_gains.1 = f32[96,256]{1,0:T(8,128)} custom-call(s32[64]{0:T(128)S(1)} %reshape.222.start_ref, s32[64]{0:T(128)S(1)} %reshape.223.count_ref, f32[32,32,128]{2,1,0:T(8,128)S(1)} %all_to_all.20.gain_ref), custom_call_target="tpu_custom_call" | custom-call | tf_op jit(solution)/shard_map/add_gains/pallas_call | solution.py:277
  (31 shorter events, 1.1 us)
Async XLA Ops:
  0.0 11.7 %copy-start.3 = (s32[1,32]{1,0:T(1,128)S(1)}, s32[1,32]{1,0:T(1,128)}, u32[]{:S(2)}) copy-start(s32[1,32]{1,0:T(1,128)} %param.10) | copy-start | bytes 388
  0.0 13.1 %copy-start.1 = (bf16[8,256,512]{2,1,0:T(8,128)(2,1)S(1)}, bf16[8,256,512]{2,1,0:T(8,128)(2,1)}, u32[]{:S(2)}) copy-start(bf16[8,256,512]{2,1,0:T(8,128)(2,1)} %ints_ref.1) | copy-start | bytes 6291460
  1.5 10.3 %collective-permute-start = (bf16[128,768]{1,0:T(8,128)(2,1)S(1)}, bf16[128,768]{1,0:T(8,128)(2,1)S(1)}, u32[]{:S(2)}, u32[]{:S(2)}) collective-permute-start(bf16[128,768]{1,0:T(8,128)(2,1)S(1)} %bitcast.30), channel_id=1, source_target_pairs={{0,8},{8,16},{16,24},{24,32},{32,40},{40,48},{48,56},{56,64},{64,7... | collective-permute-start | bytes 589832 | tf_op jit(solution)/shard_map/ppermute | solution.py:319
  6.1 7.0 %collective-permute-start.1 = (bf16[128,768]{1,0:T(8,128)(2,1)S(1)}, bf16[128,768]{1,0:T(8,128)(2,1)S(1)}, u32[]{:S(2)}, u32[]{:S(2)}) collective-permute-start(bf16[128,768]{1,0:T(8,128)(2,1)S(1)} %bitcast.31), channel_id=1, source_target_pairs={{8,0},{16,8},{24,16},{32,24},{40,32},{48,40},{56,48},{64,56},{72,6... | collective-permute-start | bytes 589832 | tf_op jit(solution)/shard_map/ppermute | solution.py:320
  13.1 1.3 copy-start.2
  19.4 49.5 %all-to-all-start = ((bf16[32,400,128]{2,1,0:T(8,128)(2,1)}), bf16[32,400,128]{2,1,0:T(8,128)(2,1)S(1)}, u32[]{:S(2)}, u32[]{:S(2)}) async-start(bf16[32,400,128]{2,1,0:T(8,128)(2,1)} %fit.1), calls=%async_computation | async-start | bytes 6553600 | tf_op jit(solution)/shard_map/all_to_all | solution.py:327
  29.1 54.9 %copy-start = (s32[32,1]{0,1:T(1,128)S(1)}, s32[32,1]{0,1:T(1,128)}, u32[]{:S(2)}) copy-start(s32[32,1]{0,1:T(1,128)} %param.11) | copy-start | bytes 388
  78.4 19.9 %all-to-all-start.1 = ((bf16[32,96,128]{2,1,0:T(8,128)(2,1)}), bf16[32,96,128]{2,1,0:T(8,128)(2,1)S(1)}, u32[]{:S(2)}, u32[]{:S(2)}) async-start(bf16[32,96,128]{2,1,0:T(8,128)(2,1)} %pair_sums.1), calls=%async_computation.1 | async-start | bytes 1572864 | tf_op jit(solution)/shard_map/all_to_all | solution.py:367
  99.1 20.6 %all-to-all-start.2 = ((f32[8,64,128]{2,1,0:T(8,128)}), f32[8,64,128]{2,1,0:T(8,128)S(1)}, u32[]{:S(2)}, u32[]{:S(2)}) async-start(f32[8,64,128]{2,1,0:T(8,128)} %broadcast_in_dim.69), calls=%async_computation.2 | async-start | bytes 524288 | tf_op jit(solution)/shard_map/all_to_all | solution.py:370

commit v4 on v2

--- a/solution.py
+++ b/solution.py
@@ -2,7 +2,6 @@
 
 import jax
 import jax.numpy as jnp
-import numpy as np
 from jax import lax
 from jax.experimental import pallas as pl
 from jax.experimental.pallas import tpu as pltpu
@@ -32,14 +31,32 @@
 
 
 def fit_kernel(
-    ints_ref, low_ref, own_ref, high_ref, order_ref, mix_ref, meta_ref, out_ref,
-    window_ref, packed_ref, sem_ref,
+    ints_ref, low_ref, own_ref, high_ref, metric_ref, size_ref, dev_ref, atom_ref, out_ref,
+    window_ref, packed_ref, meta_ref, sem_ref,
 ):
+    u, v = iota((256, 256), 0), iota((256, 256), 1)
+    main_order = u == ((v % 128) // 64) * 128 + (v // 128) * 64 + v % 64
+    side_order = u == ((v % 64) // 32) * 128 + (v // 64) * 32 + v % 32
+    main_order = jnp.where(main_order, 1.0, 0.0).astype(jnp.bfloat16)
+    side_order = jnp.where(side_order, 1.0, 0.0).astype(jnp.bfloat16)
     at = 0
     for part_ref in (low_ref, own_ref, high_ref):
         rows = part_ref.shape[0]
-        window_ref[at : at + rows] = dot(part_ref[...], order_ref[...]).astype(jnp.bfloat16)
+        half = part_ref.shape[1] // 2
+        for t in range(3):
+            real = part_ref[:, t * 128 : (t + 1) * 128]
+            imag = part_ref[:, half + t * 128 : half + (t + 1) * 128]
+            order = side_order if t == 2 else main_order
+            value = dot(jnp.concatenate([real, imag], axis=1), order)
+            window_ref[at : at + rows, t * 256 : (t + 1) * 256] = value.astype(jnp.bfloat16)
         at += rows
+    member = iota((256, 8), 0) // ROWBLK == iota((256, 8), 1)
+    member = jnp.where(member, 1.0, 0.0).astype(jnp.bfloat16)
+    mix = dot_nt(dot_nt(member, metric_ref[...]).astype(jnp.bfloat16), member)
+    mix = jnp.where(u % ROWBLK == v % ROWBLK, mix, 0.0).astype(jnp.bfloat16)
+    meta_ref[...] = jnp.zeros(meta_ref.shape, jnp.float32)
+    for row, value_ref in enumerate((size_ref, dev_ref, atom_ref)):
+        meta_ref[row : row + 1, 0 : value_ref.shape[1]] = value_ref[...].astype(jnp.float32)
     aux_dev, bas_dev, span = ints_ref.shape
     blocks = bas_dev // ROWBLK
     left = iota((ROWBLK // 2, 128), 1) < 64
@@ -47,7 +64,7 @@
     for u in range(blocks):
         ints = ints_ref[:, u * ROWBLK : (u + 1) * ROWBLK].reshape(aux_dev * ROWBLK, span)
         half = dot(ints, window_ref[...]).astype(jnp.bfloat16)
-        fitted = dot(mix_ref[...], half)
+        fitted = dot(mix, half)
         main = slice(u * PACKED, u * PACKED + ROWBLK)
         side = slice(u * PACKED + ROWBLK, (u + 1) * PACKED)
         for p in range(aux_dev):
@@ -64,7 +81,9 @@
                 packed_ref[p * 4 + 2 * k + 1, side] = odd.astype(jnp.bfloat16)
         if u == blocks - 1:
             for d in range(4 * aux_dev):
-                packed_ref[d, blocks * PACKED : blocks * PACKED + 16] = meta_ref[...]
+                packed_ref[d, blocks * PACKED : blocks * PACKED + 16] = meta_ref[...].astype(
+                    jnp.bfloat16
+                )
         if u % 2 == 1:
             first = (u - 1) * PACKED
             span_rows = pl.ds(first, 2 * PACKED + (16 if u == blocks - 1 else 0))
@@ -125,8 +144,9 @@
                             here = value[top + j * 16 : top + j * 16 + 16, at : at + 128]
                             part = jnp.where(lane_pair == j, here, part)
                         parts.append(part)
-                sums_ref[g, 0:16, h * 128 : (h + 1) * 128] = parts[0] + parts[3]
-                sums_ref[g, 16:32, h * 128 : (h + 1) * 128] = parts[2] - parts[1]
+                real, imag = parts[0] + parts[3], parts[2] - parts[1]
+                sums_ref[g, h * 32 : h * 32 + 16] = real.astype(jnp.bfloat16)
+                sums_ref[g, h * 32 + 16 : h * 32 + 32] = imag.astype(jnp.bfloat16)
         send(step).start()
         return carry
 
@@ -144,21 +164,23 @@
     for z in range(1, parts_ref.shape[0]):
         total = total + parts_ref[z].astype(jnp.float32)
     kernel = (total * scale).astype(jnp.bfloat16)
-    same = iota((256, 256), 0) // MAXBF == iota((256, 256), 1) // MAXBF
-    u, v = iota((256, 128), 0), iota((256, 128), 1)
+    u, v = iota((128, 128), 0), iota((128, 128), 1)
+    same = u // MAXBF == v // MAXBF
     spot = v % 64 - (v // 64) * MAXBF
-    first = jnp.zeros((256, 128), jnp.float32)
-    for c in range(2):
-        half = kernel[c * MAXBF : (c + 1) * MAXBF].astype(jnp.float32)
-        wide = jnp.concatenate([half] * MAXBF, axis=0)
-        wide = jnp.where(same, wide, 0.0).astype(jnp.bfloat16)
-        fold = jnp.where(spot == c * 32 + u % MAXBF, 1.0, 0.0).astype(jnp.bfloat16)
-        first = first + dot(wide, fold)
+    folds = [jnp.where(spot == c * 32 + u % MAXBF, 1.0, 0.0).astype(jnp.bfloat16) for c in range(2)]
     u, v = iota((32, 128), 0), iota((32, 128), 1)
     spot = v % 64 - (v // 64) * MAXBF
-    fold = jnp.where(spot == (u // MAXBF) * 32 + u % MAXBF, jnp.where(u < MAXBF, 1.0, -1.0), 0.0)
-    tile_ref[0:256] = first
-    tile_ref[256:512] = dot_tn(kernel, fold.astype(jnp.bfloat16))
+    turned = jnp.where(spot == (u // MAXBF) * 32 + u % MAXBF, jnp.where(u < MAXBF, 1.0, -1.0), 0.0)
+    turned = turned.astype(jnp.bfloat16)
+    for h in range(2):
+        block = kernel[h * 32 : (h + 1) * 32]
+        first = jnp.zeros((128, 128), jnp.float32)
+        for c in range(2):
+            tile = block[c * MAXBF : (c + 1) * MAXBF].astype(jnp.float32)
+            wide = jnp.where(same, jnp.concatenate([tile] * 8, axis=0), 0.0)
+            first = first + dot(wide.astype(jnp.bfloat16), folds[c])
+        tile_ref[h * 128 : (h + 1) * 128] = first
+        tile_ref[256 + h * 128 : 384 + h * 128] = dot_tn(block, turned)
     tile_ref[512:528] = jnp.zeros((MAXBF, 128), jnp.float32)
     left = iota((8, 128), 1) < 64
     for d in range(out_ref.shape[0]):
@@ -168,26 +190,27 @@
         out_ref[d] = jnp.where(left, both[0:8], pltpu.roll(both[8:16], 64, 1))
 
 
-def coef_kernel(row_ref, count_ref, coef_ref, out_ref):
-    u, v = iota((96, 96), 0), iota((96, 96), 1)
-    turn = jnp.where(u == (v + 48) % 96, jnp.where(v < 48, -1.0, 1.0), 0.0).astype(jnp.bfloat16)
-    row_id = iota((MAXBF, 96), 0)
+def coef_kernel(block_ref, start_ref, count_ref, coef_ref, out_ref):
+    width, bas_dev = coef_ref.shape[1:]
+    u, v = iota((width, width), 0), iota((width, width), 1)
+    half = width // 2
+    turn = jnp.where(u == (v + half) % width, jnp.where(v < half, -1.0, 1.0), 0.0)
+    turn = turn.astype(jnp.bfloat16)
+    row, spot = iota((MAXBF, bas_dev), 0), iota((MAXBF, bas_dev), 1)
 
     def owner(g, carry):
         picked = []
         for r in range(2):
-            row = row_ref[2 * g + r]
-            base = jnp.minimum((row // 16) * 16, coef_ref.shape[0] - 32)
-            base = pl.multiple_of(base, 16)
-            wide = coef_ref[pl.ds(base, 32)].astype(jnp.float32)
-            rows = pltpu.roll(wide, lax.rem(32 - (row - base), 32), 0)[0:MAXBF]
-            picked.append(jnp.where(row_id < count_ref[2 * g + r], rows, 0.0))
+            s = 2 * g + r
+            hit = (spot == start_ref[s] + row) & (row < count_ref[s])
+            hit = jnp.where(hit, 1.0, 0.0).astype(jnp.bfloat16)
+            picked.append(dot_nt(hit, coef_ref[block_ref[s]]))
         rows = jnp.concatenate(picked, axis=0).astype(jnp.bfloat16)
         out_ref[g, 0:32] = rows
         out_ref[g, 32:64] = dot(rows, turn).astype(jnp.bfloat16)
         return carry
 
-    lax.fori_loop(0, out_ref.shape[0], owner, 0)
+    lax.fori_loop(0, out_ref.shape[0], owner, 0, unroll=4)
 
 
 def gain_kernel(row_ref, count_ref, slot_ref, coef_ref, out_ref, sum_ref):
@@ -206,7 +229,7 @@
             part = jnp.where(row_id < count_ref[2 * g + r], part, 0.0)
             where = pl.ds(row_ref[2 * g + r], MAXBF)
             sum_ref[where, 0:96] = sum_ref[where, 0:96] + part
-    out_ref[...] = sum_ref[0:256].T[0:96]
+    out_ref[...] = sum_ref[0 : out_ref.shape[1]].T[0 : out_ref.shape[0]]
 
 
 def vmem_spec():
@@ -221,19 +244,20 @@
     return pltpu.CompilerParams(vmem_limit_bytes=mib * MIB)
 
 
-def fit(integrals, low, own, high, order, mix, meta):
+def fit(integrals, low, own, high, metric, sizes, devices, atoms):
     aux_dev, bas_dev, window = integrals.shape
     width = own.shape[1]
     blocks = bas_dev // ROWBLK
     shape = (4 * aux_dev, blocks * PACKED + 16, 128)
     return pl.pallas_call(
         fit_kernel,
-        in_specs=[vmem_spec()] * 7,
+        in_specs=[vmem_spec()] * 8,
         out_specs=pl.BlockSpec(memory_space=pltpu.HBM),
-        out_shape=jax.ShapeDtypeStruct(shape, jnp.bfloat16),
+        out_shape=pltpu.HBM(shape, jnp.bfloat16),
         scratch_shapes=[
             pltpu.VMEM((window, width), jnp.bfloat16),
             pltpu.VMEM(shape, jnp.bfloat16),
+            pltpu.VMEM((16, 128), jnp.float32),
             pltpu.SemaphoreType.DMA((blocks // 2,)),
         ],
         compiler_params=limit(32),
@@ -243,21 +267,22 @@
             transcendentals=0,
         ),
         name="fit",
-    )(integrals, low, own, high, order, mix, meta)
+    )(integrals, low, own, high, metric, sizes, devices, atoms)
 
 
 def pair_sums(end_rows, got):
     groups = got.shape[0]
     rows = groups * (got.shape[1] // PACKED) * ROWBLK + MAXBF
+    shape = (groups, 4 * MAXBF, 128)
     return pl.pallas_call(
         pair_kernel,
         in_specs=[smem_spec(), vmem_spec()],
         out_specs=pl.BlockSpec(memory_space=pltpu.HBM),
-        out_shape=jax.ShapeDtypeStruct((groups, 2 * MAXBF, 256), jnp.float32),
+        out_shape=pltpu.HBM(shape, jnp.bfloat16),
         scratch_shapes=[
             pltpu.VMEM((rows, 128), jnp.float32),
             pltpu.VMEM((rows, 128), jnp.float32),
-            pltpu.VMEM((groups, 2 * MAXBF, 256), jnp.float32),
+            pltpu.VMEM(shape, jnp.bfloat16),
             pltpu.SemaphoreType.DMA((groups // BATCH,)),
         ]
         + [pltpu.VMEM((256, 128), jnp.bfloat16)] * (4 * BATCH),
@@ -281,21 +306,23 @@
     )(places, parts)
 
 
-def partner_coef(rows, counts, coef, groups):
+def partner_coef(blocks, starts, counts, coef):
+    groups, width, _ = coef.shape
     return pl.pallas_call(
         coef_kernel,
-        in_specs=[smem_spec(), smem_spec(), vmem_spec()],
+        in_specs=[smem_spec()] * 3 + [vmem_spec()],
         out_specs=vmem_spec(),
-        out_shape=jax.ShapeDtypeStruct((groups, 64, coef.shape[1]), jnp.bfloat16),
+        out_shape=jax.ShapeDtypeStruct((groups, 64, width), jnp.bfloat16),
         compiler_params=limit(16),
+        cost_estimate=pl.CostEstimate(flops=1 << 30, bytes_accessed=2 * MIB, transcendentals=0),
         name="partner_coef",
-    )(rows, counts, coef)
+    )(blocks, starts, counts, coef)
 
 
 def add_gains(rows, counts, slots, partner, bas_dev):
     return pl.pallas_call(
         gain_kernel,
-        in_specs=[smem_spec(), smem_spec(), vmem_spec(), vmem_spec()],
+        in_specs=[smem_spec()] * 2 + [vmem_spec()] * 2,
         out_specs=vmem_spec(),
         out_shape=jax.ShapeDtypeStruct((partner.shape[2], bas_dev), jnp.float32),
         scratch_shapes=[pltpu.VMEM((bas_dev + MAXBF, 128), jnp.float32)],
@@ -306,18 +333,6 @@
 
 def pick(hit, values):
     return jnp.sum(jnp.where(hit, values, 0), axis=-1)
-
-
-def column_order(occ):
-    order = np.zeros((2 * occ, 2 * occ), np.float32)
-    spot = 0
-    for first, count in ((0, 64), (4 * 64, 32)):
-        for k in range(4):
-            for c in range(2):
-                for i in range(count):
-                    order[c * occ + first + k * count + i, spot] = 1.0
-                    spot += 1
-    return order.astype(jnp.bfloat16)
 
 
 def per_device(integrals, coeffs, metric, atom_sizes, pair_device, pair_atom):
@@ -338,22 +353,19 @@
     low = lax.ppermute(own[bas_dev - halo :], "atom", forward)
     high = lax.ppermute(own[:halo], "atom", backward)
 
-    meta = jnp.concatenate([atom_sizes[0], pair_device[:, 0], pair_atom]).astype(jnp.bfloat16)
-    meta = jnp.pad(meta[None], ((0, 15), (0, 128 - meta.shape[0])))
-    mix = metric.T[:, None, :, None] * jnp.eye(ROWBLK, dtype=jnp.bfloat16)[None, :, None, :]
-    mix = mix.reshape(aux_dev * ROWBLK, aux_dev * ROWBLK)
-    packed = fit(integrals, low, own, high, jnp.asarray(column_order(occ)), mix, meta)
-    coef_part, packed = lax.optimization_barrier((coeffs, packed))
+    coef_part = lax.dynamic_slice_in_dim(
+        coeffs, lax.axis_index("aux") * occ_part, occ_part, 2
+    )
+    coef_part = coef_part.transpose(1, 2, 0).reshape(1, 2 * occ_part, bas_dev)
+    all_coef = lax.all_gather(coef_part, "atom", axis=0, tiled=True)
+
+    packed = fit(
+        integrals, low, own, high, metric, atom_sizes, pair_device.T, pair_atom[None]
+    )
     got = lax.all_to_all(packed, "atom", split_axis=0, concat_axis=0, tiled=True)
-    coef_part = lax.dynamic_slice_in_dim(
-        coef_part, lax.axis_index("aux") * occ_part, occ_part, 2
-    ).reshape(bas_dev, 2 * occ_part)
-    all_coef = lax.all_gather(coef_part, "atom", axis=0, tiled=True)
-
-    all_meta = got[:, got.shape[1] - 16, : 2 * occ_part].astype(jnp.int32)
-    sizes = all_meta[:, :atom_count]
-    devices = all_meta[:, atom_count : atom_count + ref_count]
-    atoms = all_meta[:, atom_count + ref_count :]
+
+    all_meta = got[:, got.shape[1] - 16 : got.shape[1] - 13, :32].astype(jnp.int32)
+    sizes, devices, atoms = all_meta[:, 0, :atom_count], all_meta[:, 1], all_meta[:, 2]
     starts = jnp.cumsum(sizes, axis=1) - sizes
     atom_range = jnp.arange(atom_count, dtype=jnp.int32)
     block_range = jnp.arange(groups, dtype=jnp.int32)
@@ -372,14 +384,13 @@
     slot = here[:, None, :] & (rank[:, None, :] == jnp.arange(2, dtype=jnp.int32)[None, :, None])
     end_start, end_size = end_start.reshape(groups, ref_count), end_size.reshape(groups, ref_count)
 
-    def partner(x):
-        return x.reshape(groups, ref_count // 2, 2)[:, :, ::-1].reshape(groups, ref_count)
-
-    gather_rows = devices * bas_dev + end_start
     slot_start = pick(slot, end_start[:, None, :]).reshape(-1)
     slot_size = pick(slot, end_size[:, None, :]).reshape(-1)
-    other_row = pick(slot, partner(gather_rows)[:, None, :]).reshape(-1)
-    other_size = pick(slot, partner(end_size)[:, None, :]).reshape(-1)
+
+    packed_end = (devices * 256 + end_start) * 32 + end_size
+    other = packed_end.reshape(groups, ref_count // 2, 2)[:, :, ::-1].reshape(groups, ref_count)
+    other = pick(slot, other[:, None, :]).reshape(-1)
+    other_block, other_start, other_size = other // 8192, other // 32 % 256, other % 32
 
     targets = pair_device[:, 0]
     order = jnp.arange(ref_count, dtype=jnp.int32)
@@ -390,16 +401,16 @@
     asked_hit = asked[None, :] == jnp.arange(2 * groups, dtype=jnp.int32)[:, None]
     places = 512 + pick(asked_hit, place[None, :] - 512)
 
-    partial_sums = pair_sums(end_rows, got)
-    owned = lax.all_to_all(partial_sums, "atom", split_axis=0, concat_axis=0, tiled=True)
-    partner_rows = partner_coef(other_row, other_size, all_coef, groups)
-    owned = jnp.sum(owned, axis=0).astype(jnp.bfloat16)
-    shared = jnp.broadcast_to(owned[None], (aux_count,) + owned.shape)
+    sent = pair_sums(end_rows, got)
+    owned = lax.all_to_all(sent, "atom", split_axis=0, concat_axis=0, tiled=True)
+    own_sums = jnp.sum(owned.astype(jnp.float32), axis=0).astype(jnp.bfloat16)
+    shared = jnp.broadcast_to(own_sums[None], (aux_count,) + own_sums.shape)
     parts = lax.all_to_all(shared, "aux", split_axis=0, concat_axis=0, tiled=True)
+    partner = partner_coef(other_block, other_start, other_size, all_coef)
     slots = make_slots(scale, places, parts, groups)
     slots = lax.all_to_all(slots, "atom", split_axis=0, concat_axis=0, tiled=True)
-    gains = add_gains(slot_start, slot_size, slots, partner_rows, bas_dev)
-    return gains.reshape(2, occ_part, bas_dev).transpose(2, 0, 1)
+    result = add_gains(slot_start, slot_size, slots, partner, bas_dev)
+    return result.reshape(2, occ_part, bas_dev).transpose(2, 0, 1)
 
 
 def solution(mesh):

time: 153 us -> 149 us (0.974)
  waiting for transfers between devices: 66.2 us -> 62 us
    all_to_all x1, waiting for transfers between devices: 18.9 us -> 11 us  [per_device(): lax.all_to_all(sent, 'atom', split_axis=0, concat_axis=0, tiled=True)]
    ppermute x1, waiting for transfers between devices: 1.35 us -> 4 us  [per_device(): high = lax.ppermute(own[:halo], 'atom', backward)]
    optimization_barrier x1 -> x0, local copies, waits for them, and re-layouts: 1.95 us -> none  [per_device(): coef_part, packed = lax.optimization_barrier((coeffs, packed))]
    unnamed x17 -> x21, local copies, waits for them, and re-layouts: 6.63 us -> 7.36 us
  transfers between devices with their start and end apart: 7 -> 7, of which waited for: 4 -> 4; matrix products, arithmetic and copies ran while one was open for 8% -> 6% of each run, Pallas kernels for 9% -> 10%
where the time goes in v4:
time: 149 us; the launch traced here: 148 us
  waiting for transfers between devices  62 us (42%)
  starting transfers between devices  34.1 us (23%)
  Pallas kernels  21.4 us (14%)
  local copies, waits for them, and re-layouts  13.9 us (9%)
  between operations  13.7 us (9%)
  other arithmetic  3.31 us (2%)
    all_to_all x1, waiting for transfers between devices, per_device(): lax.all_to_all(packed, 'atom', split_axis=0, concat_axis=0, tiled=True)  39.6 us
    all_to_all x1, waiting for transfers between devices, per_device(): lax.all_to_all(sent, 'atom', split_axis=0, concat_axis=0, tiled=True)  11 us
    all_to_all x1, starting transfers between devices, per_device(): lax.all_to_all(packed, 'atom', split_axis=0, concat_axis=0, tiled=True)  8.42 us
    all_to_all x1, starting transfers between devices, per_device(): lax.all_to_all(shared, 'aux', split_axis=0, concat_axis=0, tiled=True)  8.36 us
    all_to_all x1, waiting for transfers between devices, per_device(): lax.all_to_all(shared, 'aux', split_axis=0, concat_axis=0, tiled=True)  7.38 us
    unnamed x21, local copies, waits for them, and re-layouts  7.36 us
    pallas_call x1, Pallas kernels, pair_sums(): pl.pallas_call(pair_kernel, in_specs=[smem_spec(), vmem_spec()], out_spec...  7.24 us
    pallas_call x1, Pallas kernels, partner_coef(): pl.pallas_call(coef_kernel, in_specs=[smem_spec()] * 3 + [vmem_spec()], o...  5.99 us
  transfers between devices with their start and end apart: 7, of which 4 were waited for; matrix products, arithmetic and copies ran while one was open for 6% of the time, Pallas kernels for 10%

profile of v4, /device:TPU:1, one launch (start us, length us, event | category | flops | bytes accessed | tf_op | source)
XLA Modules:
  0.0 148.3 jit_solution(10602942663773538214)
XLA Ops:
  6.5 1.3 fusion.15
  7.9 4.6 %collective-permute-start = (bf16[128,768]{1,0:T(8,128)(2,1)S(1)}, bf16[128,768]{1,0:T(8,128)(2,1)S(1)}, u32[]{:S(2)}, u32[]{:S(2)}) collective-permute-start(bf16[128,768]{1,0:T(8,128)(2,1)S(1)} %bitcast.30), channel_id=1, source_target_pairs={{0,8},{8,16},{16,24},{24,32},{32,40},{40,48},{48,56},{56,64},{64,7... | collective-permute-start | bytes 589832 | tf_op jit(solution)/shard_map/ppermute | solution.py:353
  12.5 1.9 %collective-permute-start.1 = (bf16[128,768]{1,0:T(8,128)(2,1)S(1)}, bf16[128,768]{1,0:T(8,128)(2,1)S(1)}, u32[]{:S(2)}, u32[]{:S(2)}) collective-permute-start(bf16[128,768]{1,0:T(8,128)(2,1)S(1)} %bitcast.31), channel_id=1, source_target_pairs={{8,0},{16,8},{24,16},{32,24},{40,32},{48,40},{56,48},{64,56},{72,6... | collective-permute-start | bytes 589832 | tf_op jit(solution)/shard_map/ppermute | solution.py:354
  14.4 1.0 copy.45
  15.5 4.0 %collective-permute-done.1.high_ref = bf16[128,768]{1,0:T(8,128)(2,1)S(1)} collective-permute-done((bf16[128,768]{1,0:T(8,128)(2,1)S(1)}, bf16[128,768]{1,0:T(8,128)(2,1)S(1)}, u32[]{:S(2)}, u32[]{:S(2)}) %collective-permute-start.1) | collective-permute-done | bytes 196640 | tf_op jit(solution)/shard_map/ppermute | solution.py:354
  19.5 1.6 %copy-done = bf16[8,256,512]{2,1,0:T(8,128)(2,1)S(1)} copy-done((bf16[8,256,512]{2,1,0:T(8,128)(2,1)S(1)}, bf16[8,256,512]{2,1,0:T(8,128)(2,1)}, u32[]{:S(2)}) %copy-start) | copy-done | bytes 2097176
  21.1 0.7 copy-done.2
  21.8 0.7 copy-done.3
  22.4 0.7 copy-done.4
  23.1 0.7 copy-done.5
  23.7 4.8 %fit.1 = bf16[32,400,128]{2,1,0:T(8,128)(2,1)} custom-call(bf16[8,256,512]{2,1,0:T(8,128)(2,1)S(1)} %copy-done, bf16[128,768]{1,0:T(8,128)(2,1)S(1)} %collective-permute-done.low_ref, bf16[256,768]{1,0:T(8,128)(2,1)S(1)} %bitcast.23, bf16[128,768]{1,0:T(8,128)(2,1)S(1)} %collective-permute-done.1.high_ref, bf16[8,8]{1,0:T(8,128)(2,1)S(1)} %copy-done.2, ...), custom_call_target="tpu_custom_call" | custom-call | flops 2415919104 | bytes 6291456 | tf_op jit(solution)/shard_map/fit/pallas_call | solution.py:252
  28.5 8.4 %all-to-all-start = ((bf16[32,400,128]{2,1,0:T(8,128)(2,1)}), bf16[32,400,128]{2,1,0:T(8,128)(2,1)S(1)}, u32[]{:S(2)}, u32[]{:S(2)}) async-start(bf16[32,400,128]{2,1,0:T(8,128)(2,1)} %fit.1), calls=%async_computation | async-start | bytes 6553600 | tf_op jit(solution)/shard_map/all_to_all | solution.py:365
  37.0 1.2 dynamic-slice_bitcast_fusion
  38.2 0.7 copy.42
  39.2 39.6 %all-to-all-done.got_ref = bf16[32,400,128]{2,1,0:T(8,128)(2,1)S(1)} async-done(((bf16[32,400,128]{2,1,0:T(8,128)(2,1)}), bf16[32,400,128]{2,1,0:T(8,128)(2,1)S(1)}, u32[]{:S(2)}, u32[]{:S(2)}) %all-to-all-start) | async-done | bytes 3276832 | tf_op jit(solution)/shard_map/all_to_all | solution.py:365
  78.8 0.6 copy-done.7
  79.4 0.6 slice_reduce_fusion.1
  80.5 0.7 select_reduce_fusion
  81.4 0.8 copy.36
  82.1 0.8 copy.35
  82.9 7.2 %pair_sums.1 = bf16[32,64,128]{2,1,0:T(8,128)(2,1)} custom-call(s32[1024]{0:T(1024)S(1)} %fusion.7.row_ref, bf16[32,400,128]{2,1,0:T(8,128)(2,1)S(1)} %all-to-all-done.got_ref), custom_call_target="tpu_custom_call" | custom-call | tf_op jit(solution)/shard_map/pair_sums/pallas_call | solution.py:277
  90.2 4.9 %all-to-all-start.1 = ((bf16[32,64,128]{2,1,0:T(8,128)(2,1)}), bf16[32,64,128]{2,1,0:T(8,128)(2,1)S(1)}, u32[]{:S(2)}, u32[]{:S(2)}) async-start(bf16[32,64,128]{2,1,0:T(8,128)(2,1)} %pair_sums.1), calls=%async_computation.1 | async-start | bytes 1048576 | tf_op jit(solution)/shard_map/all_to_all | solution.py:405
  95.1 0.9 broadcast_compare_fusion
  96.5 11.0 %all-to-all-done.1 = bf16[32,64,128]{2,1,0:T(8,128)(2,1)S(1)} async-done(((bf16[32,64,128]{2,1,0:T(8,128)(2,1)}), bf16[32,64,128]{2,1,0:T(8,128)(2,1)S(1)}, u32[]{:S(2)}, u32[]{:S(2)}) %all-to-all-start.1) | async-done | bytes 524320 | tf_op jit(solution)/shard_map/all_to_all | solution.py:405
  107.6 0.7 broadcast_in_dim.78
  108.3 8.4 %all-to-all-start.2 = ((bf16[8,64,128]{2,1,0:T(8,128)(2,1)}), bf16[8,64,128]{2,1,0:T(8,128)(2,1)S(1)}, u32[]{:S(2)}, u32[]{:S(2)}) async-start(bf16[8,64,128]{2,1,0:T(8,128)(2,1)} %broadcast_in_dim.78), calls=%async_computation.2 | async-start | bytes 262144 | tf_op jit(solution)/shard_map/all_to_all | solution.py:408
  117.0 7.4 %all-to-all-done.2.refs_1_ = bf16[8,64,128]{2,1,0:T(8,128)(2,1)S(1)} async-done(((bf16[8,64,128]{2,1,0:T(8,128)(2,1)}), bf16[8,64,128]{2,1,0:T(8,128)(2,1)S(1)}, u32[]{:S(2)}, u32[]{:S(2)}) %all-to-all-start.2) | async-done | bytes 131104 | tf_op jit(solution)/shard_map/all_to_all | solution.py:408
  124.4 1.6 %make_slots.1 = f32[32,8,128]{2,1,0:T(8,128)} custom-call(s32[64]{0:T(128)S(1)} %broadcast_add_fusion.1.refs_0_, bf16[8,64,128]{2,1,0:T(8,128)(2,1)S(1)} %all-to-all-done.2.refs_1_), custom_call_target="tpu_custom_call" | custom-call | tf_op jit(solution)/shard_map/make_slots/pallas_call | solution.py:298
  126.0 5.8 %all-to-all-start.3 = ((f32[32,8,128]{2,1,0:T(8,128)}), f32[32,8,128]{2,1,0:T(8,128)S(1)}, u32[]{:S(2)}, u32[]{:S(2)}) async-start(f32[32,8,128]{2,1,0:T(8,128)} %make_slots.1), calls=%async_computation.3 | async-start | bytes 262144 | tf_op jit(solution)/shard_map/all_to_all | solution.py:411
  132.3 1.4 copy-done.1
  133.7 6.0 %partner_coef.1.coef_ref = bf16[32,64,96]{2,1,0:T(8,128)(2,1)S(1)} custom-call(s32[64]{0:T(128)S(1)} %get-tuple-element.20.block_ref, s32[64]{0:T(128)S(1)} %get-tuple-element.19.start_ref, s32[64]{0:T(128)S(1)} %get-tuple-element.18.count_ref, bf16[32,96,256]{2,1,0:T(8,128)(2,1)S(1)} %copy-done.1), custom_call_target="tpu_custom_call" | custom-call | flops 1073741824 | bytes 2097152 | tf_op jit(solution)/shard_map/partner_coef/pallas_call | solution.py:311
  139.6 1.8 %add_gains.1 = f32[96,256]{1,0:T(8,128)} custom-call(s32[64]{0:T(128)S(1)} %reshape.192.row_ref, s32[64]{0:T(128)S(1)} %reshape.193.count_ref, f32[32,8,128]{2,1,0:T(8,128)S(1)} %all-to-all-done.3.slot_ref, bf16[32,64,96]{2,1,0:T(8,128)(2,1)S(1)} %partner_coef.1.coef_ref), custom_call_target="tpu_custom_call" | custom-call | tf_op jit(solution)/shard_map/add_gains/pallas_call | solution.py:323
  (49 shorter events, 2.4 us)
Async XLA Ops:
  7.9 7.6 %collective-permute-start = (bf16[128,768]{1,0:T(8,128)(2,1)S(1)}, bf16[128,768]{1,0:T(8,128)(2,1)S(1)}, u32[]{:S(2)}, u32[]{:S(2)}) collective-permute-start(bf16[128,768]{1,0:T(8,128)(2,1)S(1)} %bitcast.30), channel_id=1, source_target_pairs={{0,8},{8,16},{16,24},{24,32},{32,40},{40,48},{48,56},{56,64},{64,7... | collective-permute-start | bytes 589832 | tf_op jit(solution)/shard_map/ppermute | solution.py:353
  12.5 7.0 %collective-permute-start.1 = (bf16[128,768]{1,0:T(8,128)(2,1)S(1)}, bf16[128,768]{1,0:T(8,128)(2,1)S(1)}, u32[]{:S(2)}, u32[]{:S(2)}) collective-permute-start(bf16[128,768]{1,0:T(8,128)(2,1)S(1)} %bitcast.31), channel_id=1, source_target_pairs={{8,0},{16,8},{24,16},{32,24},{40,32},{48,40},{56,48},{64,56},{72,6... | collective-permute-start | bytes 589832 | tf_op jit(solution)/shard_map/ppermute | solution.py:354
  19.5 1.6 %copy-start = (bf16[8,256,512]{2,1,0:T(8,128)(2,1)S(1)}, bf16[8,256,512]{2,1,0:T(8,128)(2,1)}, u32[]{:S(2)}) copy-start(bf16[8,256,512]{2,1,0:T(8,128)(2,1)} %ints_ref.1) | copy-start | bytes 6291460
  21.1 0.7 copy-start.2
  21.8 0.7 copy-start.3
  22.4 0.7 copy-start.4
  23.1 0.7 copy-start.5
  28.5 10.4 %copy-start.6 = (s32[32,1]{0,1:T(1,128)S(1)}, s32[32,1]{0,1:T(1,128)}, u32[]{:S(2)}) copy-start(s32[32,1]{0,1:T(1,128)} %param.10) | copy-start | bytes 388
  28.5 50.3 %all-to-all-start = ((bf16[32,400,128]{2,1,0:T(8,128)(2,1)}), bf16[32,400,128]{2,1,0:T(8,128)(2,1)S(1)}, u32[]{:S(2)}, u32[]{:S(2)}) async-start(bf16[32,400,128]{2,1,0:T(8,128)(2,1)} %fit.1), calls=%async_computation | async-start | bytes 6553600 | tf_op jit(solution)/shard_map/all_to_all | solution.py:365
  36.9 95.3 %all-gather.2.cloned.1.call-start = ((), (), s32[]{:S(2)}) async-start(), calls=%async_computation.4 | async-start | bytes 1622016 | tf_op jit(solution)/shard_map/all_gather | solution.py:360
  78.8 0.6 copy-start.7
  82.1 13.9 %copy-start.8 = (s32[32,16,2]{0,2,1:T(2,128)S(1)}, s32[32,16,2]{0,2,1:T(2,128)}, u32[]{:S(2)}) copy-start(s32[32,16,2]{0,2,1:T(2,128)} %copy.36) | copy-start | bytes 12292
  90.2 17.3 %all-to-all-start.1 = ((bf16[32,64,128]{2,1,0:T(8,128)(2,1)}), bf16[32,64,128]{2,1,0:T(8,128)(2,1)S(1)}, u32[]{:S(2)}, u32[]{:S(2)}) async-start(bf16[32,64,128]{2,1,0:T(8,128)(2,1)} %pair_sums.1), calls=%async_computation.1 | async-start | bytes 1048576 | tf_op jit(solution)/shard_map/all_to_all | solution.py:405
  108.3 16.1 %all-to-all-start.2 = ((bf16[8,64,128]{2,1,0:T(8,128)(2,1)}), bf16[8,64,128]{2,1,0:T(8,128)(2,1)S(1)}, u32[]{:S(2)}, u32[]{:S(2)}) async-start(bf16[8,64,128]{2,1,0:T(8,128)(2,1)} %broadcast_in_dim.78), calls=%async_computation.2 | async-start | bytes 262144 | tf_op jit(solution)/shard_map/all_to_all | solution.py:408
  126.0 13.6 %all-to-all-start.3 = ((f32[32,8,128]{2,1,0:T(8,128)}), f32[32,8,128]{2,1,0:T(8,128)S(1)}, u32[]{:S(2)}, u32[]{:S(2)}) async-start(f32[32,8,128]{2,1,0:T(8,128)} %make_slots.1), calls=%async_computation.3 | async-start | bytes 262144 | tf_op jit(solution)/shard_map/all_to_all | solution.py:411
  132.2 1.4 copy-start.1
Sparse Core Ops, SparseCore 0:
  40.3 65.5 all-gather.1

commit v5 on v4

v5 whole, which is shorter than its diff:
```python
import math

import jax
import jax.numpy as jnp
from jax import lax
from jax.experimental import pallas as pl
from jax.experimental.pallas import tpu as pltpu
from jax.sharding import PartitionSpec as P

MAXBF = 16
ROWBLK = 32
PACKED = ROWBLK + ROWBLK // 2
BATCH = 8
MIB = 1 << 20


def iota(shape, dim):
    return lax.broadcasted_iota(jnp.int32, shape, dim)


def dot(a, b):
    return jnp.dot(a, b, preferred_element_type=jnp.float32)


def dot_nt(a, b):
    return lax.dot_general(a, b, (((1,), (1,)), ((), ())), preferred_element_type=jnp.float32)


def dot_tn(a, b):
    return lax.dot_general(a, b, (((0,), (0,)), ((), ())), preferred_element_type=jnp.float32)


def fit_kernel(
    low_ref, own_ref, high_ref, ints_hbm, metric_hbm, size_hbm, dev_hbm, atom_hbm, out_ref,
    ints_ref, metric_ref, size_ref, dev_ref, atom_ref, window_ref, packed_ref, meta_ref,
    in_sem, out_sem,
):
    small = [(metric_hbm, metric_ref), (size_hbm, size_ref), (dev_hbm, dev_ref), (atom_hbm, atom_ref)]
    fetches = [pltpu.make_async_copy(a, b, in_sem.at[i]) for i, (a, b) in enumerate(small)]
    aux_dev, bas_dev, span = ints_ref.shape
    blocks = bas_dev // ROWBLK
    for u in range(blocks // 2):
        rows = pl.ds(2 * u * ROWBLK, 2 * ROWBLK)
        fetches.append(
            pltpu.make_async_copy(ints_hbm.at[:, rows], ints_ref.at[:, rows], in_sem.at[4 + u])
        )
    for fetch in fetches:
        fetch.start()
    u, v = iota((256, 256), 0), iota((256, 256), 1)
    main_order = u == ((v % 128) // 64) * 128 + (v // 128) * 64 + v % 64
    side_order = u == ((v % 64) // 32) * 128 + (v // 64) * 32 + v % 32
    main_order = jnp.where(main_order, 1.0, 0.0).astype(jnp.bfloat16)
    side_order = jnp.where(side_order, 1.0, 0.0).astype(jnp.bfloat16)
    at = 0
    for part_ref in (low_ref, own_ref, high_ref):
        rows = part_ref.shape[0]
        half = part_ref.shape[1] // 2
        for t in range(3):
            real = part_ref[:, t * 128 : (t + 1) * 128]
            imag = part_ref[:, half + t * 128 : half + (t + 1) * 128]
            order = side_order if t == 2 else main_order
            value = dot(jnp.concatenate([real, imag], axis=1), order)
            window_ref[at : at + rows, t * 256 : (t + 1) * 256] = value.astype(jnp.bfloat16)
        at += rows
    for fetch in fetches[:4]:
        fetch.wait()
    member = iota((256, 8), 0) // ROWBLK == iota((256, 8), 1)
    member = jnp.where(member, 1.0, 0.0).astype(jnp.bfloat16)
    mix = dot_nt(dot_nt(member, metric_ref[...]).astype(jnp.bfloat16), member)
    mix = jnp.where(u % ROWBLK == v % ROWBLK, mix, 0.0).astype(jnp.bfloat16)
    meta_ref[...] = jnp.zeros(meta_ref.shape, jnp.float32)
    for row, value_ref in enumerate((size_ref, dev_ref, atom_ref)):
        meta_ref[row : row + 1, 0 : value_ref.shape[1]] = value_ref[...].astype(jnp.float32)
    left = iota((ROWBLK // 2, 128), 1) < 64
    copies = []
    for u in range(blocks):
        if u % 2 == 0:
            fetches[4 + u // 2].wait()
        ints = ints_ref[:, u * ROWBLK : (u + 1) * ROWBLK].reshape(aux_dev * ROWBLK, span)
        half = dot(ints, window_ref[...]).astype(jnp.bfloat16)
        fitted = dot(mix, half)
        main = slice(u * PACKED, u * PACKED + ROWBLK)
        side = slice(u * PACKED + ROWBLK, (u + 1) * PACKED)
        for p in range(aux_dev):
            rows = fitted[p * ROWBLK : (p + 1) * ROWBLK]
            for k in range(4):
                tile = rows[:, k * 128 : (k + 1) * 128]
                packed_ref[p * 4 + k, main] = tile.astype(jnp.bfloat16)
            for k in range(2):
                shared = rows[:, 512 + k * 128 : 640 + k * 128]
                top, bottom = shared[: ROWBLK // 2], shared[ROWBLK // 2 :]
                even = jnp.where(left, top, pltpu.roll(bottom, 64, 1))
                odd = jnp.where(left, pltpu.roll(top, 64, 1), bottom)
                packed_ref[p * 4 + 2 * k, side] = even.astype(jnp.bfloat16)
                packed_ref[p * 4 + 2 * k + 1, side] = odd.astype(jnp.bfloat16)
        if u == blocks - 1:
            for d in range(4 * aux_dev):
                packed_ref[d, blocks * PACKED : blocks * PACKED + 16] = meta_ref[...].astype(
                    jnp.bfloat16
                )
        if u % 2 == 1:
            first = (u - 1) * PACKED
            span_rows = pl.ds(first, 2 * PACKED + (16 if u == blocks - 1 else 0))
            copies.append(
                pltpu.make_async_copy(
                    packed_ref.at[:, span_rows], out_ref.at[:, span_rows], out_sem.at[u // 2]
                )
            )
            copies[-1].start()
    for copy in copies:
        copy.wait()


def end_table(me, got_ref, size_ref, dev_ref, atom_ref):
    groups, at = got_ref.shape[0], got_ref.shape[1] - 16
    for d in range(groups):
        rows = got_ref[d, at : at + 16].astype(jnp.float32)
        for i, dest in enumerate((size_ref, dev_ref, atom_ref)):
            dest[d : d + 1] = rows[i : i + 1]
    before = jnp.where(iota((128, 128), 0) < iota((128, 128), 1), 1.0, 0.0).astype(jnp.bfloat16)
    sizes = size_ref[...]
    packed = dot(sizes.astype(jnp.bfloat16), before) * 32.0 + sizes
    devices = dev_ref[...].astype(jnp.int32)
    atoms = atom_ref[...].astype(jnp.int32)
    found = jnp.zeros(packed.shape, jnp.float32)
    for d in range(groups):
        row = jnp.broadcast_to(packed[d : d + 1], packed.shape)
        found = jnp.where(devices == d, jnp.take_along_axis(row, atoms, axis=1), found)
    found = found.astype(jnp.int32)
    starts, counts = found // 32, found % 32
    lane = iota(found.shape, 1)
    here = (devices == me) & (lane < 32)
    rank = dot(jnp.where(here, 1.0, 0.0).astype(jnp.bfloat16), before)
    table = jnp.where(lane < 32, devices * 256 + starts, 0)
    for i, value in enumerate((starts, counts)):
        value = value.astype(jnp.float32)
        for r in range(2):
            one = jnp.sum(jnp.where(here & (rank == r), value, 0.0), axis=1, keepdims=True)
            table = jnp.where(lane == 32 + 2 * i + r, one.astype(jnp.int32), table)
    return table


def pair_kernel(
    me_ref, coef_ref, got_ref, table_ref, out_ref, real_ref, imag_ref, rows_ref, sums_ref,
    size_ref, dev_ref, atom_ref, row_ref, table_sem, sem_ref, *sides,
):
    table_ref[...] = end_table(me_ref[0], got_ref, size_ref, dev_ref, atom_ref)
    fetch = pltpu.make_async_copy(table_ref, row_ref, table_sem)
    fetch.start()
    groups, blocks = got_ref.shape[0], got_ref.shape[1] // PACKED
    lane = iota((ROWBLK // 2, 128), 1)
    left, valid = lane < 64, lane < 96

    def unpack(b, carry):
        for i in range(blocks):
            base = pl.multiple_of(b * (blocks * ROWBLK) + i * ROWBLK, ROWBLK)
            shared = got_ref[b, i * PACKED + ROWBLK : (i + 1) * PACKED].astype(jnp.float32)
            for h in range(2):
                at = i * PACKED + h * 16
                main = got_ref[b, at : at + 16].astype(jnp.float32)
                real = shared if h else pltpu.roll(shared, 64, 1)
                imag = pltpu.roll(shared, 96 if h else 32, 1)
                real = jnp.where(left, main, jnp.where(valid, real, 0.0))
                imag = jnp.where(left, pltpu.roll(main, 64, 1), jnp.where(valid, imag, 0.0))
                real_ref[pl.ds(base + h * 16, 16)] = real
                imag_ref[pl.ds(base + h * 16, 16)] = imag
        return carry

    lax.fori_loop(0, groups, unpack, 0, unroll=2)
    tail = groups * blocks * ROWBLK
    real_ref[tail : tail + MAXBF] = jnp.zeros((MAXBF, 128), jnp.float32)
    imag_ref[tail : tail + MAXBF] = jnp.zeros((MAXBF, 128), jnp.float32)
    bas_dev, width = coef_ref.shape
    rows_ref[...] = jnp.zeros(rows_ref.shape, jnp.float32)
    rows_ref[0:bas_dev, 0:width] = coef_ref[...].astype(jnp.float32)
    row_id = iota((MAXBF, 128), 0)
    lane_pair = lane // MAXBF
    batch = len(sides) // 4
    fetch.wait()

    def group(step, carry):
        for u in range(batch):
            g = step * batch + u
            for h in range(2):
                first_ref, second_ref = sides[u * 4 + h * 2], sides[u * 4 + h * 2 + 1]
                for j in range(16):
                    row = row_ref[g, h * 16 + j]
                    dest = second_ref if j % 2 else first_ref
                    place = (j // 2) * MAXBF
                    dest[place : place + 16] = real_ref[pl.ds(row, 16)].astype(jnp.bfloat16)
                    dest[128 + place : 144 + place] = imag_ref[pl.ds(row, 16)].astype(jnp.bfloat16)
                value = dot_nt(first_ref[...], second_ref[...])
                parts = []
                for top in (0, 128):
                    for at in (0, 128):
                        part = value[top : top + 16, at : at + 128]
                        for j in range(1, 8):
                            here = value[top + j * 16 : top + j * 16 + 16, at : at + 128]
                            part = jnp.where(lane_pair == j, here, part)
                        parts.append(part)
                real, imag = parts[0] + parts[3], parts[2] - parts[1]
                sums_ref[g, h * 32 : h * 32 + 16] = real.astype(jnp.bfloat16)
                sums_ref[g, h * 32 + 16 : h * 32 + 32] = imag.astype(jnp.bfloat16)
                rows = rows_ref[pl.ds(row_ref[g, 32 + h], MAXBF)]
                rows = jnp.where(row_id < row_ref[g, 34 + h], rows, 0.0)
                sums_ref[g, 64 + h * 16 : 80 + h * 16] = rows.astype(jnp.bfloat16)
        send(step).start()
        return carry

    def send(step):
        done = pl.ds(step * batch, batch)
        return pltpu.make_async_copy(sums_ref.at[done], out_ref.at[done], sem_ref.at[step])

    lax.fori_loop(0, groups // batch, group, 0)
    for step in range(groups // batch):
        send(step).wait()


def slot_kernel(scale, target_ref, rank_ref, place_ref, parts_ref, got_ref, out_ref, tile_ref):
    total = parts_ref[0].astype(jnp.float32)
    for z in range(1, parts_ref.shape[0]):
        total = total + parts_ref[z].astype(jnp.float32)
    kernel = (total * scale).astype(jnp.bfloat16)
    u, v = iota((128, 128), 0), iota((128, 128), 1)
    same = u // MAXBF == v // MAXBF
    folds = [jnp.where(v == 96 + c * 16 + u % 16, 1.0, 0.0).astype(jnp.bfloat16) for c in range(2)]
    u, v = iota((32, 128), 0), iota((32, 128), 1)
    turned = jnp.where(v == 96 + u, jnp.where(u < MAXBF, 1.0, -1.0), 0.0).astype(jnp.bfloat16)

    def coef(e):
        at = pl.multiple_of(64 + rank_ref[e] * MAXBF, MAXBF)
        return got_ref[target_ref[e], pl.ds(at, MAXBF)].astype(jnp.float32)

    for h in range(2):
        block = kernel[h * 32 : (h + 1) * 32]
        first = jnp.zeros((128, 128), jnp.float32)
        for c in range(2):
            tile = block[c * MAXBF : (c + 1) * MAXBF].astype(jnp.float32)
            wide = jnp.where(same, jnp.concatenate([tile] * 8, axis=0), 0.0)
            first = first + dot(wide.astype(jnp.bfloat16), folds[c])
        second = dot_tn(block, turned)
        for j in range(8):
            pair, rows = h * 8 + j, slice(j * MAXBF, (j + 1) * MAXBF)
            at = pair * MAXBF
            tile_ref[at : at + MAXBF] = first[rows] + coef(2 * pair + 1)
            tile_ref[256 + at : 256 + at + MAXBF] = second[rows] + coef(2 * pair)
    tile_ref[512:528] = jnp.zeros((MAXBF, 128), jnp.float32)
    for s in range(2 * out_ref.shape[0]):
        rows = tile_ref[pl.ds(pl.multiple_of(place_ref[s], MAXBF), MAXBF)]
        out_ref[s // 2, (s % 2) * MAXBF : (s % 2 + 1) * MAXBF] = rows.astype(jnp.bfloat16)


def gain_kernel(row_ref, count_ref, slot_ref, out_ref, plain_ref, turned_ref):
    plain_ref[...] = jnp.zeros(plain_ref.shape, jnp.float32)
    turned_ref[...] = jnp.zeros(turned_ref.shape, jnp.float32)
    lane, row_id = iota((MAXBF, 128), 1), iota((MAXBF, 128), 0)
    masks = [lane < MAXBF, (lane >= MAXBF) & (lane < 2 * MAXBF)]
    for g in range(slot_ref.shape[0]):
        slots = slot_ref[g]
        wide = slots.astype(jnp.float32)
        tiles = []
        for c in range(2):
            for r in range(2):
                tile = wide[r * MAXBF : (r + 1) * MAXBF]
                tile = pltpu.roll(tile, 32 + 16 * (r - c), 1)
                tiles.append(jnp.where(masks[r], tile, 0.0))
        tiles = jnp.concatenate(tiles, axis=0)[:, 0:32].astype(jnp.bfloat16)
        gains = dot(tiles, slots)
        for c, sum_ref in enumerate((plain_ref, turned_ref)):
            for r in range(2):
                at = (2 * c + r) * MAXBF
                part = jnp.where(row_id < count_ref[2 * g + r], gains[at : at + MAXBF], 0.0)
                where = pl.ds(row_ref[2 * g + r], MAXBF)
                sum_ref[where] = sum_ref[where] + part
    width, bas_dev = out_ref.shape
    half = width // 2
    plain = plain_ref[0:bas_dev].T
    turned = turned_ref[0:bas_dev].T
    out_ref[0:half] = plain[0:half] - turned[half:width]
    out_ref[half:width] = plain[half:width] + turned[0:half]


def vmem_spec():
    return pl.BlockSpec(memory_space=pltpu.VMEM)


def smem_spec():
    return pl.BlockSpec(memory_space=pltpu.SMEM)


def limit(mib):
    return pltpu.CompilerParams(vmem_limit_bytes=mib * MIB)


def in_hbm(array):
    return pltpu.with_memory_space_constraint(array, pltpu.HBM)


def fit(low, own, high, *fetched):
    aux_dev, bas_dev, window = fetched[0].shape
    width = own.shape[1]
    blocks = bas_dev // ROWBLK
    shape = (4 * aux_dev, blocks * PACKED + 16, 128)
    return pl.pallas_call(
        fit_kernel,
        in_specs=[vmem_spec()] * 3 + [pl.BlockSpec(memory_space=pltpu.HBM)] * len(fetched),
        out_specs=pl.BlockSpec(memory_space=pltpu.HBM),
        out_shape=pltpu.HBM(shape, jnp.bfloat16),
        scratch_shapes=[pltpu.VMEM(x.shape, x.dtype) for x in fetched]
        + [
            pltpu.VMEM((window, width), jnp.bfloat16),
            pltpu.VMEM(shape, jnp.bfloat16),
            pltpu.VMEM((16, 128), jnp.float32),
            pltpu.SemaphoreType.DMA((4 + blocks // 2,)),
            pltpu.SemaphoreType.DMA((blocks // 2,)),
        ],
        compiler_params=limit(32),
        cost_estimate=pl.CostEstimate(
            flops=2 * aux_dev * bas_dev * width * (window + 256),
            bytes_accessed=6 * MIB,
            transcendentals=0,
        ),
        name="fit",
    )(low, own, high, *[in_hbm(x) for x in fetched])


def pair_sums(me, coef, got):
    groups = got.shape[0]
    rows = groups * (got.shape[1] // PACKED) * ROWBLK + MAXBF
    shape = (groups, 6 * MAXBF, 128)
    return pl.pallas_call(
        pair_kernel,
        in_specs=[smem_spec(), vmem_spec(), vmem_spec()],
        out_specs=[vmem_spec(), pl.BlockSpec(memory_space=pltpu.HBM)],
        out_shape=[
            jax.ShapeDtypeStruct((groups, 128), jnp.int32),
            pltpu.HBM(shape, jnp.bfloat16),
        ],
        scratch_shapes=[
            pltpu.VMEM((rows, 128), jnp.float32),
            pltpu.VMEM((rows, 128), jnp.float32),
            pltpu.VMEM((coef.shape[0] + MAXBF, 128), jnp.float32),
            pltpu.VMEM(shape, jnp.bfloat16),
            pltpu.VMEM((groups, 128), jnp.float32),
            pltpu.VMEM((groups, 128), jnp.float32),
            pltpu.VMEM((groups, 128), jnp.float32),
            pltpu.SMEM((groups, 128), jnp.int32),
            pltpu.SemaphoreType.DMA,
            pltpu.SemaphoreType.DMA((groups // BATCH,)),
        ]
        + [pltpu.VMEM((256, 128), jnp.bfloat16)] * (4 * BATCH),
        compiler_params=limit(40),
        name="pair_sums",
    )(me, coef, got)


def make_slots(scale, targets, ranks, places, parts, got):
    def body(*refs):
        slot_kernel(scale, *refs)

    return pl.pallas_call(
        body,
        in_specs=[smem_spec()] * 3 + [vmem_spec()] * 2,
        out_specs=vmem_spec(),
        out_shape=jax.ShapeDtypeStruct((got.shape[0], 2 * MAXBF, 128), jnp.bfloat16),
        scratch_shapes=[pltpu.VMEM((528, 128), jnp.float32)],
        compiler_params=limit(16),
        name="make_slots",
    )(targets, ranks, places, parts, got)


def add_gains(rows, counts, slots, width, bas_dev):
    return pl.pallas_call(
        gain_kernel,
        in_specs=[smem_spec()] * 2 + [vmem_spec()],
        out_specs=vmem_spec(),
        out_shape=jax.ShapeDtypeStruct((width, bas_dev), jnp.float32),
        scratch_shapes=[pltpu.VMEM((bas_dev + MAXBF, 128), jnp.float32)] * 2,
        compiler_params=limit(16),
        name="add_gains",
    )(rows, counts, slots)


def pick(hit, values):
    return jnp.sum(jnp.where(hit, values, 0), axis=-1)


def per_device(integrals, coeffs, metric, atom_sizes, pair_device, pair_atom):
    aux_dev, bas_dev, window = integrals.shape
    occ = coeffs.shape[2]
    groups = lax.axis_size("atom")
    aux_count = lax.axis_size("aux")
    occ_part = occ // aux_count
    ref_count = pair_atom.shape[0]
    halo = (window - bas_dev) // 2
    scale = 1.0 / math.sqrt(2 * occ * aux_dev * aux_count * MAXBF)
    me = lax.axis_index("atom")

    own = coeffs.reshape(bas_dev, 2 * occ)
    forward = [(i, i + 1) for i in range(groups - 1)]
    backward = [(i + 1, i) for i in range(groups - 1)]
    low = lax.ppermute(own[bas_dev - halo :], "atom", forward)
    high = lax.ppermute(own[:halo], "atom", backward)

    packed = fit(
        low, own, high, integrals, metric, atom_sizes, pair_device.T, pair_atom[None]
    )
    got = lax.all_to_all(packed, "atom", split_axis=0, concat_axis=0, tiled=True)
    coef_part = lax.dynamic_slice_in_dim(
        coeffs, lax.axis_index("aux") * occ_part, occ_part, 2
    ).reshape(bas_dev, 2 * occ_part)
    me = jnp.full((1,), lax.axis_index("atom"), jnp.int32)

    targets = pair_device[:, 0]
    order = jnp.arange(ref_count, dtype=jnp.int32)
    earlier = (targets[:, None] == targets[None, :]) & (order[None, :] < order[:, None])
    ranks = jnp.sum(earlier.astype(jnp.int32), axis=1)
    asked = targets * 2 + ranks
    place = (order % 2) * 256 + (order // 2) * MAXBF
    asked_hit = asked[None, :] == jnp.arange(2 * groups, dtype=jnp.int32)[:, None]
    places = 512 + pick(asked_hit, place[None, :] - 512)

    table, sent = pair_sums(me, coef_part, got)
    owned = lax.all_to_all(sent, "atom", split_axis=0, concat_axis=0, tiled=True)
    own_sums = jnp.sum(owned[:, : 4 * MAXBF].astype(jnp.float32), axis=0).astype(jnp.bfloat16)
    shared = jnp.broadcast_to(own_sums[None], (aux_count,) + own_sums.shape)
    parts = lax.all_to_all(shared, "aux", split_axis=0, concat_axis=0, tiled=True)
    slots = make_slots(scale, targets, ranks, places, parts, owned)
    slots = lax.all_to_all(slots, "atom", split_axis=0, concat_axis=0, tiled=True)
    rows, counts = table[:, 32:34].reshape(-1), table[:, 34:36].reshape(-1)
    result = add_gains(rows, counts, slots, 2 * occ_part, bas_dev)
    return result.reshape(2, occ_part, bas_dev).transpose(2, 0, 1)


def solution(mesh):
    placed = (
        P("aux", "atom", None),
        P("atom", None, None),
        P("aux", None),
        P("atom", None),
        P("atom", None),
        P("atom"),
    )
    return jax.shard_map(
        per_device, mesh=mesh, in_specs=placed, out_specs=P("atom", None, "aux"), check_vma=False
    )
```

time: 149 us -> 132 us (0.89)
  between operations: 13.7 us -> 0.15 us
  waiting for transfers between devices: 62 us -> 75 us
  local copies, waits for them, and re-layouts: 13.9 us -> 4.72 us
  Pallas kernels: 21.4 us -> 17.6 us
  other arithmetic: 3.31 us -> 0.37 us
    all_to_all x1, waiting for transfers between devices: 0.01 us -> 8.81 us  [per_device(): lax.all_to_all(slots, 'atom', split_axis=0, concat_axis=0, tiled=True)]
    unnamed x21 -> x6, local copies, waits for them, and re-layouts: 7.36 us -> 1.19 us
    pallas_call x5 -> x4, Pallas kernels: 21.4 us -> 17.6 us  [the longest x1 7.38 us: pair_sums(): pl.pallas_call(pair_kernel, in_specs=[smem_spec(), vmem_spec(), vmem_spec...]
    all_to_all x1, waiting for transfers between devices: 11 us -> 14 us  [per_device(): lax.all_to_all(sent, 'atom', split_axis=0, concat_axis=0, tiled=True)]
    transpose x2 -> x0, local copies, waits for them, and re-layouts: 1.88 us -> none  [per_device(): coef_part = coef_part.transpose(1, 2, 0).reshape(1, 2 * occ_part, bas_dev)]
  transfers between devices with their start and end apart: 7 -> 6, of which waited for: 4 -> 5; matrix products, arithmetic and copies ran while one was open for 6% -> 2% of each run, Pallas kernels for 10% -> 0%
where the time goes in v5:
time: 132 us
  waiting for transfers between devices  75 us (57%)
  starting transfers between devices  33.7 us (26%)
  Pallas kernels  17.6 us (13%)
  local copies, waits for them, and re-layouts  4.72 us (4%)
    all_to_all x1, waiting for transfers between devices, per_device(): lax.all_to_all(packed, 'atom', split_axis=0, concat_axis=0, tiled=True)  39.7 us
    all_to_all x1, waiting for transfers between devices, per_device(): lax.all_to_all(sent, 'atom', split_axis=0, concat_axis=0, tiled=True)  14 us
    all_to_all x1, waiting for transfers between devices, per_device(): lax.all_to_all(slots, 'atom', split_axis=0, concat_axis=0, tiled=True)  8.81 us
    all_to_all x1, waiting for transfers between devices, per_device(): lax.all_to_all(shared, 'aux', split_axis=0, concat_axis=0, tiled=True)  8.54 us
    all_to_all x1, starting transfers between devices, per_device(): lax.all_to_all(packed, 'atom', split_axis=0, concat_axis=0, tiled=True)  8.42 us
    all_to_all x1, starting transfers between devices, per_device(): lax.all_to_all(shared, 'aux', split_axis=0, concat_axis=0, tiled=True)  8.18 us
    pallas_call x1, Pallas kernels, pair_sums(): pl.pallas_call(pair_kernel, in_specs=[smem_spec(), vmem_spec(), vmem_spec...  7.38 us
    pallas_call x1, Pallas kernels, fit(): pl.pallas_call(fit_kernel, in_specs=[vmem_spec()] * 3 + [pl.BlockSpec(mem...  6.81 us
  transfers between devices with their start and end apart: 6, of which 5 were waited for; matrix products, arithmetic and copies ran while one was open for 2% of the time, Pallas kernels for 0%

profile of v5, /device:TPU:1, one launch (start us, length us, event | category | flops | bytes accessed | tf_op | source)
XLA Modules:
  0.0 131.6 jit_solution(8875306581190715528)
XLA Ops:
  0.0 1.3 fusion.5
  1.3 4.6 %collective-permute-start = (bf16[128,768]{1,0:T(8,128)(2,1)S(1)}, bf16[128,768]{1,0:T(8,128)(2,1)S(1)}, u32[]{:S(2)}, u32[]{:S(2)}) collective-permute-start(bf16[128,768]{1,0:T(8,128)(2,1)S(1)} %bitcast.22), channel_id=1, source_target_pairs={{0,8},{8,16},{16,24},{24,32},{32,40},{40,48},{48,56},{56,64},{64,7... | collective-permute-start | bytes 589832 | tf_op jit(solution)/shard_map/ppermute | solution.py:402
  6.0 1.9 %collective-permute-start.1 = (bf16[128,768]{1,0:T(8,128)(2,1)S(1)}, bf16[128,768]{1,0:T(8,128)(2,1)S(1)}, u32[]{:S(2)}, u32[]{:S(2)}) collective-permute-start(bf16[128,768]{1,0:T(8,128)(2,1)S(1)} %bitcast.23), channel_id=1, source_target_pairs={{8,0},{16,8},{24,16},{32,24},{40,32},{48,40},{56,48},{64,56},{72,6... | collective-permute-start | bytes 589832 | tf_op jit(solution)/shard_map/ppermute | solution.py:403
  7.9 1.0 copy.13
  8.9 0.0 collective-permute-done.low_ref
  9.0 4.0 %collective-permute-done.1.high_ref = bf16[128,768]{1,0:T(8,128)(2,1)S(1)} collective-permute-done((bf16[128,768]{1,0:T(8,128)(2,1)S(1)}, bf16[128,768]{1,0:T(8,128)(2,1)S(1)}, u32[]{:S(2)}, u32[]{:S(2)}) %collective-permute-start.1) | collective-permute-done | bytes 196640 | tf_op jit(solution)/shard_map/ppermute | solution.py:403
  13.0 6.8 %fit.1 = bf16[32,400,128]{2,1,0:T(8,128)(2,1)} custom-call(bf16[128,768]{1,0:T(8,128)(2,1)S(1)} %collective-permute-done.low_ref, bf16[256,768]{1,0:T(8,128)(2,1)S(1)} %bitcast.15, bf16[128,768]{1,0:T(8,128)(2,1)S(1)} %collective-permute-done.1.high_ref, bf16[8,256,512]{2,1,0:T(8,128)(2,1)} %ints_hbm.1, bf16[8,8]{1,0:T(8,128)(2,1)} %metric_hbm.1, ...), custom_call_target="tpu_custom_call" | custom-call | flops 2415919104 | bytes 6291456 | tf_op jit(solution)/shard_map/fit/pallas_call | solution.py:304
  19.8 8.4 %all-to-all-start = ((bf16[32,400,128]{2,1,0:T(8,128)(2,1)}), bf16[32,400,128]{2,1,0:T(8,128)(2,1)S(1)}, u32[]{:S(2)}, u32[]{:S(2)}) async-start(bf16[32,400,128]{2,1,0:T(8,128)(2,1)} %fit.1), calls=%async_computation | async-start | bytes 6553600 | tf_op jit(solution)/shard_map/all_to_all | solution.py:408
  28.2 0.0 copy-start
  28.2 1.2 constant_dynamic-slice_fusion
  29.4 0.1 copy.11
  29.5 0.1 copy.10.coef_ref
  29.6 39.7 %all-to-all-done.got_ref = bf16[32,400,128]{2,1,0:T(8,128)(2,1)S(1)} async-done(((bf16[32,400,128]{2,1,0:T(8,128)(2,1)}), bf16[32,400,128]{2,1,0:T(8,128)(2,1)S(1)}, u32[]{:S(2)}, u32[]{:S(2)}) %all-to-all-start) | async-done | bytes 3276832 | tf_op jit(solution)/shard_map/all_to_all | solution.py:408
  69.3 7.4 %pair_sums.1 = (s32[32,128]{1,0:T(8,128)S(1)}, bf16[32,96,128]{2,1,0:T(8,128)(2,1)}) custom-call(s32[1]{0:T(128)} %bitcast.me_ref, bf16[256,96]{1,0:T(8,128)(2,1)S(1)} %copy.10.coef_ref, bf16[32,400,128]{2,1,0:T(8,128)(2,1)S(1)} %all-to-all-done.got_ref), custom_call_target="tpu_custom_call" | custom-call | tf_op jit(solution)/shard_map/pair_sums/pallas_call | solution.py:331
  76.7 5.7 %all-to-all-start.1 = ((bf16[32,96,128]{2,1,0:T(8,128)(2,1)}), bf16[32,96,128]{2,1,0:T(8,128)(2,1)S(1)}, u32[]{:S(2)}, u32[]{:S(2)}) async-start(bf16[32,96,128]{2,1,0:T(8,128)(2,1)} %get-tuple-element.8), calls=%async_computation.1 | async-start | bytes 1572864 | tf_op jit(solution)/shard_map/all_to_all | solution.py:424
  82.4 0.0 copy-done
  82.4 0.2 convert_reduce_fusion.refs_1_
  82.6 14.0 %all-to-all-done.1.refs_4_ = bf16[32,96,128]{2,1,0:T(8,128)(2,1)S(1)} async-done(((bf16[32,96,128]{2,1,0:T(8,128)(2,1)}), bf16[32,96,128]{2,1,0:T(8,128)(2,1)S(1)}, u32[]{:S(2)}, u32[]{:S(2)}) %all-to-all-start.1) | async-done | bytes 786464 | tf_op jit(solution)/shard_map/all_to_all | solution.py:424
  96.6 0.1 slice_reduce_fusion
  96.7 0.7 broadcast_in_dim.33
  97.3 8.2 %all-to-all-start.2 = ((bf16[8,64,128]{2,1,0:T(8,128)(2,1)}), bf16[8,64,128]{2,1,0:T(8,128)(2,1)S(1)}, u32[]{:S(2)}, u32[]{:S(2)}) async-start(bf16[8,64,128]{2,1,0:T(8,128)(2,1)} %broadcast_in_dim.33), calls=%async_computation.2 | async-start | bytes 262144 | tf_op jit(solution)/shard_map/all_to_all | solution.py:427
  105.5 0.1 select_reduce_fusion
  105.6 8.5 %all-to-all-done.2.refs_3_ = bf16[8,64,128]{2,1,0:T(8,128)(2,1)S(1)} async-done(((bf16[8,64,128]{2,1,0:T(8,128)(2,1)}), bf16[8,64,128]{2,1,0:T(8,128)(2,1)S(1)}, u32[]{:S(2)}, u32[]{:S(2)}) %all-to-all-start.2) | async-done | bytes 131104 | tf_op jit(solution)/shard_map/all_to_all | solution.py:427
  114.2 1.5 %make_slots.1 = bf16[32,32,128]{2,1,0:T(8,128)(2,1)} custom-call(s32[32]{0:T(128)S(1)} %bitcast.18, s32[32]{0:T(128)S(1)} %convert_reduce_fusion.refs_1_, s32[64]{0:T(128)S(1)} %broadcast_add_fusion.refs_2_, bf16[8,64,128]{2,1,0:T(8,128)(2,1)S(1)} %all-to-all-done.2.refs_3_, bf16[32,96,128]{2,1,0:T(8,128)(2,1)S(1)} %all-to-all-done.1.refs_4_), custom_call_target="tpu_custom_call" | custom-call | tf_op jit(solution)/shard_map/make_slots/pallas_call | solution.py:361
  115.7 4.9 %all-to-all-start.3 = ((bf16[32,32,128]{2,1,0:T(8,128)(2,1)}), bf16[32,32,128]{2,1,0:T(8,128)(2,1)S(1)}, u32[]{:S(2)}, u32[]{:S(2)}) async-start(bf16[32,32,128]{2,1,0:T(8,128)(2,1)} %make_slots.1), calls=%async_computation.3 | async-start | bytes 524288 | tf_op jit(solution)/shard_map/all_to_all | solution.py:429
  120.6 0.1 fusion.6
  120.7 0.1 reshape.54.row_ref
  120.8 0.1 reshape.55.count_ref
  120.9 8.8 %all-to-all-done.3.slot_ref = bf16[32,32,128]{2,1,0:T(8,128)(2,1)S(1)} async-done(((bf16[32,32,128]{2,1,0:T(8,128)(2,1)}), bf16[32,32,128]{2,1,0:T(8,128)(2,1)S(1)}, u32[]{:S(2)}, u32[]{:S(2)}) %all-to-all-start.3) | async-done | bytes 262176 | tf_op jit(solution)/shard_map/all_to_all | solution.py:429
  129.7 1.9 %add_gains.1 = f32[96,256]{1,0:T(8,128)} custom-call(s32[64]{0:T(128)S(1)} %reshape.54.row_ref, s32[64]{0:T(128)S(1)} %reshape.55.count_ref, bf16[32,32,128]{2,1,0:T(8,128)(2,1)S(1)} %all-to-all-done.3.slot_ref), custom_call_target="tpu_custom_call" | custom-call | tf_op jit(solution)/shard_map/add_gains/pallas_call | solution.py:373
  (5 shorter events, 0.1 us)
Async XLA Ops:
  1.3 7.6 %collective-permute-start = (bf16[128,768]{1,0:T(8,128)(2,1)S(1)}, bf16[128,768]{1,0:T(8,128)(2,1)S(1)}, u32[]{:S(2)}, u32[]{:S(2)}) collective-permute-start(bf16[128,768]{1,0:T(8,128)(2,1)S(1)} %bitcast.22), channel_id=1, source_target_pairs={{0,8},{8,16},{16,24},{24,32},{32,40},{40,48},{48,56},{56,64},{64,7... | collective-permute-start | bytes 589832 | tf_op jit(solution)/shard_map/ppermute | solution.py:402
  6.0 7.0 %collective-permute-start.1 = (bf16[128,768]{1,0:T(8,128)(2,1)S(1)}, bf16[128,768]{1,0:T(8,128)(2,1)S(1)}, u32[]{:S(2)}, u32[]{:S(2)}) collective-permute-start(bf16[128,768]{1,0:T(8,128)(2,1)S(1)} %bitcast.23), channel_id=1, source_target_pairs={{8,0},{16,8},{24,16},{32,24},{40,32},{48,40},{56,48},{64,56},{72,6... | collective-permute-start | bytes 589832 | tf_op jit(solution)/shard_map/ppermute | solution.py:403
  19.8 49.5 %all-to-all-start = ((bf16[32,400,128]{2,1,0:T(8,128)(2,1)}), bf16[32,400,128]{2,1,0:T(8,128)(2,1)S(1)}, u32[]{:S(2)}, u32[]{:S(2)}) async-start(bf16[32,400,128]{2,1,0:T(8,128)(2,1)} %fit.1), calls=%async_computation | async-start | bytes 6553600 | tf_op jit(solution)/shard_map/all_to_all | solution.py:408
  28.2 54.2 %copy-start = (s32[32,1]{0,1:T(1,128)S(1)}, s32[32,1]{0,1:T(1,128)}, u32[]{:S(2)}) copy-start(s32[32,1]{0,1:T(1,128)} %param.10) | copy-start | bytes 388
  76.7 19.9 %all-to-all-start.1 = ((bf16[32,96,128]{2,1,0:T(8,128)(2,1)}), bf16[32,96,128]{2,1,0:T(8,128)(2,1)S(1)}, u32[]{:S(2)}, u32[]{:S(2)}) async-start(bf16[32,96,128]{2,1,0:T(8,128)(2,1)} %get-tuple-element.8), calls=%async_computation.1 | async-start | bytes 1572864 | tf_op jit(solution)/shard_map/all_to_all | solution.py:424
  97.3 16.8 %all-to-all-start.2 = ((bf16[8,64,128]{2,1,0:T(8,128)(2,1)}), bf16[8,64,128]{2,1,0:T(8,128)(2,1)S(1)}, u32[]{:S(2)}, u32[]{:S(2)}) async-start(bf16[8,64,128]{2,1,0:T(8,128)(2,1)} %broadcast_in_dim.33), calls=%async_computation.2 | async-start | bytes 262144 | tf_op jit(solution)/shard_map/all_to_all | solution.py:427
  115.7 14.0 %all-to-all-start.3 = ((bf16[32,32,128]{2,1,0:T(8,128)(2,1)}), bf16[32,32,128]{2,1,0:T(8,128)(2,1)S(1)}, u32[]{:S(2)}, u32[]{:S(2)}) async-start(bf16[32,32,128]{2,1,0:T(8,128)(2,1)} %make_slots.1), calls=%async_computation.3 | async-start | bytes 524288 | tf_op jit(solution)/shard_map/all_to_all | solution.py:429

commit v6 on v5

--- a/solution.py
+++ b/solution.py
@@ -30,54 +30,67 @@
     return lax.dot_general(a, b, (((0,), (0,)), ((), ())), preferred_element_type=jnp.float32)
 
 
-def fit_kernel(
-    low_ref, own_ref, high_ref, ints_hbm, metric_hbm, size_hbm, dev_hbm, atom_hbm, out_ref,
-    ints_ref, metric_ref, size_ref, dev_ref, atom_ref, window_ref, packed_ref, meta_ref,
-    in_sem, out_sem,
+def ordered(part_ref, order_ref, window_ref, at):
+    rows = part_ref.shape[0]
+    half = part_ref.shape[1] // 2
+    for t in range(3):
+        real = part_ref[:, t * 128 : (t + 1) * 128]
+        imag = part_ref[:, half + t * 128 : half + (t + 1) * 128]
+        value = dot(jnp.concatenate([real, imag], axis=1), order_ref[t // 2])
+        window_ref[at : at + rows, t * 256 : (t + 1) * 256] = value.astype(jnp.bfloat16)
+
+
+def stage_kernel(
+    own_ref, ints_hbm, metric_hbm, size_hbm, dev_hbm, atom_hbm,
+    ints_ref, window_ref, order_ref, mix_ref, meta_ref,
+    metric_ref, size_ref, dev_ref, atom_ref, rows_ref, sem_ref,
 ):
-    small = [(metric_hbm, metric_ref), (size_hbm, size_ref), (dev_hbm, dev_ref), (atom_hbm, atom_ref)]
-    fetches = [pltpu.make_async_copy(a, b, in_sem.at[i]) for i, (a, b) in enumerate(small)]
-    aux_dev, bas_dev, span = ints_ref.shape
-    blocks = bas_dev // ROWBLK
-    for u in range(blocks // 2):
-        rows = pl.ds(2 * u * ROWBLK, 2 * ROWBLK)
-        fetches.append(
-            pltpu.make_async_copy(ints_hbm.at[:, rows], ints_ref.at[:, rows], in_sem.at[4 + u])
-        )
+    sources = (ints_hbm, metric_hbm, size_hbm, dev_hbm, atom_hbm)
+    targets = (ints_ref, metric_ref, size_ref, dev_ref, atom_ref)
+    fetches = [
+        pltpu.make_async_copy(a, b, sem_ref.at[i]) for i, (a, b) in enumerate(zip(sources, targets))
+    ]
     for fetch in fetches:
         fetch.start()
     u, v = iota((256, 256), 0), iota((256, 256), 1)
     main_order = u == ((v % 128) // 64) * 128 + (v // 128) * 64 + v % 64
     side_order = u == ((v % 64) // 32) * 128 + (v // 64) * 32 + v % 32
-    main_order = jnp.where(main_order, 1.0, 0.0).astype(jnp.bfloat16)
-    side_order = jnp.where(side_order, 1.0, 0.0).astype(jnp.bfloat16)
-    at = 0
-    for part_ref in (low_ref, own_ref, high_ref):
-        rows = part_ref.shape[0]
-        half = part_ref.shape[1] // 2
-        for t in range(3):
-            real = part_ref[:, t * 128 : (t + 1) * 128]
-            imag = part_ref[:, half + t * 128 : half + (t + 1) * 128]
-            order = side_order if t == 2 else main_order
-            value = dot(jnp.concatenate([real, imag], axis=1), order)
-            window_ref[at : at + rows, t * 256 : (t + 1) * 256] = value.astype(jnp.bfloat16)
-        at += rows
-    for fetch in fetches[:4]:
+    order_ref[0] = jnp.where(main_order, 1.0, 0.0).astype(jnp.bfloat16)
+    order_ref[1] = jnp.where(side_order, 1.0, 0.0).astype(jnp.bfloat16)
+    ordered(own_ref, order_ref, window_ref, 0)
+    for fetch in fetches[1:]:
         fetch.wait()
     member = iota((256, 8), 0) // ROWBLK == iota((256, 8), 1)
     member = jnp.where(member, 1.0, 0.0).astype(jnp.bfloat16)
     mix = dot_nt(dot_nt(member, metric_ref[...]).astype(jnp.bfloat16), member)
-    mix = jnp.where(u % ROWBLK == v % ROWBLK, mix, 0.0).astype(jnp.bfloat16)
-    meta_ref[...] = jnp.zeros(meta_ref.shape, jnp.float32)
+    mix_ref[...] = jnp.where(u % ROWBLK == v % ROWBLK, mix, 0.0).astype(jnp.bfloat16)
+    rows_ref[...] = jnp.zeros(rows_ref.shape, jnp.float32)
     for row, value_ref in enumerate((size_ref, dev_ref, atom_ref)):
-        meta_ref[row : row + 1, 0 : value_ref.shape[1]] = value_ref[...].astype(jnp.float32)
+        rows_ref[row : row + 1, 0 : value_ref.shape[1]] = value_ref[...].astype(jnp.float32)
+    meta_ref[...] = rows_ref[...].astype(jnp.bfloat16)
+    fetches[0].wait()
+
+
+def fit_kernel(
+    low_ref, high_ref, own_ref, ints_ref, order_ref, mix_ref, meta_ref, out_ref,
+    window_ref, packed_ref, out_sem,
+):
+    aux_dev, bas_dev, span = ints_ref.shape
+    blocks = bas_dev // ROWBLK
+    halo = low_ref.shape[0]
+    ordered(low_ref, order_ref, window_ref, 0)
+    window_ref[halo : halo + bas_dev] = own_ref[...]
+    ordered(high_ref, order_ref, window_ref, halo + bas_dev)
+    mix = mix_ref[...]
     left = iota((ROWBLK // 2, 128), 1) < 64
     copies = []
     for u in range(blocks):
-        if u % 2 == 0:
-            fetches[4 + u // 2].wait()
-        ints = ints_ref[:, u * ROWBLK : (u + 1) * ROWBLK].reshape(aux_dev * ROWBLK, span)
-        half = dot(ints, window_ref[...]).astype(jnp.bfloat16)
+        if u % 4 == 0:
+            ints = ints_ref[:, u * ROWBLK : (u + 4) * ROWBLK].reshape(-1, span)
+            wide = dot(ints, window_ref[...]).astype(jnp.bfloat16)
+            wide = wide.reshape(aux_dev, 4 * ROWBLK, -1)
+        at = (u % 4) * ROWBLK
+        half = wide[:, at : at + ROWBLK].reshape(aux_dev * ROWBLK, -1)
         fitted = dot(mix, half)
         main = slice(u * PACKED, u * PACKED + ROWBLK)
         side = slice(u * PACKED + ROWBLK, (u + 1) * PACKED)
@@ -95,9 +108,7 @@
                 packed_ref[p * 4 + 2 * k + 1, side] = odd.astype(jnp.bfloat16)
         if u == blocks - 1:
             for d in range(4 * aux_dev):
-                packed_ref[d, blocks * PACKED : blocks * PACKED + 16] = meta_ref[...].astype(
-                    jnp.bfloat16
-                )
+                packed_ref[d, blocks * PACKED : blocks * PACKED + 16] = meta_ref[...]
         if u % 2 == 1:
             first = (u - 1) * PACKED
             span_rows = pl.ds(first, 2 * PACKED + (16 if u == blocks - 1 else 0))
@@ -166,7 +177,7 @@
                 imag_ref[pl.ds(base + h * 16, 16)] = imag
         return carry
 
-    lax.fori_loop(0, groups, unpack, 0, unroll=2)
+    lax.fori_loop(0, groups, unpack, 0, unroll=4)
     tail = groups * blocks * ROWBLK
     real_ref[tail : tail + MAXBF] = jnp.zeros((MAXBF, 128), jnp.float32)
     imag_ref[tail : tail + MAXBF] = jnp.zeros((MAXBF, 128), jnp.float32)
@@ -184,23 +195,26 @@
             for h in range(2):
                 first_ref, second_ref = sides[u * 4 + h * 2], sides[u * 4 + h * 2 + 1]
                 for j in range(16):
-                    row = row_ref[g, h * 16 + j]
-                    dest = second_ref if j % 2 else first_ref
+                    row = pl.ds(row_ref[g, h * 16 + j], 16)
                     place = (j // 2) * MAXBF
-                    dest[place : place + 16] = real_ref[pl.ds(row, 16)].astype(jnp.bfloat16)
-                    dest[128 + place : 144 + place] = imag_ref[pl.ds(row, 16)].astype(jnp.bfloat16)
+                    real, imag = real_ref[row], imag_ref[row]
+                    if j % 2:
+                        second_ref[place : place + 16, 0:128] = real.astype(jnp.bfloat16)
+                        second_ref[place : place + 16, 128:256] = imag.astype(jnp.bfloat16)
+                    else:
+                        first_ref[place : place + 16, 0:128] = real.astype(jnp.bfloat16)
+                        first_ref[place : place + 16, 128:256] = imag.astype(jnp.bfloat16)
+                        place += 128
+                        first_ref[place : place + 16, 0:128] = imag.astype(jnp.bfloat16)
+                        first_ref[place : place + 16, 128:256] = (-real).astype(jnp.bfloat16)
                 value = dot_nt(first_ref[...], second_ref[...])
-                parts = []
-                for top in (0, 128):
-                    for at in (0, 128):
-                        part = value[top : top + 16, at : at + 128]
-                        for j in range(1, 8):
-                            here = value[top + j * 16 : top + j * 16 + 16, at : at + 128]
-                            part = jnp.where(lane_pair == j, here, part)
-                        parts.append(part)
-                real, imag = parts[0] + parts[3], parts[2] - parts[1]
-                sums_ref[g, h * 32 : h * 32 + 16] = real.astype(jnp.bfloat16)
-                sums_ref[g, h * 32 + 16 : h * 32 + 32] = imag.astype(jnp.bfloat16)
+                for c in range(2):
+                    part = value[c * 128 : c * 128 + 16]
+                    for j in range(1, 8):
+                        here = value[c * 128 + j * 16 : c * 128 + j * 16 + 16]
+                        part = jnp.where(lane_pair == j, here, part)
+                    at = h * 32 + c * 16
+                    sums_ref[g, at : at + 16] = part.astype(jnp.bfloat16)
                 rows = rows_ref[pl.ds(row_ref[g, 32 + h], MAXBF)]
                 rows = jnp.where(row_id < row_ref[g, 34 + h], rows, 0.0)
                 sums_ref[g, 64 + h * 16 : 80 + h * 16] = rows.astype(jnp.bfloat16)
@@ -296,22 +310,34 @@
     return pltpu.with_memory_space_constraint(array, pltpu.HBM)
 
 
-def fit(low, own, high, *fetched):
-    aux_dev, bas_dev, window = fetched[0].shape
-    width = own.shape[1]
+def stage(own, *fetched):
+    shapes = [fetched[0].shape, own.shape, (2, 256, 256), (256, 256), (16, 128)]
+    return pl.pallas_call(
+        stage_kernel,
+        in_specs=[vmem_spec()] + [pl.BlockSpec(memory_space=pltpu.HBM)] * len(fetched),
+        out_specs=[vmem_spec()] * len(shapes),
+        out_shape=[pltpu.VMEM(shape, jnp.bfloat16) for shape in shapes],
+        scratch_shapes=[pltpu.VMEM(x.shape, x.dtype) for x in fetched[1:]]
+        + [pltpu.VMEM((16, 128), jnp.float32), pltpu.SemaphoreType.DMA((len(fetched),))],
+        compiler_params=limit(16),
+        cost_estimate=pl.CostEstimate(flops=1 << 28, bytes_accessed=5 * MIB, transcendentals=0),
+        name="stage",
+    )(own, *[in_hbm(x) for x in fetched])
+
+
+def fit(low, high, window_rows, ints, order, mix, meta):
+    aux_dev, bas_dev, window = ints.shape
+    width = low.shape[1]
     blocks = bas_dev // ROWBLK
     shape = (4 * aux_dev, blocks * PACKED + 16, 128)
     return pl.pallas_call(
         fit_kernel,
-        in_specs=[vmem_spec()] * 3 + [pl.BlockSpec(memory_space=pltpu.HBM)] * len(fetched),
+        in_specs=[vmem_spec()] * 7,
         out_specs=pl.BlockSpec(memory_space=pltpu.HBM),
         out_shape=pltpu.HBM(shape, jnp.bfloat16),
-        scratch_shapes=[pltpu.VMEM(x.shape, x.dtype) for x in fetched]
-        + [
+        scratch_shapes=[
             pltpu.VMEM((window, width), jnp.bfloat16),
             pltpu.VMEM(shape, jnp.bfloat16),
-            pltpu.VMEM((16, 128), jnp.float32),
-            pltpu.SemaphoreType.DMA((4 + blocks // 2,)),
             pltpu.SemaphoreType.DMA((blocks // 2,)),
         ],
         compiler_params=limit(32),
@@ -321,7 +347,7 @@
             transcendentals=0,
         ),
         name="fit",
-    )(low, own, high, *[in_hbm(x) for x in fetched])
+    )(low, high, window_rows, ints, order, mix, meta)
 
 
 def pair_sums(me, coef, got):
@@ -348,7 +374,7 @@
             pltpu.SemaphoreType.DMA,
             pltpu.SemaphoreType.DMA((groups // BATCH,)),
         ]
-        + [pltpu.VMEM((256, 128), jnp.bfloat16)] * (4 * BATCH),
+        + [pltpu.VMEM((256, 256), jnp.bfloat16), pltpu.VMEM((128, 256), jnp.bfloat16)] * (2 * BATCH),
         compiler_params=limit(40),
         name="pair_sums",
     )(me, coef, got)
@@ -402,9 +428,10 @@
     low = lax.ppermute(own[bas_dev - halo :], "atom", forward)
     high = lax.ppermute(own[:halo], "atom", backward)
 
-    packed = fit(
-        low, own, high, integrals, metric, atom_sizes, pair_device.T, pair_atom[None]
+    ints, window_rows, order, mix, meta = stage(
+        own, integrals, metric, atom_sizes, pair_device.T, pair_atom[None]
     )
+    packed = fit(low, high, window_rows, ints, order, mix, meta)
     got = lax.all_to_all(packed, "atom", split_axis=0, concat_axis=0, tiled=True)
     coef_part = lax.dynamic_slice_in_dim(
         coeffs, lax.axis_index("aux") * occ_part, occ_part, 2

time: 132 us -> 129 us (0.977)
  waiting for transfers between devices: 75 us -> 73.2 us
    ppermute x1, waiting for transfers between devices: 4 us -> 2.17 us  [per_device(): high = lax.ppermute(own[:halo], 'atom', backward)]
    pallas_call x1 -> x2, Pallas kernels: 6.81 us -> 6.4 us  [the longest x1 4.58 us: fit(): pl.pallas_call(fit_kernel, in_specs=[vmem_spec()] * 7, out_specs=pl.Block...]
  transfers between devices with their start and end apart: 6 -> 6, of which waited for: 5 -> 5; matrix products, arithmetic and copies ran while one was open for 2% -> 2% of each run, Pallas kernels for 0% -> 1%
where the time goes in v6:
time: 129 us
  waiting for transfers between devices  73.2 us (57%)
  starting transfers between devices  33.7 us (26%)
  Pallas kernels  16.5 us (13%)
  local copies, waits for them, and re-layouts  4.73 us (4%)
    all_to_all x1, waiting for transfers between devices, per_device(): lax.all_to_all(packed, 'atom', split_axis=0, concat_axis=0, tiled=True)  39.7 us
    all_to_all x1, waiting for transfers between devices, per_device(): lax.all_to_all(sent, 'atom', split_axis=0, concat_axis=0, tiled=True)  14 us
    all_to_all x1, waiting for transfers between devices, per_device(): lax.all_to_all(slots, 'atom', split_axis=0, concat_axis=0, tiled=True)  8.81 us
    all_to_all x1, waiting for transfers between devices, per_device(): lax.all_to_all(shared, 'aux', split_axis=0, concat_axis=0, tiled=True)  8.54 us
    all_to_all x1, starting transfers between devices, per_device(): lax.all_to_all(packed, 'atom', split_axis=0, concat_axis=0, tiled=True)  8.42 us
    all_to_all x1, starting transfers between devices, per_device(): lax.all_to_all(shared, 'aux', split_axis=0, concat_axis=0, tiled=True)  8.18 us
    pallas_call x1, Pallas kernels, pair_sums(): pl.pallas_call(pair_kernel, in_specs=[smem_spec(), vmem_spec(), vmem_spec...  6.7 us
    all_to_all x1, starting transfers between devices, per_device(): lax.all_to_all(sent, 'atom', split_axis=0, concat_axis=0, tiled=True)  5.68 us
  transfers between devices with their start and end apart: 6, of which 5 were waited for; matrix products, arithmetic and copies ran while one was open for 2% of the time, Pallas kernels for 1%

profile of v6, /device:TPU:1, one launch (start us, length us, event | category | flops | bytes accessed | tf_op | source)
XLA Modules:
  0.0 128.7 jit_solution(13376895554369193310)
XLA Ops:
  0.0 1.3 %fusion.5 = (bf16[128,2,384]{2,1,0:T(2,128)(2,1)S(1)}, bf16[128,2,384]{2,1,0:T(2,128)(2,1)S(1)}) fusion(bf16[256,2,384]{2,1,0:T(2,128)(2,1)} %param.7), kind=kLoop, calls=%fused_computation.18 | loop fusion | bytes 786432 | tf_op jit(solution)/shard_map/slice | solution.py:429
  1.3 4.6 %collective-permute-start = (bf16[128,768]{1,0:T(8,128)(2,1)S(1)}, bf16[128,768]{1,0:T(8,128)(2,1)S(1)}, u32[]{:S(2)}, u32[]{:S(2)}) collective-permute-start(bf16[128,768]{1,0:T(8,128)(2,1)S(1)} %bitcast.22), channel_id=1, source_target_pairs={{0,8},{8,16},{16,24},{24,32},{32,40},{40,48},{48,56},{56,64},{64,7... | collective-permute-start | bytes 589832 | tf_op jit(solution)/shard_map/ppermute | solution.py:428
  6.0 1.9 %collective-permute-start.1 = (bf16[128,768]{1,0:T(8,128)(2,1)S(1)}, bf16[128,768]{1,0:T(8,128)(2,1)S(1)}, u32[]{:S(2)}, u32[]{:S(2)}) collective-permute-start(bf16[128,768]{1,0:T(8,128)(2,1)S(1)} %bitcast.23), channel_id=1, source_target_pairs={{8,0},{16,8},{24,16},{32,24},{40,32},{48,40},{56,48},{64,56},{72,6... | collective-permute-start | bytes 589832 | tf_op jit(solution)/shard_map/ppermute | solution.py:429
  7.9 1.0 copy.14
  8.9 1.8 %stage.1 = (bf16[8,256,512]{2,1,0:T(8,128)(2,1)S(1)}, bf16[256,768]{1,0:T(8,128)(2,1)S(1)}, bf16[2,256,256]{2,1,0:T(8,128)(2,1)S(1)}, bf16[256,256]{1,0:T(8,128)(2,1)S(1)}, bf16[16,128]{1,0:T(8,128)(2,1)S(1)}) custom-call(bf16[256,768]{1,0:T(8,128)(2,1)S(1)} %bitcast.15, bf16[8,256,512]{2,1,0:T(8,128)(2,1)} %ints_hbm.1, bf16[8,8]{1,0:T(8,128)(2,1)} %metric_hbm.1, ...), custom_call_target="tpu_custom_call" | custom-call | flops 268435456 | bytes 5242880 | tf_op jit(solution)/shard_map/stage/pallas_call | solution.py:315
  10.8 0.0 collective-permute-done.low_ref
  10.8 2.2 %collective-permute-done.1.high_ref = bf16[128,768]{1,0:T(8,128)(2,1)S(1)} collective-permute-done((bf16[128,768]{1,0:T(8,128)(2,1)S(1)}, bf16[128,768]{1,0:T(8,128)(2,1)S(1)}, u32[]{:S(2)}, u32[]{:S(2)}) %collective-permute-start.1) | collective-permute-done | bytes 196640 | tf_op jit(solution)/shard_map/ppermute | solution.py:429
  13.0 4.6 %fit.1 = bf16[32,400,128]{2,1,0:T(8,128)(2,1)} custom-call(bf16[128,768]{1,0:T(8,128)(2,1)S(1)} %collective-permute-done.low_ref, bf16[128,768]{1,0:T(8,128)(2,1)S(1)} %collective-permute-done.1.high_ref, bf16[256,768]{1,0:T(8,128)(2,1)S(1)} %get-tuple-element.12.own_ref, bf16[8,256,512]{2,1,0:T(8,128)(2,1)S(1)} %get-tuple-element.13.ints_ref, ...), custom_call_target="tpu_custom_call" | custom-call | flops 2415919104 | bytes 6291456 | tf_op jit(solution)/shard_map/fit/pallas_call | solution.py:333
  17.5 8.4 %all-to-all-start = ((bf16[32,400,128]{2,1,0:T(8,128)(2,1)}), bf16[32,400,128]{2,1,0:T(8,128)(2,1)S(1)}, u32[]{:S(2)}, u32[]{:S(2)}) async-start(bf16[32,400,128]{2,1,0:T(8,128)(2,1)} %fit.1), calls=%async_computation | async-start | bytes 6553600 | tf_op jit(solution)/shard_map/all_to_all | solution.py:435
  26.0 0.0 copy-start
  26.0 1.2 constant_dynamic-slice_fusion
  27.2 0.1 copy.11
  27.3 0.1 copy.10.coef_ref
  27.4 39.7 %all-to-all-done.got_ref = bf16[32,400,128]{2,1,0:T(8,128)(2,1)S(1)} async-done(((bf16[32,400,128]{2,1,0:T(8,128)(2,1)}), bf16[32,400,128]{2,1,0:T(8,128)(2,1)S(1)}, u32[]{:S(2)}, u32[]{:S(2)}) %all-to-all-start) | async-done | bytes 3276832 | tf_op jit(solution)/shard_map/all_to_all | solution.py:435
  67.1 6.7 %pair_sums.1 = (s32[32,128]{1,0:T(8,128)S(1)}, bf16[32,96,128]{2,1,0:T(8,128)(2,1)}) custom-call(s32[1]{0:T(128)} %bitcast.me_ref, bf16[256,96]{1,0:T(8,128)(2,1)S(1)} %copy.10.coef_ref, bf16[32,400,128]{2,1,0:T(8,128)(2,1)S(1)} %all-to-all-done.got_ref), custom_call_target="tpu_custom_call" | custom-call | tf_op jit(solution)/shard_map/pair_sums/pallas_call | solution.py:357
  73.8 5.7 %all-to-all-start.1 = ((bf16[32,96,128]{2,1,0:T(8,128)(2,1)}), bf16[32,96,128]{2,1,0:T(8,128)(2,1)S(1)}, u32[]{:S(2)}, u32[]{:S(2)}) async-start(bf16[32,96,128]{2,1,0:T(8,128)(2,1)} %get-tuple-element.18), calls=%async_computation.1 | async-start | bytes 1572864 | tf_op jit(solution)/shard_map/all_to_all | solution.py:451
  79.5 0.0 copy-done
  79.5 0.2 convert_reduce_fusion.refs_1_
  79.7 14.0 %all-to-all-done.1.refs_4_ = bf16[32,96,128]{2,1,0:T(8,128)(2,1)S(1)} async-done(((bf16[32,96,128]{2,1,0:T(8,128)(2,1)}), bf16[32,96,128]{2,1,0:T(8,128)(2,1)S(1)}, u32[]{:S(2)}, u32[]{:S(2)}) %all-to-all-start.1) | async-done | bytes 786464 | tf_op jit(solution)/shard_map/all_to_all | solution.py:451
  93.7 0.1 slice_reduce_fusion
  93.8 0.7 broadcast_in_dim.33
  94.4 8.2 %all-to-all-start.2 = ((bf16[8,64,128]{2,1,0:T(8,128)(2,1)}), bf16[8,64,128]{2,1,0:T(8,128)(2,1)S(1)}, u32[]{:S(2)}, u32[]{:S(2)}) async-start(bf16[8,64,128]{2,1,0:T(8,128)(2,1)} %broadcast_in_dim.33), calls=%async_computation.2 | async-start | bytes 262144 | tf_op jit(solution)/shard_map/all_to_all | solution.py:454
  102.6 0.1 select_reduce_fusion
  102.7 8.5 %all-to-all-done.2.refs_3_ = bf16[8,64,128]{2,1,0:T(8,128)(2,1)S(1)} async-done(((bf16[8,64,128]{2,1,0:T(8,128)(2,1)}), bf16[8,64,128]{2,1,0:T(8,128)(2,1)S(1)}, u32[]{:S(2)}, u32[]{:S(2)}) %all-to-all-start.2) | async-done | bytes 131104 | tf_op jit(solution)/shard_map/all_to_all | solution.py:454
  111.3 1.5 %make_slots.1 = bf16[32,32,128]{2,1,0:T(8,128)(2,1)} custom-call(s32[32]{0:T(128)S(1)} %bitcast.18, s32[32]{0:T(128)S(1)} %convert_reduce_fusion.refs_1_, s32[64]{0:T(128)S(1)} %broadcast_add_fusion.refs_2_, bf16[8,64,128]{2,1,0:T(8,128)(2,1)S(1)} %all-to-all-done.2.refs_3_, bf16[32,96,128]{2,1,0:T(8,128)(2,1)S(1)} %all-to-all-done.1.refs_4_), custom_call_target="tpu_custom_call" | custom-call | tf_op jit(solution)/shard_map/make_slots/pallas_call | solution.py:387
  112.8 4.9 %all-to-all-start.3 = ((bf16[32,32,128]{2,1,0:T(8,128)(2,1)}), bf16[32,32,128]{2,1,0:T(8,128)(2,1)S(1)}, u32[]{:S(2)}, u32[]{:S(2)}) async-start(bf16[32,32,128]{2,1,0:T(8,128)(2,1)} %make_slots.1), calls=%async_computation.3 | async-start | bytes 524288 | tf_op jit(solution)/shard_map/all_to_all | solution.py:456
  117.7 0.1 fusion.6
  117.8 0.1 reshape.54.row_ref
  117.9 0.1 reshape.55.count_ref
  118.0 8.8 %all-to-all-done.3.slot_ref = bf16[32,32,128]{2,1,0:T(8,128)(2,1)S(1)} async-done(((bf16[32,32,128]{2,1,0:T(8,128)(2,1)}), bf16[32,32,128]{2,1,0:T(8,128)(2,1)S(1)}, u32[]{:S(2)}, u32[]{:S(2)}) %all-to-all-start.3) | async-done | bytes 262176 | tf_op jit(solution)/shard_map/all_to_all | solution.py:456
  126.8 1.9 %add_gains.1 = f32[96,256]{1,0:T(8,128)} custom-call(s32[64]{0:T(128)S(1)} %reshape.54.row_ref, s32[64]{0:T(128)S(1)} %reshape.55.count_ref, bf16[32,32,128]{2,1,0:T(8,128)(2,1)S(1)} %all-to-all-done.3.slot_ref), custom_call_target="tpu_custom_call" | custom-call | tf_op jit(solution)/shard_map/add_gains/pallas_call | solution.py:399
  (4 shorter events, 0.1 us)
Async XLA Ops:
  1.3 9.4 %collective-permute-start = (bf16[128,768]{1,0:T(8,128)(2,1)S(1)}, bf16[128,768]{1,0:T(8,128)(2,1)S(1)}, u32[]{:S(2)}, u32[]{:S(2)}) collective-permute-start(bf16[128,768]{1,0:T(8,128)(2,1)S(1)} %bitcast.22), channel_id=1, source_target_pairs={{0,8},{8,16},{16,24},{24,32},{32,40},{40,48},{48,56},{56,64},{64,7... | collective-permute-start | bytes 589832 | tf_op jit(solution)/shard_map/ppermute | solution.py:428
  6.0 7.0 %collective-permute-start.1 = (bf16[128,768]{1,0:T(8,128)(2,1)S(1)}, bf16[128,768]{1,0:T(8,128)(2,1)S(1)}, u32[]{:S(2)}, u32[]{:S(2)}) collective-permute-start(bf16[128,768]{1,0:T(8,128)(2,1)S(1)} %bitcast.23), channel_id=1, source_target_pairs={{8,0},{16,8},{24,16},{32,24},{40,32},{48,40},{56,48},{64,56},{72,6... | collective-permute-start | bytes 589832 | tf_op jit(solution)/shard_map/ppermute | solution.py:429
  17.5 49.5 %all-to-all-start = ((bf16[32,400,128]{2,1,0:T(8,128)(2,1)}), bf16[32,400,128]{2,1,0:T(8,128)(2,1)S(1)}, u32[]{:S(2)}, u32[]{:S(2)}) async-start(bf16[32,400,128]{2,1,0:T(8,128)(2,1)} %fit.1), calls=%async_computation | async-start | bytes 6553600 | tf_op jit(solution)/shard_map/all_to_all | solution.py:435
  26.0 53.5 %copy-start = (s32[32,1]{0,1:T(1,128)S(1)}, s32[32,1]{0,1:T(1,128)}, u32[]{:S(2)}) copy-start(s32[32,1]{0,1:T(1,128)} %param.10) | copy-start | bytes 388
  73.8 19.9 %all-to-all-start.1 = ((bf16[32,96,128]{2,1,0:T(8,128)(2,1)}), bf16[32,96,128]{2,1,0:T(8,128)(2,1)S(1)}, u32[]{:S(2)}, u32[]{:S(2)}) async-start(bf16[32,96,128]{2,1,0:T(8,128)(2,1)} %get-tuple-element.18), calls=%async_computation.1 | async-start | bytes 1572864 | tf_op jit(solution)/shard_map/all_to_all | solution.py:451
  94.4 16.8 %all-to-all-start.2 = ((bf16[8,64,128]{2,1,0:T(8,128)(2,1)}), bf16[8,64,128]{2,1,0:T(8,128)(2,1)S(1)}, u32[]{:S(2)}, u32[]{:S(2)}) async-start(bf16[8,64,128]{2,1,0:T(8,128)(2,1)} %broadcast_in_dim.33), calls=%async_computation.2 | async-start | bytes 262144 | tf_op jit(solution)/shard_map/all_to_all | solution.py:454
  112.8 14.0 %all-to-all-start.3 = ((bf16[32,32,128]{2,1,0:T(8,128)(2,1)}), bf16[32,32,128]{2,1,0:T(8,128)(2,1)S(1)}, u32[]{:S(2)}, u32[]{:S(2)}) async-start(bf16[32,32,128]{2,1,0:T(8,128)(2,1)} %make_slots.1), calls=%async_computation.3 | async-start | bytes 524288 | tf_op jit(solution)/shard_map/all_to_all | solution.py:456

commit v7 on v6

--- a/solution.py
+++ b/solution.py
@@ -37,7 +37,8 @@
         real = part_ref[:, t * 128 : (t + 1) * 128]
         imag = part_ref[:, half + t * 128 : half + (t + 1) * 128]
         value = dot(jnp.concatenate([real, imag], axis=1), order_ref[t // 2])
-        window_ref[at : at + rows, t * 256 : (t + 1) * 256] = value.astype(jnp.bfloat16)
+        place = pl.ds(at if isinstance(at, int) else pl.multiple_of(at, 128), rows)
+        window_ref[place, t * 256 : (t + 1) * 256] = value.astype(jnp.bfloat16)
 
 
 def stage_kernel(
@@ -72,15 +73,16 @@
 
 
 def fit_kernel(
-    low_ref, high_ref, own_ref, ints_ref, order_ref, mix_ref, meta_ref, out_ref,
+    odd_ref, near_ref, far_ref, own_ref, ints_ref, order_ref, mix_ref, meta_ref, out_ref,
     window_ref, packed_ref, out_sem,
 ):
     aux_dev, bas_dev, span = ints_ref.shape
     blocks = bas_dev // ROWBLK
-    halo = low_ref.shape[0]
-    ordered(low_ref, order_ref, window_ref, 0)
+    halo = near_ref.shape[0]
+    far_at = odd_ref[0] * (halo + bas_dev)
+    ordered(near_ref, order_ref, window_ref, halo + bas_dev - far_at)
     window_ref[halo : halo + bas_dev] = own_ref[...]
-    ordered(high_ref, order_ref, window_ref, halo + bas_dev)
+    ordered(far_ref, order_ref, window_ref, far_at)
     mix = mix_ref[...]
     left = iota((ROWBLK // 2, 128), 1) < 64
     copies = []
@@ -264,34 +266,34 @@
         out_ref[s // 2, (s % 2) * MAXBF : (s % 2 + 1) * MAXBF] = rows.astype(jnp.bfloat16)
 
 
-def gain_kernel(row_ref, count_ref, slot_ref, out_ref, plain_ref, turned_ref):
-    plain_ref[...] = jnp.zeros(plain_ref.shape, jnp.float32)
-    turned_ref[...] = jnp.zeros(turned_ref.shape, jnp.float32)
+def gain_kernel(row_ref, count_ref, slot_ref, out_ref, sum_ref, turned_ref):
+    groups, rows, _ = slot_ref.shape
+    width, bas_dev = out_ref.shape
+    half = width // 2
+    u, v = iota((128, 128), 0), iota((128, 128), 1)
+    turn = jnp.where((v < half) & (u == v + half), -1.0, 0.0)
+    turn = jnp.where((v >= half) & (v < width) & (u == v - half), 1.0, turn).astype(jnp.bfloat16)
+    turned = dot(slot_ref[...].reshape(groups * rows, 128), turn).astype(jnp.bfloat16)
+    turned_ref[...] = turned.reshape(groups, rows, 128)
+    sum_ref[...] = jnp.zeros(sum_ref.shape, jnp.float32)
     lane, row_id = iota((MAXBF, 128), 1), iota((MAXBF, 128), 0)
-    masks = [lane < MAXBF, (lane >= MAXBF) & (lane < 2 * MAXBF)]
-    for g in range(slot_ref.shape[0]):
+    for g in range(groups):
         slots = slot_ref[g]
         wide = slots.astype(jnp.float32)
         tiles = []
-        for c in range(2):
-            for r in range(2):
-                tile = wide[r * MAXBF : (r + 1) * MAXBF]
-                tile = pltpu.roll(tile, 32 + 16 * (r - c), 1)
-                tiles.append(jnp.where(masks[r], tile, 0.0))
-        tiles = jnp.concatenate(tiles, axis=0)[:, 0:32].astype(jnp.bfloat16)
-        gains = dot(tiles, slots)
-        for c, sum_ref in enumerate((plain_ref, turned_ref)):
-            for r in range(2):
-                at = (2 * c + r) * MAXBF
-                part = jnp.where(row_id < count_ref[2 * g + r], gains[at : at + MAXBF], 0.0)
-                where = pl.ds(row_ref[2 * g + r], MAXBF)
-                sum_ref[where] = sum_ref[where] + part
-    width, bas_dev = out_ref.shape
-    half = width // 2
-    plain = plain_ref[0:bas_dev].T
-    turned = turned_ref[0:bas_dev].T
-    out_ref[0:half] = plain[0:half] - turned[half:width]
-    out_ref[half:width] = plain[half:width] + turned[0:half]
+        for r in range(2):
+            tile = wide[r * MAXBF : (r + 1) * MAXBF]
+            real = jnp.where(lane // MAXBF == r, pltpu.roll(tile, 32 + 16 * r, 1), 0.0)
+            imag = jnp.where(lane // MAXBF == 2 + r, pltpu.roll(tile, 48 + 16 * r, 1), 0.0)
+            tiles.append(real + imag)
+        tiles = jnp.concatenate(tiles, axis=0)[:, 0:64].astype(jnp.bfloat16)
+        gains = dot(tiles, jnp.concatenate([slots, turned_ref[g]], axis=0))
+        for r in range(2):
+            part = gains[r * MAXBF : (r + 1) * MAXBF]
+            part = jnp.where(row_id < count_ref[2 * g + r], part, 0.0)
+            where = pl.ds(row_ref[2 * g + r], MAXBF)
+            sum_ref[where] = sum_ref[where] + part
+    out_ref[...] = sum_ref[0:bas_dev].T[0:width]
 
 
 def vmem_spec():
@@ -325,14 +327,14 @@
     )(own, *[in_hbm(x) for x in fetched])
 
 
-def fit(low, high, window_rows, ints, order, mix, meta):
+def fit(odd, near, far, window_rows, ints, order, mix, meta):
     aux_dev, bas_dev, window = ints.shape
-    width = low.shape[1]
+    width = near.shape[1]
     blocks = bas_dev // ROWBLK
     shape = (4 * aux_dev, blocks * PACKED + 16, 128)
     return pl.pallas_call(
         fit_kernel,
-        in_specs=[vmem_spec()] * 7,
+        in_specs=[smem_spec()] + [vmem_spec()] * 7,
         out_specs=pl.BlockSpec(memory_space=pltpu.HBM),
         out_shape=pltpu.HBM(shape, jnp.bfloat16),
         scratch_shapes=[
@@ -347,7 +349,7 @@
             transcendentals=0,
         ),
         name="fit",
-    )(low, high, window_rows, ints, order, mix, meta)
+    )(odd, near, far, window_rows, ints, order, mix, meta)
 
 
 def pair_sums(me, coef, got):
@@ -401,7 +403,10 @@
         in_specs=[smem_spec()] * 2 + [vmem_spec()],
         out_specs=vmem_spec(),
         out_shape=jax.ShapeDtypeStruct((width, bas_dev), jnp.float32),
-        scratch_shapes=[pltpu.VMEM((bas_dev + MAXBF, 128), jnp.float32)] * 2,
+        scratch_shapes=[
+            pltpu.VMEM((bas_dev + MAXBF, 128), jnp.float32),
+            pltpu.VMEM(slots.shape, jnp.bfloat16),
+        ],
         compiler_params=limit(16),
         name="add_gains",
     )(rows, counts, slots)
@@ -423,15 +428,18 @@
     me = lax.axis_index("atom")
 
     own = coeffs.reshape(bas_dev, 2 * occ)
-    forward = [(i, i + 1) for i in range(groups - 1)]
-    backward = [(i + 1, i) for i in range(groups - 1)]
-    low = lax.ppermute(own[bas_dev - halo :], "atom", forward)
-    high = lax.ppermute(own[:halo], "atom", backward)
+    odd = lax.axis_index("atom") % 2
+    near = lax.dynamic_slice_in_dim(own, (1 - odd) * halo, halo, 0)
+    near = lax.ppermute(near, "atom", [(i, i ^ 1) for i in range(groups)])
+    far = lax.dynamic_slice_in_dim(own, odd * halo, halo, 0)
+    inner = range(1, groups - 1)
+    far = lax.ppermute(far, "atom", [(i, i + 1 if i % 2 else i - 1) for i in inner])
 
     ints, window_rows, order, mix, meta = stage(
         own, integrals, metric, atom_sizes, pair_device.T, pair_atom[None]
     )
-    packed = fit(low, high, window_rows, ints, order, mix, meta)
+    odd = jnp.full((1,), odd, jnp.int32)
+    packed = fit(odd, near, far, window_rows, ints, order, mix, meta)
     got = lax.all_to_all(packed, "atom", split_axis=0, concat_axis=0, tiled=True)
     coef_part = lax.dynamic_slice_in_dim(
         coeffs, lax.axis_index("aux") * occ_part, occ_part, 2

time: 129 us -> 127 us (0.984)
  starting transfers between devices: 33.7 us -> 31.4 us
  local copies, waits for them, and re-layouts: 4.73 us -> 3.42 us
    slice x1 -> x0, local copies, waits for them, and re-layouts: 1.29 us -> none  [per_device(): high = lax.ppermute(own[:halo], 'atom', backward)]
where the time goes in v7:
time: 127 us; the launch traced here: 126 us
  waiting for transfers between devices  74.3 us (59%)
  starting transfers between devices  31.4 us (25%)
  Pallas kernels  16.6 us (13%)
  local copies, waits for them, and re-layouts  3.42 us (3%)
    all_to_all x1, waiting for transfers between devices, per_device(): lax.all_to_all(packed, 'atom', split_axis=0, concat_axis=0, tiled=True)  39.7 us
    all_to_all x1, waiting for transfers between devices, per_device(): lax.all_to_all(sent, 'atom', split_axis=0, concat_axis=0, tiled=True)  14 us
    all_to_all x1, waiting for transfers between devices, per_device(): lax.all_to_all(slots, 'atom', split_axis=0, concat_axis=0, tiled=True)  8.81 us
    all_to_all x1, waiting for transfers between devices, per_device(): lax.all_to_all(shared, 'aux', split_axis=0, concat_axis=0, tiled=True)  8.54 us
    all_to_all x1, starting transfers between devices, per_device(): lax.all_to_all(shared, 'aux', split_axis=0, concat_axis=0, tiled=True)  8.19 us
    all_to_all x1, starting transfers between devices, per_device(): lax.all_to_all(packed, 'atom', split_axis=0, concat_axis=0, tiled=True)  7.41 us
    pallas_call x1, Pallas kernels, pair_sums(): pl.pallas_call(pair_kernel, in_specs=[smem_spec(), vmem_spec(), vmem_spec...  6.69 us
    all_to_all x1, starting transfers between devices, per_device(): lax.all_to_all(sent, 'atom', split_axis=0, concat_axis=0, tiled=True)  5.68 us
  transfers between devices with their start and end apart: 6, of which 5 were waited for; matrix products, arithmetic and copies ran while one was open for 2% of the time, Pallas kernels for 1%

profile of v7, /device:TPU:1, one launch (start us, length us, event | category | flops | bytes accessed | tf_op | source)
XLA Modules:
  0.0 126.2 jit_solution(851143003707626331)
XLA Ops:
  0.0 1.0 copy.12
  1.1 3.3 %collective-permute-start = (bf16[128,768]{1,0:T(8,128)(2,1)S(1)}, bf16[128,768]{1,0:T(8,128)(2,1)S(1)}, u32[]{:S(2)}, u32[]{:S(2)}) collective-permute-start(bf16[128,768]{1,0:T(8,128)(2,1)S(1)} %get-tuple-element.20), channel_id=1, source_target_pairs={{0,8},{8,0},{16,24},{24,16},{32,40},{40,32},{48,56},{56,48},{64,72... | collective-permute-start | bytes 589832 | tf_op jit(solution)/shard_map/ppermute | solution.py:433
  4.4 1.9 %collective-permute-start.1 = (bf16[128,768]{1,0:T(8,128)(2,1)S(1)}, bf16[128,768]{1,0:T(8,128)(2,1)S(1)}, u32[]{:S(2)}, u32[]{:S(2)}) collective-permute-start(bf16[128,768]{1,0:T(8,128)(2,1)S(1)} %get-tuple-element.19), channel_id=1, source_target_pairs={{8,16},{16,8},{24,32},{32,24},{40,48},{48,40},{56,64},{64,56},{72,... | collective-permute-start | bytes 589832 | tf_op jit(solution)/shard_map/ppermute | solution.py:436
  6.3 1.8 %stage.1 = (bf16[8,256,512]{2,1,0:T(8,128)(2,1)S(1)}, bf16[256,768]{1,0:T(8,128)(2,1)S(1)}, bf16[2,256,256]{2,1,0:T(8,128)(2,1)S(1)}, bf16[256,256]{1,0:T(8,128)(2,1)S(1)}, bf16[16,128]{1,0:T(8,128)(2,1)S(1)}) custom-call(bf16[256,768]{1,0:T(8,128)(2,1)S(1)} %bitcast.13, bf16[8,256,512]{2,1,0:T(8,128)(2,1)} %ints_hbm.1, bf16[8,8]{1,0:T(8,128)(2,1)} %metric_hbm.1, ...), custom_call_target="tpu_custom_call" | custom-call | flops 268435456 | bytes 5242880 | tf_op jit(solution)/shard_map/stage/pallas_call | solution.py:317
  8.2 0.0 collective-permute-done.near_ref
  8.2 3.2 %collective-permute-done.1.far_ref = bf16[128,768]{1,0:T(8,128)(2,1)S(1)} collective-permute-done((bf16[128,768]{1,0:T(8,128)(2,1)S(1)}, bf16[128,768]{1,0:T(8,128)(2,1)S(1)}, u32[]{:S(2)}, u32[]{:S(2)}) %collective-permute-start.1) | collective-permute-done | bytes 196640 | tf_op jit(solution)/shard_map/ppermute | solution.py:436
  11.4 4.7 %fit.1 = bf16[32,400,128]{2,1,0:T(8,128)(2,1)} custom-call(s32[1]{0:T(128)} %bitcast.2.odd_ref, bf16[128,768]{1,0:T(8,128)(2,1)S(1)} %collective-permute-done.near_ref, bf16[128,768]{1,0:T(8,128)(2,1)S(1)} %collective-permute-done.1.far_ref, bf16[256,768]{1,0:T(8,128)(2,1)S(1)} %get-tuple-element.12.own_ref, ...), custom_call_target="tpu_custom_call" | custom-call | flops 2415919104 | bytes 6291456 | tf_op jit(solution)/shard_map/fit/pallas_call | solution.py:335
  16.1 7.4 %all-to-all-start = ((bf16[32,400,128]{2,1,0:T(8,128)(2,1)}), bf16[32,400,128]{2,1,0:T(8,128)(2,1)S(1)}, u32[]{:S(2)}, u32[]{:S(2)}) async-start(bf16[32,400,128]{2,1,0:T(8,128)(2,1)} %fit.1), calls=%async_computation | async-start | bytes 6553600 | tf_op jit(solution)/shard_map/all_to_all | solution.py:443
  23.5 0.0 copy-start
  23.5 1.2 constant_dynamic-slice_fusion.2
  24.7 0.1 copy.11
  24.8 0.1 copy.10.coef_ref
  24.9 39.7 %all-to-all-done.got_ref = bf16[32,400,128]{2,1,0:T(8,128)(2,1)S(1)} async-done(((bf16[32,400,128]{2,1,0:T(8,128)(2,1)}), bf16[32,400,128]{2,1,0:T(8,128)(2,1)S(1)}, u32[]{:S(2)}, u32[]{:S(2)}) %all-to-all-start) | async-done | bytes 3276832 | tf_op jit(solution)/shard_map/all_to_all | solution.py:443
  64.6 6.7 %pair_sums.1 = (s32[32,128]{1,0:T(8,128)S(1)}, bf16[32,96,128]{2,1,0:T(8,128)(2,1)}) custom-call(s32[1]{0:T(128)} %bitcast.me_ref, bf16[256,96]{1,0:T(8,128)(2,1)S(1)} %copy.10.coef_ref, bf16[32,400,128]{2,1,0:T(8,128)(2,1)S(1)} %all-to-all-done.got_ref), custom_call_target="tpu_custom_call" | custom-call | tf_op jit(solution)/shard_map/pair_sums/pallas_call | solution.py:359
  71.3 5.7 %all-to-all-start.1 = ((bf16[32,96,128]{2,1,0:T(8,128)(2,1)}), bf16[32,96,128]{2,1,0:T(8,128)(2,1)S(1)}, u32[]{:S(2)}, u32[]{:S(2)}) async-start(bf16[32,96,128]{2,1,0:T(8,128)(2,1)} %get-tuple-element.18), calls=%async_computation.1 | async-start | bytes 1572864 | tf_op jit(solution)/shard_map/all_to_all | solution.py:459
  77.0 0.0 copy-done
  77.0 0.2 convert_reduce_fusion.refs_1_
  77.2 14.0 %all-to-all-done.1.refs_4_ = bf16[32,96,128]{2,1,0:T(8,128)(2,1)S(1)} async-done(((bf16[32,96,128]{2,1,0:T(8,128)(2,1)}), bf16[32,96,128]{2,1,0:T(8,128)(2,1)S(1)}, u32[]{:S(2)}, u32[]{:S(2)}) %all-to-all-start.1) | async-done | bytes 786464 | tf_op jit(solution)/shard_map/all_to_all | solution.py:459
  91.2 0.1 slice_reduce_fusion
  91.3 0.7 broadcast_in_dim.37
  92.0 8.2 %all-to-all-start.2 = ((bf16[8,64,128]{2,1,0:T(8,128)(2,1)}), bf16[8,64,128]{2,1,0:T(8,128)(2,1)S(1)}, u32[]{:S(2)}, u32[]{:S(2)}) async-start(bf16[8,64,128]{2,1,0:T(8,128)(2,1)} %broadcast_in_dim.37), calls=%async_computation.2 | async-start | bytes 262144 | tf_op jit(solution)/shard_map/all_to_all | solution.py:462
  100.1 0.1 select_reduce_fusion
  100.2 8.5 %all-to-all-done.2.refs_3_ = bf16[8,64,128]{2,1,0:T(8,128)(2,1)S(1)} async-done(((bf16[8,64,128]{2,1,0:T(8,128)(2,1)}), bf16[8,64,128]{2,1,0:T(8,128)(2,1)S(1)}, u32[]{:S(2)}, u32[]{:S(2)}) %all-to-all-start.2) | async-done | bytes 131104 | tf_op jit(solution)/shard_map/all_to_all | solution.py:462
  108.8 1.5 %make_slots.1 = bf16[32,32,128]{2,1,0:T(8,128)(2,1)} custom-call(s32[32]{0:T(128)S(1)} %bitcast.16, s32[32]{0:T(128)S(1)} %convert_reduce_fusion.refs_1_, s32[64]{0:T(128)S(1)} %broadcast_add_fusion.refs_2_, bf16[8,64,128]{2,1,0:T(8,128)(2,1)S(1)} %all-to-all-done.2.refs_3_, bf16[32,96,128]{2,1,0:T(8,128)(2,1)S(1)} %all-to-all-done.1.refs_4_), custom_call_target="tpu_custom_call" | custom-call | tf_op jit(solution)/shard_map/make_slots/pallas_call | solution.py:389
  110.3 4.9 %all-to-all-start.3 = ((bf16[32,32,128]{2,1,0:T(8,128)(2,1)}), bf16[32,32,128]{2,1,0:T(8,128)(2,1)S(1)}, u32[]{:S(2)}, u32[]{:S(2)}) async-start(bf16[32,32,128]{2,1,0:T(8,128)(2,1)} %make_slots.1), calls=%async_computation.3 | async-start | bytes 524288 | tf_op jit(solution)/shard_map/all_to_all | solution.py:464
  115.2 0.1 fusion.5
  115.3 0.1 reshape.52.row_ref
  115.4 0.1 reshape.53.count_ref
  115.5 8.8 %all-to-all-done.3.slot_ref = bf16[32,32,128]{2,1,0:T(8,128)(2,1)S(1)} async-done(((bf16[32,32,128]{2,1,0:T(8,128)(2,1)}), bf16[32,32,128]{2,1,0:T(8,128)(2,1)S(1)}, u32[]{:S(2)}, u32[]{:S(2)}) %all-to-all-start.3) | async-done | bytes 262176 | tf_op jit(solution)/shard_map/all_to_all | solution.py:464
  124.3 1.9 %add_gains.1 = f32[96,256]{1,0:T(8,128)} custom-call(s32[64]{0:T(128)S(1)} %reshape.52.row_ref, s32[64]{0:T(128)S(1)} %reshape.53.count_ref, bf16[32,32,128]{2,1,0:T(8,128)(2,1)S(1)} %all-to-all-done.3.slot_ref), custom_call_target="tpu_custom_call" | custom-call | tf_op jit(solution)/shard_map/add_gains/pallas_call | solution.py:401
  (3 shorter events, 0.0 us)
Async XLA Ops:
  1.1 7.1 %collective-permute-start = (bf16[128,768]{1,0:T(8,128)(2,1)S(1)}, bf16[128,768]{1,0:T(8,128)(2,1)S(1)}, u32[]{:S(2)}, u32[]{:S(2)}) collective-permute-start(bf16[128,768]{1,0:T(8,128)(2,1)S(1)} %get-tuple-element.20), channel_id=1, source_target_pairs={{0,8},{8,0},{16,24},{24,16},{32,40},{40,32},{48,56},{56,48},{64,72... | collective-permute-start | bytes 589832 | tf_op jit(solution)/shard_map/ppermute | solution.py:433
  4.4 7.0 %collective-permute-start.1 = (bf16[128,768]{1,0:T(8,128)(2,1)S(1)}, bf16[128,768]{1,0:T(8,128)(2,1)S(1)}, u32[]{:S(2)}, u32[]{:S(2)}) collective-permute-start(bf16[128,768]{1,0:T(8,128)(2,1)S(1)} %get-tuple-element.19), channel_id=1, source_target_pairs={{8,16},{16,8},{24,32},{32,24},{40,48},{48,40},{56,64},{64,56},{72,... | collective-permute-start | bytes 589832 | tf_op jit(solution)/shard_map/ppermute | solution.py:436
  16.1 48.5 %all-to-all-start = ((bf16[32,400,128]{2,1,0:T(8,128)(2,1)}), bf16[32,400,128]{2,1,0:T(8,128)(2,1)S(1)}, u32[]{:S(2)}, u32[]{:S(2)}) async-start(bf16[32,400,128]{2,1,0:T(8,128)(2,1)} %fit.1), calls=%async_computation | async-start | bytes 6553600 | tf_op jit(solution)/shard_map/all_to_all | solution.py:443
  23.5 53.5 %copy-start = (s32[32,1]{0,1:T(1,128)S(1)}, s32[32,1]{0,1:T(1,128)}, u32[]{:S(2)}) copy-start(s32[32,1]{0,1:T(1,128)} %param.10) | copy-start | bytes 388
  71.3 19.9 %all-to-all-start.1 = ((bf16[32,96,128]{2,1,0:T(8,128)(2,1)}), bf16[32,96,128]{2,1,0:T(8,128)(2,1)S(1)}, u32[]{:S(2)}, u32[]{:S(2)}) async-start(bf16[32,96,128]{2,1,0:T(8,128)(2,1)} %get-tuple-element.18), calls=%async_computation.1 | async-start | bytes 1572864 | tf_op jit(solution)/shard_map/all_to_all | solution.py:459
  92.0 16.8 %all-to-all-start.2 = ((bf16[8,64,128]{2,1,0:T(8,128)(2,1)}), bf16[8,64,128]{2,1,0:T(8,128)(2,1)S(1)}, u32[]{:S(2)}, u32[]{:S(2)}) async-start(bf16[8,64,128]{2,1,0:T(8,128)(2,1)} %broadcast_in_dim.37), calls=%async_computation.2 | async-start | bytes 262144 | tf_op jit(solution)/shard_map/all_to_all | solution.py:462
  110.3 14.0 %all-to-all-start.3 = ((bf16[32,32,128]{2,1,0:T(8,128)(2,1)}), bf16[32,32,128]{2,1,0:T(8,128)(2,1)S(1)}, u32[]{:S(2)}, u32[]{:S(2)}) async-start(bf16[32,32,128]{2,1,0:T(8,128)(2,1)} %make_slots.1), calls=%async_computation.3 | async-start | bytes 524288 | tf_op jit(solution)/shard_map/all_to_all | solution.py:464

commit v8 on v7

--- a/solution.py
+++ b/solution.py
@@ -10,7 +10,7 @@
 MAXBF = 16
 ROWBLK = 32
 PACKED = ROWBLK + ROWBLK // 2
-BATCH = 8
+BATCH = 16
 MIB = 1 << 20
 
 
@@ -179,7 +179,7 @@
                 imag_ref[pl.ds(base + h * 16, 16)] = imag
         return carry
 
-    lax.fori_loop(0, groups, unpack, 0, unroll=4)
+    lax.fori_loop(0, groups, unpack, 0, unroll=8)
     tail = groups * blocks * ROWBLK
     real_ref[tail : tail + MAXBF] = jnp.zeros((MAXBF, 128), jnp.float32)
     imag_ref[tail : tail + MAXBF] = jnp.zeros((MAXBF, 128), jnp.float32)
@@ -245,7 +245,7 @@
 
     def coef(e):
         at = pl.multiple_of(64 + rank_ref[e] * MAXBF, MAXBF)
-        return got_ref[target_ref[e], pl.ds(at, MAXBF)].astype(jnp.float32)
+        return got_ref[target_ref[e], pl.ds(at, MAXBF)]
 
     for h in range(2):
         block = kernel[h * 32 : (h + 1) * 32]
@@ -254,16 +254,17 @@
             tile = block[c * MAXBF : (c + 1) * MAXBF].astype(jnp.float32)
             wide = jnp.where(same, jnp.concatenate([tile] * 8, axis=0), 0.0)
             first = first + dot(wide.astype(jnp.bfloat16), folds[c])
-        second = dot_tn(block, turned)
+        first = first.astype(jnp.bfloat16)
+        second = dot_tn(block, turned).astype(jnp.bfloat16)
         for j in range(8):
             pair, rows = h * 8 + j, slice(j * MAXBF, (j + 1) * MAXBF)
             at = pair * MAXBF
             tile_ref[at : at + MAXBF] = first[rows] + coef(2 * pair + 1)
             tile_ref[256 + at : 256 + at + MAXBF] = second[rows] + coef(2 * pair)
-    tile_ref[512:528] = jnp.zeros((MAXBF, 128), jnp.float32)
+    tile_ref[512:528] = jnp.zeros((MAXBF, 128), jnp.bfloat16)
     for s in range(2 * out_ref.shape[0]):
         rows = tile_ref[pl.ds(pl.multiple_of(place_ref[s], MAXBF), MAXBF)]
-        out_ref[s // 2, (s % 2) * MAXBF : (s % 2 + 1) * MAXBF] = rows.astype(jnp.bfloat16)
+        out_ref[s // 2, (s % 2) * MAXBF : (s % 2 + 1) * MAXBF] = rows
 
 
 def gain_kernel(row_ref, count_ref, slot_ref, out_ref, sum_ref, turned_ref):
@@ -391,7 +392,7 @@
         in_specs=[smem_spec()] * 3 + [vmem_spec()] * 2,
         out_specs=vmem_spec(),
         out_shape=jax.ShapeDtypeStruct((got.shape[0], 2 * MAXBF, 128), jnp.bfloat16),
-        scratch_shapes=[pltpu.VMEM((528, 128), jnp.float32)],
+        scratch_shapes=[pltpu.VMEM((528, 128), jnp.bfloat16)],
         compiler_params=limit(16),
         name="make_slots",
     )(targets, ranks, places, parts, got)
@@ -429,11 +430,11 @@
 
     own = coeffs.reshape(bas_dev, 2 * occ)
     odd = lax.axis_index("atom") % 2
+    inner = range(1, groups - 1)
+    far = lax.dynamic_slice_in_dim(own, odd * halo, halo, 0)
+    far = lax.ppermute(far, "atom", [(i, i + 1 if i % 2 else i - 1) for i in inner])
     near = lax.dynamic_slice_in_dim(own, (1 - odd) * halo, halo, 0)
     near = lax.ppermute(near, "atom", [(i, i ^ 1) for i in range(groups)])
-    far = lax.dynamic_slice_in_dim(own, odd * halo, halo, 0)
-    inner = range(1, groups - 1)
-    far = lax.ppermute(far, "atom", [(i, i + 1 if i % 2 else i - 1) for i in inner])
 
     ints, window_rows, order, mix, meta = stage(
         own, integrals, metric, atom_sizes, pair_device.T, pair_atom[None]

time: 127 us -> 126 us (level)
  no operation moved by 1% of the time
where the time goes in v8:
time: 126 us
  waiting for transfers between devices  74.3 us (59%)
  starting transfers between devices  31.4 us (25%)
  Pallas kernels  16.1 us (13%)
  local copies, waits for them, and re-layouts  3.42 us (3%)
    all_to_all x1, waiting for transfers between devices, per_device(): lax.all_to_all(packed, 'atom', split_axis=0, concat_axis=0, tiled=True)  39.7 us
    all_to_all x1, waiting for transfers between devices, per_device(): lax.all_to_all(sent, 'atom', split_axis=0, concat_axis=0, tiled=True)  14 us
    all_to_all x1, waiting for transfers between devices, per_device(): lax.all_to_all(slots, 'atom', split_axis=0, concat_axis=0, tiled=True)  8.81 us
    all_to_all x1, waiting for transfers between devices, per_device(): lax.all_to_all(shared, 'aux', split_axis=0, concat_axis=0, tiled=True)  8.54 us
    all_to_all x1, starting transfers between devices, per_device(): lax.all_to_all(shared, 'aux', split_axis=0, concat_axis=0, tiled=True)  8.18 us
    all_to_all x1, starting transfers between devices, per_device(): lax.all_to_all(packed, 'atom', split_axis=0, concat_axis=0, tiled=True)  7.41 us
    pallas_call x1, Pallas kernels, pair_sums(): pl.pallas_call(pair_kernel, in_specs=[smem_spec(), vmem_spec(), vmem_spec...  6.23 us
    all_to_all x1, starting transfers between devices, per_device(): lax.all_to_all(sent, 'atom', split_axis=0, concat_axis=0, tiled=True)  5.68 us
  transfers between devices with their start and end apart: 6, of which 5 were waited for; matrix products, arithmetic and copies ran while one was open for 2% of the time, Pallas kernels for 1%

profile of v8, /device:TPU:1, one launch (start us, length us, event | category | flops | bytes accessed | tf_op | source)
XLA Modules:
  0.0 125.8 jit_solution(15457417067095798352)
XLA Ops:
  0.0 1.0 copy.12
  1.1 3.3 %collective-permute-start = (bf16[128,768]{1,0:T(8,128)(2,1)S(1)}, bf16[128,768]{1,0:T(8,128)(2,1)S(1)}, u32[]{:S(2)}, u32[]{:S(2)}) collective-permute-start(bf16[128,768]{1,0:T(8,128)(2,1)S(1)} %get-tuple-element.20), channel_id=1, source_target_pairs={{0,8},{8,0},{16,24},{24,16},{32,40},{40,32},{48,56},{56,48},{64,72... | collective-permute-start | bytes 589832 | tf_op jit(solution)/shard_map/ppermute | solution.py:437
  4.4 1.9 %collective-permute-start.1 = (bf16[128,768]{1,0:T(8,128)(2,1)S(1)}, bf16[128,768]{1,0:T(8,128)(2,1)S(1)}, u32[]{:S(2)}, u32[]{:S(2)}) collective-permute-start(bf16[128,768]{1,0:T(8,128)(2,1)S(1)} %get-tuple-element.19), channel_id=1, source_target_pairs={{8,16},{16,8},{24,32},{32,24},{40,48},{48,40},{56,64},{64,56},{72,... | collective-permute-start | bytes 589832 | tf_op jit(solution)/shard_map/ppermute | solution.py:435
  6.3 1.8 %stage.1 = (bf16[8,256,512]{2,1,0:T(8,128)(2,1)S(1)}, bf16[256,768]{1,0:T(8,128)(2,1)S(1)}, bf16[2,256,256]{2,1,0:T(8,128)(2,1)S(1)}, bf16[256,256]{1,0:T(8,128)(2,1)S(1)}, bf16[16,128]{1,0:T(8,128)(2,1)S(1)}) custom-call(bf16[256,768]{1,0:T(8,128)(2,1)S(1)} %bitcast.13, bf16[8,256,512]{2,1,0:T(8,128)(2,1)} %ints_hbm.1, bf16[8,8]{1,0:T(8,128)(2,1)} %metric_hbm.1, ...), custom_call_target="tpu_custom_call" | custom-call | flops 268435456 | bytes 5242880 | tf_op jit(solution)/shard_map/stage/pallas_call | solution.py:318
  8.2 0.0 collective-permute-done.near_ref
  8.2 3.2 %collective-permute-done.1.far_ref = bf16[128,768]{1,0:T(8,128)(2,1)S(1)} collective-permute-done((bf16[128,768]{1,0:T(8,128)(2,1)S(1)}, bf16[128,768]{1,0:T(8,128)(2,1)S(1)}, u32[]{:S(2)}, u32[]{:S(2)}) %collective-permute-start.1) | collective-permute-done | bytes 196640 | tf_op jit(solution)/shard_map/ppermute | solution.py:435
  11.4 4.7 %fit.1 = bf16[32,400,128]{2,1,0:T(8,128)(2,1)} custom-call(s32[1]{0:T(128)} %bitcast.2.odd_ref, bf16[128,768]{1,0:T(8,128)(2,1)S(1)} %collective-permute-done.near_ref, bf16[128,768]{1,0:T(8,128)(2,1)S(1)} %collective-permute-done.1.far_ref, bf16[256,768]{1,0:T(8,128)(2,1)S(1)} %get-tuple-element.12.own_ref, ...), custom_call_target="tpu_custom_call" | custom-call | flops 2415919104 | bytes 6291456 | tf_op jit(solution)/shard_map/fit/pallas_call | solution.py:336
  16.1 7.4 %all-to-all-start = ((bf16[32,400,128]{2,1,0:T(8,128)(2,1)}), bf16[32,400,128]{2,1,0:T(8,128)(2,1)S(1)}, u32[]{:S(2)}, u32[]{:S(2)}) async-start(bf16[32,400,128]{2,1,0:T(8,128)(2,1)} %fit.1), calls=%async_computation | async-start | bytes 6553600 | tf_op jit(solution)/shard_map/all_to_all | solution.py:444
  23.5 0.0 copy-start
  23.5 1.2 constant_dynamic-slice_fusion.2
  24.7 0.1 copy.11
  24.8 0.1 copy.10.coef_ref
  24.9 39.7 %all-to-all-done.got_ref = bf16[32,400,128]{2,1,0:T(8,128)(2,1)S(1)} async-done(((bf16[32,400,128]{2,1,0:T(8,128)(2,1)}), bf16[32,400,128]{2,1,0:T(8,128)(2,1)S(1)}, u32[]{:S(2)}, u32[]{:S(2)}) %all-to-all-start) | async-done | bytes 3276832 | tf_op jit(solution)/shard_map/all_to_all | solution.py:444
  64.6 6.2 %pair_sums.1 = (s32[32,128]{1,0:T(8,128)S(1)}, bf16[32,96,128]{2,1,0:T(8,128)(2,1)}) custom-call(s32[1]{0:T(128)} %bitcast.me_ref, bf16[256,96]{1,0:T(8,128)(2,1)S(1)} %copy.10.coef_ref, bf16[32,400,128]{2,1,0:T(8,128)(2,1)S(1)} %all-to-all-done.got_ref), custom_call_target="tpu_custom_call" | custom-call | tf_op jit(solution)/shard_map/pair_sums/pallas_call | solution.py:360
  70.8 5.7 %all-to-all-start.1 = ((bf16[32,96,128]{2,1,0:T(8,128)(2,1)}), bf16[32,96,128]{2,1,0:T(8,128)(2,1)S(1)}, u32[]{:S(2)}, u32[]{:S(2)}) async-start(bf16[32,96,128]{2,1,0:T(8,128)(2,1)} %get-tuple-element.18), calls=%async_computation.1 | async-start | bytes 1572864 | tf_op jit(solution)/shard_map/all_to_all | solution.py:460
  76.5 0.0 copy-done
  76.5 0.2 convert_reduce_fusion.refs_1_
  76.7 14.0 %all-to-all-done.1.refs_4_ = bf16[32,96,128]{2,1,0:T(8,128)(2,1)S(1)} async-done(((bf16[32,96,128]{2,1,0:T(8,128)(2,1)}), bf16[32,96,128]{2,1,0:T(8,128)(2,1)S(1)}, u32[]{:S(2)}, u32[]{:S(2)}) %all-to-all-start.1) | async-done | bytes 786464 | tf_op jit(solution)/shard_map/all_to_all | solution.py:460
  90.7 0.1 slice_reduce_fusion
  90.8 0.7 broadcast_in_dim.37
  91.5 8.2 %all-to-all-start.2 = ((bf16[8,64,128]{2,1,0:T(8,128)(2,1)}), bf16[8,64,128]{2,1,0:T(8,128)(2,1)S(1)}, u32[]{:S(2)}, u32[]{:S(2)}) async-start(bf16[8,64,128]{2,1,0:T(8,128)(2,1)} %broadcast_in_dim.37), calls=%async_computation.2 | async-start | bytes 262144 | tf_op jit(solution)/shard_map/all_to_all | solution.py:463
  99.7 0.1 select_reduce_fusion
  99.8 8.5 %all-to-all-done.2.refs_3_ = bf16[8,64,128]{2,1,0:T(8,128)(2,1)S(1)} async-done(((bf16[8,64,128]{2,1,0:T(8,128)(2,1)}), bf16[8,64,128]{2,1,0:T(8,128)(2,1)S(1)}, u32[]{:S(2)}, u32[]{:S(2)}) %all-to-all-start.2) | async-done | bytes 131104 | tf_op jit(solution)/shard_map/all_to_all | solution.py:463
  108.3 1.5 %make_slots.1 = bf16[32,32,128]{2,1,0:T(8,128)(2,1)} custom-call(s32[32]{0:T(128)S(1)} %bitcast.16, s32[32]{0:T(128)S(1)} %convert_reduce_fusion.refs_1_, s32[64]{0:T(128)S(1)} %broadcast_add_fusion.refs_2_, bf16[8,64,128]{2,1,0:T(8,128)(2,1)S(1)} %all-to-all-done.2.refs_3_, bf16[32,96,128]{2,1,0:T(8,128)(2,1)S(1)} %all-to-all-done.1.refs_4_), custom_call_target="tpu_custom_call" | custom-call | tf_op jit(solution)/shard_map/make_slots/pallas_call | solution.py:390
  109.8 4.9 %all-to-all-start.3 = ((bf16[32,32,128]{2,1,0:T(8,128)(2,1)}), bf16[32,32,128]{2,1,0:T(8,128)(2,1)S(1)}, u32[]{:S(2)}, u32[]{:S(2)}) async-start(bf16[32,32,128]{2,1,0:T(8,128)(2,1)} %make_slots.1), calls=%async_computation.3 | async-start | bytes 524288 | tf_op jit(solution)/shard_map/all_to_all | solution.py:465
  114.7 0.1 fusion.5
  114.8 0.1 reshape.52.row_ref
  114.9 0.1 reshape.53.count_ref
  115.0 8.8 %all-to-all-done.3.slot_ref = bf16[32,32,128]{2,1,0:T(8,128)(2,1)S(1)} async-done(((bf16[32,32,128]{2,1,0:T(8,128)(2,1)}), bf16[32,32,128]{2,1,0:T(8,128)(2,1)S(1)}, u32[]{:S(2)}, u32[]{:S(2)}) %all-to-all-start.3) | async-done | bytes 262176 | tf_op jit(solution)/shard_map/all_to_all | solution.py:465
  123.8 1.9 %add_gains.1 = f32[96,256]{1,0:T(8,128)} custom-call(s32[64]{0:T(128)S(1)} %reshape.52.row_ref, s32[64]{0:T(128)S(1)} %reshape.53.count_ref, bf16[32,32,128]{2,1,0:T(8,128)(2,1)S(1)} %all-to-all-done.3.slot_ref), custom_call_target="tpu_custom_call" | custom-call | tf_op jit(solution)/shard_map/add_gains/pallas_call | solution.py:402
  (3 shorter events, 0.0 us)
Async XLA Ops:
  1.1 7.1 %collective-permute-start = (bf16[128,768]{1,0:T(8,128)(2,1)S(1)}, bf16[128,768]{1,0:T(8,128)(2,1)S(1)}, u32[]{:S(2)}, u32[]{:S(2)}) collective-permute-start(bf16[128,768]{1,0:T(8,128)(2,1)S(1)} %get-tuple-element.20), channel_id=1, source_target_pairs={{0,8},{8,0},{16,24},{24,16},{32,40},{40,32},{48,56},{56,48},{64,72... | collective-permute-start | bytes 589832 | tf_op jit(solution)/shard_map/ppermute | solution.py:437
  4.4 7.0 %collective-permute-start.1 = (bf16[128,768]{1,0:T(8,128)(2,1)S(1)}, bf16[128,768]{1,0:T(8,128)(2,1)S(1)}, u32[]{:S(2)}, u32[]{:S(2)}) collective-permute-start(bf16[128,768]{1,0:T(8,128)(2,1)S(1)} %get-tuple-element.19), channel_id=1, source_target_pairs={{8,16},{16,8},{24,32},{32,24},{40,48},{48,40},{56,64},{64,56},{72,... | collective-permute-start | bytes 589832 | tf_op jit(solution)/shard_map/ppermute | solution.py:435
  16.1 48.5 %all-to-all-start = ((bf16[32,400,128]{2,1,0:T(8,128)(2,1)}), bf16[32,400,128]{2,1,0:T(8,128)(2,1)S(1)}, u32[]{:S(2)}, u32[]{:S(2)}) async-start(bf16[32,400,128]{2,1,0:T(8,128)(2,1)} %fit.1), calls=%async_computation | async-start | bytes 6553600 | tf_op jit(solution)/shard_map/all_to_all | solution.py:444
  23.5 53.0 %copy-start = (s32[32,1]{0,1:T(1,128)S(1)}, s32[32,1]{0,1:T(1,128)}, u32[]{:S(2)}) copy-start(s32[32,1]{0,1:T(1,128)} %param.10) | copy-start | bytes 388
  70.8 19.9 %all-to-all-start.1 = ((bf16[32,96,128]{2,1,0:T(8,128)(2,1)}), bf16[32,96,128]{2,1,0:T(8,128)(2,1)S(1)}, u32[]{:S(2)}, u32[]{:S(2)}) async-start(bf16[32,96,128]{2,1,0:T(8,128)(2,1)} %get-tuple-element.18), calls=%async_computation.1 | async-start | bytes 1572864 | tf_op jit(solution)/shard_map/all_to_all | solution.py:460
  91.5 16.8 %all-to-all-start.2 = ((bf16[8,64,128]{2,1,0:T(8,128)(2,1)}), bf16[8,64,128]{2,1,0:T(8,128)(2,1)S(1)}, u32[]{:S(2)}, u32[]{:S(2)}) async-start(bf16[8,64,128]{2,1,0:T(8,128)(2,1)} %broadcast_in_dim.37), calls=%async_computation.2 | async-start | bytes 262144 | tf_op jit(solution)/shard_map/all_to_all | solution.py:463
  109.8 14.0 %all-to-all-start.3 = ((bf16[32,32,128]{2,1,0:T(8,128)(2,1)}), bf16[32,32,128]{2,1,0:T(8,128)(2,1)S(1)}, u32[]{:S(2)}, u32[]{:S(2)}) async-start(bf16[32,32,128]{2,1,0:T(8,128)(2,1)} %make_slots.1), calls=%async_computation.3 | async-start | bytes 524288 | tf_op jit(solution)/shard_map/all_to_all | solution.py:465

commit v9 on v8

--- a/solution.py
+++ b/solution.py
@@ -9,7 +9,7 @@
 
 MAXBF = 16
 ROWBLK = 32
-PACKED = ROWBLK + ROWBLK // 2
+WORDS = ROWBLK * 3 // 4
 BATCH = 16
 MIB = 1 << 20
 
@@ -44,7 +44,7 @@
 def stage_kernel(
     own_ref, ints_hbm, metric_hbm, size_hbm, dev_hbm, atom_hbm,
     ints_ref, window_ref, order_ref, mix_ref, meta_ref,
-    metric_ref, size_ref, dev_ref, atom_ref, rows_ref, sem_ref,
+    metric_ref, size_ref, dev_ref, atom_ref, sem_ref,
 ):
     sources = (ints_hbm, metric_hbm, size_hbm, dev_hbm, atom_hbm)
     targets = (ints_ref, metric_ref, size_ref, dev_ref, atom_ref)
@@ -65,16 +65,25 @@
     member = jnp.where(member, 1.0, 0.0).astype(jnp.bfloat16)
     mix = dot_nt(dot_nt(member, metric_ref[...]).astype(jnp.bfloat16), member)
     mix_ref[...] = jnp.where(u % ROWBLK == v % ROWBLK, mix, 0.0).astype(jnp.bfloat16)
-    rows_ref[...] = jnp.zeros(rows_ref.shape, jnp.float32)
+    meta_ref[...] = jnp.zeros(meta_ref.shape, jnp.int32)
     for row, value_ref in enumerate((size_ref, dev_ref, atom_ref)):
-        rows_ref[row : row + 1, 0 : value_ref.shape[1]] = value_ref[...].astype(jnp.float32)
-    meta_ref[...] = rows_ref[...].astype(jnp.bfloat16)
+        meta_ref[row + 2 : row + 3, 0 : value_ref.shape[1]] = value_ref[...]
     fetches[0].wait()
+
+
+def join(high, low):
+    return (high << 16) + low
+
+
+def split(words):
+    high = (words + 32768) >> 16
+    low = (words << 16) >> 16
+    return high.astype(jnp.float32), low.astype(jnp.float32)
 
 
 def fit_kernel(
     odd_ref, near_ref, far_ref, own_ref, ints_ref, order_ref, mix_ref, meta_ref, out_ref,
-    window_ref, packed_ref, out_sem,
+    window_ref, packed_ref, power_ref, out_sem,
 ):
     aux_dev, bas_dev, span = ints_ref.shape
     blocks = bas_dev // ROWBLK
@@ -85,7 +94,13 @@
     ordered(far_ref, order_ref, window_ref, far_at)
     mix = mix_ref[...]
     left = iota((ROWBLK // 2, 128), 1) < 64
+    power_ref[...] = jnp.zeros(power_ref.shape, jnp.float32)
+    spot = iota((aux_dev * ROWBLK, 128), 1) - iota((aux_dev * ROWBLK, 128), 0) % ROWBLK
     copies = []
+
+    def whole(values):
+        return jnp.round(values).astype(jnp.int32)
+
     for u in range(blocks):
         if u % 4 == 0:
             ints = ints_ref[:, u * ROWBLK : (u + 4) * ROWBLK].reshape(-1, span)
@@ -94,26 +109,41 @@
         at = (u % 4) * ROWBLK
         half = wide[:, at : at + ROWBLK].reshape(aux_dev * ROWBLK, -1)
         fitted = dot(mix, half)
-        main = slice(u * PACKED, u * PACKED + ROWBLK)
-        side = slice(u * PACKED + ROWBLK, (u + 1) * PACKED)
+        largest = jnp.abs(fitted[:, 0:128])
+        for t in range(1, 6):
+            largest = jnp.maximum(largest, jnp.abs(fitted[:, t * 128 : (t + 1) * 128]))
+        largest = jnp.maximum(jnp.max(largest, axis=1, keepdims=True), 1e-30)
+        power = jnp.floor(jnp.log2(largest) + 1.5e-4) - 14.0
+        fitted = fitted * jnp.exp2(-power)
+        powers = jnp.where(spot == at, jnp.broadcast_to(power, spot.shape), 0.0)
+        for p in range(aux_dev):
+            row = 2 * p + u // 4
+            mine = jnp.sum(powers[p * ROWBLK : (p + 1) * ROWBLK], axis=0, keepdims=True)
+            power_ref[row : row + 1] = power_ref[row : row + 1] + mine
         for p in range(aux_dev):
             rows = fitted[p * ROWBLK : (p + 1) * ROWBLK]
+            top, bottom = rows[: ROWBLK // 2], rows[ROWBLK // 2 :]
+            main = join(whole(top[:, 0:512]), whole(bottom[:, 0:512]))
+            first = u * WORDS
             for k in range(4):
-                tile = rows[:, k * 128 : (k + 1) * 128]
-                packed_ref[p * 4 + k, main] = tile.astype(jnp.bfloat16)
+                packed_ref[p * 4 + k, first : first + 16] = main[:, k * 128 : (k + 1) * 128]
             for k in range(2):
-                shared = rows[:, 512 + k * 128 : 640 + k * 128]
-                top, bottom = shared[: ROWBLK // 2], shared[ROWBLK // 2 :]
-                even = jnp.where(left, top, pltpu.roll(bottom, 64, 1))
-                odd = jnp.where(left, pltpu.roll(top, 64, 1), bottom)
-                packed_ref[p * 4 + 2 * k, side] = even.astype(jnp.bfloat16)
-                packed_ref[p * 4 + 2 * k + 1, side] = odd.astype(jnp.bfloat16)
+                lanes = slice(512 + k * 128, 640 + k * 128)
+                even = jnp.where(left, top[:, lanes], pltpu.roll(bottom[:, lanes], 64, 1))
+                odd = jnp.where(left, pltpu.roll(top[:, lanes], 64, 1), bottom[:, lanes])
+                for d, side in ((2 * k, whole(even)), (2 * k + 1, whole(odd))):
+                    packed_ref[p * 4 + d, first + 16 : first + 24] = join(side[0:8], side[8:16])
         if u == blocks - 1:
-            for d in range(4 * aux_dev):
-                packed_ref[d, blocks * PACKED : blocks * PACKED + 16] = meta_ref[...]
+            row = iota((8, 128), 0)
+            for p in range(aux_dev):
+                tail = meta_ref[...]
+                for i in range(2):
+                    power = power_ref[2 * p + i : 2 * p + i + 1].astype(jnp.int32)
+                    tail = jnp.where(row == i, jnp.broadcast_to(power, tail.shape), tail)
+                for k in range(4):
+                    packed_ref[p * 4 + k, blocks * WORDS : blocks * WORDS + 8] = tail
         if u % 2 == 1:
-            first = (u - 1) * PACKED
-            span_rows = pl.ds(first, 2 * PACKED + (16 if u == blocks - 1 else 0))
+            span_rows = pl.ds((u - 1) * WORDS, 2 * WORDS + (8 if u == blocks - 1 else 0))
             copies.append(
                 pltpu.make_async_copy(
                     packed_ref.at[:, span_rows], out_ref.at[:, span_rows], out_sem.at[u // 2]
@@ -125,11 +155,11 @@
 
 
 def end_table(me, got_ref, size_ref, dev_ref, atom_ref):
-    groups, at = got_ref.shape[0], got_ref.shape[1] - 16
+    groups, at = got_ref.shape[0], got_ref.shape[1] - 8
     for d in range(groups):
-        rows = got_ref[d, at : at + 16].astype(jnp.float32)
+        rows = got_ref[d, at : at + 8].astype(jnp.float32)
         for i, dest in enumerate((size_ref, dev_ref, atom_ref)):
-            dest[d : d + 1] = rows[i : i + 1]
+            dest[d : d + 1] = rows[i + 2 : i + 3]
     before = jnp.where(iota((128, 128), 0) < iota((128, 128), 1), 1.0, 0.0).astype(jnp.bfloat16)
     sizes = size_ref[...]
     packed = dot(sizes.astype(jnp.bfloat16), before) * 32.0 + sizes
@@ -160,23 +190,34 @@
     table_ref[...] = end_table(me_ref[0], got_ref, size_ref, dev_ref, atom_ref)
     fetch = pltpu.make_async_copy(table_ref, row_ref, table_sem)
     fetch.start()
-    groups, blocks = got_ref.shape[0], got_ref.shape[1] // PACKED
+    groups, blocks = got_ref.shape[0], got_ref.shape[1] // WORDS
     lane = iota((ROWBLK // 2, 128), 1)
     left, valid = lane < 64, lane < 96
 
+    row = iota((16, 256), 0)
+    spread = jnp.where(row == iota((16, 256), 1) // 128, 1.0, 0.0).astype(jnp.bfloat16)
+    row = iota((8, 128), 0)
+
     def unpack(b, carry):
+        powers = got_ref[b, blocks * WORDS : blocks * WORDS + 8]
+        powers = jnp.exp2(jnp.where(row < 2, powers, 0).astype(jnp.float32))
+        powers = jnp.concatenate([powers, jnp.zeros((8, 128), jnp.float32)], axis=0)
+        scales = dot_tn(powers.astype(jnp.bfloat16), spread)
         for i in range(blocks):
             base = pl.multiple_of(b * (blocks * ROWBLK) + i * ROWBLK, ROWBLK)
-            shared = got_ref[b, i * PACKED + ROWBLK : (i + 1) * PACKED].astype(jnp.float32)
+            mains = split(got_ref[b, i * WORDS : i * WORDS + 16])
+            shared = split(got_ref[b, i * WORDS + 16 : (i + 1) * WORDS])
+            shared = jnp.concatenate(shared, axis=0)
             for h in range(2):
-                at = i * PACKED + h * 16
-                main = got_ref[b, at : at + 16].astype(jnp.float32)
+                main = mains[h]
+                at = (i % 4) * ROWBLK + h * 16
+                scale = scales[at : at + 16, (i // 4) * 128 : (i // 4 + 1) * 128]
                 real = shared if h else pltpu.roll(shared, 64, 1)
                 imag = pltpu.roll(shared, 96 if h else 32, 1)
                 real = jnp.where(left, main, jnp.where(valid, real, 0.0))
                 imag = jnp.where(left, pltpu.roll(main, 64, 1), jnp.where(valid, imag, 0.0))
-                real_ref[pl.ds(base + h * 16, 16)] = real
-                imag_ref[pl.ds(base + h * 16, 16)] = imag
+                real_ref[pl.ds(base + h * 16, 16)] = real * scale
+                imag_ref[pl.ds(base + h * 16, 16)] = imag * scale
         return carry
 
     lax.fori_loop(0, groups, unpack, 0, unroll=8)
@@ -314,14 +355,15 @@
 
 
 def stage(own, *fetched):
-    shapes = [fetched[0].shape, own.shape, (2, 256, 256), (256, 256), (16, 128)]
+    shapes = [fetched[0].shape, own.shape, (2, 256, 256), (256, 256)]
     return pl.pallas_call(
         stage_kernel,
         in_specs=[vmem_spec()] + [pl.BlockSpec(memory_space=pltpu.HBM)] * len(fetched),
-        out_specs=[vmem_spec()] * len(shapes),
-        out_shape=[pltpu.VMEM(shape, jnp.bfloat16) for shape in shapes],
+        out_specs=[vmem_spec()] * 5,
+        out_shape=[pltpu.VMEM(shape, jnp.bfloat16) for shape in shapes]
+        + [pltpu.VMEM((8, 128), jnp.int32)],
         scratch_shapes=[pltpu.VMEM(x.shape, x.dtype) for x in fetched[1:]]
-        + [pltpu.VMEM((16, 128), jnp.float32), pltpu.SemaphoreType.DMA((len(fetched),))],
+        + [pltpu.SemaphoreType.DMA((len(fetched),))],
         compiler_params=limit(16),
         cost_estimate=pl.CostEstimate(flops=1 << 28, bytes_accessed=5 * MIB, transcendentals=0),
         name="stage",
@@ -332,15 +374,16 @@
     aux_dev, bas_dev, window = ints.shape
     width = near.shape[1]
     blocks = bas_dev // ROWBLK
-    shape = (4 * aux_dev, blocks * PACKED + 16, 128)
+    shape = (4 * aux_dev, blocks * WORDS + 8, 128)
     return pl.pallas_call(
         fit_kernel,
         in_specs=[smem_spec()] + [vmem_spec()] * 7,
         out_specs=pl.BlockSpec(memory_space=pltpu.HBM),
-        out_shape=pltpu.HBM(shape, jnp.bfloat16),
+        out_shape=pltpu.HBM(shape, jnp.int32),
         scratch_shapes=[
             pltpu.VMEM((window, width), jnp.bfloat16),
-            pltpu.VMEM(shape, jnp.bfloat16),
+            pltpu.VMEM(shape, jnp.int32),
+            pltpu.VMEM((2 * aux_dev, 128), jnp.float32),
             pltpu.SemaphoreType.DMA((blocks // 2,)),
         ],
         compiler_params=limit(32),
@@ -355,7 +398,7 @@
 
 def pair_sums(me, coef, got):
     groups = got.shape[0]
-    rows = groups * (got.shape[1] // PACKED) * ROWBLK + MAXBF
+    rows = groups * (got.shape[1] // WORDS) * ROWBLK + MAXBF
     shape = (groups, 6 * MAXBF, 128)
     return pl.pallas_call(
         pair_kernel,

time: 126 us -> 129 us (1.024)
  Pallas kernels: 16.1 us -> 18.7 us
    pallas_call x1, Pallas kernels: 6.23 us -> 8.2 us  [pair_sums(): pl.pallas_call(pair_kernel, in_specs=[smem_spec(), vmem_spec(), vmem_spec...]
where the time goes in v9:
time: 129 us; the launch traced here: 128 us
  waiting for transfers between devices  74.3 us (58%)
  starting transfers between devices  31.4 us (24%)
  Pallas kernels  18.7 us (14%)
  local copies, waits for them, and re-layouts  3.42 us (3%)
    all_to_all x1, waiting for transfers between devices, per_device(): lax.all_to_all(packed, 'atom', split_axis=0, concat_axis=0, tiled=True)  39.7 us
    all_to_all x1, waiting for transfers between devices, per_device(): lax.all_to_all(sent, 'atom', split_axis=0, concat_axis=0, tiled=True)  14 us
    all_to_all x1, waiting for transfers between devices, per_device(): lax.all_to_all(slots, 'atom', split_axis=0, concat_axis=0, tiled=True)  8.81 us
    all_to_all x1, waiting for transfers between devices, per_device(): lax.all_to_all(shared, 'aux', split_axis=0, concat_axis=0, tiled=True)  8.54 us
    pallas_call x1, Pallas kernels, pair_sums(): pl.pallas_call(pair_kernel, in_specs=[smem_spec(), vmem_spec(), vmem_spec...  8.2 us
    all_to_all x1, starting transfers between devices, per_device(): lax.all_to_all(shared, 'aux', split_axis=0, concat_axis=0, tiled=True)  8.19 us
    all_to_all x1, starting transfers between devices, per_device(): lax.all_to_all(packed, 'atom', split_axis=0, concat_axis=0, tiled=True)  7.41 us
    all_to_all x1, starting transfers between devices, per_device(): lax.all_to_all(sent, 'atom', split_axis=0, concat_axis=0, tiled=True)  5.68 us
  transfers between devices with their start and end apart: 6, of which 5 were waited for; matrix products, arithmetic and copies ran while one was open for 2% of the time, Pallas kernels for 1%

profile of v9, /device:TPU:1, one launch (start us, length us, event | category | flops | bytes accessed | tf_op | source)
XLA Modules:
  0.0 128.4 jit_solution(3071482054835434261)
XLA Ops:
  0.0 1.0 copy.12
  1.1 3.3 %collective-permute-start = (bf16[128,768]{1,0:T(8,128)(2,1)S(1)}, bf16[128,768]{1,0:T(8,128)(2,1)S(1)}, u32[]{:S(2)}, u32[]{:S(2)}) collective-permute-start(bf16[128,768]{1,0:T(8,128)(2,1)S(1)} %get-tuple-element.20), channel_id=1, source_target_pairs={{0,8},{8,0},{16,24},{24,16},{32,40},{40,32},{48,56},{56,48},{64,72... | collective-permute-start | bytes 589832 | tf_op jit(solution)/shard_map/ppermute | solution.py:480
  4.4 1.9 %collective-permute-start.1 = (bf16[128,768]{1,0:T(8,128)(2,1)S(1)}, bf16[128,768]{1,0:T(8,128)(2,1)S(1)}, u32[]{:S(2)}, u32[]{:S(2)}) collective-permute-start(bf16[128,768]{1,0:T(8,128)(2,1)S(1)} %get-tuple-element.19), channel_id=1, source_target_pairs={{8,16},{16,8},{24,32},{32,24},{40,48},{48,40},{56,64},{64,56},{72,... | collective-permute-start | bytes 589832 | tf_op jit(solution)/shard_map/ppermute | solution.py:478
  6.3 1.8 %stage.1 = (bf16[8,256,512]{2,1,0:T(8,128)(2,1)S(1)}, bf16[256,768]{1,0:T(8,128)(2,1)S(1)}, bf16[2,256,256]{2,1,0:T(8,128)(2,1)S(1)}, bf16[256,256]{1,0:T(8,128)(2,1)S(1)}, s32[8,128]{1,0:T(8,128)S(1)}) custom-call(bf16[256,768]{1,0:T(8,128)(2,1)S(1)} %bitcast.13, bf16[8,256,512]{2,1,0:T(8,128)(2,1)} %ints_hbm.1, bf16[8,8]{1,0:T(8,128)(2,1)} %metric_hbm.1, ...), custom_call_target="tpu_custom_call" | custom-call | flops 268435456 | bytes 5242880 | tf_op jit(solution)/shard_map/stage/pallas_call | solution.py:359
  8.2 0.0 collective-permute-done.near_ref
  8.2 3.2 %collective-permute-done.1.far_ref = bf16[128,768]{1,0:T(8,128)(2,1)S(1)} collective-permute-done((bf16[128,768]{1,0:T(8,128)(2,1)S(1)}, bf16[128,768]{1,0:T(8,128)(2,1)S(1)}, u32[]{:S(2)}, u32[]{:S(2)}) %collective-permute-start.1) | collective-permute-done | bytes 196640 | tf_op jit(solution)/shard_map/ppermute | solution.py:478
  11.4 5.3 %fit.1 = s32[32,200,128]{2,1,0:T(8,128)} custom-call(s32[1]{0:T(128)} %bitcast.2.odd_ref, bf16[128,768]{1,0:T(8,128)(2,1)S(1)} %collective-permute-done.near_ref, bf16[128,768]{1,0:T(8,128)(2,1)S(1)} %collective-permute-done.1.far_ref, bf16[256,768]{1,0:T(8,128)(2,1)S(1)} %get-tuple-element.12.own_ref, bf16[8,256,512]{2,1,0:T(8,128)(2,1)S(1)} %get-tuple-element.13.ints_ref, ...), custom_call_target="tpu_custom_call" | custom-call | flops 2415919104 | bytes 6291456 | tf_op jit(solution)/shard_map/fit/pallas_call | solution.py:378
  16.7 7.4 %all-to-all-start = ((s32[32,200,128]{2,1,0:T(8,128)}), s32[32,200,128]{2,1,0:T(8,128)S(1)}, u32[]{:S(2)}, u32[]{:S(2)}) async-start(s32[32,200,128]{2,1,0:T(8,128)} %fit.1), calls=%async_computation | async-start | bytes 6553600 | tf_op jit(solution)/shard_map/all_to_all | solution.py:487
  24.1 0.0 copy-start
  24.1 1.2 constant_dynamic-slice_fusion.2
  25.3 0.1 copy.11
  25.4 0.1 copy.10.coef_ref
  25.5 39.7 %all-to-all-done.got_ref = s32[32,200,128]{2,1,0:T(8,128)S(1)} async-done(((s32[32,200,128]{2,1,0:T(8,128)}), s32[32,200,128]{2,1,0:T(8,128)S(1)}, u32[]{:S(2)}, u32[]{:S(2)}) %all-to-all-start) | async-done | bytes 3276832 | tf_op jit(solution)/shard_map/all_to_all | solution.py:487
  65.2 8.2 %pair_sums.1 = (s32[32,128]{1,0:T(8,128)S(1)}, bf16[32,96,128]{2,1,0:T(8,128)(2,1)}) custom-call(s32[1]{0:T(128)} %bitcast.me_ref, bf16[256,96]{1,0:T(8,128)(2,1)S(1)} %copy.10.coef_ref, s32[32,200,128]{2,1,0:T(8,128)S(1)} %all-to-all-done.got_ref), custom_call_target="tpu_custom_call" | custom-call | tf_op jit(solution)/shard_map/pair_sums/pallas_call | solution.py:403
  73.4 5.7 %all-to-all-start.1 = ((bf16[32,96,128]{2,1,0:T(8,128)(2,1)}), bf16[32,96,128]{2,1,0:T(8,128)(2,1)S(1)}, u32[]{:S(2)}, u32[]{:S(2)}) async-start(bf16[32,96,128]{2,1,0:T(8,128)(2,1)} %get-tuple-element.18), calls=%async_computation.1 | async-start | bytes 1572864 | tf_op jit(solution)/shard_map/all_to_all | solution.py:503
  79.1 0.0 copy-done
  79.1 0.2 convert_reduce_fusion.refs_1_
  79.3 14.0 %all-to-all-done.1.refs_4_ = bf16[32,96,128]{2,1,0:T(8,128)(2,1)S(1)} async-done(((bf16[32,96,128]{2,1,0:T(8,128)(2,1)}), bf16[32,96,128]{2,1,0:T(8,128)(2,1)S(1)}, u32[]{:S(2)}, u32[]{:S(2)}) %all-to-all-start.1) | async-done | bytes 786464 | tf_op jit(solution)/shard_map/all_to_all | solution.py:503
  93.3 0.1 slice_reduce_fusion
  93.4 0.7 broadcast_in_dim.37
  94.1 8.2 %all-to-all-start.2 = ((bf16[8,64,128]{2,1,0:T(8,128)(2,1)}), bf16[8,64,128]{2,1,0:T(8,128)(2,1)S(1)}, u32[]{:S(2)}, u32[]{:S(2)}) async-start(bf16[8,64,128]{2,1,0:T(8,128)(2,1)} %broadcast_in_dim.37), calls=%async_computation.2 | async-start | bytes 262144 | tf_op jit(solution)/shard_map/all_to_all | solution.py:506
  102.3 0.1 select_reduce_fusion
  102.4 8.5 %all-to-all-done.2.refs_3_ = bf16[8,64,128]{2,1,0:T(8,128)(2,1)S(1)} async-done(((bf16[8,64,128]{2,1,0:T(8,128)(2,1)}), bf16[8,64,128]{2,1,0:T(8,128)(2,1)S(1)}, u32[]{:S(2)}, u32[]{:S(2)}) %all-to-all-start.2) | async-done | bytes 131104 | tf_op jit(solution)/shard_map/all_to_all | solution.py:506
  110.9 1.5 %make_slots.1 = bf16[32,32,128]{2,1,0:T(8,128)(2,1)} custom-call(s32[32]{0:T(128)S(1)} %bitcast.16, s32[32]{0:T(128)S(1)} %convert_reduce_fusion.refs_1_, s32[64]{0:T(128)S(1)} %broadcast_add_fusion.refs_2_, bf16[8,64,128]{2,1,0:T(8,128)(2,1)S(1)} %all-to-all-done.2.refs_3_, bf16[32,96,128]{2,1,0:T(8,128)(2,1)S(1)} %all-to-all-done.1.refs_4_), custom_call_target="tpu_custom_call" | custom-call | tf_op jit(solution)/shard_map/make_slots/pallas_call | solution.py:433
  112.5 4.9 %all-to-all-start.3 = ((bf16[32,32,128]{2,1,0:T(8,128)(2,1)}), bf16[32,32,128]{2,1,0:T(8,128)(2,1)S(1)}, u32[]{:S(2)}, u32[]{:S(2)}) async-start(bf16[32,32,128]{2,1,0:T(8,128)(2,1)} %make_slots.1), calls=%async_computation.3 | async-start | bytes 524288 | tf_op jit(solution)/shard_map/all_to_all | solution.py:508
  117.4 0.1 fusion.5
  117.4 0.1 reshape.52.row_ref
  117.6 0.1 reshape.53.count_ref
  117.7 8.8 %all-to-all-done.3.slot_ref = bf16[32,32,128]{2,1,0:T(8,128)(2,1)S(1)} async-done(((bf16[32,32,128]{2,1,0:T(8,128)(2,1)}), bf16[32,32,128]{2,1,0:T(8,128)(2,1)S(1)}, u32[]{:S(2)}, u32[]{:S(2)}) %all-to-all-start.3) | async-done | bytes 262176 | tf_op jit(solution)/shard_map/all_to_all | solution.py:508
  126.5 1.9 %add_gains.1 = f32[96,256]{1,0:T(8,128)} custom-call(s32[64]{0:T(128)S(1)} %reshape.52.row_ref, s32[64]{0:T(128)S(1)} %reshape.53.count_ref, bf16[32,32,128]{2,1,0:T(8,128)(2,1)S(1)} %all-to-all-done.3.slot_ref), custom_call_target="tpu_custom_call" | custom-call | tf_op jit(solution)/shard_map/add_gains/pallas_call | solution.py:445
  (3 shorter events, 0.0 us)
Async XLA Ops:
  1.1 7.1 %collective-permute-start = (bf16[128,768]{1,0:T(8,128)(2,1)S(1)}, bf16[128,768]{1,0:T(8,128)(2,1)S(1)}, u32[]{:S(2)}, u32[]{:S(2)}) collective-permute-start(bf16[128,768]{1,0:T(8,128)(2,1)S(1)} %get-tuple-element.20), channel_id=1, source_target_pairs={{0,8},{8,0},{16,24},{24,16},{32,40},{40,32},{48,56},{56,48},{64,72... | collective-permute-start | bytes 589832 | tf_op jit(solution)/shard_map/ppermute | solution.py:480
  4.4 7.0 %collective-permute-start.1 = (bf16[128,768]{1,0:T(8,128)(2,1)S(1)}, bf16[128,768]{1,0:T(8,128)(2,1)S(1)}, u32[]{:S(2)}, u32[]{:S(2)}) collective-permute-start(bf16[128,768]{1,0:T(8,128)(2,1)S(1)} %get-tuple-element.19), channel_id=1, source_target_pairs={{8,16},{16,8},{24,32},{32,24},{40,48},{48,40},{56,64},{64,56},{72,... | collective-permute-start | bytes 589832 | tf_op jit(solution)/shard_map/ppermute | solution.py:478
  16.7 48.5 %all-to-all-start = ((s32[32,200,128]{2,1,0:T(8,128)}), s32[32,200,128]{2,1,0:T(8,128)S(1)}, u32[]{:S(2)}, u32[]{:S(2)}) async-start(s32[32,200,128]{2,1,0:T(8,128)} %fit.1), calls=%async_computation | async-start | bytes 6553600 | tf_op jit(solution)/shard_map/all_to_all | solution.py:487
  24.1 55.0 %copy-start = (s32[32,1]{0,1:T(1,128)S(1)}, s32[32,1]{0,1:T(1,128)}, u32[]{:S(2)}) copy-start(s32[32,1]{0,1:T(1,128)} %param.10) | copy-start | bytes 388
  73.4 19.9 %all-to-all-start.1 = ((bf16[32,96,128]{2,1,0:T(8,128)(2,1)}), bf16[32,96,128]{2,1,0:T(8,128)(2,1)S(1)}, u32[]{:S(2)}, u32[]{:S(2)}) async-start(bf16[32,96,128]{2,1,0:T(8,128)(2,1)} %get-tuple-element.18), calls=%async_computation.1 | async-start | bytes 1572864 | tf_op jit(solution)/shard_map/all_to_all | solution.py:503
  94.1 16.8 %all-to-all-start.2 = ((bf16[8,64,128]{2,1,0:T(8,128)(2,1)}), bf16[8,64,128]{2,1,0:T(8,128)(2,1)S(1)}, u32[]{:S(2)}, u32[]{:S(2)}) async-start(bf16[8,64,128]{2,1,0:T(8,128)(2,1)} %broadcast_in_dim.37), calls=%async_computation.2 | async-start | bytes 262144 | tf_op jit(solution)/shard_map/all_to_all | solution.py:506
  112.5 14.0 %all-to-all-start.3 = ((bf16[32,32,128]{2,1,0:T(8,128)(2,1)}), bf16[32,32,128]{2,1,0:T(8,128)(2,1)S(1)}, u32[]{:S(2)}, u32[]{:S(2)}) async-start(bf16[32,32,128]{2,1,0:T(8,128)(2,1)} %make_slots.1), calls=%async_computation.3 | async-start | bytes 524288 | tf_op jit(solution)/shard_map/all_to_all | solution.py:508

commit v10 on v8

--- a/solution.py
+++ b/solution.py
@@ -154,8 +154,8 @@
 
 
 def pair_kernel(
-    me_ref, coef_ref, got_ref, table_ref, out_ref, real_ref, imag_ref, rows_ref, sums_ref,
-    size_ref, dev_ref, atom_ref, row_ref, table_sem, sem_ref, *sides,
+    me_ref, coef_ref, got_ref, table_ref, out_ref, real_ref, imag_ref, rows_ref,
+    size_ref, dev_ref, atom_ref, row_ref, table_sem, *sides,
 ):
     table_ref[...] = end_table(me_ref[0], got_ref, size_ref, dev_ref, atom_ref)
     fetch = pltpu.make_async_copy(table_ref, row_ref, table_sem)
@@ -216,20 +216,13 @@
                         here = value[c * 128 + j * 16 : c * 128 + j * 16 + 16]
                         part = jnp.where(lane_pair == j, here, part)
                     at = h * 32 + c * 16
-                    sums_ref[g, at : at + 16] = part.astype(jnp.bfloat16)
+                    out_ref[g, at : at + 16] = part.astype(jnp.bfloat16)
                 rows = rows_ref[pl.ds(row_ref[g, 32 + h], MAXBF)]
                 rows = jnp.where(row_id < row_ref[g, 34 + h], rows, 0.0)
-                sums_ref[g, 64 + h * 16 : 80 + h * 16] = rows.astype(jnp.bfloat16)
-        send(step).start()
+                out_ref[g, 64 + h * 16 : 80 + h * 16] = rows.astype(jnp.bfloat16)
         return carry
 
-    def send(step):
-        done = pl.ds(step * batch, batch)
-        return pltpu.make_async_copy(sums_ref.at[done], out_ref.at[done], sem_ref.at[step])
-
     lax.fori_loop(0, groups // batch, group, 0)
-    for step in range(groups // batch):
-        send(step).wait()
 
 
 def slot_kernel(scale, target_ref, rank_ref, place_ref, parts_ref, got_ref, out_ref, tile_ref):
@@ -267,7 +260,7 @@
         out_ref[s // 2, (s % 2) * MAXBF : (s % 2 + 1) * MAXBF] = rows
 
 
-def gain_kernel(row_ref, count_ref, slot_ref, out_ref, sum_ref, turned_ref):
+def gain_kernel(table_ref, slot_ref, out_ref, sum_ref, turned_ref):
     groups, rows, _ = slot_ref.shape
     width, bas_dev = out_ref.shape
     half = width // 2
@@ -291,8 +284,8 @@
         gains = dot(tiles, jnp.concatenate([slots, turned_ref[g]], axis=0))
         for r in range(2):
             part = gains[r * MAXBF : (r + 1) * MAXBF]
-            part = jnp.where(row_id < count_ref[2 * g + r], part, 0.0)
-            where = pl.ds(row_ref[2 * g + r], MAXBF)
+            part = jnp.where(row_id < table_ref[g, 34 + r], part, 0.0)
+            where = pl.ds(table_ref[g, 32 + r], MAXBF)
             sum_ref[where] = sum_ref[where] + part
     out_ref[...] = sum_ref[0:bas_dev].T[0:width]
 
@@ -360,22 +353,20 @@
     return pl.pallas_call(
         pair_kernel,
         in_specs=[smem_spec(), vmem_spec(), vmem_spec()],
-        out_specs=[vmem_spec(), pl.BlockSpec(memory_space=pltpu.HBM)],
+        out_specs=[vmem_spec()] * 2,
         out_shape=[
             jax.ShapeDtypeStruct((groups, 128), jnp.int32),
-            pltpu.HBM(shape, jnp.bfloat16),
+            jax.ShapeDtypeStruct(shape, jnp.bfloat16),
         ],
         scratch_shapes=[
             pltpu.VMEM((rows, 128), jnp.float32),
             pltpu.VMEM((rows, 128), jnp.float32),
             pltpu.VMEM((coef.shape[0] + MAXBF, 128), jnp.float32),
-            pltpu.VMEM(shape, jnp.bfloat16),
             pltpu.VMEM((groups, 128), jnp.float32),
             pltpu.VMEM((groups, 128), jnp.float32),
             pltpu.VMEM((groups, 128), jnp.float32),
             pltpu.SMEM((groups, 128), jnp.int32),
             pltpu.SemaphoreType.DMA,
-            pltpu.SemaphoreType.DMA((groups // BATCH,)),
         ]
         + [pltpu.VMEM((256, 256), jnp.bfloat16), pltpu.VMEM((128, 256), jnp.bfloat16)] * (2 * BATCH),
         compiler_params=limit(40),
@@ -398,10 +389,10 @@
     )(targets, ranks, places, parts, got)
 
 
-def add_gains(rows, counts, slots, width, bas_dev):
+def add_gains(table, slots, width, bas_dev):
     return pl.pallas_call(
         gain_kernel,
-        in_specs=[smem_spec()] * 2 + [vmem_spec()],
+        in_specs=[smem_spec(), vmem_spec()],
         out_specs=vmem_spec(),
         out_shape=jax.ShapeDtypeStruct((width, bas_dev), jnp.float32),
         scratch_shapes=[
@@ -410,7 +401,7 @@
         ],
         compiler_params=limit(16),
         name="add_gains",
-    )(rows, counts, slots)
+    )(table, slots)
 
 
 def pick(hit, values):
@@ -456,6 +447,9 @@
     asked_hit = asked[None, :] == jnp.arange(2 * groups, dtype=jnp.int32)[:, None]
     places = 512 + pick(asked_hit, place[None, :] - 512)
 
+    me, coef_part, got, targets, ranks, places = lax.optimization_barrier(
+        (me, coef_part, got, targets, ranks, places)
+    )
     table, sent = pair_sums(me, coef_part, got)
     owned = lax.all_to_all(sent, "atom", split_axis=0, concat_axis=0, tiled=True)
     own_sums = jnp.sum(owned[:, : 4 * MAXBF].astype(jnp.float32), axis=0).astype(jnp.bfloat16)
@@ -463,8 +457,7 @@
     parts = lax.all_to_all(shared, "aux", split_axis=0, concat_axis=0, tiled=True)
     slots = make_slots(scale, targets, ranks, places, parts, owned)
     slots = lax.all_to_all(slots, "atom", split_axis=0, concat_axis=0, tiled=True)
-    rows, counts = table[:, 32:34].reshape(-1), table[:, 34:36].reshape(-1)
-    result = add_gains(rows, counts, slots, 2 * occ_part, bas_dev)
+    result = add_gains(table, slots, 2 * occ_part, bas_dev)
     return result.reshape(2, occ_part, bas_dev).transpose(2, 0, 1)
 
 

time: 126 us -> 124 us (0.984)
  blocking collectives: 0 us -> 50 us
  waiting for transfers between devices: 74.3 us -> 42.7 us
  starting transfers between devices: 31.4 us -> 12.6 us
    all_to_all x0 -> x3, blocking collectives: none -> 50 us  [the longest x1 19.7 us: per_device(): lax.all_to_all(sent, 'atom', split_axis=0, concat_axis=0, tiled=True)]
    all_to_all x3 -> x0, waiting for transfers between devices: 31.4 us -> none  [the longest x1 14 us: per_device(): lax.all_to_all(sent, 'atom', split_axis=0, concat_axis=0, tiled=True)]
    all_to_all x3 -> x0, starting transfers between devices: 18.8 us -> none  [the longest x1 8.18 us: per_device(): lax.all_to_all(shared, 'aux', split_axis=0, concat_axis=0, tiled=True)]
  transfers between devices with their start and end apart: 6 -> 3, of which waited for: 5 -> 2; matrix products, arithmetic and copies ran while one was open for 2% -> 1% of each run, Pallas kernels for 1% -> 1%
where the time goes in v10:
time: 124 us; the launch traced here: 123 us
  blocking collectives  50 us (40%)
  waiting for transfers between devices  42.7 us (34%)
  Pallas kernels  15.1 us (12%)
  starting transfers between devices  12.6 us (10%)
  local copies, waits for them, and re-layouts  2.48 us (2%)
    all_to_all x1, waiting for transfers between devices, per_device(): lax.all_to_all(packed, 'atom', split_axis=0, concat_axis=0, tiled=True)  39.5 us
    all_to_all x1, blocking collectives, per_device(): lax.all_to_all(sent, 'atom', split_axis=0, concat_axis=0, tiled=True)  19.7 us
    all_to_all x1, blocking collectives, per_device(): lax.all_to_all(shared, 'aux', split_axis=0, concat_axis=0, tiled=True)  16.6 us
    all_to_all x1, blocking collectives, per_device(): lax.all_to_all(slots, 'atom', split_axis=0, concat_axis=0, tiled=True)  13.7 us
    all_to_all x1, starting transfers between devices, per_device(): lax.all_to_all(packed, 'atom', split_axis=0, concat_axis=0, tiled=True)  7.41 us
    pallas_call x1, Pallas kernels, pair_sums(): pl.pallas_call(pair_kernel, in_specs=[smem_spec(), vmem_spec(), vmem_spec...  5.58 us
    pallas_call x1, Pallas kernels, fit(): pl.pallas_call(fit_kernel, in_specs=[smem_spec()] + [vmem_spec()] * 7, ou...  4.71 us
    ppermute x1, starting transfers between devices, per_device(): near = lax.ppermute(near, 'atom', [(i, i ^ 1) for i in range(groups)])  3.33 us
  transfers between devices with their start and end apart: 3, of which 2 were waited for; matrix products, arithmetic and copies ran while one was open for 1% of the time, Pallas kernels for 1%

profile of v10, /device:TPU:1, one launch (start us, length us, event | category | flops | bytes accessed | tf_op | source)
XLA Modules:
  0.0 123.4 jit_solution(14474473159850345407)
XLA Ops:
  0.0 1.0 copy.12
  1.1 3.3 %collective-permute-start = (bf16[128,768]{1,0:T(8,128)(2,1)S(1)}, bf16[128,768]{1,0:T(8,128)(2,1)S(1)}, u32[]{:S(2)}, u32[]{:S(2)}) collective-permute-start(bf16[128,768]{1,0:T(8,128)(2,1)S(1)} %get-tuple-element.32), channel_id=1, source_target_pairs={{0,8},{8,0},{16,24},{24,16},{32,40},{40,32},{48,56},{56,48},{64,72... | collective-permute-start | bytes 589832 | tf_op jit(solution)/shard_map/ppermute | solution.py:428
  4.4 1.9 %collective-permute-start.1 = (bf16[128,768]{1,0:T(8,128)(2,1)S(1)}, bf16[128,768]{1,0:T(8,128)(2,1)S(1)}, u32[]{:S(2)}, u32[]{:S(2)}) collective-permute-start(bf16[128,768]{1,0:T(8,128)(2,1)S(1)} %get-tuple-element.31), channel_id=1, source_target_pairs={{8,16},{16,8},{24,32},{32,24},{40,48},{48,40},{56,64},{64,56},{72,... | collective-permute-start | bytes 589832 | tf_op jit(solution)/shard_map/ppermute | solution.py:426
  6.3 1.8 %stage.1 = (bf16[8,256,512]{2,1,0:T(8,128)(2,1)S(1)}, bf16[256,768]{1,0:T(8,128)(2,1)S(1)}, bf16[2,256,256]{2,1,0:T(8,128)(2,1)S(1)}, bf16[256,256]{1,0:T(8,128)(2,1)S(1)}, bf16[16,128]{1,0:T(8,128)(2,1)S(1)}) custom-call(bf16[256,768]{1,0:T(8,128)(2,1)S(1)} %bitcast.13, bf16[8,256,512]{2,1,0:T(8,128)(2,1)} %ints_hbm.1, bf16[8,8]{1,0:T(8,128)(2,1)} %metric_hbm.1, ...), custom_call_target="tpu_custom_call" | custom-call | flops 268435456 | bytes 5242880 | tf_op jit(solution)/shard_map/stage/pallas_call | solution.py:311
  8.2 0.0 collective-permute-done.near_ref
  8.2 3.2 %collective-permute-done.1.far_ref = bf16[128,768]{1,0:T(8,128)(2,1)S(1)} collective-permute-done((bf16[128,768]{1,0:T(8,128)(2,1)S(1)}, bf16[128,768]{1,0:T(8,128)(2,1)S(1)}, u32[]{:S(2)}, u32[]{:S(2)}) %collective-permute-start.1) | collective-permute-done | bytes 196640 | tf_op jit(solution)/shard_map/ppermute | solution.py:426
  11.4 4.7 %fit.1 = bf16[32,400,128]{2,1,0:T(8,128)(2,1)} custom-call(s32[1]{0:T(128)} %bitcast.2.odd_ref, bf16[128,768]{1,0:T(8,128)(2,1)S(1)} %collective-permute-done.near_ref, bf16[128,768]{1,0:T(8,128)(2,1)S(1)} %collective-permute-done.1.far_ref, bf16[256,768]{1,0:T(8,128)(2,1)S(1)} %get-tuple-element.18.own_ref, ...), custom_call_target="tpu_custom_call" | custom-call | flops 2415919104 | bytes 6291456 | tf_op jit(solution)/shard_map/fit/pallas_call | solution.py:329
  16.1 0.0 copy-start
  16.1 7.4 %all-to-all-start = ((bf16[32,400,128]{2,1,0:T(8,128)(2,1)}), bf16[32,400,128]{2,1,0:T(8,128)(2,1)S(1)}, u32[]{:S(2)}, u32[]{:S(2)}) async-start(bf16[32,400,128]{2,1,0:T(8,128)(2,1)} %fit.1), calls=%async_computation | async-start | bytes 6553600 | tf_op jit(solution)/shard_map/all_to_all | solution.py:435
  23.5 1.2 constant_dynamic-slice_fusion.2
  24.7 0.1 copy.11
  24.8 0.0 copy-done
  24.8 0.2 convert_reduce_fusion.refs_1_
  25.0 0.1 select_reduce_fusion
  25.1 39.5 %all-to-all-done.got_ref = bf16[32,400,128]{2,1,0:T(8,128)(2,1)S(1)} async-done(((bf16[32,400,128]{2,1,0:T(8,128)(2,1)}), bf16[32,400,128]{2,1,0:T(8,128)(2,1)S(1)}, u32[]{:S(2)}, u32[]{:S(2)}) %all-to-all-start) | async-done | bytes 3276832 | tf_op jit(solution)/shard_map/all_to_all | solution.py:435
  64.6 0.1 copy.10.coef_ref
  64.8 5.6 %pair_sums.1 = (s32[32,128]{1,0:T(8,128)S(1)}, bf16[32,96,128]{2,1,0:T(8,128)(2,1)S(1)}) custom-call(s32[1]{0:T(128)} %bitcast.me_ref, bf16[256,96]{1,0:T(8,128)(2,1)S(1)} %copy.10.coef_ref, bf16[32,400,128]{2,1,0:T(8,128)(2,1)S(1)} %all-to-all-done.got_ref), custom_call_target="tpu_custom_call" | custom-call | tf_op jit(solution)/shard_map/pair_sums/pallas_call | solution.py:353
  70.3 19.7 %all_to_all.20.refs_4_ = bf16[32,96,128]{2,1,0:T(8,128)(2,1)S(1)} all-to-all(bf16[32,96,128]{2,1,0:T(8,128)(2,1)S(1)} %get-tuple-element.30), channel_id=1, replica_groups=mesh['atom'=32,'aux'=8] {'atom'}, dimensions={0} | all-to-all | bytes 1572864 | tf_op jit(solution)/shard_map/all_to_all | solution.py:454
  90.0 0.1 slice_reduce_fusion
  90.1 16.6 %all_to_all.21.refs_3_ = bf16[8,64,128]{2,1,0:T(8,128)(2,1)S(1)} all-to-all(bf16[8,64,128]{2,1,0:T(8,128)(2,1)S(1)} %broadcast_in_dim.37), channel_id=1, replica_groups=mesh['atom'=32,'aux'=8] {'aux'}, dimensions={0} | all-to-all | bytes 262144 | tf_op jit(solution)/shard_map/all_to_all | solution.py:457
  106.8 0.8 make_slots.1
  107.6 13.7 %all_to_all.22.slot_ref = bf16[32,32,128]{2,1,0:T(8,128)(2,1)S(1)} all-to-all(bf16[32,32,128]{2,1,0:T(8,128)(2,1)S(1)} %make_slots.1), channel_id=1, replica_groups=mesh['atom'=32,'aux'=8] {'atom'}, dimensions={0} | all-to-all | bytes 524288 | tf_op jit(solution)/shard_map/all_to_all | solution.py:459
  121.3 2.2 %add_gains.1 = f32[96,256]{1,0:T(8,128)} custom-call(s32[32,128]{1,0:T(8,128)S(1)} %get-tuple-element.26.table_ref, bf16[32,32,128]{2,1,0:T(8,128)(2,1)S(1)} %all_to_all.22.slot_ref), custom_call_target="tpu_custom_call" | custom-call | tf_op jit(solution)/shard_map/add_gains/pallas_call | solution.py:393
  (4 shorter events, 0.1 us)
Async XLA Ops:
  1.1 7.1 %collective-permute-start = (bf16[128,768]{1,0:T(8,128)(2,1)S(1)}, bf16[128,768]{1,0:T(8,128)(2,1)S(1)}, u32[]{:S(2)}, u32[]{:S(2)}) collective-permute-start(bf16[128,768]{1,0:T(8,128)(2,1)S(1)} %get-tuple-element.32), channel_id=1, source_target_pairs={{0,8},{8,0},{16,24},{24,16},{32,40},{40,32},{48,56},{56,48},{64,72... | collective-permute-start | bytes 589832 | tf_op jit(solution)/shard_map/ppermute | solution.py:428
  4.4 7.0 %collective-permute-start.1 = (bf16[128,768]{1,0:T(8,128)(2,1)S(1)}, bf16[128,768]{1,0:T(8,128)(2,1)S(1)}, u32[]{:S(2)}, u32[]{:S(2)}) collective-permute-start(bf16[128,768]{1,0:T(8,128)(2,1)S(1)} %get-tuple-element.31), channel_id=1, source_target_pairs={{8,16},{16,8},{24,32},{32,24},{40,48},{48,40},{56,64},{64,56},{72,... | collective-permute-start | bytes 589832 | tf_op jit(solution)/shard_map/ppermute | solution.py:426
  16.1 8.7 %copy-start = (s32[32,1]{0,1:T(1,128)S(1)}, s32[32,1]{0,1:T(1,128)}, u32[]{:S(2)}) copy-start(s32[32,1]{0,1:T(1,128)} %param.10) | copy-start | bytes 388
  16.1 48.5 %all-to-all-start = ((bf16[32,400,128]{2,1,0:T(8,128)(2,1)}), bf16[32,400,128]{2,1,0:T(8,128)(2,1)S(1)}, u32[]{:S(2)}, u32[]{:S(2)}) async-start(bf16[32,400,128]{2,1,0:T(8,128)(2,1)} %fit.1), calls=%async_computation | async-start | bytes 6553600 | tf_op jit(solution)/shard_map/all_to_all | solution.py:435

commit v11 on v10

--- a/solution.py
+++ b/solution.py
@@ -42,8 +42,8 @@
 
 
 def stage_kernel(
-    own_ref, ints_hbm, metric_hbm, size_hbm, dev_hbm, atom_hbm,
-    ints_ref, window_ref, order_ref, mix_ref, meta_ref,
+    part_ref, own_ref, ints_hbm, metric_hbm, size_hbm, dev_hbm, atom_hbm,
+    ints_ref, window_ref, order_ref, mix_ref, meta_ref, coef_ref,
     metric_ref, size_ref, dev_ref, atom_ref, rows_ref, sem_ref,
 ):
     sources = (ints_hbm, metric_hbm, size_hbm, dev_hbm, atom_hbm)
@@ -59,6 +59,12 @@
     order_ref[0] = jnp.where(main_order, 1.0, 0.0).astype(jnp.bfloat16)
     order_ref[1] = jnp.where(side_order, 1.0, 0.0).astype(jnp.bfloat16)
     ordered(own_ref, order_ref, window_ref, 0)
+    width = own_ref.shape[1]
+    part = width // 16
+    row, lane = iota((width, 128), 0), iota((width, 128), 1)
+    source = part_ref[0] * part + jnp.where(lane < part, lane, lane + width // 2 - part)
+    chosen = jnp.where((row == source) & (lane < 2 * part), 1.0, 0.0).astype(jnp.bfloat16)
+    coef_ref[...] = dot(own_ref[...], chosen).astype(jnp.bfloat16)
     for fetch in fetches[1:]:
         fetch.wait()
     member = iota((256, 8), 0) // ROWBLK == iota((256, 8), 1)
@@ -74,7 +80,7 @@
 
 def fit_kernel(
     odd_ref, near_ref, far_ref, own_ref, ints_ref, order_ref, mix_ref, meta_ref, out_ref,
-    window_ref, packed_ref, out_sem,
+    window_ref,
 ):
     aux_dev, bas_dev, span = ints_ref.shape
     blocks = bas_dev // ROWBLK
@@ -85,7 +91,6 @@
     ordered(far_ref, order_ref, window_ref, far_at)
     mix = mix_ref[...]
     left = iota((ROWBLK // 2, 128), 1) < 64
-    copies = []
     for u in range(blocks):
         if u % 4 == 0:
             ints = ints_ref[:, u * ROWBLK : (u + 4) * ROWBLK].reshape(-1, span)
@@ -100,28 +105,17 @@
             rows = fitted[p * ROWBLK : (p + 1) * ROWBLK]
             for k in range(4):
                 tile = rows[:, k * 128 : (k + 1) * 128]
-                packed_ref[p * 4 + k, main] = tile.astype(jnp.bfloat16)
+                out_ref[p * 4 + k, main] = tile.astype(jnp.bfloat16)
             for k in range(2):
                 shared = rows[:, 512 + k * 128 : 640 + k * 128]
                 top, bottom = shared[: ROWBLK // 2], shared[ROWBLK // 2 :]
                 even = jnp.where(left, top, pltpu.roll(bottom, 64, 1))
                 odd = jnp.where(left, pltpu.roll(top, 64, 1), bottom)
-                packed_ref[p * 4 + 2 * k, side] = even.astype(jnp.bfloat16)
-                packed_ref[p * 4 + 2 * k + 1, side] = odd.astype(jnp.bfloat16)
+                out_ref[p * 4 + 2 * k, side] = even.astype(jnp.bfloat16)
+                out_ref[p * 4 + 2 * k + 1, side] = odd.astype(jnp.bfloat16)
         if u == blocks - 1:
             for d in range(4 * aux_dev):
-                packed_ref[d, blocks * PACKED : blocks * PACKED + 16] = meta_ref[...]
-        if u % 2 == 1:
-            first = (u - 1) * PACKED
-            span_rows = pl.ds(first, 2 * PACKED + (16 if u == blocks - 1 else 0))
-            copies.append(
-                pltpu.make_async_copy(
-                    packed_ref.at[:, span_rows], out_ref.at[:, span_rows], out_sem.at[u // 2]
-                )
-            )
-            copies[-1].start()
-    for copy in copies:
-        copy.wait()
+                out_ref[d, blocks * PACKED : blocks * PACKED + 16] = meta_ref[...]
 
 
 def end_table(me, got_ref, size_ref, dev_ref, atom_ref):
@@ -183,9 +177,9 @@
     tail = groups * blocks * ROWBLK
     real_ref[tail : tail + MAXBF] = jnp.zeros((MAXBF, 128), jnp.float32)
     imag_ref[tail : tail + MAXBF] = jnp.zeros((MAXBF, 128), jnp.float32)
-    bas_dev, width = coef_ref.shape
+    bas_dev = coef_ref.shape[0]
     rows_ref[...] = jnp.zeros(rows_ref.shape, jnp.float32)
-    rows_ref[0:bas_dev, 0:width] = coef_ref[...].astype(jnp.float32)
+    rows_ref[0:bas_dev] = coef_ref[...].astype(jnp.float32)
     row_id = iota((MAXBF, 128), 0)
     lane_pair = lane // MAXBF
     batch = len(sides) // 4
@@ -225,7 +219,7 @@
     lax.fori_loop(0, groups // batch, group, 0)
 
 
-def slot_kernel(scale, target_ref, rank_ref, place_ref, parts_ref, got_ref, out_ref, tile_ref):
+def slot_kernel(scale, asked_ref, place_ref, parts_ref, got_ref, out_ref, tile_ref):
     total = parts_ref[0].astype(jnp.float32)
     for z in range(1, parts_ref.shape[0]):
         total = total + parts_ref[z].astype(jnp.float32)
@@ -237,8 +231,8 @@
     turned = jnp.where(v == 96 + u, jnp.where(u < MAXBF, 1.0, -1.0), 0.0).astype(jnp.bfloat16)
 
     def coef(e):
-        at = pl.multiple_of(64 + rank_ref[e] * MAXBF, MAXBF)
-        return got_ref[target_ref[e], pl.ds(at, MAXBF)]
+        at = pl.multiple_of(64 + (asked_ref[e] % 2) * MAXBF, MAXBF)
+        return got_ref[asked_ref[e] // 2, pl.ds(at, MAXBF)]
 
     for h in range(2):
         block = kernel[h * 32 : (h + 1) * 32]
@@ -306,11 +300,13 @@
     return pltpu.with_memory_space_constraint(array, pltpu.HBM)
 
 
-def stage(own, *fetched):
+def stage(part, own, *fetched):
     shapes = [fetched[0].shape, own.shape, (2, 256, 256), (256, 256), (16, 128)]
+    shapes.append((own.shape[0], 128))
     return pl.pallas_call(
         stage_kernel,
-        in_specs=[vmem_spec()] + [pl.BlockSpec(memory_space=pltpu.HBM)] * len(fetched),
+        in_specs=[smem_spec(), vmem_spec()]
+        + [pl.BlockSpec(memory_space=pltpu.HBM)] * len(fetched),
         out_specs=[vmem_spec()] * len(shapes),
         out_shape=[pltpu.VMEM(shape, jnp.bfloat16) for shape in shapes],
         scratch_shapes=[pltpu.VMEM(x.shape, x.dtype) for x in fetched[1:]]
@@ -318,7 +314,7 @@
         compiler_params=limit(16),
         cost_estimate=pl.CostEstimate(flops=1 << 28, bytes_accessed=5 * MIB, transcendentals=0),
         name="stage",
-    )(own, *[in_hbm(x) for x in fetched])
+    )(part, own, *[in_hbm(x) for x in fetched])
 
 
 def fit(odd, near, far, window_rows, ints, order, mix, meta):
@@ -329,13 +325,9 @@
     return pl.pallas_call(
         fit_kernel,
         in_specs=[smem_spec()] + [vmem_spec()] * 7,
-        out_specs=pl.BlockSpec(memory_space=pltpu.HBM),
-        out_shape=pltpu.HBM(shape, jnp.bfloat16),
-        scratch_shapes=[
-            pltpu.VMEM((window, width), jnp.bfloat16),
-            pltpu.VMEM(shape, jnp.bfloat16),
-            pltpu.SemaphoreType.DMA((blocks // 2,)),
-        ],
+        out_specs=vmem_spec(),
+        out_shape=jax.ShapeDtypeStruct(shape, jnp.bfloat16),
+        scratch_shapes=[pltpu.VMEM((window, width), jnp.bfloat16)],
         compiler_params=limit(32),
         cost_estimate=pl.CostEstimate(
             flops=2 * aux_dev * bas_dev * width * (window + 256),
@@ -374,19 +366,19 @@
     )(me, coef, got)
 
 
-def make_slots(scale, targets, ranks, places, parts, got):
+def make_slots(scale, asked, places, parts, got):
     def body(*refs):
         slot_kernel(scale, *refs)
 
     return pl.pallas_call(
         body,
-        in_specs=[smem_spec()] * 3 + [vmem_spec()] * 2,
+        in_specs=[smem_spec()] * 2 + [vmem_spec()] * 2,
         out_specs=vmem_spec(),
         out_shape=jax.ShapeDtypeStruct((got.shape[0], 2 * MAXBF, 128), jnp.bfloat16),
         scratch_shapes=[pltpu.VMEM((528, 128), jnp.bfloat16)],
         compiler_params=limit(16),
         name="make_slots",
-    )(targets, ranks, places, parts, got)
+    )(asked, places, parts, got)
 
 
 def add_gains(table, slots, width, bas_dev):
@@ -427,15 +419,10 @@
     near = lax.dynamic_slice_in_dim(own, (1 - odd) * halo, halo, 0)
     near = lax.ppermute(near, "atom", [(i, i ^ 1) for i in range(groups)])
 
-    ints, window_rows, order, mix, meta = stage(
-        own, integrals, metric, atom_sizes, pair_device.T, pair_atom[None]
+    part = jnp.full((1,), lax.axis_index("aux"), jnp.int32)
+    ints, window_rows, columns, mix, meta, coef_part = stage(
+        part, own, integrals, metric, atom_sizes, pair_device.T, pair_atom[None]
     )
-    odd = jnp.full((1,), odd, jnp.int32)
-    packed = fit(odd, near, far, window_rows, ints, order, mix, meta)
-    got = lax.all_to_all(packed, "atom", split_axis=0, concat_axis=0, tiled=True)
-    coef_part = lax.dynamic_slice_in_dim(
-        coeffs, lax.axis_index("aux") * occ_part, occ_part, 2
-    ).reshape(bas_dev, 2 * occ_part)
     me = jnp.full((1,), lax.axis_index("atom"), jnp.int32)
 
     targets = pair_device[:, 0]
@@ -447,15 +434,18 @@
     asked_hit = asked[None, :] == jnp.arange(2 * groups, dtype=jnp.int32)[:, None]
     places = 512 + pick(asked_hit, place[None, :] - 512)
 
-    me, coef_part, got, targets, ranks, places = lax.optimization_barrier(
-        (me, coef_part, got, targets, ranks, places)
+    near, far, me, coef_part, asked, places = lax.optimization_barrier(
+        (near, far, me, coef_part, asked, places)
     )
+    odd = jnp.full((1,), odd, jnp.int32)
+    packed = fit(odd, near, far, window_rows, ints, columns, mix, meta)
+    got = lax.all_to_all(packed, "atom", split_axis=0, concat_axis=0, tiled=True)
     table, sent = pair_sums(me, coef_part, got)
     owned = lax.all_to_all(sent, "atom", split_axis=0, concat_axis=0, tiled=True)
     own_sums = jnp.sum(owned[:, : 4 * MAXBF].astype(jnp.float32), axis=0).astype(jnp.bfloat16)
     shared = jnp.broadcast_to(own_sums[None], (aux_count,) + own_sums.shape)
     parts = lax.all_to_all(shared, "aux", split_axis=0, concat_axis=0, tiled=True)
-    slots = make_slots(scale, targets, ranks, places, parts, owned)
+    slots = make_slots(scale, asked, places, parts, owned)
     slots = lax.all_to_all(slots, "atom", split_axis=0, concat_axis=0, tiled=True)
     result = add_gains(table, slots, 2 * occ_part, bas_dev)
     return result.reshape(2, occ_part, bas_dev).transpose(2, 0, 1)

time: 124 us -> 120 us (0.968)
  blocking collectives: 50 us -> 98.1 us
  waiting for transfers between devices: 42.7 us -> 0.01 us
  starting transfers between devices: 12.6 us -> 4.69 us
  other arithmetic: 0.37 us -> 1.76 us
  local copies, waits for them, and re-layouts: 2.48 us -> 1.1 us
    all_to_all x0 -> x1, blocking collectives: none -> 50 us  [per_device(): lax.all_to_all(packed, 'atom', split_axis=0, concat_axis=0, tiled=True)]
    all_to_all x1 -> x0, waiting for transfers between devices: 39.5 us -> none  [per_device(): lax.all_to_all(packed, 'atom', split_axis=0, concat_axis=0, tiled=True)]
    all_to_all x1 -> x0, starting transfers between devices: 7.41 us -> none  [per_device(): lax.all_to_all(packed, 'atom', split_axis=0, concat_axis=0, tiled=True)]
    ppermute x1, starting transfers between devices: 3.33 us -> 0.09 us  [per_device(): near = lax.ppermute(near, 'atom', [(i, i ^ 1) for i in range(groups)])]
    ppermute x1, waiting for transfers between devices: 3.22 us -> 0.01 us  [per_device(): lax.ppermute(far, 'atom', [(i, i + 1 if i % 2 else i - 1) for i in inner])]
    ppermute x1, starting transfers between devices: 1.91 us -> 4.59 us  [per_device(): lax.ppermute(far, 'atom', [(i, i + 1 if i % 2 else i - 1) for i in inner])]
    all_to_all x1, blocking collectives: 19.7 us -> 17.8 us  [per_device(): lax.all_to_all(sent, 'atom', split_axis=0, concat_axis=0, tiled=True)]
  transfers between devices with their start and end apart: 3 -> 2, of which waited for: 2 -> 0; matrix products, arithmetic and copies ran while one was open for 1% -> 1% of each run, Pallas kernels for 1% -> 1%
where the time goes in v11:
time: 120 us
  blocking collectives  98.1 us (82%)
  Pallas kernels  14 us (12%)
  starting transfers between devices  4.69 us (4%)
  other arithmetic  1.76 us (1%)
    all_to_all x1, blocking collectives, per_device(): lax.all_to_all(packed, 'atom', split_axis=0, concat_axis=0, tiled=True)  50 us
    all_to_all x1, blocking collectives, per_device(): lax.all_to_all(sent, 'atom', split_axis=0, concat_axis=0, tiled=True)  17.8 us
    all_to_all x1, blocking collectives, per_device(): lax.all_to_all(shared, 'aux', split_axis=0, concat_axis=0, tiled=True)  16.6 us
    all_to_all x1, blocking collectives, per_device(): lax.all_to_all(slots, 'atom', split_axis=0, concat_axis=0, tiled=True)  13.7 us
    pallas_call x1, Pallas kernels, pair_sums(): pl.pallas_call(pair_kernel, in_specs=[smem_spec(), vmem_spec(), vmem_spec...  5.57 us
    ppermute x1, starting transfers between devices, per_device(): lax.ppermute(far, 'atom', [(i, i + 1 if i % 2 else i - 1) for i in inner])  4.59 us
    pallas_call x1, Pallas kernels, fit(): pl.pallas_call(fit_kernel, in_specs=[smem_spec()] + [vmem_spec()] * 7, ou...  3.62 us
  transfers between devices with their start and end apart: 2, of which 0 were waited for; matrix products, arithmetic and copies ran while one was open for 1% of the time, Pallas kernels for 1%

profile of v11, /device:TPU:1, one launch (start us, length us, event | category | flops | bytes accessed | tf_op | source)
XLA Modules:
  0.0 119.7 jit_solution(10793921109672810515)
XLA Ops:
  0.0 1.0 copy.7
  1.1 4.6 %collective-permute-start.1 = (bf16[128,768]{1,0:T(8,128)(2,1)S(1)}, bf16[128,768]{1,0:T(8,128)(2,1)S(1)}, u32[]{:S(2)}, u32[]{:S(2)}) collective-permute-start(bf16[128,768]{1,0:T(8,128)(2,1)S(1)} %get-tuple-element.33), channel_id=1, source_target_pairs={{8,16},{16,8},{24,32},{32,24},{40,48},{48,40},{56,64},{64,56},{72,... | collective-permute-start | bytes 589832 | tf_op jit(solution)/shard_map/ppermute | solution.py:418
  5.7 0.1 collective-permute-start
  5.8 0.9 convert_reduce_fusion
  6.7 0.7 multiply_add_fusion.refs_0_
  7.4 0.1 select_reduce_fusion
  7.5 1.7 %stage.1 = (bf16[8,256,512]{2,1,0:T(8,128)(2,1)S(1)}, bf16[256,768]{1,0:T(8,128)(2,1)S(1)}, bf16[2,256,256]{2,1,0:T(8,128)(2,1)S(1)}, bf16[256,256]{1,0:T(8,128)...) custom-call(s32[1]{0:T(128)} %bitcast.1.part_ref, bf16[256,768]{1,0:T(8,128)(2,1)S(1)} %bitcast.13, ...), custom_call_target="tpu_custom_call" | custom-call | flops 268435456 | bytes 5242880 | tf_op jit(solution)/shard_map/stage/pallas_call | solution.py:306
  9.2 0.0 collective-permute-done.1.far_ref
  9.2 0.0 collective-permute-done.near_ref
  9.2 3.6 %fit.1 = bf16[32,400,128]{2,1,0:T(8,128)(2,1)S(1)} custom-call(s32[1]{0:T(128)} %bitcast.5.odd_ref, bf16[128,768]{1,0:T(8,128)(2,1)S(1)} %collective-permute-done.near_ref, bf16[128,768]{1,0:T(8,128)(2,1)S(1)} %collective-permute-done.1.far_ref, bf16[256,768]{1,0:T(8,128)(2,1)S(1)} %get-tuple-element.24.own_ref, ...), custom_call_target="tpu_custom_call" | custom-call | flops 2415919104 | bytes 6291456 | tf_op jit(solution)/shard_map/fit/pallas_call | solution.py:325
  12.9 50.0 %all_to_all.20.got_ref = bf16[32,400,128]{2,1,0:T(8,128)(2,1)S(1)} all-to-all(bf16[32,400,128]{2,1,0:T(8,128)(2,1)S(1)} %fit.1), channel_id=1, replica_groups=mesh['atom'=32,'aux'=8] {'atom'}, dimensions={0} | all-to-all | bytes 6553600 | tf_op jit(solution)/shard_map/all_to_all | solution.py:442
  62.9 5.6 %pair_sums.1 = (s32[32,128]{1,0:T(8,128)S(1)}, bf16[32,96,128]{2,1,0:T(8,128)(2,1)S(1)}) custom-call(s32[1]{0:T(128)} %bitcast.me_ref, bf16[256,128]{1,0:T(8,128)(2,1)S(1)} %get-tuple-element.21.coef_ref, bf16[32,400,128]{2,1,0:T(8,128)(2,1)S(1)} %all_to_all.20.got_ref), custom_call_target="tpu_custom_call" | custom-call | tf_op jit(solution)/shard_map/pair_sums/pallas_call | solution.py:345
  68.5 17.8 %all_to_all.21.refs_3_ = bf16[32,96,128]{2,1,0:T(8,128)(2,1)S(1)} all-to-all(bf16[32,96,128]{2,1,0:T(8,128)(2,1)S(1)} %get-tuple-element.32), channel_id=1, replica_groups=mesh['atom'=32,'aux'=8] {'atom'}, dimensions={0} | all-to-all | bytes 1572864 | tf_op jit(solution)/shard_map/all_to_all | solution.py:444
  86.3 0.1 slice_reduce_fusion
  86.4 16.6 %all_to_all.22.refs_2_ = bf16[8,64,128]{2,1,0:T(8,128)(2,1)S(1)} all-to-all(bf16[8,64,128]{2,1,0:T(8,128)(2,1)S(1)} %broadcast_in_dim.41), channel_id=1, replica_groups=mesh['atom'=32,'aux'=8] {'aux'}, dimensions={0} | all-to-all | bytes 262144 | tf_op jit(solution)/shard_map/all_to_all | solution.py:447
  103.0 0.9 make_slots.1
  103.9 13.7 %all_to_all.23.slot_ref = bf16[32,32,128]{2,1,0:T(8,128)(2,1)S(1)} all-to-all(bf16[32,32,128]{2,1,0:T(8,128)(2,1)S(1)} %make_slots.1), channel_id=1, replica_groups=mesh['atom'=32,'aux'=8] {'atom'}, dimensions={0} | all-to-all | bytes 524288 | tf_op jit(solution)/shard_map/all_to_all | solution.py:449
  117.6 2.1 %add_gains.1 = f32[96,256]{1,0:T(8,128)} custom-call(s32[32,128]{1,0:T(8,128)S(1)} %get-tuple-element.29.table_ref, bf16[32,32,128]{2,1,0:T(8,128)(2,1)S(1)} %all_to_all.23.slot_ref), custom_call_target="tpu_custom_call" | custom-call | tf_op jit(solution)/shard_map/add_gains/pallas_call | solution.py:385
  (4 shorter events, 0.1 us)
Async XLA Ops:
  1.1 8.1 %collective-permute-start.1 = (bf16[128,768]{1,0:T(8,128)(2,1)S(1)}, bf16[128,768]{1,0:T(8,128)(2,1)S(1)}, u32[]{:S(2)}, u32[]{:S(2)}) collective-permute-start(bf16[128,768]{1,0:T(8,128)(2,1)S(1)} %get-tuple-element.33), channel_id=1, source_target_pairs={{8,16},{16,8},{24,32},{32,24},{40,48},{48,40},{56,64},{64,56},{72,... | collective-permute-start | bytes 589832 | tf_op jit(solution)/shard_map/ppermute | solution.py:418
  5.7 3.5 %collective-permute-start = (bf16[128,768]{1,0:T(8,128)(2,1)S(1)}, bf16[128,768]{1,0:T(8,128)(2,1)S(1)}, u32[]{:S(2)}, u32[]{:S(2)}) collective-permute-start(bf16[128,768]{1,0:T(8,128)(2,1)S(1)} %get-tuple-element.34), channel_id=1, source_target_pairs={{0,8},{8,0},{16,24},{24,16},{32,40},{40,32},{48,56},{56,48},{64,72... | collective-permute-start | bytes 589832 | tf_op jit(solution)/shard_map/ppermute | solution.py:420

commit v12 on v11

--- a/solution.py
+++ b/solution.py
@@ -115,13 +115,13 @@
                 out_ref[p * 4 + 2 * k + 1, side] = odd.astype(jnp.bfloat16)
         if u == blocks - 1:
             for d in range(4 * aux_dev):
-                out_ref[d, blocks * PACKED : blocks * PACKED + 16] = meta_ref[...]
+                out_ref[d, blocks * PACKED : blocks * PACKED + 8] = meta_ref[...]
 
 
 def end_table(me, got_ref, size_ref, dev_ref, atom_ref):
-    groups, at = got_ref.shape[0], got_ref.shape[1] - 16
+    groups, at = got_ref.shape[0], got_ref.shape[1] - 8
     for d in range(groups):
-        rows = got_ref[d, at : at + 16].astype(jnp.float32)
+        rows = got_ref[d, at : at + 8].astype(jnp.float32)
         for i, dest in enumerate((size_ref, dev_ref, atom_ref)):
             dest[d : d + 1] = rows[i : i + 1]
     before = jnp.where(iota((128, 128), 0) < iota((128, 128), 1), 1.0, 0.0).astype(jnp.bfloat16)
@@ -148,10 +148,13 @@
 
 
 def pair_kernel(
-    me_ref, coef_ref, got_ref, table_ref, out_ref, real_ref, imag_ref, rows_ref,
+    me_ref, coef_ref, got_ref, slot_ref, out_ref, real_ref, imag_ref, rows_ref, table_ref,
     size_ref, dev_ref, atom_ref, row_ref, table_sem, *sides,
 ):
-    table_ref[...] = end_table(me_ref[0], got_ref, size_ref, dev_ref, atom_ref)
+    table = end_table(me_ref[0], got_ref, size_ref, dev_ref, atom_ref)
+    table_ref[...] = table
+    slot_ref[...] = jnp.zeros(slot_ref.shape, jnp.int32)
+    slot_ref[:, 0 : table.shape[0]] = table.astype(jnp.float32).T[32:40].astype(jnp.int32)
     fetch = pltpu.make_async_copy(table_ref, row_ref, table_sem)
     fetch.start()
     groups, blocks = got_ref.shape[0], got_ref.shape[1] // PACKED
@@ -278,8 +281,8 @@
         gains = dot(tiles, jnp.concatenate([slots, turned_ref[g]], axis=0))
         for r in range(2):
             part = gains[r * MAXBF : (r + 1) * MAXBF]
-            part = jnp.where(row_id < table_ref[g, 34 + r], part, 0.0)
-            where = pl.ds(table_ref[g, 32 + r], MAXBF)
+            part = jnp.where(row_id < table_ref[2 + r, g], part, 0.0)
+            where = pl.ds(table_ref[r, g], MAXBF)
             sum_ref[where] = sum_ref[where] + part
     out_ref[...] = sum_ref[0:bas_dev].T[0:width]
 
@@ -301,7 +304,7 @@
 
 
 def stage(part, own, *fetched):
-    shapes = [fetched[0].shape, own.shape, (2, 256, 256), (256, 256), (16, 128)]
+    shapes = [fetched[0].shape, own.shape, (2, 256, 256), (256, 256), (8, 128)]
     shapes.append((own.shape[0], 128))
     return pl.pallas_call(
         stage_kernel,
@@ -310,7 +313,7 @@
         out_specs=[vmem_spec()] * len(shapes),
         out_shape=[pltpu.VMEM(shape, jnp.bfloat16) for shape in shapes],
         scratch_shapes=[pltpu.VMEM(x.shape, x.dtype) for x in fetched[1:]]
-        + [pltpu.VMEM((16, 128), jnp.float32), pltpu.SemaphoreType.DMA((len(fetched),))],
+        + [pltpu.VMEM((8, 128), jnp.float32), pltpu.SemaphoreType.DMA((len(fetched),))],
         compiler_params=limit(16),
         cost_estimate=pl.CostEstimate(flops=1 << 28, bytes_accessed=5 * MIB, transcendentals=0),
         name="stage",
@@ -321,7 +324,7 @@
     aux_dev, bas_dev, window = ints.shape
     width = near.shape[1]
     blocks = bas_dev // ROWBLK
-    shape = (4 * aux_dev, blocks * PACKED + 16, 128)
+    shape = (4 * aux_dev, blocks * PACKED + 8, 128)
     return pl.pallas_call(
         fit_kernel,
         in_specs=[smem_spec()] + [vmem_spec()] * 7,
@@ -347,13 +350,14 @@
         in_specs=[smem_spec(), vmem_spec(), vmem_spec()],
         out_specs=[vmem_spec()] * 2,
         out_shape=[
-            jax.ShapeDtypeStruct((groups, 128), jnp.int32),
+            jax.ShapeDtypeStruct((8, 128), jnp.int32),
             jax.ShapeDtypeStruct(shape, jnp.bfloat16),
         ],
         scratch_shapes=[
             pltpu.VMEM((rows, 128), jnp.float32),
             pltpu.VMEM((rows, 128), jnp.float32),
             pltpu.VMEM((coef.shape[0] + MAXBF, 128), jnp.float32),
+            pltpu.VMEM((groups, 128), jnp.int32),
             pltpu.VMEM((groups, 128), jnp.float32),
             pltpu.VMEM((groups, 128), jnp.float32),
             pltpu.VMEM((groups, 128), jnp.float32),

time: 120 us -> 120 us (level)
  no operation moved by 1% of the time
where the time goes in v12:
time: 120 us; the launch traced here: 119 us
  blocking collectives  97.5 us (81%)
  Pallas kernels  14.2 us (12%)
  starting transfers between devices  4.69 us (4%)
  other arithmetic  1.76 us (1%)
    all_to_all x1, blocking collectives, per_device(): lax.all_to_all(packed, 'atom', split_axis=0, concat_axis=0, tiled=True)  49.5 us
    all_to_all x1, blocking collectives, per_device(): lax.all_to_all(sent, 'atom', split_axis=0, concat_axis=0, tiled=True)  17.7 us
    all_to_all x1, blocking collectives, per_device(): lax.all_to_all(shared, 'aux', split_axis=0, concat_axis=0, tiled=True)  16.6 us
    all_to_all x1, blocking collectives, per_device(): lax.all_to_all(slots, 'atom', split_axis=0, concat_axis=0, tiled=True)  13.7 us
    pallas_call x1, Pallas kernels, pair_sums(): pl.pallas_call(pair_kernel, in_specs=[smem_spec(), vmem_spec(), vmem_spec...  6.03 us
    ppermute x1, starting transfers between devices, per_device(): lax.ppermute(far, 'atom', [(i, i + 1 if i % 2 else i - 1) for i in inner])  4.59 us
    pallas_call x1, Pallas kernels, fit(): pl.pallas_call(fit_kernel, in_specs=[smem_spec()] + [vmem_spec()] * 7, ou...  3.62 us
  transfers between devices with their start and end apart: 2, of which 0 were waited for; matrix products, arithmetic and copies ran while one was open for 1% of the time, Pallas kernels for 1%

profile of v12, /device:TPU:1, one launch (start us, length us, event | category | flops | bytes accessed | tf_op | source)
XLA Modules:
  0.0 119.4 jit_solution(2567180564122823122)
XLA Ops:
  0.0 1.0 copy.7
  1.1 4.6 %collective-permute-start.1 = (bf16[128,768]{1,0:T(8,128)(2,1)S(1)}, bf16[128,768]{1,0:T(8,128)(2,1)S(1)}, u32[]{:S(2)}, u32[]{:S(2)}) collective-permute-start(bf16[128,768]{1,0:T(8,128)(2,1)S(1)} %get-tuple-element.33), channel_id=1, source_target_pairs={{8,16},{16,8},{24,32},{32,24},{40,48},{48,40},{56,64},{64,56},{72,... | collective-permute-start | bytes 589832 | tf_op jit(solution)/shard_map/ppermute | solution.py:422
  5.7 0.1 collective-permute-start
  5.8 0.9 convert_reduce_fusion
  6.7 0.7 multiply_add_fusion.refs_0_
  7.4 0.1 select_reduce_fusion
  7.5 1.7 %stage.1 = (bf16[8,256,512]{2,1,0:T(8,128)(2,1)S(1)}, bf16[256,768]{1,0:T(8,128)(2,1)S(1)}, bf16[2,256,256]{2,1,0:T(8,128)(2,1)S(1)}, bf16[256,256]{1,0:T(8,128)...) custom-call(s32[1]{0:T(128)} %bitcast.1.part_ref, bf16[256,768]{1,0:T(8,128)(2,1)S(1)} %bitcast.13, ...), custom_call_target="tpu_custom_call" | custom-call | flops 268435456 | bytes 5242880 | tf_op jit(solution)/shard_map/stage/pallas_call | solution.py:309
  9.2 0.0 collective-permute-done.1.far_ref
  9.2 0.0 collective-permute-done.near_ref
  9.2 3.6 %fit.1 = bf16[32,392,128]{2,1,0:T(8,128)(2,1)S(1)} custom-call(s32[1]{0:T(128)} %bitcast.5.odd_ref, bf16[128,768]{1,0:T(8,128)(2,1)S(1)} %collective-permute-done.near_ref, bf16[128,768]{1,0:T(8,128)(2,1)S(1)} %collective-permute-done.1.far_ref, bf16[256,768]{1,0:T(8,128)(2,1)S(1)} %get-tuple-element.24.own_ref, ...), custom_call_target="tpu_custom_call" | custom-call | flops 2415919104 | bytes 6291456 | tf_op jit(solution)/shard_map/fit/pallas_call | solution.py:328
  12.9 49.5 %all_to_all.20.got_ref = bf16[32,392,128]{2,1,0:T(8,128)(2,1)S(1)} all-to-all(bf16[32,392,128]{2,1,0:T(8,128)(2,1)S(1)} %fit.1), channel_id=1, replica_groups=mesh['atom'=32,'aux'=8] {'atom'}, dimensions={0} | all-to-all | bytes 6422528 | tf_op jit(solution)/shard_map/all_to_all | solution.py:446
  62.4 6.0 %pair_sums.1 = (s32[8,128]{1,0:T(8,128)S(1)}, bf16[32,96,128]{2,1,0:T(8,128)(2,1)S(1)}) custom-call(s32[1]{0:T(128)} %bitcast.me_ref, bf16[256,128]{1,0:T(8,128)(2,1)S(1)} %get-tuple-element.21.coef_ref, bf16[32,392,128]{2,1,0:T(8,128)(2,1)S(1)} %all_to_all.20.got_ref), custom_call_target="tpu_custom_call" | custom-call | tf_op jit(solution)/shard_map/pair_sums/pallas_call | solution.py:348
  68.4 17.7 %all_to_all.21.refs_3_ = bf16[32,96,128]{2,1,0:T(8,128)(2,1)S(1)} all-to-all(bf16[32,96,128]{2,1,0:T(8,128)(2,1)S(1)} %get-tuple-element.32), channel_id=1, replica_groups=mesh['atom'=32,'aux'=8] {'atom'}, dimensions={0} | all-to-all | bytes 1572864 | tf_op jit(solution)/shard_map/all_to_all | solution.py:448
  86.1 0.1 slice_reduce_fusion
  86.2 16.6 %all_to_all.22.refs_2_ = bf16[8,64,128]{2,1,0:T(8,128)(2,1)S(1)} all-to-all(bf16[8,64,128]{2,1,0:T(8,128)(2,1)S(1)} %broadcast_in_dim.41), channel_id=1, replica_groups=mesh['atom'=32,'aux'=8] {'aux'}, dimensions={0} | all-to-all | bytes 262144 | tf_op jit(solution)/shard_map/all_to_all | solution.py:451
  102.9 0.9 make_slots.1
  103.8 13.7 %all_to_all.23.slot_ref = bf16[32,32,128]{2,1,0:T(8,128)(2,1)S(1)} all-to-all(bf16[32,32,128]{2,1,0:T(8,128)(2,1)S(1)} %make_slots.1), channel_id=1, replica_groups=mesh['atom'=32,'aux'=8] {'atom'}, dimensions={0} | all-to-all | bytes 524288 | tf_op jit(solution)/shard_map/all_to_all | solution.py:453
  117.4 1.9 %add_gains.1 = f32[96,256]{1,0:T(8,128)} custom-call(s32[8,128]{1,0:T(8,128)S(1)} %get-tuple-element.29.table_ref, bf16[32,32,128]{2,1,0:T(8,128)(2,1)S(1)} %all_to_all.23.slot_ref), custom_call_target="tpu_custom_call" | custom-call | tf_op jit(solution)/shard_map/add_gains/pallas_call | solution.py:389
  (4 shorter events, 0.1 us)
Async XLA Ops:
  1.1 8.1 %collective-permute-start.1 = (bf16[128,768]{1,0:T(8,128)(2,1)S(1)}, bf16[128,768]{1,0:T(8,128)(2,1)S(1)}, u32[]{:S(2)}, u32[]{:S(2)}) collective-permute-start(bf16[128,768]{1,0:T(8,128)(2,1)S(1)} %get-tuple-element.33), channel_id=1, source_target_pairs={{8,16},{16,8},{24,32},{32,24},{40,48},{48,40},{56,64},{64,56},{72,... | collective-permute-start | bytes 589832 | tf_op jit(solution)/shard_map/ppermute | solution.py:422
  5.7 3.5 %collective-permute-start = (bf16[128,768]{1,0:T(8,128)(2,1)S(1)}, bf16[128,768]{1,0:T(8,128)(2,1)S(1)}, u32[]{:S(2)}, u32[]{:S(2)}) collective-permute-start(bf16[128,768]{1,0:T(8,128)(2,1)S(1)} %get-tuple-element.34), channel_id=1, source_target_pairs={{0,8},{8,0},{16,24},{24,16},{32,40},{40,32},{48,56},{56,48},{64,72... | collective-permute-start | bytes 589832 | tf_op jit(solution)/shard_map/ppermute | solution.py:424

commit v13 on v12

--- a/solution.py
+++ b/solution.py
@@ -153,8 +153,6 @@
 ):
     table = end_table(me_ref[0], got_ref, size_ref, dev_ref, atom_ref)
     table_ref[...] = table
-    slot_ref[...] = jnp.zeros(slot_ref.shape, jnp.int32)
-    slot_ref[:, 0 : table.shape[0]] = table.astype(jnp.float32).T[32:40].astype(jnp.int32)
     fetch = pltpu.make_async_copy(table_ref, row_ref, table_sem)
     fetch.start()
     groups, blocks = got_ref.shape[0], got_ref.shape[1] // PACKED
@@ -186,6 +184,8 @@
     row_id = iota((MAXBF, 128), 0)
     lane_pair = lane // MAXBF
     batch = len(sides) // 4
+    slot_ref[...] = jnp.zeros(slot_ref.shape, jnp.int32)
+    slot_ref[:, 0:groups] = table.astype(jnp.float32).T[32:40].astype(jnp.int32)
     fetch.wait()
 
     def group(step, carry):
@@ -214,9 +214,14 @@
                         part = jnp.where(lane_pair == j, here, part)
                     at = h * 32 + c * 16
                     out_ref[g, at : at + 16] = part.astype(jnp.bfloat16)
-                rows = rows_ref[pl.ds(row_ref[g, 32 + h], MAXBF)]
-                rows = jnp.where(row_id < row_ref[g, 34 + h], rows, 0.0)
-                out_ref[g, 64 + h * 16 : 80 + h * 16] = rows.astype(jnp.bfloat16)
+            rows = []
+            for r in range(2):
+                value = rows_ref[pl.ds(row_ref[g, 32 + r], MAXBF)]
+                rows.append(jnp.where(row_id < row_ref[g, 34 + r], value, 0.0))
+            rest = pltpu.roll(rows[1], 96, 1)
+            out_ref[g, 64:80] = jnp.where(valid, rows[0], rest).astype(jnp.bfloat16)
+            rest = jnp.where(left[0:8], rest[0:8], pltpu.roll(rest[8:16], 64, 1))
+            out_ref[g, 80:88] = rest.astype(jnp.bfloat16)
         return carry
 
     lax.fori_loop(0, groups // batch, group, 0)
@@ -233,9 +238,17 @@
     u, v = iota((32, 128), 0), iota((32, 128), 1)
     turned = jnp.where(v == 96 + u, jnp.where(u < MAXBF, 1.0, -1.0), 0.0).astype(jnp.bfloat16)
 
+    lane = iota((MAXBF, 128), 1)
+
     def coef(e):
-        at = pl.multiple_of(64 + (asked_ref[e] % 2) * MAXBF, MAXBF)
-        return got_ref[asked_ref[e] // 2, pl.ds(at, MAXBF)]
+        source = asked_ref[e] // 2
+        rows = got_ref[source, 64:80].astype(jnp.float32)
+        rest = got_ref[source, 80:88].astype(jnp.float32)
+        rest = jnp.concatenate([rest, pltpu.roll(rest, 64, 1)], axis=0)
+        second = jnp.where(lane < 64, rest, jnp.where(lane < 96, 0.0, rows))
+        second = pltpu.roll(second, 32, 1)
+        first = jnp.where(lane < 96, rows, 0.0)
+        return jnp.where(asked_ref[e] % 2 == 1, second, first)
 
     for h in range(2):
         block = kernel[h * 32 : (h + 1) * 32]
@@ -244,13 +257,14 @@
             tile = block[c * MAXBF : (c + 1) * MAXBF].astype(jnp.float32)
             wide = jnp.where(same, jnp.concatenate([tile] * 8, axis=0), 0.0)
             first = first + dot(wide.astype(jnp.bfloat16), folds[c])
-        first = first.astype(jnp.bfloat16)
-        second = dot_tn(block, turned).astype(jnp.bfloat16)
+        second = dot_tn(block, turned)
         for j in range(8):
             pair, rows = h * 8 + j, slice(j * MAXBF, (j + 1) * MAXBF)
             at = pair * MAXBF
-            tile_ref[at : at + MAXBF] = first[rows] + coef(2 * pair + 1)
-            tile_ref[256 + at : 256 + at + MAXBF] = second[rows] + coef(2 * pair)
+            tile = first[rows] + coef(2 * pair + 1)
+            tile_ref[at : at + MAXBF] = tile.astype(jnp.bfloat16)
+            tile = second[rows] + coef(2 * pair)
+            tile_ref[256 + at : 256 + at + MAXBF] = tile.astype(jnp.bfloat16)
     tile_ref[512:528] = jnp.zeros((MAXBF, 128), jnp.bfloat16)
     for s in range(2 * out_ref.shape[0]):
         rows = tile_ref[pl.ds(pl.multiple_of(place_ref[s], MAXBF), MAXBF)]
@@ -344,7 +358,7 @@
 def pair_sums(me, coef, got):
     groups = got.shape[0]
     rows = groups * (got.shape[1] // PACKED) * ROWBLK + MAXBF
-    shape = (groups, 6 * MAXBF, 128)
+    shape = (groups, 88, 128)
     return pl.pallas_call(
         pair_kernel,
         in_specs=[smem_spec(), vmem_spec(), vmem_spec()],

time: 120 us -> 119 us (level)
  no operation moved by 1% of the time
where the time goes in v13:
time: 119 us; the launch traced here: 118 us
  blocking collectives  96.8 us (81%)
  Pallas kernels  13.7 us (12%)
  starting transfers between devices  4.69 us (4%)
  other arithmetic  1.76 us (1%)
    all_to_all x1, blocking collectives, per_device(): lax.all_to_all(packed, 'atom', split_axis=0, concat_axis=0, tiled=True)  49.5 us
    all_to_all x1, blocking collectives, per_device(): lax.all_to_all(sent, 'atom', split_axis=0, concat_axis=0, tiled=True)  17.1 us
    all_to_all x1, blocking collectives, per_device(): lax.all_to_all(shared, 'aux', split_axis=0, concat_axis=0, tiled=True)  16.8 us
    all_to_all x1, blocking collectives, per_device(): lax.all_to_all(slots, 'atom', split_axis=0, concat_axis=0, tiled=True)  13.4 us
    pallas_call x1, Pallas kernels, pair_sums(): pl.pallas_call(pair_kernel, in_specs=[smem_spec(), vmem_spec(), vmem_spec...  5.52 us
    ppermute x1, starting transfers between devices, per_device(): lax.ppermute(far, 'atom', [(i, i + 1 if i % 2 else i - 1) for i in inner])  4.59 us
    pallas_call x1, Pallas kernels, fit(): pl.pallas_call(fit_kernel, in_specs=[smem_spec()] + [vmem_spec()] * 7, ou...  3.62 us
  transfers between devices with their start and end apart: 2, of which 0 were waited for; matrix products, arithmetic and copies ran while one was open for 1% of the time, Pallas kernels for 1%

profile of v13, /device:TPU:1, one launch (start us, length us, event | category | flops | bytes accessed | tf_op | source)
XLA Modules:
  0.0 118.2 jit_solution(4046547660007543442)
XLA Ops:
  0.0 1.0 copy.7
  1.1 4.6 %collective-permute-start.1 = (bf16[128,768]{1,0:T(8,128)(2,1)S(1)}, bf16[128,768]{1,0:T(8,128)(2,1)S(1)}, u32[]{:S(2)}, u32[]{:S(2)}) collective-permute-start(bf16[128,768]{1,0:T(8,128)(2,1)S(1)} %get-tuple-element.33), channel_id=1, source_target_pairs={{8,16},{16,8},{24,32},{32,24},{40,48},{48,40},{56,64},{64,56},{72,... | collective-permute-start | bytes 589832 | tf_op jit(solution)/shard_map/ppermute | solution.py:436
  5.7 0.1 collective-permute-start
  5.8 0.9 convert_reduce_fusion
  6.7 0.7 multiply_add_fusion.refs_0_
  7.4 0.1 select_reduce_fusion
  7.5 1.7 %stage.1 = (bf16[8,256,512]{2,1,0:T(8,128)(2,1)S(1)}, bf16[256,768]{1,0:T(8,128)(2,1)S(1)}, bf16[2,256,256]{2,1,0:T(8,128)(2,1)S(1)}, bf16[256,256]{1,0:T(8,128)...) custom-call(s32[1]{0:T(128)} %bitcast.1.part_ref, bf16[256,768]{1,0:T(8,128)(2,1)S(1)} %bitcast.13, ...), custom_call_target="tpu_custom_call" | custom-call | flops 268435456 | bytes 5242880 | tf_op jit(solution)/shard_map/stage/pallas_call | solution.py:323
  9.2 0.0 collective-permute-done.1.far_ref
  9.2 0.0 collective-permute-done.near_ref
  9.2 3.6 %fit.1 = bf16[32,392,128]{2,1,0:T(8,128)(2,1)S(1)} custom-call(s32[1]{0:T(128)} %bitcast.5.odd_ref, bf16[128,768]{1,0:T(8,128)(2,1)S(1)} %collective-permute-done.near_ref, bf16[128,768]{1,0:T(8,128)(2,1)S(1)} %collective-permute-done.1.far_ref, bf16[256,768]{1,0:T(8,128)(2,1)S(1)} %get-tuple-element.24.own_ref, ...), custom_call_target="tpu_custom_call" | custom-call | flops 2415919104 | bytes 6291456 | tf_op jit(solution)/shard_map/fit/pallas_call | solution.py:342
  12.9 49.5 %all_to_all.20.got_ref = bf16[32,392,128]{2,1,0:T(8,128)(2,1)S(1)} all-to-all(bf16[32,392,128]{2,1,0:T(8,128)(2,1)S(1)} %fit.1), channel_id=1, replica_groups=mesh['atom'=32,'aux'=8] {'atom'}, dimensions={0} | all-to-all | bytes 6422528 | tf_op jit(solution)/shard_map/all_to_all | solution.py:460
  62.4 5.5 %pair_sums.1 = (s32[8,128]{1,0:T(8,128)S(1)}, bf16[32,88,128]{2,1,0:T(8,128)(2,1)S(1)}) custom-call(s32[1]{0:T(128)} %bitcast.me_ref, bf16[256,128]{1,0:T(8,128)(2,1)S(1)} %get-tuple-element.21.coef_ref, bf16[32,392,128]{2,1,0:T(8,128)(2,1)S(1)} %all_to_all.20.got_ref), custom_call_target="tpu_custom_call" | custom-call | tf_op jit(solution)/shard_map/pair_sums/pallas_call | solution.py:362
  67.9 17.1 %all_to_all.21.refs_3_ = bf16[32,88,128]{2,1,0:T(8,128)(2,1)S(1)} all-to-all(bf16[32,88,128]{2,1,0:T(8,128)(2,1)S(1)} %get-tuple-element.32), channel_id=1, replica_groups=mesh['atom'=32,'aux'=8] {'atom'}, dimensions={0} | all-to-all | bytes 1441792 | tf_op jit(solution)/shard_map/all_to_all | solution.py:462
  85.0 0.1 slice_reduce_fusion
  85.1 16.8 %all_to_all.22.refs_2_ = bf16[8,64,128]{2,1,0:T(8,128)(2,1)S(1)} all-to-all(bf16[8,64,128]{2,1,0:T(8,128)(2,1)S(1)} %broadcast_in_dim.41), channel_id=1, replica_groups=mesh['atom'=32,'aux'=8] {'aux'}, dimensions={0} | all-to-all | bytes 262144 | tf_op jit(solution)/shard_map/all_to_all | solution.py:465
  101.9 0.9 make_slots.1
  102.8 13.4 %all_to_all.23.slot_ref = bf16[32,32,128]{2,1,0:T(8,128)(2,1)S(1)} all-to-all(bf16[32,32,128]{2,1,0:T(8,128)(2,1)S(1)} %make_slots.1), channel_id=1, replica_groups=mesh['atom'=32,'aux'=8] {'atom'}, dimensions={0} | all-to-all | bytes 524288 | tf_op jit(solution)/shard_map/all_to_all | solution.py:467
  116.2 1.9 %add_gains.1 = f32[96,256]{1,0:T(8,128)} custom-call(s32[8,128]{1,0:T(8,128)S(1)} %get-tuple-element.29.table_ref, bf16[32,32,128]{2,1,0:T(8,128)(2,1)S(1)} %all_to_all.23.slot_ref), custom_call_target="tpu_custom_call" | custom-call | tf_op jit(solution)/shard_map/add_gains/pallas_call | solution.py:403
  (4 shorter events, 0.1 us)
Async XLA Ops:
  1.1 8.1 %collective-permute-start.1 = (bf16[128,768]{1,0:T(8,128)(2,1)S(1)}, bf16[128,768]{1,0:T(8,128)(2,1)S(1)}, u32[]{:S(2)}, u32[]{:S(2)}) collective-permute-start(bf16[128,768]{1,0:T(8,128)(2,1)S(1)} %get-tuple-element.33), channel_id=1, source_target_pairs={{8,16},{16,8},{24,32},{32,24},{40,48},{48,40},{56,64},{64,56},{72,... | collective-permute-start | bytes 589832 | tf_op jit(solution)/shard_map/ppermute | solution.py:436
  5.7 3.5 %collective-permute-start = (bf16[128,768]{1,0:T(8,128)(2,1)S(1)}, bf16[128,768]{1,0:T(8,128)(2,1)S(1)}, u32[]{:S(2)}, u32[]{:S(2)}) collective-permute-start(bf16[128,768]{1,0:T(8,128)(2,1)S(1)} %get-tuple-element.34), channel_id=1, source_target_pairs={{0,8},{8,0},{16,24},{24,16},{32,40},{40,32},{48,56},{56,48},{64,72... | collective-permute-start | bytes 589832 | tf_op jit(solution)/shard_map/ppermute | solution.py:438

commit v14 on v13

--- a/solution.py
+++ b/solution.py
@@ -10,7 +10,7 @@
 MAXBF = 16
 ROWBLK = 32
 PACKED = ROWBLK + ROWBLK // 2
-BATCH = 16
+BATCH = 32
 MIB = 1 << 20
 
 
@@ -43,8 +43,8 @@
 
 def stage_kernel(
     part_ref, own_ref, ints_hbm, metric_hbm, size_hbm, dev_hbm, atom_hbm,
-    ints_ref, window_ref, order_ref, mix_ref, meta_ref, coef_ref,
-    metric_ref, size_ref, dev_ref, atom_ref, rows_ref, sem_ref,
+    half_ref, ints_ref, order_ref, mix_ref, meta_ref, coef_ref,
+    window_ref, metric_ref, size_ref, dev_ref, atom_ref, rows_ref, sem_ref,
 ):
     sources = (ints_hbm, metric_hbm, size_hbm, dev_hbm, atom_hbm)
     targets = (ints_ref, metric_ref, size_ref, dev_ref, atom_ref)
@@ -76,25 +76,34 @@
         rows_ref[row : row + 1, 0 : value_ref.shape[1]] = value_ref[...].astype(jnp.float32)
     meta_ref[...] = rows_ref[...].astype(jnp.bfloat16)
     fetches[0].wait()
+    aux_dev, bas_dev, span = ints_ref.shape
+    halo = (span - bas_dev) // 2
+    step = bas_dev // 2
+    for u in range(2):
+        rows = slice(u * step, (u + 1) * step)
+        ints = ints_ref[:, rows, halo : halo + bas_dev].reshape(aux_dev * step, bas_dev)
+        half_ref[:, rows] = dot(ints, window_ref[...]).reshape(aux_dev, step, -1)
 
 
 def fit_kernel(
-    odd_ref, near_ref, far_ref, own_ref, ints_ref, order_ref, mix_ref, meta_ref, out_ref,
+    odd_ref, near_ref, far_ref, half_ref, ints_ref, order_ref, mix_ref, meta_ref, out_ref,
     window_ref,
 ):
     aux_dev, bas_dev, span = ints_ref.shape
     blocks = bas_dev // ROWBLK
     halo = near_ref.shape[0]
-    far_at = odd_ref[0] * (halo + bas_dev)
-    ordered(near_ref, order_ref, window_ref, halo + bas_dev - far_at)
-    window_ref[halo : halo + bas_dev] = own_ref[...]
+    far_at = odd_ref[0] * halo
+    ordered(near_ref, order_ref, window_ref, halo - far_at)
     ordered(far_ref, order_ref, window_ref, far_at)
     mix = mix_ref[...]
     left = iota((ROWBLK // 2, 128), 1) < 64
     for u in range(blocks):
         if u % 4 == 0:
-            ints = ints_ref[:, u * ROWBLK : (u + 4) * ROWBLK].reshape(-1, span)
-            wide = dot(ints, window_ref[...]).astype(jnp.bfloat16)
+            rows = slice(u * ROWBLK, (u + 4) * ROWBLK)
+            low, high = ints_ref[:, rows, 0:halo], ints_ref[:, rows, span - halo : span]
+            ints = jnp.concatenate([low, high], axis=2).reshape(-1, 2 * halo)
+            wide = dot(ints, window_ref[...]) + half_ref[:, rows].reshape(ints.shape[0], -1)
+            wide = wide.astype(jnp.bfloat16)
             wide = wide.reshape(aux_dev, 4 * ROWBLK, -1)
         at = (u % 4) * ROWBLK
         half = wide[:, at : at + ROWBLK].reshape(aux_dev * ROWBLK, -1)
@@ -174,7 +183,7 @@
                 imag_ref[pl.ds(base + h * 16, 16)] = imag
         return carry
 
-    lax.fori_loop(0, groups, unpack, 0, unroll=8)
+    lax.fori_loop(0, groups, unpack, 0, unroll=16)
     tail = groups * blocks * ROWBLK
     real_ref[tail : tail + MAXBF] = jnp.zeros((MAXBF, 128), jnp.float32)
     imag_ref[tail : tail + MAXBF] = jnp.zeros((MAXBF, 128), jnp.float32)
@@ -318,23 +327,25 @@
 
 
 def stage(part, own, *fetched):
-    shapes = [fetched[0].shape, own.shape, (2, 256, 256), (256, 256), (8, 128)]
-    shapes.append((own.shape[0], 128))
+    shapes = [fetched[0].shape, (2, 256, 256), (256, 256), (8, 128), (own.shape[0], 128)]
+    half = fetched[0].shape[:2] + own.shape[1:]
     return pl.pallas_call(
         stage_kernel,
         in_specs=[smem_spec(), vmem_spec()]
         + [pl.BlockSpec(memory_space=pltpu.HBM)] * len(fetched),
-        out_specs=[vmem_spec()] * len(shapes),
-        out_shape=[pltpu.VMEM(shape, jnp.bfloat16) for shape in shapes],
-        scratch_shapes=[pltpu.VMEM(x.shape, x.dtype) for x in fetched[1:]]
+        out_specs=[vmem_spec()] * (len(shapes) + 1),
+        out_shape=[pltpu.VMEM(half, jnp.float32)]
+        + [pltpu.VMEM(shape, jnp.bfloat16) for shape in shapes],
+        scratch_shapes=[pltpu.VMEM(own.shape, jnp.bfloat16)]
+        + [pltpu.VMEM(x.shape, x.dtype) for x in fetched[1:]]
         + [pltpu.VMEM((8, 128), jnp.float32), pltpu.SemaphoreType.DMA((len(fetched),))],
-        compiler_params=limit(16),
+        compiler_params=limit(24),
         cost_estimate=pl.CostEstimate(flops=1 << 28, bytes_accessed=5 * MIB, transcendentals=0),
         name="stage",
     )(part, own, *[in_hbm(x) for x in fetched])
 
 
-def fit(odd, near, far, window_rows, ints, order, mix, meta):
+def fit(odd, near, far, half, ints, order, mix, meta):
     aux_dev, bas_dev, window = ints.shape
     width = near.shape[1]
     blocks = bas_dev // ROWBLK
@@ -344,7 +355,7 @@
         in_specs=[smem_spec()] + [vmem_spec()] * 7,
         out_specs=vmem_spec(),
         out_shape=jax.ShapeDtypeStruct(shape, jnp.bfloat16),
-        scratch_shapes=[pltpu.VMEM((window, width), jnp.bfloat16)],
+        scratch_shapes=[pltpu.VMEM((window - bas_dev, width), jnp.bfloat16)],
         compiler_params=limit(32),
         cost_estimate=pl.CostEstimate(
             flops=2 * aux_dev * bas_dev * width * (window + 256),
@@ -352,7 +363,7 @@
             transcendentals=0,
         ),
         name="fit",
-    )(odd, near, far, window_rows, ints, order, mix, meta)
+    )(odd, near, far, half, ints, order, mix, meta)
 
 
 def pair_sums(me, coef, got):
@@ -438,7 +449,7 @@
     near = lax.ppermute(near, "atom", [(i, i ^ 1) for i in range(groups)])
 
     part = jnp.full((1,), lax.axis_index("aux"), jnp.int32)
-    ints, window_rows, columns, mix, meta, coef_part = stage(
+    half, ints, columns, mix, meta, coef_part = stage(
         part, own, integrals, metric, atom_sizes, pair_device.T, pair_atom[None]
     )
     me = jnp.full((1,), lax.axis_index("atom"), jnp.int32)
@@ -456,7 +467,7 @@
         (near, far, me, coef_part, asked, places)
     )
     odd = jnp.full((1,), odd, jnp.int32)
-    packed = fit(odd, near, far, window_rows, ints, columns, mix, meta)
+    packed = fit(odd, near, far, half, ints, columns, mix, meta)
     got = lax.all_to_all(packed, "atom", split_axis=0, concat_axis=0, tiled=True)
     table, sent = pair_sums(me, coef_part, got)
     owned = lax.all_to_all(sent, "atom", split_axis=0, concat_axis=0, tiled=True)

time: 119 us -> 117 us (0.983)
  transfers between devices with their start and end apart: 2 -> 2, of which waited for: 0 -> 0; matrix products, arithmetic and copies ran while one was open for 1% -> 1% of each run, Pallas kernels for 1% -> 2%
where the time goes in v14:
time: 117 us
  blocking collectives  95.8 us (82%)
  Pallas kernels  13.3 us (11%)
  starting transfers between devices  4.69 us (4%)
  other arithmetic  1.76 us (2%)
    all_to_all x1, blocking collectives, per_device(): lax.all_to_all(packed, 'atom', split_axis=0, concat_axis=0, tiled=True)  48.5 us
    all_to_all x1, blocking collectives, per_device(): lax.all_to_all(sent, 'atom', split_axis=0, concat_axis=0, tiled=True)  17.1 us
    all_to_all x1, blocking collectives, per_device(): lax.all_to_all(shared, 'aux', split_axis=0, concat_axis=0, tiled=True)  16.8 us
    all_to_all x1, blocking collectives, per_device(): lax.all_to_all(slots, 'atom', split_axis=0, concat_axis=0, tiled=True)  13.4 us
    pallas_call x1, Pallas kernels, pair_sums(): pl.pallas_call(pair_kernel, in_specs=[smem_spec(), vmem_spec(), vmem_spec...  5.27 us
    ppermute x1, starting transfers between devices, per_device(): lax.ppermute(far, 'atom', [(i, i + 1 if i % 2 else i - 1) for i in inner])  4.59 us
    pallas_call x1, Pallas kernels, stage(): pl.pallas_call(stage_kernel, in_specs=[smem_spec(), vmem_spec()] + [pl.Bl...  2.68 us
    pallas_call x1, Pallas kernels, fit(): pl.pallas_call(fit_kernel, in_specs=[smem_spec()] + [vmem_spec()] * 7, ou...  2.52 us
  transfers between devices with their start and end apart: 2, of which 0 were waited for; matrix products, arithmetic and copies ran while one was open for 1% of the time, Pallas kernels for 2%

profile of v14, /device:TPU:1, one launch (start us, length us, event | category | flops | bytes accessed | tf_op | source)
XLA Modules:
  0.0 116.8 jit_solution(8152074735626313735)
XLA Ops:
  0.0 1.0 copy.7
  1.1 4.6 %collective-permute-start.1 = (bf16[128,768]{1,0:T(8,128)(2,1)S(1)}, bf16[128,768]{1,0:T(8,128)(2,1)S(1)}, u32[]{:S(2)}, u32[]{:S(2)}) collective-permute-start(bf16[128,768]{1,0:T(8,128)(2,1)S(1)} %get-tuple-element.33), channel_id=1, source_target_pairs={{8,16},{16,8},{24,32},{32,24},{40,48},{48,40},{56,64},{64,56},{72,... | collective-permute-start | bytes 589832 | tf_op jit(solution)/shard_map/ppermute | solution.py:447
  5.7 0.1 collective-permute-start
  5.8 0.9 convert_reduce_fusion
  6.7 0.7 multiply_add_fusion.refs_0_
  7.4 0.1 select_reduce_fusion
  7.5 2.7 %stage.1 = (f32[8,256,768]{2,1,0:T(8,128)S(1)}, bf16[8,256,512]{2,1,0:T(8,128)(2,1)S(1)}, bf16[2,256,256]{2,1,0:T(8,128)(2,1)S(1)}, bf16[256,256]{1,0:T(8,128)(2...) custom-call(s32[1]{0:T(128)} %bitcast.1.part_ref, bf16[256,768]{1,0:T(8,128)(2,1)S(1)} %bitcast.13, ...), custom_call_target="tpu_custom_call" | custom-call | flops 268435456 | bytes 5242880 | tf_op jit(solution)/shard_map/stage/pallas_call | solution.py:332
  10.2 0.0 collective-permute-done.1.far_ref
  10.2 0.0 collective-permute-done.near_ref
  10.2 2.5 %fit.1 = bf16[32,392,128]{2,1,0:T(8,128)(2,1)S(1)} custom-call(s32[1]{0:T(128)} %bitcast.5.odd_ref, bf16[128,768]{1,0:T(8,128)(2,1)S(1)} %collective-permute-done.near_ref, bf16[128,768]{1,0:T(8,128)(2,1)S(1)} %collective-permute-done.1.far_ref, f32[8,256,768]{2,1,0:T(8,128)S(1)} %get-tuple-element.24.half_ref, ...), custom_call_target="tpu_custom_call" | custom-call | flops 2415919104 | bytes 6291456 | tf_op jit(solution)/shard_map/fit/pallas_call | solution.py:353
  12.7 48.5 %all_to_all.20.got_ref = bf16[32,392,128]{2,1,0:T(8,128)(2,1)S(1)} all-to-all(bf16[32,392,128]{2,1,0:T(8,128)(2,1)S(1)} %fit.1), channel_id=1, replica_groups=mesh['atom'=32,'aux'=8] {'atom'}, dimensions={0} | all-to-all | bytes 6422528 | tf_op jit(solution)/shard_map/all_to_all | solution.py:471
  61.3 5.3 %pair_sums.1 = (s32[8,128]{1,0:T(8,128)S(1)}, bf16[32,88,128]{2,1,0:T(8,128)(2,1)S(1)}) custom-call(s32[1]{0:T(128)} %bitcast.me_ref, bf16[256,128]{1,0:T(8,128)(2,1)S(1)} %get-tuple-element.21.coef_ref, bf16[32,392,128]{2,1,0:T(8,128)(2,1)S(1)} %all_to_all.20.got_ref), custom_call_target="tpu_custom_call" | custom-call | tf_op jit(solution)/shard_map/pair_sums/pallas_call | solution.py:373
  66.5 17.1 %all_to_all.21.refs_3_ = bf16[32,88,128]{2,1,0:T(8,128)(2,1)S(1)} all-to-all(bf16[32,88,128]{2,1,0:T(8,128)(2,1)S(1)} %get-tuple-element.32), channel_id=1, replica_groups=mesh['atom'=32,'aux'=8] {'atom'}, dimensions={0} | all-to-all | bytes 1441792 | tf_op jit(solution)/shard_map/all_to_all | solution.py:473
  83.6 0.1 slice_reduce_fusion
  83.7 16.8 %all_to_all.22.refs_2_ = bf16[8,64,128]{2,1,0:T(8,128)(2,1)S(1)} all-to-all(bf16[8,64,128]{2,1,0:T(8,128)(2,1)S(1)} %broadcast_in_dim.41), channel_id=1, replica_groups=mesh['atom'=32,'aux'=8] {'aux'}, dimensions={0} | all-to-all | bytes 262144 | tf_op jit(solution)/shard_map/all_to_all | solution.py:476
  100.5 0.9 make_slots.1
  101.5 13.4 %all_to_all.23.slot_ref = bf16[32,32,128]{2,1,0:T(8,128)(2,1)S(1)} all-to-all(bf16[32,32,128]{2,1,0:T(8,128)(2,1)S(1)} %make_slots.1), channel_id=1, replica_groups=mesh['atom'=32,'aux'=8] {'atom'}, dimensions={0} | all-to-all | bytes 524288 | tf_op jit(solution)/shard_map/all_to_all | solution.py:478
  114.9 1.9 %add_gains.1 = f32[96,256]{1,0:T(8,128)} custom-call(s32[8,128]{1,0:T(8,128)S(1)} %get-tuple-element.29.table_ref, bf16[32,32,128]{2,1,0:T(8,128)(2,1)S(1)} %all_to_all.23.slot_ref), custom_call_target="tpu_custom_call" | custom-call | tf_op jit(solution)/shard_map/add_gains/pallas_call | solution.py:414
  (4 shorter events, 0.1 us)
Async XLA Ops:
  1.1 9.1 %collective-permute-start.1 = (bf16[128,768]{1,0:T(8,128)(2,1)S(1)}, bf16[128,768]{1,0:T(8,128)(2,1)S(1)}, u32[]{:S(2)}, u32[]{:S(2)}) collective-permute-start(bf16[128,768]{1,0:T(8,128)(2,1)S(1)} %get-tuple-element.33), channel_id=1, source_target_pairs={{8,16},{16,8},{24,32},{32,24},{40,48},{48,40},{56,64},{64,56},{72,... | collective-permute-start | bytes 589832 | tf_op jit(solution)/shard_map/ppermute | solution.py:447
  5.7 4.5 %collective-permute-start = (bf16[128,768]{1,0:T(8,128)(2,1)S(1)}, bf16[128,768]{1,0:T(8,128)(2,1)S(1)}, u32[]{:S(2)}, u32[]{:S(2)}) collective-permute-start(bf16[128,768]{1,0:T(8,128)(2,1)S(1)} %get-tuple-element.34), channel_id=1, source_target_pairs={{0,8},{8,0},{16,24},{24,16},{32,40},{40,32},{48,56},{56,48},{64,72... | collective-permute-start | bytes 589832 | tf_op jit(solution)/shard_map/ppermute | solution.py:449

commit v15 on v14

--- a/solution.py
+++ b/solution.py
@@ -37,7 +37,7 @@
         real = part_ref[:, t * 128 : (t + 1) * 128]
         imag = part_ref[:, half + t * 128 : half + (t + 1) * 128]
         value = dot(jnp.concatenate([real, imag], axis=1), order_ref[t // 2])
-        place = pl.ds(at if isinstance(at, int) else pl.multiple_of(at, 128), rows)
+        place = pl.ds(at if isinstance(at, int) else pl.multiple_of(at, 64), rows)
         window_ref[place, t * 256 : (t + 1) * 256] = value.astype(jnp.bfloat16)
 
 
@@ -86,7 +86,7 @@
 
 
 def fit_kernel(
-    odd_ref, near_ref, far_ref, half_ref, ints_ref, order_ref, mix_ref, meta_ref, out_ref,
+    odd_ref, near_ref, far_ref, rest_ref, half_ref, ints_ref, order_ref, mix_ref, meta_ref, out_ref,
     window_ref,
 ):
     aux_dev, bas_dev, span = ints_ref.shape
@@ -95,6 +95,7 @@
     far_at = odd_ref[0] * halo
     ordered(near_ref, order_ref, window_ref, halo - far_at)
     ordered(far_ref, order_ref, window_ref, far_at)
+    ordered(rest_ref, order_ref, window_ref, far_at + halo // 2)
     mix = mix_ref[...]
     left = iota((ROWBLK // 2, 128), 1) < 64
     for u in range(blocks):
@@ -345,14 +346,14 @@
     )(part, own, *[in_hbm(x) for x in fetched])
 
 
-def fit(odd, near, far, half, ints, order, mix, meta):
+def fit(odd, near, far, rest, half, ints, order, mix, meta):
     aux_dev, bas_dev, window = ints.shape
     width = near.shape[1]
     blocks = bas_dev // ROWBLK
     shape = (4 * aux_dev, blocks * PACKED + 8, 128)
     return pl.pallas_call(
         fit_kernel,
-        in_specs=[smem_spec()] + [vmem_spec()] * 7,
+        in_specs=[smem_spec()] + [vmem_spec()] * 8,
         out_specs=vmem_spec(),
         out_shape=jax.ShapeDtypeStruct(shape, jnp.bfloat16),
         scratch_shapes=[pltpu.VMEM((window - bas_dev, width), jnp.bfloat16)],
@@ -363,7 +364,7 @@
             transcendentals=0,
         ),
         name="fit",
-    )(odd, near, far, half, ints, order, mix, meta)
+    )(odd, near, far, rest, half, ints, order, mix, meta)
 
 
 def pair_sums(me, coef, got):
@@ -444,7 +445,9 @@
     odd = lax.axis_index("atom") % 2
     inner = range(1, groups - 1)
     far = lax.dynamic_slice_in_dim(own, odd * halo, halo, 0)
-    far = lax.ppermute(far, "atom", [(i, i + 1 if i % 2 else i - 1) for i in inner])
+    across = [(i, i + 1 if i % 2 else i - 1) for i in inner]
+    rest = lax.ppermute(far[halo // 2 :], "atom", across)
+    far = lax.ppermute(far[: halo // 2], "atom", across)
     near = lax.dynamic_slice_in_dim(own, (1 - odd) * halo, halo, 0)
     near = lax.ppermute(near, "atom", [(i, i ^ 1) for i in range(groups)])
 
@@ -463,11 +466,11 @@
     asked_hit = asked[None, :] == jnp.arange(2 * groups, dtype=jnp.int32)[:, None]
     places = 512 + pick(asked_hit, place[None, :] - 512)
 
-    near, far, me, coef_part, asked, places = lax.optimization_barrier(
-        (near, far, me, coef_part, asked, places)
+    near, far, rest, me, coef_part, asked, places = lax.optimization_barrier(
+        (near, far, rest, me, coef_part, asked, places)
     )
     odd = jnp.full((1,), odd, jnp.int32)
-    packed = fit(odd, near, far, half, ints, columns, mix, meta)
+    packed = fit(odd, near, far, rest, half, ints, columns, mix, meta)
     got = lax.all_to_all(packed, "atom", split_axis=0, concat_axis=0, tiled=True)
     table, sent = pair_sums(me, coef_part, got)
     owned = lax.all_to_all(sent, "atom", split_axis=0, concat_axis=0, tiled=True)

time: 117 us -> 121 us (1.034)
  starting transfers between devices: 4.69 us -> 6.61 us
  blocking collectives: 95.8 us -> 97.4 us
    ppermute x1 -> x2, starting transfers between devices: 4.59 us -> 6.52 us  [the longest x1 4.59 us: per_device(): rest = lax.ppermute(far[halo // 2:], 'atom', across)]
    all_to_all x1, blocking collectives: 48.5 us -> 50.1 us  [per_device(): lax.all_to_all(packed, 'atom', split_axis=0, concat_axis=0, tiled=True)]
  transfers between devices with their start and end apart: 2 -> 3, of which waited for: 0 -> 0; matrix products, arithmetic and copies ran while one was open for 1% -> 1% of each run, Pallas kernels for 2% -> 2%
where the time goes in v15:
time: 121 us; the launch traced here: 120 us
  blocking collectives  97.4 us (80%)
  Pallas kernels  13.4 us (11%)
  starting transfers between devices  6.61 us (5%)
  other arithmetic  1.76 us (1%)
    all_to_all x1, blocking collectives, per_device(): lax.all_to_all(packed, 'atom', split_axis=0, concat_axis=0, tiled=True)  50.1 us
    all_to_all x1, blocking collectives, per_device(): lax.all_to_all(sent, 'atom', split_axis=0, concat_axis=0, tiled=True)  17.1 us
    all_to_all x1, blocking collectives, per_device(): lax.all_to_all(shared, 'aux', split_axis=0, concat_axis=0, tiled=True)  16.8 us
    all_to_all x1, blocking collectives, per_device(): lax.all_to_all(slots, 'atom', split_axis=0, concat_axis=0, tiled=True)  13.4 us
    pallas_call x1, Pallas kernels, pair_sums(): pl.pallas_call(pair_kernel, in_specs=[smem_spec(), vmem_spec(), vmem_spec...  5.23 us
    ppermute x1, starting transfers between devices, per_device(): rest = lax.ppermute(far[halo // 2:], 'atom', across)  4.59 us
    pallas_call x1, Pallas kernels, stage(): pl.pallas_call(stage_kernel, in_specs=[smem_spec(), vmem_spec()] + [pl.Bl...  2.69 us
    pallas_call x1, Pallas kernels, fit(): pl.pallas_call(fit_kernel, in_specs=[smem_spec()] + [vmem_spec()] * 8, ou...  2.57 us
  transfers between devices with their start and end apart: 3, of which 0 were waited for; matrix products, arithmetic and copies ran while one was open for 1% of the time, Pallas kernels for 2%

profile of v15, /device:TPU:1, one launch (start us, length us, event | category | flops | bytes accessed | tf_op | source)
XLA Modules:
  0.0 120.4 jit_solution(14265795424121157968)
XLA Ops:
  0.0 1.0 copy.7
  1.1 4.6 %collective-permute-start.2 = (bf16[64,768]{1,0:T(8,128)(2,1)S(1)}, bf16[64,768]{1,0:T(8,128)(2,1)S(1)}, u32[]{:S(2)}, u32[]{:S(2)}) collective-permute-start(bf16[64,768]{1,0:T(8,128)(2,1)S(1)} %get-tuple-element.35), channel_id=1, source_target_pairs={{8,16},{16,8},{24,32},{32,24},{40,48},{48,40},{56,64},{64,56},{72,... | collective-permute-start | bytes 294920 | tf_op jit(solution)/shard_map/ppermute | solution.py:449
  5.7 1.9 %collective-permute-start.1 = (bf16[64,768]{1,0:T(8,128)(2,1)S(1)}, bf16[64,768]{1,0:T(8,128)(2,1)S(1)}, u32[]{:S(2)}, u32[]{:S(2)}) collective-permute-start(bf16[64,768]{1,0:T(8,128)(2,1)S(1)} %get-tuple-element.36), channel_id=1, source_target_pairs={{8,16},{16,8},{24,32},{32,24},{40,48},{48,40},{56,64},{64,56},{72,... | collective-permute-start | bytes 294920 | tf_op jit(solution)/shard_map/ppermute | solution.py:450
  7.7 0.1 collective-permute-start
  7.8 0.9 convert_reduce_fusion
  8.7 0.7 multiply_add_fusion.refs_0_
  9.3 0.1 select_reduce_fusion
  9.4 2.7 %stage.1 = (f32[8,256,768]{2,1,0:T(8,128)S(1)}, bf16[8,256,512]{2,1,0:T(8,128)(2,1)S(1)}, bf16[2,256,256]{2,1,0:T(8,128)(2,1)S(1)}, bf16[256,256]{1,0:T(8,128)(2...) custom-call(s32[1]{0:T(128)} %bitcast.1.part_ref, bf16[256,768]{1,0:T(8,128)(2,1)S(1)} %bitcast.14, ...), custom_call_target="tpu_custom_call" | custom-call | flops 268435456 | bytes 5242880 | tf_op jit(solution)/shard_map/stage/pallas_call | solution.py:333
  12.1 0.0 collective-permute-done.2.rest_ref
  12.1 0.0 collective-permute-done.1.far_ref
  12.2 0.0 collective-permute-done.near_ref
  12.2 2.6 %fit.1 = bf16[32,392,128]{2,1,0:T(8,128)(2,1)S(1)} custom-call(s32[1]{0:T(128)} %bitcast.5.odd_ref, bf16[128,768]{1,0:T(8,128)(2,1)S(1)} %collective-permute-done.near_ref, bf16[64,768]{1,0:T(8,128)(2,1)S(1)} %collective-permute-done.1.far_ref, bf16[64,768]{1,0:T(8,128)(2,1)S(1)} %collective-permute-done.2.rest_ref, ...), custom_call_target="tpu_custom_call" | custom-call | flops 2415919104 | bytes 6291456 | tf_op jit(solution)/shard_map/fit/pallas_call | solution.py:354
  14.7 50.1 %all_to_all.20.got_ref = bf16[32,392,128]{2,1,0:T(8,128)(2,1)S(1)} all-to-all(bf16[32,392,128]{2,1,0:T(8,128)(2,1)S(1)} %fit.1), channel_id=1, replica_groups=mesh['atom'=32,'aux'=8] {'atom'}, dimensions={0} | all-to-all | bytes 6422528 | tf_op jit(solution)/shard_map/all_to_all | solution.py:474
  64.8 5.2 %pair_sums.1 = (s32[8,128]{1,0:T(8,128)S(1)}, bf16[32,88,128]{2,1,0:T(8,128)(2,1)S(1)}) custom-call(s32[1]{0:T(128)} %bitcast.me_ref, bf16[256,128]{1,0:T(8,128)(2,1)S(1)} %get-tuple-element.22.coef_ref, bf16[32,392,128]{2,1,0:T(8,128)(2,1)S(1)} %all_to_all.20.got_ref), custom_call_target="tpu_custom_call" | custom-call | tf_op jit(solution)/shard_map/pair_sums/pallas_call | solution.py:374
  70.0 17.1 %all_to_all.21.refs_3_ = bf16[32,88,128]{2,1,0:T(8,128)(2,1)S(1)} all-to-all(bf16[32,88,128]{2,1,0:T(8,128)(2,1)S(1)} %get-tuple-element.34), channel_id=1, replica_groups=mesh['atom'=32,'aux'=8] {'atom'}, dimensions={0} | all-to-all | bytes 1441792 | tf_op jit(solution)/shard_map/all_to_all | solution.py:476
  87.1 0.1 slice_reduce_fusion
  87.2 16.8 %all_to_all.22.refs_2_ = bf16[8,64,128]{2,1,0:T(8,128)(2,1)S(1)} all-to-all(bf16[8,64,128]{2,1,0:T(8,128)(2,1)S(1)} %broadcast_in_dim.41), channel_id=1, replica_groups=mesh['atom'=32,'aux'=8] {'aux'}, dimensions={0} | all-to-all | bytes 262144 | tf_op jit(solution)/shard_map/all_to_all | solution.py:479
  104.1 0.9 make_slots.1
  105.0 13.4 %all_to_all.23.slot_ref = bf16[32,32,128]{2,1,0:T(8,128)(2,1)S(1)} all-to-all(bf16[32,32,128]{2,1,0:T(8,128)(2,1)S(1)} %make_slots.1), channel_id=1, replica_groups=mesh['atom'=32,'aux'=8] {'atom'}, dimensions={0} | all-to-all | bytes 524288 | tf_op jit(solution)/shard_map/all_to_all | solution.py:481
  118.4 2.0 %add_gains.1 = f32[96,256]{1,0:T(8,128)} custom-call(s32[8,128]{1,0:T(8,128)S(1)} %get-tuple-element.31.table_ref, bf16[32,32,128]{2,1,0:T(8,128)(2,1)S(1)} %all_to_all.23.slot_ref), custom_call_target="tpu_custom_call" | custom-call | tf_op jit(solution)/shard_map/add_gains/pallas_call | solution.py:415
  (5 shorter events, 0.1 us)
Async XLA Ops:
  1.1 11.1 %collective-permute-start.2 = (bf16[64,768]{1,0:T(8,128)(2,1)S(1)}, bf16[64,768]{1,0:T(8,128)(2,1)S(1)}, u32[]{:S(2)}, u32[]{:S(2)}) collective-permute-start(bf16[64,768]{1,0:T(8,128)(2,1)S(1)} %get-tuple-element.35), channel_id=1, source_target_pairs={{8,16},{16,8},{24,32},{32,24},{40,48},{48,40},{56,64},{64,56},{72,... | collective-permute-start | bytes 294920 | tf_op jit(solution)/shard_map/ppermute | solution.py:449
  5.7 6.5 %collective-permute-start.1 = (bf16[64,768]{1,0:T(8,128)(2,1)S(1)}, bf16[64,768]{1,0:T(8,128)(2,1)S(1)}, u32[]{:S(2)}, u32[]{:S(2)}) collective-permute-start(bf16[64,768]{1,0:T(8,128)(2,1)S(1)} %get-tuple-element.36), channel_id=1, source_target_pairs={{8,16},{16,8},{24,32},{32,24},{40,48},{48,40},{56,64},{64,56},{72,... | collective-permute-start | bytes 294920 | tf_op jit(solution)/shard_map/ppermute | solution.py:450
  7.7 4.5 %collective-permute-start = (bf16[128,768]{1,0:T(8,128)(2,1)S(1)}, bf16[128,768]{1,0:T(8,128)(2,1)S(1)}, u32[]{:S(2)}, u32[]{:S(2)}) collective-permute-start(bf16[128,768]{1,0:T(8,128)(2,1)S(1)} %constant_dynamic-slice_fusion.2), channel_id=1, source_target_pairs={{0,8},{8,0},{16,24},{24,16},{32,40},{40,32},{48,56},{56,48},{64,72... | collective-permute-start | bytes 589832 | tf_op jit(solution)/shard_map/ppermute | solution.py:452

commit v16 on v14

--- a/solution.py
+++ b/solution.py
@@ -457,8 +457,8 @@
     targets = pair_device[:, 0]
     order = jnp.arange(ref_count, dtype=jnp.int32)
     earlier = (targets[:, None] == targets[None, :]) & (order[None, :] < order[:, None])
-    ranks = jnp.sum(earlier.astype(jnp.int32), axis=1)
-    asked = targets * 2 + ranks
+    own_block = jnp.where(order[None, :] == order[:, None], 2 * targets[None, :], 0)
+    asked = jnp.sum(earlier.astype(jnp.int32) + own_block, axis=1)
     place = (order % 2) * 256 + (order // 2) * MAXBF
     asked_hit = asked[None, :] == jnp.arange(2 * groups, dtype=jnp.int32)[:, None]
     places = 512 + pick(asked_hit, place[None, :] - 512)

time: 117 us -> 117 us (level)
  no operation moved by 1% of the time
where the time goes in v16:
time: 117 us
  blocking collectives  95.9 us (82%)
  Pallas kernels  13.3 us (11%)
  starting transfers between devices  4.69 us (4%)
  other arithmetic  1.76 us (2%)
    all_to_all x1, blocking collectives, per_device(): lax.all_to_all(packed, 'atom', split_axis=0, concat_axis=0, tiled=True)  48.5 us
    all_to_all x1, blocking collectives, per_device(): lax.all_to_all(sent, 'atom', split_axis=0, concat_axis=0, tiled=True)  17.1 us
    all_to_all x1, blocking collectives, per_device(): lax.all_to_all(shared, 'aux', split_axis=0, concat_axis=0, tiled=True)  16.8 us
    all_to_all x1, blocking collectives, per_device(): lax.all_to_all(slots, 'atom', split_axis=0, concat_axis=0, tiled=True)  13.4 us
    pallas_call x1, Pallas kernels, pair_sums(): pl.pallas_call(pair_kernel, in_specs=[smem_spec(), vmem_spec(), vmem_spec...  5.24 us
    ppermute x1, starting transfers between devices, per_device(): lax.ppermute(far, 'atom', [(i, i + 1 if i % 2 else i - 1) for i in inner])  4.59 us
    pallas_call x1, Pallas kernels, stage(): pl.pallas_call(stage_kernel, in_specs=[smem_spec(), vmem_spec()] + [pl.Bl...  2.69 us
    pallas_call x1, Pallas kernels, fit(): pl.pallas_call(fit_kernel, in_specs=[smem_spec()] + [vmem_spec()] * 7, ou...  2.52 us
  transfers between devices with their start and end apart: 2, of which 0 were waited for; matrix products, arithmetic and copies ran while one was open for 1% of the time, Pallas kernels for 2%

profile of v16, /device:TPU:1, one launch (start us, length us, event | category | flops | bytes accessed | tf_op | source)
XLA Modules:
  0.0 116.8 jit_solution(4169967234745656652)
XLA Ops:
  0.0 1.0 copy.7
  1.1 4.6 %collective-permute-start.1 = (bf16[128,768]{1,0:T(8,128)(2,1)S(1)}, bf16[128,768]{1,0:T(8,128)(2,1)S(1)}, u32[]{:S(2)}, u32[]{:S(2)}) collective-permute-start(bf16[128,768]{1,0:T(8,128)(2,1)S(1)} %get-tuple-element.33), channel_id=1, source_target_pairs={{8,16},{16,8},{24,32},{32,24},{40,48},{48,40},{56,64},{64,56},{72,... | collective-permute-start | bytes 589832 | tf_op jit(solution)/shard_map/ppermute | solution.py:447
  5.7 0.1 collective-permute-start
  5.8 0.7 broadcast_multiply_fusion
  6.5 0.9 add_reduce_fusion.refs_0_
  7.4 0.1 select_reduce_fusion
  7.5 2.7 %stage.1 = (f32[8,256,768]{2,1,0:T(8,128)S(1)}, bf16[8,256,512]{2,1,0:T(8,128)(2,1)S(1)}, bf16[2,256,256]{2,1,0:T(8,128)(2,1)S(1)}, bf16[256,256]{1,0:T(8,128)(2...) custom-call(s32[1]{0:T(128)} %bitcast.1.part_ref, bf16[256,768]{1,0:T(8,128)(2,1)S(1)} %bitcast.13, ...), custom_call_target="tpu_custom_call" | custom-call | flops 268435456 | bytes 5242880 | tf_op jit(solution)/shard_map/stage/pallas_call | solution.py:332
  10.2 0.0 collective-permute-done.1.far_ref
  10.2 0.0 collective-permute-done.near_ref
  10.2 2.5 %fit.1 = bf16[32,392,128]{2,1,0:T(8,128)(2,1)S(1)} custom-call(s32[1]{0:T(128)} %bitcast.5.odd_ref, bf16[128,768]{1,0:T(8,128)(2,1)S(1)} %collective-permute-done.near_ref, bf16[128,768]{1,0:T(8,128)(2,1)S(1)} %collective-permute-done.1.far_ref, f32[8,256,768]{2,1,0:T(8,128)S(1)} %get-tuple-element.24.half_ref, ...), custom_call_target="tpu_custom_call" | custom-call | flops 2415919104 | bytes 6291456 | tf_op jit(solution)/shard_map/fit/pallas_call | solution.py:353
  12.7 48.5 %all_to_all.20.got_ref = bf16[32,392,128]{2,1,0:T(8,128)(2,1)S(1)} all-to-all(bf16[32,392,128]{2,1,0:T(8,128)(2,1)S(1)} %fit.1), channel_id=1, replica_groups=mesh['atom'=32,'aux'=8] {'atom'}, dimensions={0} | all-to-all | bytes 6422528 | tf_op jit(solution)/shard_map/all_to_all | solution.py:471
  61.3 5.2 %pair_sums.1 = (s32[8,128]{1,0:T(8,128)S(1)}, bf16[32,88,128]{2,1,0:T(8,128)(2,1)S(1)}) custom-call(s32[1]{0:T(128)} %bitcast.me_ref, bf16[256,128]{1,0:T(8,128)(2,1)S(1)} %get-tuple-element.21.coef_ref, bf16[32,392,128]{2,1,0:T(8,128)(2,1)S(1)} %all_to_all.20.got_ref), custom_call_target="tpu_custom_call" | custom-call | tf_op jit(solution)/shard_map/pair_sums/pallas_call | solution.py:373
  66.5 17.1 %all_to_all.21.refs_3_ = bf16[32,88,128]{2,1,0:T(8,128)(2,1)S(1)} all-to-all(bf16[32,88,128]{2,1,0:T(8,128)(2,1)S(1)} %get-tuple-element.32), channel_id=1, replica_groups=mesh['atom'=32,'aux'=8] {'atom'}, dimensions={0} | all-to-all | bytes 1441792 | tf_op jit(solution)/shard_map/all_to_all | solution.py:473
  83.6 0.1 slice_reduce_fusion
  83.7 16.8 %all_to_all.22.refs_2_ = bf16[8,64,128]{2,1,0:T(8,128)(2,1)S(1)} all-to-all(bf16[8,64,128]{2,1,0:T(8,128)(2,1)S(1)} %broadcast_in_dim.57), channel_id=1, replica_groups=mesh['atom'=32,'aux'=8] {'aux'}, dimensions={0} | all-to-all | bytes 262144 | tf_op jit(solution)/shard_map/all_to_all | solution.py:476
  100.5 0.9 make_slots.1
  101.4 13.4 %all_to_all.23.slot_ref = bf16[32,32,128]{2,1,0:T(8,128)(2,1)S(1)} all-to-all(bf16[32,32,128]{2,1,0:T(8,128)(2,1)S(1)} %make_slots.1), channel_id=1, replica_groups=mesh['atom'=32,'aux'=8] {'atom'}, dimensions={0} | all-to-all | bytes 524288 | tf_op jit(solution)/shard_map/all_to_all | solution.py:478
  114.9 2.0 %add_gains.1 = f32[96,256]{1,0:T(8,128)} custom-call(s32[8,128]{1,0:T(8,128)S(1)} %get-tuple-element.29.table_ref, bf16[32,32,128]{2,1,0:T(8,128)(2,1)S(1)} %all_to_all.23.slot_ref), custom_call_target="tpu_custom_call" | custom-call | tf_op jit(solution)/shard_map/add_gains/pallas_call | solution.py:414
  (4 shorter events, 0.1 us)
Async XLA Ops:
  1.1 9.1 %collective-permute-start.1 = (bf16[128,768]{1,0:T(8,128)(2,1)S(1)}, bf16[128,768]{1,0:T(8,128)(2,1)S(1)}, u32[]{:S(2)}, u32[]{:S(2)}) collective-permute-start(bf16[128,768]{1,0:T(8,128)(2,1)S(1)} %get-tuple-element.33), channel_id=1, source_target_pairs={{8,16},{16,8},{24,32},{32,24},{40,48},{48,40},{56,64},{64,56},{72,... | collective-permute-start | bytes 589832 | tf_op jit(solution)/shard_map/ppermute | solution.py:447
  5.7 4.5 %collective-permute-start = (bf16[128,768]{1,0:T(8,128)(2,1)S(1)}, bf16[128,768]{1,0:T(8,128)(2,1)S(1)}, u32[]{:S(2)}, u32[]{:S(2)}) collective-permute-start(bf16[128,768]{1,0:T(8,128)(2,1)S(1)} %get-tuple-element.34), channel_id=1, source_target_pairs={{0,8},{8,0},{16,24},{24,16},{32,40},{40,32},{48,56},{56,48},{64,72... | collective-permute-start | bytes 589832 | tf_op jit(solution)/shard_map/ppermute | solution.py:449
